TPU v7x, 32 devices: a whole 2x2x4 slice. The times are simulated.
32 devices in a mesh: src: 8 (over z, x), row: 4 (over y, core).
Axes of the slice: x: 2, y: 2, z: 4, core: 2. Of those that a mesh axis runs over, the one named last changes fastest.
Arguments:
- factor: float32 [10240, 1024], P(('row', 'src')), as said below
- right_side: float32 [10240, 4096], P('row', 'src'), may hold values from -6 to 6
Outputs:
- advanced: float32 [10240, 4096], P('row', 'src')
Inputs may be any that keep to these rules, and one draw needn't show every extreme that they name: factor is zero where its column index exceeds its row index, and its entries where the two are equal lie between 1 and 2.
All inputs are finite; a program needn't handle non-finite values.
Results may differ from a plain program's by a relative error of at most 0.0001.
Values sent between devices are 32-bit elements; how exact they have to be, the bound alone decides.
No kernel may reach another device: no remote copies, remote signals or barrier semaphores. Data moves between devices by JAX's collectives and lax.ppermute only.
A program may use at most 64 MiB of HBM per device.

v0:
```python
import functools
import math

import jax
import jax.numpy as jnp
from jax import lax
from jax.experimental import pallas as pl
from jax.experimental.pallas import tpu as pltpu
from jax.sharding import PartitionSpec as P

VMEM_BYTES = 40 * 1024 * 1024
LANES = 128
RING_LIMIT = 16

ANY = pl.BlockSpec(memory_space=pl.ANY)
SCALARS = pl.BlockSpec(memory_space=pltpu.SMEM)
WHOLE = pl.BlockSpec(memory_space=pltpu.VMEM)


def dot32(a, b):
    return jnp.dot(a, b, preferred_element_type=jnp.float32, precision=lax.Precision.HIGHEST)


def split16(value):
    high = value.astype(jnp.bfloat16)
    return high, (value - high.astype(jnp.float32)).astype(jnp.bfloat16)


def dot_split(a, b):
    (a_high, a_low), (b_high, b_low) = a, b
    dot = functools.partial(jnp.dot, preferred_element_type=jnp.float32)
    return dot(a_high, b_high) + dot(a_high, b_low) + dot(a_low, b_high)


def grid_ids(size):
    return [lax.broadcasted_iota(jnp.int32, (size, size), axis) for axis in range(2)]


def below_blocks(half, row, col):
    return (row // half % 2 == 1) & (col // half == row // half - 1)


def invert_lower(blocks):
    size = blocks[0].shape[0]
    row, col = grid_ids(size)
    inverses = []
    for block in blocks:
        diag = jnp.where(row == col, block, 0.0)
        down = 1.0 / jnp.sum(diag, axis=1, keepdims=True)
        across = 1.0 / jnp.sum(diag, axis=0, keepdims=True)
        below = below_blocks(1, row, col)
        inverses.append(
            jnp.where(row == col, down, 0.0) - jnp.where(below, down * block * across, 0.0)
        )
    half = 2
    while half < size:
        below = below_blocks(half, row, col)
        inner = [
            dot32(jnp.where(below, block, 0.0), inverse) for block, inverse in zip(blocks, inverses)
        ]
        inverses = [inverse - dot32(inverse, part) for inverse, part in zip(inverses, inner)]
        half *= 2
    return inverses


def prepare_kernel(rows, block, depth, me, place, factor, out):
    width = depth // 2
    out[...] = factor[:, width:]
    first = me[0] * rows

    @pl.when((place[0] == 0) & (first < depth))
    def _():
        blocks = []
        for j in range(0, rows, block):
            at = jnp.minimum(first + j, depth - block)
            near = pl.multiple_of(at // LANES * LANES, LANES)
            value = factor[j : j + block, pl.ds(near, LANES)]
            value = pltpu.roll(value, (LANES - at % LANES) % LANES, 1)
            blocks.append(value[:, :block])
        row, col = grid_ids(block)
        blocks = [
            jnp.where(first + i * block < depth, value, jnp.where(row == col, 1.0, 0.0))
            for i, value in enumerate(blocks)
        ]
        for i, inverse in enumerate(invert_lower(blocks)):

            @pl.when(first + i * block < depth)
            def _(i=i, inverse=inverse):
                out[i * block : (i + 1) * block, width - block :] = inverse


def prepare(me, place, factor, block):
    rows, depth = factor.shape
    return pl.pallas_call(
        functools.partial(prepare_kernel, rows, block, depth),
        out_shape=jax.ShapeDtypeStruct((rows, depth // 2), jnp.float32),
        in_specs=[SCALARS] * 2 + [WHOLE],
        out_specs=WHOLE,
        compiler_params=pltpu.CompilerParams(vmem_limit_bytes=VMEM_BYTES // 2),
        cost_estimate=pl.CostEstimate(
            flops=24 * rows * block * block, bytes_accessed=6 * rows * depth, transcendentals=0
        ),
    )(me, place, factor)


def solve_kernel(pieces, rows, width, chunk, block, panel, ids, place, *refs):
    held, refs = refs[: 2 * pieces], refs[2 * pieces :]
    rhs, refs = refs[0], refs[1:]
    earlier, refs = refs[:panel], refs[panel:]
    solved, lower, piece_sem, rhs_sem = refs
    first, last = panel * width, (panel + 1) * width
    side = lower.shape[1] - LANES

    @pl.when(place[0] == 0)
    def _():
        def copies(i):
            at = pl.ds(pl.multiple_of(ids[i] * rows, 8), rows)
            cut = 0 if panel else width - LANES
            return [
                pltpu.make_async_copy(
                    held[i], lower.at[at, pl.ds(0, width)], piece_sem.at[0, i]
                ),
                pltpu.make_async_copy(
                    held[pieces + i].at[:, pl.ds(cut, width - cut)],
                    lower.at[at, pl.ds(width, width - cut)],
                    piece_sem.at[1, i],
                ),
            ]

        def needed(i):
            return (ids[i] * rows < last) & ((ids[i] + 1) * rows > first)

        for i in range(pieces):

            @pl.when(needed(i))
            def _(i=i):
                for copy in copies(i):
                    copy.start()

        load = pltpu.make_async_copy(rhs.at[pl.ds(first, width)], solved, rhs_sem)
        load.start()
        for i in range(pieces):

            @pl.when(needed(i))
            def _(i=i):
                for copy in copies(i):
                    copy.wait()

        load.wait()
        row, col = grid_ids(chunk)
        lane = lax.broadcasted_iota(jnp.int32, (chunk, LANES), 1)
        starts = range(0, width, chunk)
        inverses = []
        for j in starts:
            value = lower[first + j : first + j + chunk, side:]
            value = jnp.where(lane >= LANES - block, value, 0.0)
            shift = block
            while shift < LANES:
                value = value + pltpu.roll(value, LANES - shift, 1)
                shift *= 2
            value = jnp.concatenate([value] * (chunk // LANES), axis=1)
            inverses.append(jnp.where(row // block == col // block, value, 0.0))
        half = block
        while half < chunk:
            below = below_blocks(half, row, col)
            parts = [split16(inverse) for inverse in inverses]
            inner = [
                dot_split(
                    split16(
                        jnp.where(
                            below,
                            lower[first + j : first + j + chunk, first + j : first + j + chunk],
                            0.0,
                        )
                    ),
                    part,
                )
                for j, part in zip(starts, parts)
            ]
            inverses = [
                inverse - dot_split(part, split16(value))
                for inverse, part, value in zip(inverses, parts, inner)
            ]
            half *= 2
        for k in range(panel):
            solved[...] = solved[...] - dot_split(
                split16(lower[first:last, k * width : (k + 1) * width]), split16(earlier[k][...])
            )
        for j in starts:
            value = solved[j : j + chunk]
            if j:
                at = slice(first + j, first + j + chunk)
                value = value - dot_split(
                    split16(lower[at, first : first + j]), split16(solved[:j])
                )
            solved[j : j + chunk] = dot_split(split16(inverses[j // chunk]), split16(value))


def solve_panel(panel, ids, place, held, rhs, earlier, width, block):
    pieces = len(held[0])
    rows = held[0][0].shape[0]
    columns = rhs.shape[1]
    tall = -(-(panel + 1) * width // rows) * rows
    chunk = math.gcd(width, 2 * LANES)
    return pl.pallas_call(
        functools.partial(solve_kernel, pieces, rows, width, chunk, block, panel),
        out_shape=jax.ShapeDtypeStruct((width, columns), jnp.float32),
        in_specs=[SCALARS] * 2 + [ANY] * (2 * pieces + 1) + [WHOLE] * panel,
        out_specs=WHOLE,
        scratch_shapes=[
            pltpu.VMEM((tall, 2 * width if panel else width + LANES), jnp.float32),
            pltpu.SemaphoreType.DMA((2, pieces)),
            pltpu.SemaphoreType.DMA,
        ],
        compiler_params=pltpu.CompilerParams(vmem_limit_bytes=VMEM_BYTES // 2),
        cost_estimate=pl.CostEstimate(
            flops=6 * (panel + 1) * width * width * columns,
            bytes_accessed=12 * width * columns,
            transcendentals=0,
        ),
    )(ids, place, *held[0], *held[1], rhs, *earlier)


def update_kernel(pieces, rows, width, tile, step, places, panel, ids, place, *refs):
    held, refs = refs[:pieces], refs[pieces:]
    current, refs = refs[0], refs[1:]
    solved, refs = refs[:places], refs[places:]
    out, lower, block, found, high, low, product, piece_sem, block_sem, found_sem, out_sem = refs
    first, last = panel * width, (panel + 1) * width
    start = place[0] * current.shape[0]

    def fetch(r):
        return pltpu.make_async_copy(solved[r], found, found_sem)

    for r in range(places):

        @pl.when(place[0] == r)
        def _(r=r):
            fetch(r).start()

    def at(i):
        return pl.ds(pl.multiple_of(ids[i] * rows, 8), rows)

    def loads(i, source):
        return [
            pltpu.make_async_copy(held[source], lower.at[i], piece_sem.at[i]),
            pltpu.make_async_copy(current.at[at(i)], block.at[i], block_sem.at[i]),
        ]

    def store(i):
        return pltpu.make_async_copy(block.at[i], out.at[at(i)], out_sem.at[i])

    for i in range(pieces):
        for load in loads(i, i):
            load.start()
    fetch(0).wait()
    high[...], low[...] = split16(found[...])

    @pl.loop(0, pieces)
    def _(i):
        for load in loads(i, 0):
            load.wait()

        @pl.loop(0, rows // tile)
        def _(t):
            inside = pl.multiple_of(t * tile, 8)
            top = start + ids[i] * rows + inside
            product[...] = dot_split(
                split16(lower[i, pl.ds(inside, tile)]), (high[...], low[...])
            )

            @pl.when(top >= last)
            def _():
                block[i, pl.ds(inside, tile)] = block[i, pl.ds(inside, tile)] - product[...]

            @pl.when(top < last)
            def _():
                @pl.loop(0, tile // step)
                def _(u):
                    part = pl.multiple_of(u * step, 8)
                    row = top + part
                    here = pl.ds(inside + part, step)

                    @pl.when((row >= first) & (row < last))
                    def _():
                        block[i, here] = found[pl.ds(pl.multiple_of(row - first, 8), step)]

                    @pl.when(row >= last)
                    def _():
                        block[i, here] = block[i, here] - product[pl.ds(part, step)]

        store(i).start()

    @pl.loop(0, pieces)
    def _(i):
        store(i).wait()


def update(panel, ids, place, held, current, solved, width):
    pieces, places = len(held), len(solved)
    rows, columns = held[0].shape[0], current.shape[1]
    step = math.gcd(rows, width)
    tile = step * max(m for m in range(1, rows // step + 1) if rows // step % m == 0 and step * m <= 512)
    return pl.pallas_call(
        functools.partial(update_kernel, pieces, rows, width, tile, step, places, panel),
        out_shape=jax.ShapeDtypeStruct(current.shape, jnp.float32),
        in_specs=[SCALARS] * 2 + [ANY] * (pieces + 1 + places),
        out_specs=ANY,
        scratch_shapes=[
            pltpu.VMEM((pieces, rows, width), jnp.float32),
            pltpu.VMEM((pieces, rows, columns), jnp.float32),
            pltpu.VMEM((width, columns), jnp.float32),
            pltpu.VMEM((width, columns), jnp.bfloat16),
            pltpu.VMEM((width, columns), jnp.bfloat16),
            pltpu.VMEM((tile, columns), jnp.float32),
            pltpu.SemaphoreType.DMA((pieces,)),
            pltpu.SemaphoreType.DMA((pieces,)),
            pltpu.SemaphoreType.DMA,
            pltpu.SemaphoreType.DMA((pieces,)),
        ],
        compiler_params=pltpu.CompilerParams(vmem_limit_bytes=VMEM_BYTES),
        cost_estimate=pl.CostEstimate(
            flops=6 * pieces * rows * width * columns,
            bytes_accessed=4 * pieces * rows * (width + 2 * columns),
            transcendentals=0,
        ),
    )(ids, place, *held, current, *solved)


def gather_pieces(panels, count):
    me = lax.axis_index("src")
    if count % 2 or count > RING_LIMIT:
        gathered = [lax.all_gather(panel, "src", axis=0, tiled=True) for panel in panels]
        return [[piece] for piece in gathered], [jnp.zeros_like(me)]
    ring = list(range(0, count, 2)) + list(range(count - 1, 0, -2))
    onward = [(ring[i], ring[(i + 1) % count]) for i in range(count)]
    back = [(b, a) for a, b in onward]
    position = jnp.where(me % 2 == 0, me // 2, count - 1 - me // 2)

    def shard_at(spot):
        spot = (spot + count) % count
        return jnp.where(spot < count // 2, 2 * spot, 2 * (count - 1 - spot) + 1)

    held = [[panel] for panel in panels]
    ids = [me]
    going = [[panel, panel] for panel in panels]
    for step in range(1, count // 2 + 1):
        last = step == count // 2
        for k in range(2):
            for way, pairs in enumerate((onward, back)):
                if last and way != k:
                    continue
                going[k][way] = lax.ppermute(going[k][way], "src", pairs)
                held[k].append(going[k][way])
        ids += [shard_at(position - step)] + ([] if last else [shard_at(position + step)])
    return held, ids


def spread_rows(block, count):
    found = {0: block}
    stride = count // 2
    while stride:
        for r in list(found):
            found[r + stride] = lax.ppermute(found[r], "row", [(r, r + stride)])
        stride //= 2
    return [found[r] for r in range(count)]


def solution(mesh):
    sources, places = mesh.shape["src"], mesh.shape["row"]

    def local(factor, right_side):
        rows, depth = factor.shape
        width = depth // 2
        block = math.gcd(math.gcd(rows, width), LANES)
        me = lax.axis_index("src").reshape(1).astype(jnp.int32)
        place = lax.axis_index("row").reshape(1).astype(jnp.int32)
        panels = [factor[:, :width], prepare(me, place, factor, block)]
        held, ids = gather_pieces(panels, sources)
        ids = jnp.stack(ids).astype(jnp.int32)
        first = solve_panel(0, ids, place, held, right_side, [], width, block)
        second = solve_panel(1, ids, place, held, right_side, [first], width, block)
        current = update(0, ids, place, held[0], right_side, spread_rows(first, places), width)
        return update(1, ids, place, held[1], current, spread_rows(second, places), width)

    placed = (P(("row", "src"), None), P("row", "src"))
    return jax.shard_map(
        local, mesh=mesh, in_specs=placed, out_specs=P("row", "src"), check_vma=False
    )
```

profile of v0, /device:TPU:0, one launch (start us, length us, event | category | flops | bytes accessed | tf_op | source)
XLA Modules:
  0.0 158.1 jit_solution(17126107325602995068)
XLA Ops:
  1.3 2.6 %shard_map.28.refs_8_.refs_0_ = f32[320,512]{1,0:T(8,128)S(1)} custom-call(s32[1]{0:T(128)} %bitcast.me, s32[1]{0:T(128)} %bitcast.8.place, f32[320,1024]{1,0:T(8,128)S(1)} %copy-done.10), custom_call_target="tpu_custom_call" | custom-call | flops 31457280 | bytes 1966080 | tf_op jit(solution)/shard_map/pallas_call | solution.py:94
  3.9 3.0 %collective-permute-start.1 = (f32[320,512]{1,0:T(8,128)S(1)}, f32[320,512]{1,0:T(8,128)S(1)}, u32[]{:S(2)}, u32[]{:S(2)}) collective-permute-start(f32[320,512]{1,0:T(8,128)S(1)} %shard_map.28.refs_8_.refs_0_), channel_id=1, source_target_pairs={{8,0},{16,8},{24,16},{28,24},{20,28},{12,20},{4,12},{0,4},{9,1},{1... | collective-permute-start | bytes 1966088 | tf_op jit(solution)/shard_map/ppermute | solution.py:353
  7.0 2.0 %collective-permute-start = (f32[320,512]{1,0:T(8,128)S(1)}, f32[320,512]{1,0:T(8,128)S(1)}, u32[]{:S(2)}, u32[]{:S(2)}) collective-permute-start(f32[320,512]{1,0:T(8,128)S(1)} %shard_map.28.refs_8_.refs_0_), channel_id=1, source_target_pairs={{0,8},{8,16},{16,24},{24,28},{28,20},{20,12},{12,4},{4,0},{1,9},{9... | collective-permute-start | bytes 1966088 | tf_op jit(solution)/shard_map/ppermute | solution.py:353
  9.1 13.5 %collective-permute-done.1.refs_10_.refs_2_ = f32[320,512]{1,0:T(8,128)S(1)} collective-permute-done((f32[320,512]{1,0:T(8,128)S(1)}, f32[320,512]{1,0:T(8,128)S(1)}, u32[]{:S(2)}, u32[]{:S(2)}) %collective-permute-start.1) | collective-permute-done | bytes 655392 | tf_op jit(solution)/shard_map/ppermute | solution.py:353
  22.6 1.9 %collective-permute-start.3 = (f32[320,512]{1,0:T(8,128)S(1)}, f32[320,512]{1,0:T(8,128)S(1)}, u32[]{:S(2)}, u32[]{:S(2)}) collective-permute-start(f32[320,512]{1,0:T(8,128)S(1)} %collective-permute-done.1.refs_10_.refs_2_), channel_id=1, source_target_pairs={{8,0},{16,8},{24,16},{28,24},{20,28},{12,20},{4,12},{0,4},{9,1},{1... | collective-permute-start | bytes 1966088 | tf_op jit(solution)/shard_map/ppermute | solution.py:353
  25.5 13.1 %collective-permute-done.refs_9_.refs_1_ = f32[320,512]{1,0:T(8,128)S(1)} collective-permute-done((f32[320,512]{1,0:T(8,128)S(1)}, f32[320,512]{1,0:T(8,128)S(1)}, u32[]{:S(2)}, u32[]{:S(2)}) %collective-permute-start) | collective-permute-done | bytes 655392 | tf_op jit(solution)/shard_map/ppermute | solution.py:353
  38.7 1.9 %collective-permute-start.10 = (f32[320,512]{1,0:T(8,128)S(1)}, f32[320,512]{1,0:T(8,128)}, u32[]{:S(2)}, u32[]{:S(2)}) collective-permute-start(f32[320,512]{1,0:T(8,128)S(1)} %collective-permute-done.8.refs_2_), channel_id=1, source_target_pairs={{8,0},{16,8},{24,16},{28,24},{20,28},{12,20},{4,12},{0,4},{9,1},{1... | collective-permute-start | bytes 1966088 | tf_op jit(solution)/shard_map/ppermute | solution.py:353
  41.5 9.1 %collective-permute-done.3.refs_12_.refs_4_ = f32[320,512]{1,0:T(8,128)S(1)} collective-permute-done((f32[320,512]{1,0:T(8,128)S(1)}, f32[320,512]{1,0:T(8,128)S(1)}, u32[]{:S(2)}, u32[]{:S(2)}) %collective-permute-start.3) | collective-permute-done | bytes 655392 | tf_op jit(solution)/shard_map/ppermute | solution.py:353
  50.7 1.9 %collective-permute-start.5 = (f32[320,512]{1,0:T(8,128)S(1)}, f32[320,512]{1,0:T(8,128)}, u32[]{:S(2)}, u32[]{:S(2)}) collective-permute-start(f32[320,512]{1,0:T(8,128)S(1)} %collective-permute-done.3.refs_12_.refs_4_), channel_id=1, source_target_pairs={{8,0},{16,8},{24,16},{28,24},{20,28},{12,20},{4,12},{0,4},{9,1},{1... | collective-permute-start | bytes 1966088 | tf_op jit(solution)/shard_map/ppermute | solution.py:353
  53.7 13.2 %collective-permute-done.2.refs_11_.refs_3_ = f32[320,512]{1,0:T(8,128)} collective-permute-done((f32[320,512]{1,0:T(8,128)S(1)}, f32[320,512]{1,0:T(8,128)}, u32[]{:S(2)}, u32[]{:S(2)}) %collective-permute-start.2) | collective-permute-done | bytes 655392 | tf_op jit(solution)/shard_map/ppermute | solution.py:353
  66.9 1.9 %collective-permute-start.12 = (f32[320,512]{1,0:T(8,128)}, f32[320,512]{1,0:T(8,128)}, u32[]{:S(2)}, u32[]{:S(2)}) collective-permute-start(f32[320,512]{1,0:T(8,128)} %collective-permute-done.10.refs_4_), channel_id=1, source_target_pairs={{8,0},{16,8},{24,16},{28,24},{20,28},{12,20},{4,12},{0,4},{9,1},{1... | collective-permute-start | bytes 1966088 | tf_op jit(solution)/shard_map/ppermute | solution.py:353
  68.9 10.0 %collective-permute-done.5.refs_14_.refs_6_ = f32[320,512]{1,0:T(8,128)} collective-permute-done((f32[320,512]{1,0:T(8,128)S(1)}, f32[320,512]{1,0:T(8,128)}, u32[]{:S(2)}, u32[]{:S(2)}) %collective-permute-start.5) | collective-permute-done | bytes 655392 | tf_op jit(solution)/shard_map/ppermute | solution.py:353
  78.8 1.9 %collective-permute-start.6 = (f32[320,512]{1,0:T(8,128)}, f32[320,512]{1,0:T(8,128)}, u32[]{:S(2)}, u32[]{:S(2)}) collective-permute-start(f32[320,512]{1,0:T(8,128)} %collective-permute-done.5.refs_14_.refs_6_), channel_id=1, source_target_pairs={{8,0},{16,8},{24,16},{28,24},{20,28},{12,20},{4,12},{0,4},{9,1},{1... | collective-permute-start | bytes 1966088 | tf_op jit(solution)/shard_map/ppermute | solution.py:353
  81.1 13.9 %collective-permute-done.4.refs_13_.refs_5_ = f32[320,512]{1,0:T(8,128)} collective-permute-done((f32[320,512]{1,0:T(8,128)}, f32[320,512]{1,0:T(8,128)}, u32[]{:S(2)}, u32[]{:S(2)}) %collective-permute-start.4) | collective-permute-done | bytes 655392 | tf_op jit(solution)/shard_map/ppermute | solution.py:353
  94.9 8.6 %collective-permute-done.6.refs_15_.refs_7_ = f32[320,512]{1,0:T(8,128)} collective-permute-done((f32[320,512]{1,0:T(8,128)}, f32[320,512]{1,0:T(8,128)}, u32[]{:S(2)}, u32[]{:S(2)}) %collective-permute-start.6) | collective-permute-done | bytes 655392 | tf_op jit(solution)/shard_map/ppermute | solution.py:353
  103.5 1.5 collective-permute-done.13.refs_7_
  105.0 2.5 %copy-done = f32[2560,512]{1,0:T(8,128)S(1)} copy-done((f32[2560,512]{1,0:T(8,128)S(1)}, f32[2560,512]{1,0:T(8,128)}, u32[]{:S(2)}) %copy-start) | copy-done | bytes 5242904
  110.8 3.5 %shard_map.29.refs_9_.refs_17_ = f32[512,512]{1,0:T(8,128)S(1)} custom-call(s32[8]{0:T(128)S(1)} %stack.35.ids, s32[1]{0:T(128)} %bitcast.8.place, f32[320,512]{1,0:T(8,128)S(1)} %slice.3.refs_0_, f32[320,512]{1,0:T(8,128)S(1)} %copy-done.2, f32[320,512]{1,0:T(8,128)S(1)} %copy-done.5, f32[320,512]{1,0:T(8,128)S(1)} %copy-done.8, ...), custom_call_target="tpu_custom_call" | custom-call | flops 805306368 | bytes 3145728 | tf_op jit(solution)/shard_map/pallas_call | solution.py:205
  114.3 1.5 collective-permute-start.15
  115.8 5.5 %shard_map.31.refs_9_ = f32[512,512]{1,0:T(8,128)S(1)} custom-call(s32[8]{0:T(128)S(1)} %stack.35.ids, s32[1]{0:T(128)} %bitcast.8.place, f32[320,512]{1,0:T(8,128)S(1)} %slice.3.refs_0_, f32[320,512]{1,0:T(8,128)S(1)} %copy-done.2, f32[320,512]{1,0:T(8,128)S(1)} %copy-done.5, f32[320,512]{1,0:T(8,128)S(1)} %copy-done.8, ...), custom_call_target="tpu_custom_call" | custom-call | flops 1610612736 | bytes 3145728 | tf_op jit(solution)/shard_map/pallas_call | solution.py:205
  124.0 4.0 %collective-permute-done.15.refs_11_ = f32[512,512]{1,0:T(8,128)S(1)} collective-permute-done((f32[512,512]{1,0:T(8,128)S(1)}, f32[512,512]{1,0:T(8,128)S(1)}, u32[]{:S(2)}, u32[]{:S(2)}) %collective-permute-start.15) | collective-permute-done | bytes 1048608 | tf_op jit(solution)/shard_map/ppermute | solution.py:364
  130.1 9.1 %collective-permute-done.18.refs_11_ = f32[512,512]{1,0:T(8,128)S(1)} collective-permute-done((f32[512,512]{1,0:T(8,128)S(1)}, f32[512,512]{1,0:T(8,128)S(1)}, u32[]{:S(2)}, u32[]{:S(2)}) %collective-permute-start.18) | collective-permute-done | bytes 1048608 | tf_op jit(solution)/shard_map/ppermute | solution.py:364
  140.0 9.0 %shard_map.30.refs_8_ = f32[2560,512]{1,0:T(8,128)} custom-call(s32[8]{0:T(128)S(1)} %stack.35.ids, s32[1]{0:T(128)} %bitcast.8.place, f32[320,512]{1,0:T(8,128)S(1)} %slice.3.refs_0_, f32[320,512]{1,0:T(8,128)S(1)} %copy-done.3, f32[320,512]{1,0:T(8,128)S(1)} %copy-done.6, f32[320,512]{1,0:T(8,128)S(1)} %copy-done.9, ...), custom_call_target="tpu_custom_call" | custom-call | flops 4026531840 | bytes 15728640 | tf_op jit(solution)/shard_map/pallas_call | solution.py:304
  149.1 9.0 %shard_map.32 = f32[2560,512]{1,0:T(8,128)} custom-call(s32[8]{0:T(128)S(1)} %stack.35.ids, s32[1]{0:T(128)} %bitcast.8.place, f32[320,512]{1,0:T(8,128)S(1)} %shard_map.28.refs_8_.refs_0_, f32[320,512]{1,0:T(8,128)S(1)} %collective-permute-done.refs_9_.refs_1_, f32[320,512]{1,0:T(8,128)S(1)} %collective-permute-done.1.refs_10_.refs_2_, ...), custom_call_target="tpu_custom_call" | custom-call | flops 4026531840 | bytes 15728640 | tf_op jit(solution)/shard_map/pallas_call | solution.py:304
  (45 shorter events, 13.8 us)
Async XLA Ops:
  3.9 18.7 %collective-permute-start.1 = (f32[320,512]{1,0:T(8,128)S(1)}, f32[320,512]{1,0:T(8,128)S(1)}, u32[]{:S(2)}, u32[]{:S(2)}) collective-permute-start(f32[320,512]{1,0:T(8,128)S(1)} %shard_map.28.refs_8_.refs_0_), channel_id=1, source_target_pairs={{8,0},{16,8},{24,16},{28,24},{20,28},{12,20},{4,12},{0,4},{9,1},{1... | collective-permute-start | bytes 1966088 | tf_op jit(solution)/shard_map/ppermute | solution.py:353
  6.9 17.7 %collective-permute-start.7 = (f32[320,512]{1,0:T(8,128)S(1)}, f32[320,512]{1,0:T(8,128)S(1)}, u32[]{:S(2)}, u32[]{:S(2)}) collective-permute-start(f32[320,512]{1,0:T(8,128)S(1)} %slice.3.refs_0_), channel_id=1, source_target_pairs={{0,8},{8,16},{16,24},{24,28},{28,20},{20,12},{12,4},{4,0},{1,9},{9... | collective-permute-start | bytes 1966088 | tf_op jit(solution)/shard_map/ppermute | solution.py:353
  7.0 31.6 %collective-permute-start = (f32[320,512]{1,0:T(8,128)S(1)}, f32[320,512]{1,0:T(8,128)S(1)}, u32[]{:S(2)}, u32[]{:S(2)}) collective-permute-start(f32[320,512]{1,0:T(8,128)S(1)} %shard_map.28.refs_8_.refs_0_), channel_id=1, source_target_pairs={{0,8},{8,16},{16,24},{24,28},{28,20},{20,12},{12,4},{4,0},{1,9},{9... | collective-permute-start | bytes 1966088 | tf_op jit(solution)/shard_map/ppermute | solution.py:353
  9.0 29.7 %collective-permute-start.8 = (f32[320,512]{1,0:T(8,128)S(1)}, f32[320,512]{1,0:T(8,128)S(1)}, u32[]{:S(2)}, u32[]{:S(2)}) collective-permute-start(f32[320,512]{1,0:T(8,128)S(1)} %slice.3.refs_0_), channel_id=1, source_target_pairs={{8,0},{16,8},{24,16},{28,24},{20,28},{12,20},{4,12},{0,4},{9,1},{1... | collective-permute-start | bytes 1966088 | tf_op jit(solution)/shard_map/ppermute | solution.py:353
  22.6 28.1 %collective-permute-start.3 = (f32[320,512]{1,0:T(8,128)S(1)}, f32[320,512]{1,0:T(8,128)S(1)}, u32[]{:S(2)}, u32[]{:S(2)}) collective-permute-start(f32[320,512]{1,0:T(8,128)S(1)} %collective-permute-done.1.refs_10_.refs_2_), channel_id=1, source_target_pairs={{8,0},{16,8},{24,16},{28,24},{20,28},{12,20},{4,12},{0,4},{9,1},{1... | collective-permute-start | bytes 1966088 | tf_op jit(solution)/shard_map/ppermute | solution.py:353
  24.6 28.1 %collective-permute-start.9 = (f32[320,512]{1,0:T(8,128)S(1)}, f32[320,512]{1,0:T(8,128)S(1)}, u32[]{:S(2)}, u32[]{:S(2)}) collective-permute-start(f32[320,512]{1,0:T(8,128)S(1)} %collective-permute-done.7.refs_1_), channel_id=1, source_target_pairs={{0,8},{8,16},{16,24},{24,28},{28,20},{20,12},{12,4},{4,0},{1,9},{9... | collective-permute-start | bytes 1966088 | tf_op jit(solution)/shard_map/ppermute | solution.py:353
  38.6 28.2 %collective-permute-start.2 = (f32[320,512]{1,0:T(8,128)S(1)}, f32[320,512]{1,0:T(8,128)}, u32[]{:S(2)}, u32[]{:S(2)}) collective-permute-start(f32[320,512]{1,0:T(8,128)S(1)} %collective-permute-done.refs_9_.refs_1_), channel_id=1, source_target_pairs={{0,8},{8,16},{16,24},{24,28},{28,20},{20,12},{12,4},{4,0},{1,9},{9... | collective-permute-start | bytes 1966088 | tf_op jit(solution)/shard_map/ppermute | solution.py:353
  38.7 28.2 %collective-permute-start.10 = (f32[320,512]{1,0:T(8,128)S(1)}, f32[320,512]{1,0:T(8,128)}, u32[]{:S(2)}, u32[]{:S(2)}) collective-permute-start(f32[320,512]{1,0:T(8,128)S(1)} %collective-permute-done.8.refs_2_), channel_id=1, source_target_pairs={{8,0},{16,8},{24,16},{28,24},{20,28},{12,20},{4,12},{0,4},{9,1},{1... | collective-permute-start | bytes 1966088 | tf_op jit(solution)/shard_map/ppermute | solution.py:353
  50.7 28.2 %collective-permute-start.5 = (f32[320,512]{1,0:T(8,128)S(1)}, f32[320,512]{1,0:T(8,128)}, u32[]{:S(2)}, u32[]{:S(2)}) collective-permute-start(f32[320,512]{1,0:T(8,128)S(1)} %collective-permute-done.3.refs_12_.refs_4_), channel_id=1, source_target_pairs={{8,0},{16,8},{24,16},{28,24},{20,28},{12,20},{4,12},{0,4},{9,1},{1... | collective-permute-start | bytes 1966088 | tf_op jit(solution)/shard_map/ppermute | solution.py:353
  52.7 28.2 %collective-permute-start.11 = (f32[320,512]{1,0:T(8,128)S(1)}, f32[320,512]{1,0:T(8,128)}, u32[]{:S(2)}, u32[]{:S(2)}) collective-permute-start(f32[320,512]{1,0:T(8,128)S(1)} %collective-permute-done.9.refs_3_), channel_id=1, source_target_pairs={{0,8},{8,16},{16,24},{24,28},{28,20},{20,12},{12,4},{4,0},{1,9},{9... | collective-permute-start | bytes 1966088 | tf_op jit(solution)/shard_map/ppermute | solution.py:353
  66.8 28.1 %collective-permute-start.4 = (f32[320,512]{1,0:T(8,128)}, f32[320,512]{1,0:T(8,128)}, u32[]{:S(2)}, u32[]{:S(2)}) collective-permute-start(f32[320,512]{1,0:T(8,128)} %collective-permute-done.2.refs_11_.refs_3_), channel_id=1, source_target_pairs={{0,8},{8,16},{16,24},{24,28},{28,20},{20,12},{12,4},{4,0},{1,9},{9... | collective-permute-start | bytes 1966088 | tf_op jit(solution)/shard_map/ppermute | solution.py:353
  66.9 28.0 %collective-permute-start.12 = (f32[320,512]{1,0:T(8,128)}, f32[320,512]{1,0:T(8,128)}, u32[]{:S(2)}, u32[]{:S(2)}) collective-permute-start(f32[320,512]{1,0:T(8,128)} %collective-permute-done.10.refs_4_), channel_id=1, source_target_pairs={{8,0},{16,8},{24,16},{28,24},{20,28},{12,20},{4,12},{0,4},{9,1},{1... | collective-permute-start | bytes 1966088 | tf_op jit(solution)/shard_map/ppermute | solution.py:353
  78.8 24.7 %collective-permute-start.6 = (f32[320,512]{1,0:T(8,128)}, f32[320,512]{1,0:T(8,128)}, u32[]{:S(2)}, u32[]{:S(2)}) collective-permute-start(f32[320,512]{1,0:T(8,128)} %collective-permute-done.5.refs_14_.refs_6_), channel_id=1, source_target_pairs={{8,0},{16,8},{24,16},{28,24},{20,28},{12,20},{4,12},{0,4},{9,1},{1... | collective-permute-start | bytes 1966088 | tf_op jit(solution)/shard_map/ppermute | solution.py:353
  80.9 24.1 %collective-permute-start.13 = (f32[320,512]{1,0:T(8,128)}, f32[320,512]{1,0:T(8,128)}, u32[]{:S(2)}, u32[]{:S(2)}) collective-permute-start(f32[320,512]{1,0:T(8,128)} %collective-permute-done.11.refs_5_), channel_id=1, source_target_pairs={{0,8},{8,16},{16,24},{24,28},{28,20},{20,12},{12,4},{4,0},{1,9},{9... | collective-permute-start | bytes 1966088 | tf_op jit(solution)/shard_map/ppermute | solution.py:353
  105.0 2.5 %copy-start = (f32[2560,512]{1,0:T(8,128)S(1)}, f32[2560,512]{1,0:T(8,128)}, u32[]{:S(2)}) copy-start(f32[2560,512]{1,0:T(8,128)} %refs_16_.3) | copy-start | bytes 15728644
  114.3 25.7 %copy-start.3 = (f32[320,512]{1,0:T(8,128)S(1)}, f32[320,512]{1,0:T(8,128)}, u32[]{:S(2)}) copy-start(f32[320,512]{1,0:T(8,128)} %copy-done.1) | copy-start | bytes 1966084
  114.3 25.7 %copy-start.6 = (f32[320,512]{1,0:T(8,128)S(1)}, f32[320,512]{1,0:T(8,128)}, u32[]{:S(2)}) copy-start(f32[320,512]{1,0:T(8,128)} %copy-done.4) | copy-start | bytes 1966084
  114.3 25.7 %copy-start.9 = (f32[320,512]{1,0:T(8,128)S(1)}, f32[320,512]{1,0:T(8,128)}, u32[]{:S(2)}) copy-start(f32[320,512]{1,0:T(8,128)} %copy-done.7) | copy-start | bytes 1966084
  114.3 13.7 %collective-permute-start.15 = (f32[512,512]{1,0:T(8,128)S(1)}, f32[512,512]{1,0:T(8,128)S(1)}, u32[]{:S(2)}, u32[]{:S(2)}) collective-permute-start(f32[512,512]{1,0:T(8,128)S(1)} %shard_map.29.refs_9_.refs_17_), channel_id=1, source_target_pairs={{0,2},{4,6},{8,10},{12,14},{16,18},{20,22},{24,26},{28,30}} | collective-permute-start | bytes 3145736 | tf_op jit(solution)/shard_map/ppermute | solution.py:364
  121.3 18.0 %collective-permute-start.18 = (f32[512,512]{1,0:T(8,128)S(1)}, f32[512,512]{1,0:T(8,128)S(1)}, u32[]{:S(2)}, u32[]{:S(2)}) collective-permute-start(f32[512,512]{1,0:T(8,128)S(1)} %shard_map.31.refs_9_), channel_id=1, source_target_pairs={{0,2},{4,6},{8,10},{12,14},{16,18},{20,22},{24,26},{28,30}} | collective-permute-start | bytes 3145736 | tf_op jit(solution)/shard_map/ppermute | solution.py:364
  122.6 17.4 %collective-permute-start.14 = (f32[512,512]{1,0:T(8,128)S(1)}, f32[512,512]{1,0:T(8,128)S(1)}, u32[]{:S(2)}, u32[]{:S(2)}) collective-permute-start(f32[512,512]{1,0:T(8,128)S(1)} %shard_map.29.refs_9_.refs_17_), channel_id=1, source_target_pairs={{0,1},{4,5},{8,9},{12,13},{16,17},{20,21},{24,25},{28,29}} | collective-permute-start | bytes 3145736 | tf_op jit(solution)/shard_map/ppermute | solution.py:364
  128.0 12.0 %collective-permute-start.16 = (f32[512,512]{1,0:T(8,128)S(1)}, f32[512,512]{1,0:T(8,128)S(1)}, u32[]{:S(2)}, u32[]{:S(2)}) collective-permute-start(f32[512,512]{1,0:T(8,128)S(1)} %collective-permute-done.15.refs_11_), channel_id=1, source_target_pairs={{2,3},{6,7},{10,11},{14,15},{18,19},{22,23},{26,27},{30,31}} | collective-permute-start | bytes 3145736 | tf_op jit(solution)/shard_map/ppermute | solution.py:364
  128.7 20.3 %collective-permute-start.17 = (f32[512,512]{1,0:T(8,128)S(1)}, f32[512,512]{1,0:T(8,128)S(1)}, u32[]{:S(2)}, u32[]{:S(2)}) collective-permute-start(f32[512,512]{1,0:T(8,128)S(1)} %shard_map.31.refs_9_), channel_id=1, source_target_pairs={{0,1},{4,5},{8,9},{12,13},{16,17},{20,21},{24,25},{28,29}} | collective-permute-start | bytes 3145736 | tf_op jit(solution)/shard_map/ppermute | solution.py:364
  139.3 9.8 %collective-permute-start.19 = (f32[512,512]{1,0:T(8,128)S(1)}, f32[512,512]{1,0:T(8,128)S(1)}, u32[]{:S(2)}, u32[]{:S(2)}) collective-permute-start(f32[512,512]{1,0:T(8,128)S(1)} %collective-permute-done.18.refs_11_), channel_id=1, source_target_pairs={{2,3},{6,7},{10,11},{14,15},{18,19},{22,23},{26,27},{30,31}} | collective-permute-start | bytes 3145736 | tf_op jit(solution)/shard_map/ppermute | solution.py:364
  (7 other events, 7.1 us)
where the time goes:
time: 159 us; the launch traced here: 158 us
  waiting for transfers between devices  96.3 us (61%)
  Pallas kernels  29.5 us (19%)
  starting transfers between devices  22.3 us (14%)
  local copies, waits for them, and re-layouts  9.77 us (6%)
    ppermute x14, waiting for transfers between devices, gather_pieces(): going[k][way] = lax.ppermute(going[k][way], 'src', pairs)  83.1 us
    pallas_call x2, Pallas kernels, update(): pl.pallas_call(functools.partial(update_kernel, pieces, rows, width, tile...  18 us
    ppermute x14, starting transfers between devices, gather_pieces(): going[k][way] = lax.ppermute(going[k][way], 'src', pairs)  15.3 us
    ppermute x6, waiting for transfers between devices, spread_rows(): found[r + stride] = lax.ppermute(found[r], 'row', [(r, r + stride)])  13.2 us
    unnamed x22, local copies, waits for them, and re-layouts  9.65 us
    pallas_call x2, Pallas kernels, solve_panel(): pl.pallas_call(functools.partial(solve_kernel, pieces, rows, width, chunk...  8.94 us
    ppermute x6, starting transfers between devices, spread_rows(): found[r + stride] = lax.ppermute(found[r], 'row', [(r, r + stride)])  6.99 us
  transfers between devices with their start and end apart: 20, of which 13 were waited for; matrix products, arithmetic and copies ran while one was open for 0% of the time, Pallas kernels for 9%

commit v1 on v0

--- a/solution.py
+++ b/solution.py
@@ -8,11 +8,12 @@
 from jax.experimental.pallas import tpu as pltpu
 from jax.sharding import PartitionSpec as P
 
-VMEM_BYTES = 40 * 1024 * 1024
+VMEM_BYTES = 60 * 1024 * 1024
 LANES = 128
 RING_LIMIT = 16
-
-ANY = pl.BlockSpec(memory_space=pl.ANY)
+TOKEN_STEP = 2
+
+ANY = pl.BlockSpec(memory_space=pltpu.HBM)
 SCALARS = pl.BlockSpec(memory_space=pltpu.SMEM)
 WHOLE = pl.BlockSpec(memory_space=pltpu.VMEM)
 
@@ -63,8 +64,11 @@
     return inverses
 
 
-def prepare_kernel(rows, block, depth, me, place, factor, out):
+def prepare_kernel(rows, block, depth, me, place, source, out, factor, sem):
     width = depth // 2
+    load = pltpu.make_async_copy(source, factor, sem)
+    load.start()
+    load.wait()
     out[...] = factor[:, width:]
     first = me[0] * rows
 
@@ -94,9 +98,10 @@
     return pl.pallas_call(
         functools.partial(prepare_kernel, rows, block, depth),
         out_shape=jax.ShapeDtypeStruct((rows, depth // 2), jnp.float32),
-        in_specs=[SCALARS] * 2 + [WHOLE],
+        in_specs=[SCALARS] * 2 + [ANY],
         out_specs=WHOLE,
-        compiler_params=pltpu.CompilerParams(vmem_limit_bytes=VMEM_BYTES // 2),
+        scratch_shapes=[pltpu.VMEM((rows, depth), jnp.float32), pltpu.SemaphoreType.DMA],
+        compiler_params=pltpu.CompilerParams(vmem_limit_bytes=VMEM_BYTES),
         cost_estimate=pl.CostEstimate(
             flops=24 * rows * block * block, bytes_accessed=6 * rows * depth, transcendentals=0
         ),
@@ -212,7 +217,7 @@
             pltpu.SemaphoreType.DMA((2, pieces)),
             pltpu.SemaphoreType.DMA,
         ],
-        compiler_params=pltpu.CompilerParams(vmem_limit_bytes=VMEM_BYTES // 2),
+        compiler_params=pltpu.CompilerParams(vmem_limit_bytes=VMEM_BYTES),
         cost_estimate=pl.CostEstimate(
             flops=6 * (panel + 1) * width * width * columns,
             bytes_accessed=12 * width * columns,
@@ -221,45 +226,60 @@
     )(ids, place, *held[0], *held[1], rhs, *earlier)
 
 
-def update_kernel(pieces, rows, width, tile, step, places, panel, ids, place, *refs):
-    held, refs = refs[:pieces], refs[pieces:]
-    current, refs = refs[0], refs[1:]
-    solved, refs = refs[:places], refs[places:]
+def update_kernel(pieces, rows, width, tile, step, places, behind, ids, place, *refs):
+    held, refs = refs[: 4 * pieces], refs[4 * pieces :]
+    rhs, refs = refs[0], refs[1:]
+    solved, refs = refs[: 2 * places], refs[2 * places :]
+    refs = refs[len(refs) - 11 :]
     out, lower, block, found, high, low, product, piece_sem, block_sem, found_sem, out_sem = refs
-    first, last = panel * width, (panel + 1) * width
-    start = place[0] * current.shape[0]
-
-    def fetch(r):
-        return pltpu.make_async_copy(solved[r], found, found_sem)
+    depth = 2 * width
+    start = place[0] * rhs.shape[0]
+
+    def fetch(k, r):
+        return pltpu.make_async_copy(
+            solved[k * places + r], found.at[pl.ds(k * width, width)], found_sem.at[k]
+        )
+
+    def at(i):
+        return pl.ds(pl.multiple_of(ids[i] * rows, 8), rows)
+
+    def load(k, i, source):
+        return pltpu.make_async_copy(
+            held[source], lower.at[i, :, pl.ds(k * width, width)], piece_sem.at[k, i]
+        )
+
+    def load_block(i):
+        return pltpu.make_async_copy(rhs.at[at(i)], block.at[i], block_sem.at[i])
+
+    def store(i):
+        return pltpu.make_async_copy(block.at[i], out.at[at(i)], out_sem.at[i])
 
     for r in range(places):
 
         @pl.when(place[0] == r)
         def _(r=r):
-            fetch(r).start()
-
-    def at(i):
-        return pl.ds(pl.multiple_of(ids[i] * rows, 8), rows)
-
-    def loads(i, source):
-        return [
-            pltpu.make_async_copy(held[source], lower.at[i], piece_sem.at[i]),
-            pltpu.make_async_copy(current.at[at(i)], block.at[i], block_sem.at[i]),
-        ]
-
-    def store(i):
-        return pltpu.make_async_copy(block.at[i], out.at[at(i)], out_sem.at[i])
+            for k in range(2):
+                fetch(k, r).start()
+
+    for group in range(2):
+
+        @pl.when((place[0] == behind) == (group == 1))
+        def _(group=group):
+            for i in range(pieces):
+                for k in range(2):
+                    load(k, i, (2 * group + k) * pieces + i).start()
 
     for i in range(pieces):
-        for load in loads(i, i):
-            load.start()
-    fetch(0).wait()
+        load_block(i).start()
+    for k in range(2):
+        fetch(k, 0).wait()
     high[...], low[...] = split16(found[...])
 
     @pl.loop(0, pieces)
     def _(i):
-        for load in loads(i, 0):
-            load.wait()
+        for k in range(2):
+            load(k, i, 0).wait()
+        load_block(i).wait()
 
         @pl.loop(0, rows // tile)
         def _(t):
@@ -269,11 +289,11 @@
                 split16(lower[i, pl.ds(inside, tile)]), (high[...], low[...])
             )
 
-            @pl.when(top >= last)
+            @pl.when(top >= depth)
             def _():
                 block[i, pl.ds(inside, tile)] = block[i, pl.ds(inside, tile)] - product[...]
 
-            @pl.when(top < last)
+            @pl.when(top < depth)
             def _():
                 @pl.loop(0, tile // step)
                 def _(u):
@@ -281,11 +301,11 @@
                     row = top + part
                     here = pl.ds(inside + part, step)
 
-                    @pl.when((row >= first) & (row < last))
+                    @pl.when(row < depth)
                     def _():
-                        block[i, here] = found[pl.ds(pl.multiple_of(row - first, 8), step)]
-
-                    @pl.when(row >= last)
+                        block[i, here] = found[pl.ds(pl.multiple_of(row, 8), step)]
+
+                    @pl.when(row >= depth)
                     def _():
                         block[i, here] = block[i, here] - product[pl.ds(part, step)]
 
@@ -296,64 +316,84 @@
         store(i).wait()
 
 
-def update(panel, ids, place, held, current, solved, width):
-    pieces, places = len(held), len(solved)
-    rows, columns = held[0].shape[0], current.shape[1]
-    step = math.gcd(rows, width)
+def update(ids, place, held, rhs, solved, width, behind, written=None):
+    pieces, places = len(held[0]), len(solved[0])
+    rows, columns = held[0][0].shape[0], rhs.shape[1]
+    step = math.gcd(rows, 2 * width)
     tile = step * max(m for m in range(1, rows // step + 1) if rows // step % m == 0 and step * m <= 512)
+    operands = [ids, place, *[piece for group in held for piece in group], rhs, *solved[0], *solved[1]]
+    extra = [] if written is None else [written]
     return pl.pallas_call(
-        functools.partial(update_kernel, pieces, rows, width, tile, step, places, panel),
-        out_shape=jax.ShapeDtypeStruct(current.shape, jnp.float32),
-        in_specs=[SCALARS] * 2 + [ANY] * (pieces + 1 + places),
+        functools.partial(update_kernel, pieces, rows, width, tile, step, places, behind),
+        out_shape=jax.ShapeDtypeStruct(rhs.shape, jnp.float32),
+        in_specs=[SCALARS] * 2 + [ANY] * (len(operands) - 2 + len(extra)),
         out_specs=ANY,
+        input_output_aliases={len(operands): 0} if extra else {},
         scratch_shapes=[
-            pltpu.VMEM((pieces, rows, width), jnp.float32),
+            pltpu.VMEM((pieces, rows, 2 * width), jnp.float32),
             pltpu.VMEM((pieces, rows, columns), jnp.float32),
-            pltpu.VMEM((width, columns), jnp.float32),
-            pltpu.VMEM((width, columns), jnp.bfloat16),
-            pltpu.VMEM((width, columns), jnp.bfloat16),
+            pltpu.VMEM((2 * width, columns), jnp.float32),
+            pltpu.VMEM((2 * width, columns), jnp.bfloat16),
+            pltpu.VMEM((2 * width, columns), jnp.bfloat16),
             pltpu.VMEM((tile, columns), jnp.float32),
+            pltpu.SemaphoreType.DMA((2, pieces)),
             pltpu.SemaphoreType.DMA((pieces,)),
-            pltpu.SemaphoreType.DMA((pieces,)),
-            pltpu.SemaphoreType.DMA,
+            pltpu.SemaphoreType.DMA((2,)),
             pltpu.SemaphoreType.DMA((pieces,)),
         ],
         compiler_params=pltpu.CompilerParams(vmem_limit_bytes=VMEM_BYTES),
         cost_estimate=pl.CostEstimate(
-            flops=6 * pieces * rows * width * columns,
-            bytes_accessed=4 * pieces * rows * (width + 2 * columns),
+            flops=12 * pieces * rows * width * columns,
+            bytes_accessed=8 * pieces * rows * (width + columns),
             transcendentals=0,
         ),
-    )(ids, place, *held, current, *solved)
-
-
-def gather_pieces(panels, count):
-    me = lax.axis_index("src")
-    if count % 2 or count > RING_LIMIT:
-        gathered = [lax.all_gather(panel, "src", axis=0, tiled=True) for panel in panels]
-        return [[piece] for piece in gathered], [jnp.zeros_like(me)]
-    ring = list(range(0, count, 2)) + list(range(count - 1, 0, -2))
-    onward = [(ring[i], ring[(i + 1) % count]) for i in range(count)]
-    back = [(b, a) for a, b in onward]
-    position = jnp.where(me % 2 == 0, me // 2, count - 1 - me // 2)
-
-    def shard_at(spot):
-        spot = (spot + count) % count
-        return jnp.where(spot < count // 2, 2 * spot, 2 * (count - 1 - spot) + 1)
-
-    held = [[panel] for panel in panels]
-    ids = [me]
+    )(*operands, *extra)
+
+
+def gate_kernel(first, second, token, first_out, second_out):
+    pass
+
+
+def gate(panels, token):
+    return pl.pallas_call(
+        gate_kernel,
+        out_shape=[jax.ShapeDtypeStruct(panel.shape, panel.dtype) for panel in panels],
+        in_specs=[ANY] * 3,
+        out_specs=[ANY] * 2,
+        input_output_aliases={0: 0, 1: 1},
+        compiler_params=pltpu.CompilerParams(vmem_limit_bytes=VMEM_BYTES),
+    )(*panels, token)
+
+
+def ring_steps(panels, ring, members, number):
+    count = len(ring)
+    ways = [
+        [(number(ring[i], r), number(ring[(i + way) % count], r)) for i in range(count) for r in members]
+        for way in (1, -1)
+    ]
     going = [[panel, panel] for panel in panels]
     for step in range(1, count // 2 + 1):
-        last = step == count // 2
+        arrived = [[], []]
         for k in range(2):
-            for way, pairs in enumerate((onward, back)):
-                if last and way != k:
+            for way in range(2):
+                if step == count // 2 and way != k:
                     continue
-                going[k][way] = lax.ppermute(going[k][way], "src", pairs)
-                held[k].append(going[k][way])
-        ids += [shard_at(position - step)] + ([] if last else [shard_at(position + step)])
-    return held, ids
+                going[k][way] = lax.ppermute(going[k][way], number.axes, ways[way])
+                arrived[k].append(going[k][way])
+        yield arrived
+
+
+class Number:
+    def __init__(self, mesh):
+        self.axes = tuple(mesh.axis_names)
+        self.shape = dict(mesh.shape)
+
+    def __call__(self, source, row):
+        at = {"src": source, "row": row}
+        place = 0
+        for axis in self.axes:
+            place = place * self.shape[axis] + at[axis]
+        return place
 
 
 def spread_rows(block, count):
@@ -367,7 +407,9 @@
 
 
 def solution(mesh):
-    sources, places = mesh.shape["src"], mesh.shape["row"]
+    count, places = mesh.shape["src"], mesh.shape["row"]
+    number = Number(mesh)
+    behind = 1
 
     def local(factor, right_side):
         rows, depth = factor.shape
@@ -376,12 +418,37 @@
         me = lax.axis_index("src").reshape(1).astype(jnp.int32)
         place = lax.axis_index("row").reshape(1).astype(jnp.int32)
         panels = [factor[:, :width], prepare(me, place, factor, block)]
-        held, ids = gather_pieces(panels, sources)
-        ids = jnp.stack(ids).astype(jnp.int32)
+        if count % 2 or count > RING_LIMIT or places < 2:
+            held = [[lax.all_gather(panel, "src", axis=0, tiled=True)] for panel in panels]
+            late, ids, cut = held, jnp.zeros_like(me), 1
+        else:
+            ring = list(range(0, count, 2)) + list(range(count - 1, 0, -2))
+            spot = jnp.where(me % 2 == 0, me // 2, count - 1 - me // 2)
+            half = count // 2
+            away = [0] + [d for step in range(1, half) for d in (-step, step)] + [half]
+            spot = (spot + jnp.array(away, jnp.int32) + count) % count
+            ids = jnp.where(spot < half, 2 * spot, 2 * (count - 1 - spot) + 1)
+            held = [[panel] for panel in panels]
+            ahead = [r for r in range(places) if r != behind]
+            for step, arrived in enumerate(ring_steps(panels, ring, ahead, number)):
+                for k in range(2):
+                    held[k] += arrived[k]
+                if step == TOKEN_STEP:
+                    token = lax.ppermute(arrived[0][0][:8, :LANES], "row", [(0, behind)])
+            late = [[panel] for panel in panels]
+            for arrived in ring_steps(gate(panels, token), ring, [behind], number):
+                for k in range(2):
+                    late[k] += arrived[k]
+            cut = 5
         first = solve_panel(0, ids, place, held, right_side, [], width, block)
         second = solve_panel(1, ids, place, held, right_side, [first], width, block)
-        current = update(0, ids, place, held[0], right_side, spread_rows(first, places), width)
-        return update(1, ids, place, held[1], current, spread_rows(second, places), width)
+        solved = [spread_rows(first, places), spread_rows(second, places)]
+        result = None
+        for part in (slice(0, cut), slice(cut, None)):
+            group = [pieces[part] for pieces in held + late]
+            if group[0]:
+                result = update(ids[part], place, group, right_side, solved, width, behind, result)
+        return result
 
     placed = (P(("row", "src"), None), P("row", "src"))
     return jax.shard_map(

time: 159 us -> 180 us (1.13)
  starting transfers between devices: 22.3 us -> 99.6 us
  waiting for transfers between devices: 96.3 us -> 30.2 us
  Pallas kernels: 29.5 us -> 39.2 us
    ppermute x14 -> x29, waiting for transfers between devices: 83.1 us -> 15.2 us  [the longest x28 15.2 us: ring_steps(): going[k][way] = lax.ppermute(going[k][way], number.axes, ways[way])]
    ppermute x14 -> x29, starting transfers between devices: 15.3 us -> 61.9 us  [the longest x28 60.7 us: ring_steps(): going[k][way] = lax.ppermute(going[k][way], number.axes, ways[way])]
    ppermute x6, starting transfers between devices: 6.99 us -> 37.6 us  [spread_rows(): found[r + stride] = lax.ppermute(found[r], 'row', [(r, r + stride)])]
    pallas_call x2, Pallas kernels: 8.94 us -> 14.3 us  [solve_panel(): pl.pallas_call(functools.partial(solve_kernel, pieces, rows, width, chunk...]
    unnamed x22 -> x44, local copies, waits for them, and re-layouts: 9.65 us -> 6.56 us
    pallas_call x1, Pallas kernels: 2.56 us -> 4.78 us  [prepare(): pl.pallas_call(functools.partial(prepare_kernel, rows, block, depth), out...]
    pallas_call x2, Pallas kernels: 18 us -> 20.2 us  [update(): pl.pallas_call(functools.partial(update_kernel, pieces, rows, width, tile...]
    ppermute x6, waiting for transfers between devices: 13.2 us -> 15 us  [spread_rows(): found[r + stride] = lax.ppermute(found[r], 'row', [(r, r + stride)])]
  transfers between devices with their start and end apart: 20 -> 35, of which waited for: 13 -> 10; matrix products, arithmetic and copies ran while one was open for 0% -> 2% of each run, Pallas kernels for 9% -> 17%
where the time goes in v1:
time: 180 us; the launch traced here: 179 us
  starting transfers between devices  99.6 us (55%)
  Pallas kernels  39.2 us (22%)
  waiting for transfers between devices  30.2 us (17%)
  local copies, waits for them, and re-layouts  8.36 us (5%)
    ppermute x28, starting transfers between devices, ring_steps(): going[k][way] = lax.ppermute(going[k][way], number.axes, ways[way])  60.7 us
    ppermute x6, starting transfers between devices, spread_rows(): found[r + stride] = lax.ppermute(found[r], 'row', [(r, r + stride)])  37.6 us
    pallas_call x2, Pallas kernels, update(): pl.pallas_call(functools.partial(update_kernel, pieces, rows, width, tile...  20.2 us
    ppermute x28, waiting for transfers between devices, ring_steps(): going[k][way] = lax.ppermute(going[k][way], number.axes, ways[way])  15.2 us
    ppermute x6, waiting for transfers between devices, spread_rows(): found[r + stride] = lax.ppermute(found[r], 'row', [(r, r + stride)])  15 us
    pallas_call x2, Pallas kernels, solve_panel(): pl.pallas_call(functools.partial(solve_kernel, pieces, rows, width, chunk...  14.3 us
    unnamed x44, local copies, waits for them, and re-layouts  6.56 us
    pallas_call x1, Pallas kernels, prepare(): pl.pallas_call(functools.partial(prepare_kernel, rows, block, depth), out...  4.78 us
  transfers between devices with their start and end apart: 35, of which 10 were waited for; matrix products, arithmetic and copies ran while one was open for 2% of the time, Pallas kernels for 17%

profile of v1, /device:TPU:0, one launch (start us, length us, event | category | flops | bytes accessed | tf_op | source)
XLA Modules:
  0.0 178.7 jit_solution(6773368437205655605)
XLA Ops:
  1.2 4.9 %collective-permute-start = (f32[320,512]{1,0:T(8,128)S(1)}, f32[320,512]{1,0:T(8,128)S(1)}, u32[]{:S(2)}, u32[]{:S(2)}) collective-permute-start(f32[320,512]{1,0:T(8,128)S(1)} %slice.13.refs_0_.refs_10_), channel_id=1, source_target_pairs={{0,8},{2,10},{3,11},{8,16},{10,18},{11,19},{16,24},{18,26},{19,27}... | collective-permute-start | bytes 1966088 | tf_op jit(solution)/shard_map/ppermute | solution.py:381
  6.1 4.8 %shard_map.37.refs_8_.refs_5_.refs_15_ = f32[320,512]{1,0:T(8,128)} custom-call(s32[1]{0:T(128)} %bitcast.me, s32[1]{0:T(128)} %bitcast.2.place, f32[320,1024]{1,0:T(8,128)} %source.1), custom_call_target="tpu_custom_call" | custom-call | flops 31457280 | bytes 1966080 | tf_op jit(solution)/shard_map/pallas_call | solution.py:98
  10.9 1.9 %collective-permute-start.10 = (f32[320,512]{1,0:T(8,128)}, f32[320,512]{1,0:T(8,128)S(1)}, u32[]{:S(2)}, u32[]{:S(2)}) collective-permute-start(f32[320,512]{1,0:T(8,128)} %shard_map.37.refs_8_.refs_5_.refs_15_), channel_id=1, source_target_pairs={{0,4},{2,6},{3,7},{8,0},{10,2},{11,3},{16,8},{18,10},{19,11},{24,1... | collective-permute-start | bytes 1966088 | tf_op jit(solution)/shard_map/ppermute | solution.py:381
  12.8 3.9 %collective-permute-start.7 = (f32[320,512]{1,0:T(8,128)}, f32[320,512]{1,0:T(8,128)S(1)}, u32[]{:S(2)}, u32[]{:S(2)}) collective-permute-start(f32[320,512]{1,0:T(8,128)} %shard_map.37.refs_8_.refs_5_.refs_15_), channel_id=1, source_target_pairs={{0,8},{2,10},{3,11},{8,16},{10,18},{11,19},{16,24},{18,26},{19,27}... | collective-permute-start | bytes 1966088 | tf_op jit(solution)/shard_map/ppermute | solution.py:381
  16.7 1.9 %collective-permute-start.3 = (f32[320,512]{1,0:T(8,128)S(1)}, f32[320,512]{1,0:T(8,128)S(1)}, u32[]{:S(2)}, u32[]{:S(2)}) collective-permute-start(f32[320,512]{1,0:T(8,128)S(1)} %slice.13.refs_0_.refs_10_), channel_id=1, source_target_pairs={{0,4},{2,6},{3,7},{8,0},{10,2},{11,3},{16,8},{18,10},{19,11},{24,1... | collective-permute-start | bytes 1966088 | tf_op jit(solution)/shard_map/ppermute | solution.py:381
  18.7 3.9 %collective-permute-start.1 = (f32[320,512]{1,0:T(8,128)S(1)}, f32[320,512]{1,0:T(8,128)S(1)}, u32[]{:S(2)}, u32[]{:S(2)}) collective-permute-start(f32[320,512]{1,0:T(8,128)S(1)} %collective-permute-done.refs_1_), channel_id=1, source_target_pairs={{0,8},{2,10},{3,11},{8,16},{10,18},{11,19},{16,24},{18,26},{19,27}... | collective-permute-start | bytes 1966088 | tf_op jit(solution)/shard_map/ppermute | solution.py:381
  23.6 1.9 %collective-permute-start.11 = (f32[320,512]{1,0:T(8,128)S(1)}, f32[320,512]{1,0:T(8,128)S(1)}, u32[]{:S(2)}, u32[]{:S(2)}) collective-permute-start(f32[320,512]{1,0:T(8,128)S(1)} %collective-permute-done.10.refs_10_.refs_7_), channel_id=1, source_target_pairs={{0,4},{2,6},{3,7},{8,0},{10,2},{11,3},{16,8},{18,10},{19,11},{24,1... | collective-permute-start | bytes 1966088 | tf_op jit(solution)/shard_map/ppermute | solution.py:381
  25.5 3.9 %collective-permute-start.8 = (f32[320,512]{1,0:T(8,128)S(1)}, f32[320,512]{1,0:T(8,128)}, u32[]{:S(2)}, u32[]{:S(2)}) collective-permute-start(f32[320,512]{1,0:T(8,128)S(1)} %collective-permute-done.7.refs_9_.refs_6_), channel_id=1, source_target_pairs={{0,8},{2,10},{3,11},{8,16},{10,18},{11,19},{16,24},{18,26},{19,27}... | collective-permute-start | bytes 1966088 | tf_op jit(solution)/shard_map/ppermute | solution.py:381
  30.6 1.9 %collective-permute-start.4 = (f32[320,512]{1,0:T(8,128)S(1)}, f32[320,512]{1,0:T(8,128)}, u32[]{:S(2)}, u32[]{:S(2)}) collective-permute-start(f32[320,512]{1,0:T(8,128)S(1)} %collective-permute-done.3.refs_2_), channel_id=1, source_target_pairs={{0,4},{2,6},{3,7},{8,0},{10,2},{11,3},{16,8},{18,10},{19,11},{24,1... | collective-permute-start | bytes 1966088 | tf_op jit(solution)/shard_map/ppermute | solution.py:381
  32.5 3.9 %collective-permute-start.2 = (f32[320,512]{1,0:T(8,128)S(1)}, f32[320,512]{1,0:T(8,128)S(1)}, u32[]{:S(2)}, u32[]{:S(2)}) collective-permute-start(f32[320,512]{1,0:T(8,128)S(1)} %collective-permute-done.1.refs_3_), channel_id=1, source_target_pairs={{0,8},{2,10},{3,11},{8,16},{10,18},{11,19},{16,24},{18,26},{19,27}... | collective-permute-start | bytes 1966088 | tf_op jit(solution)/shard_map/ppermute | solution.py:381
  37.6 1.9 %collective-permute-start.12 = (f32[320,512]{1,0:T(8,128)S(1)}, f32[320,512]{1,0:T(8,128)}, u32[]{:S(2)}, u32[]{:S(2)}) collective-permute-start(f32[320,512]{1,0:T(8,128)S(1)} %collective-permute-done.11.refs_12_.refs_9_), channel_id=1, source_target_pairs={{0,4},{2,6},{3,7},{8,0},{10,2},{11,3},{16,8},{18,10},{19,11},{24,1... | collective-permute-start | bytes 1966088 | tf_op jit(solution)/shard_map/ppermute | solution.py:381
  39.7 3.9 %collective-permute-start.9 = (f32[320,512]{1,0:T(8,128)}, f32[320,512]{1,0:T(8,128)}, u32[]{:S(2)}, u32[]{:S(2)}) collective-permute-start(f32[320,512]{1,0:T(8,128)} %collective-permute-done.8.refs_11_.refs_8_), channel_id=1, source_target_pairs={{0,8},{2,10},{3,11},{8,16},{10,18},{11,19},{16,24},{18,26},{19,27}... | collective-permute-start | bytes 1966088 | tf_op jit(solution)/shard_map/ppermute | solution.py:381
  44.8 1.9 %collective-permute-start.5 = (f32[320,512]{1,0:T(8,128)}, f32[320,512]{1,0:T(8,128)}, u32[]{:S(2)}, u32[]{:S(2)}) collective-permute-start(f32[320,512]{1,0:T(8,128)} %collective-permute-done.4.refs_4_), channel_id=1, source_target_pairs={{0,4},{2,6},{3,7},{8,0},{10,2},{11,3},{16,8},{18,10},{19,11},{24,1... | collective-permute-start | bytes 1966088 | tf_op jit(solution)/shard_map/ppermute | solution.py:381
  48.0 2.0 %copy.8.second = f32[320,512]{1,0:T(8,128)} copy(f32[320,512]{1,0:T(8,128)} %shard_map.37.refs_8_.refs_5_.refs_15_) | data formatting | bytes 1310720
  51.8 2.6 %collective-permute-start.13 = (f32[320,512]{1,0:T(8,128)}, f32[320,512]{1,0:T(8,128)}, u32[]{:S(2)}, u32[]{:S(2)}) collective-permute-start(f32[320,512]{1,0:T(8,128)} %collective-permute-done.12.refs_14_.refs_4_), channel_id=1, source_target_pairs={{0,4},{2,6},{3,7},{8,0},{10,2},{11,3},{16,8},{18,10},{19,11},{24,1... | collective-permute-start | bytes 1966088 | tf_op jit(solution)/shard_map/ppermute | solution.py:381
  56.5 3.2 %collective-permute-start.6 = (f32[320,512]{1,0:T(8,128)S(1)}, f32[320,512]{1,0:T(8,128)}, u32[]{:S(2)}, u32[]{:S(2)}) collective-permute-start(f32[320,512]{1,0:T(8,128)S(1)} %collective-permute-done.2.refs_5_.refs_0_), channel_id=1, source_target_pairs={{0,8},{2,10},{3,11},{8,16},{10,18},{11,19},{16,24},{18,26},{19,27}... | collective-permute-start | bytes 1966088 | tf_op jit(solution)/shard_map/ppermute | solution.py:381
  62.8 9.1 %collective-permute-done.13.refs_15_.refs_5_ = f32[320,512]{1,0:T(8,128)} collective-permute-done((f32[320,512]{1,0:T(8,128)}, f32[320,512]{1,0:T(8,128)}, u32[]{:S(2)}, u32[]{:S(2)}) %collective-permute-start.13) | collective-permute-done | bytes 655392 | tf_op jit(solution)/shard_map/ppermute | solution.py:381
  76.1 6.0 %shard_map.39.refs_17_.refs_21_.refs_13_ = f32[512,512]{1,0:T(8,128)} custom-call(s32[8]{0:T(128)} %compare_select_fusion.2.ids, s32[1]{0:T(128)} %bitcast.2.place, f32[320,512]{1,0:T(8,128)} %copy-done, f32[320,512]{1,0:T(8,128)} %copy-done.3, f32[320,512]{1,0:T(8,128)} %copy-done.6, f32[320,512]{1,0:T(8,128)} %copy-done.7, ...), custom_call_target="tpu_custom_call" | custom-call | flops 805306368 | bytes 3145728 | tf_op jit(solution)/shard_map/pallas_call | solution.py:210
  82.2 8.2 %shard_map.40.refs_25_.refs_17_ = f32[512,512]{1,0:T(8,128)} custom-call(s32[8]{0:T(128)} %compare_select_fusion.2.ids, s32[1]{0:T(128)} %bitcast.2.place, f32[320,512]{1,0:T(8,128)} %copy-done, f32[320,512]{1,0:T(8,128)} %copy-done.3, f32[320,512]{1,0:T(8,128)} %copy-done.6, f32[320,512]{1,0:T(8,128)} %copy-done.7, ...), custom_call_target="tpu_custom_call" | custom-call | flops 1610612736 | bytes 3145728 | tf_op jit(solution)/shard_map/pallas_call | solution.py:210
  90.4 32.2 %collective-permute-start.33 = (f32[512,512]{1,0:T(8,128)}, f32[512,512]{1,0:T(8,128)S(1)}, u32[]{:S(2)}, u32[]{:S(2)}) collective-permute-start(f32[512,512]{1,0:T(8,128)} %shard_map.40.refs_25_.refs_17_), channel_id=1, source_target_pairs={{0,2},{4,6},{8,10},{12,14},{16,18},{20,22},{24,26},{28,30}} | collective-permute-start | bytes 3145736 | tf_op jit(solution)/shard_map/ppermute | solution.py:404
  130.5 4.6 %collective-permute-done.33.refs_27_.refs_19_ = f32[512,512]{1,0:T(8,128)S(1)} collective-permute-done((f32[512,512]{1,0:T(8,128)}, f32[512,512]{1,0:T(8,128)S(1)}, u32[]{:S(2)}, u32[]{:S(2)}) %collective-permute-start.33) | collective-permute-done | bytes 1048608 | tf_op jit(solution)/shard_map/ppermute | solution.py:404
  135.9 10.4 %collective-permute-done.30.refs_23_.refs_15_ = f32[512,512]{1,0:T(8,128)S(1)} collective-permute-done((f32[512,512]{1,0:T(8,128)S(1)}, f32[512,512]{1,0:T(8,128)S(1)}, u32[]{:S(2)}, u32[]{:S(2)}) %collective-permute-start.30) | collective-permute-done | bytes 1048608 | tf_op jit(solution)/shard_map/ppermute | solution.py:404
  157.2 11.9 %shard_map.41.refs_21_ = f32[2560,512]{1,0:T(8,128)} custom-call(s32[5]{0:T(128)} %bitcast.4, s32[1]{0:T(128)} %bitcast.2.place, f32[320,512]{1,0:T(8,128)} %copy-done, f32[320,512]{1,0:T(8,128)} %copy-done.3, f32[320,512]{1,0:T(8,128)} %copy-done.6, f32[320,512]{1,0:T(8,128)} %copy-done.7, f32[320,512]{1,0:T(8,128)} %collective-permute-done.4.refs_4_, ...), custom_call_target="tpu_custom_call" | custom-call | flops 5033164800 | bytes 13107200 | tf_op jit(solution)/shard_map/pallas_call | solution.py:326
  170.3 8.2 %shard_map.42 = f32[2560,512]{1,0:T(8,128)} custom-call(s32[3]{0:T(128)} %slice.12.ids, s32[1]{0:T(128)} %bitcast.2.place, f32[320,512]{1,0:T(8,128)} %copy-done.2, f32[320,512]{1,0:T(8,128)} %collective-permute-done.5.refs_6_.refs_1_, f32[320,512]{1,0:T(8,128)} %collective-permute-done.6.refs_7_.refs_2_, ...), custom_call_target="tpu_custom_call", output_to_operand_aliasing={{}: (23, {})} | custom-call | flops 3019898880 | bytes 7864320 | tf_op jit(solution)/shard_map/pallas_call | solution.py:326
  (100 shorter events, 38.7 us)
Async XLA Ops:
  1.2 17.5 %collective-permute-start = (f32[320,512]{1,0:T(8,128)S(1)}, f32[320,512]{1,0:T(8,128)S(1)}, u32[]{:S(2)}, u32[]{:S(2)}) collective-permute-start(f32[320,512]{1,0:T(8,128)S(1)} %slice.13.refs_0_.refs_10_), channel_id=1, source_target_pairs={{0,8},{2,10},{3,11},{8,16},{10,18},{11,19},{16,24},{18,26},{19,27}... | collective-permute-start | bytes 1966088 | tf_op jit(solution)/shard_map/ppermute | solution.py:381
  25.5 14.1 %collective-permute-start.8 = (f32[320,512]{1,0:T(8,128)S(1)}, f32[320,512]{1,0:T(8,128)}, u32[]{:S(2)}, u32[]{:S(2)}) collective-permute-start(f32[320,512]{1,0:T(8,128)S(1)} %collective-permute-done.7.refs_9_.refs_6_), channel_id=1, source_target_pairs={{0,8},{2,10},{3,11},{8,16},{10,18},{11,19},{16,24},{18,26},{19,27}... | collective-permute-start | bytes 1966088 | tf_op jit(solution)/shard_map/ppermute | solution.py:381
  30.6 14.1 %collective-permute-start.4 = (f32[320,512]{1,0:T(8,128)S(1)}, f32[320,512]{1,0:T(8,128)}, u32[]{:S(2)}, u32[]{:S(2)}) collective-permute-start(f32[320,512]{1,0:T(8,128)S(1)} %collective-permute-done.3.refs_2_), channel_id=1, source_target_pairs={{0,4},{2,6},{3,7},{8,0},{10,2},{11,3},{16,8},{18,10},{19,11},{24,1... | collective-permute-start | bytes 1966088 | tf_op jit(solution)/shard_map/ppermute | solution.py:381
  32.5 14.1 %collective-permute-start.2 = (f32[320,512]{1,0:T(8,128)S(1)}, f32[320,512]{1,0:T(8,128)S(1)}, u32[]{:S(2)}, u32[]{:S(2)}) collective-permute-start(f32[320,512]{1,0:T(8,128)S(1)} %collective-permute-done.1.refs_3_), channel_id=1, source_target_pairs={{0,8},{2,10},{3,11},{8,16},{10,18},{11,19},{16,24},{18,26},{19,27}... | collective-permute-start | bytes 1966088 | tf_op jit(solution)/shard_map/ppermute | solution.py:381
  37.6 14.1 %collective-permute-start.12 = (f32[320,512]{1,0:T(8,128)S(1)}, f32[320,512]{1,0:T(8,128)}, u32[]{:S(2)}, u32[]{:S(2)}) collective-permute-start(f32[320,512]{1,0:T(8,128)S(1)} %collective-permute-done.11.refs_12_.refs_9_), channel_id=1, source_target_pairs={{0,4},{2,6},{3,7},{8,0},{10,2},{11,3},{16,8},{18,10},{19,11},{24,1... | collective-permute-start | bytes 1966088 | tf_op jit(solution)/shard_map/ppermute | solution.py:381
  39.7 20.1 %collective-permute-start.9 = (f32[320,512]{1,0:T(8,128)}, f32[320,512]{1,0:T(8,128)}, u32[]{:S(2)}, u32[]{:S(2)}) collective-permute-start(f32[320,512]{1,0:T(8,128)} %collective-permute-done.8.refs_11_.refs_8_), channel_id=1, source_target_pairs={{0,8},{2,10},{3,11},{8,16},{10,18},{11,19},{16,24},{18,26},{19,27}... | collective-permute-start | bytes 1966088 | tf_op jit(solution)/shard_map/ppermute | solution.py:381
  44.8 16.5 %collective-permute-start.5 = (f32[320,512]{1,0:T(8,128)}, f32[320,512]{1,0:T(8,128)}, u32[]{:S(2)}, u32[]{:S(2)}) collective-permute-start(f32[320,512]{1,0:T(8,128)} %collective-permute-done.4.refs_4_), channel_id=1, source_target_pairs={{0,4},{2,6},{3,7},{8,0},{10,2},{11,3},{16,8},{18,10},{19,11},{24,1... | collective-permute-start | bytes 1966088 | tf_op jit(solution)/shard_map/ppermute | solution.py:381
  51.8 20.0 %collective-permute-start.13 = (f32[320,512]{1,0:T(8,128)}, f32[320,512]{1,0:T(8,128)}, u32[]{:S(2)}, u32[]{:S(2)}) collective-permute-start(f32[320,512]{1,0:T(8,128)} %collective-permute-done.12.refs_14_.refs_4_), channel_id=1, source_target_pairs={{0,4},{2,6},{3,7},{8,0},{10,2},{11,3},{16,8},{18,10},{19,11},{24,1... | collective-permute-start | bytes 1966088 | tf_op jit(solution)/shard_map/ppermute | solution.py:381
  55.0 18.4 %collective-permute-start.15 = (f32[320,512]{1,0:T(8,128)}, f32[320,512]{1,0:T(8,128)}, u32[]{:S(2)}, u32[]{:S(2)}) collective-permute-start(f32[320,512]{1,0:T(8,128)} %get-tuple-element.7), channel_id=1, source_target_pairs={{1,9},{9,17},{17,25},{25,29},{29,21},{21,13},{13,5},{5,1}} | collective-permute-start | bytes 1966088 | tf_op jit(solution)/shard_map/ppermute | solution.py:381
  56.5 19.6 %collective-permute-start.6 = (f32[320,512]{1,0:T(8,128)S(1)}, f32[320,512]{1,0:T(8,128)}, u32[]{:S(2)}, u32[]{:S(2)}) collective-permute-start(f32[320,512]{1,0:T(8,128)S(1)} %collective-permute-done.2.refs_5_.refs_0_), channel_id=1, source_target_pairs={{0,8},{2,10},{3,11},{8,16},{10,18},{11,19},{16,24},{18,26},{19,27}... | collective-permute-start | bytes 1966088 | tf_op jit(solution)/shard_map/ppermute | solution.py:381
  59.7 62.8 %collective-permute-start.18 = (f32[320,512]{1,0:T(8,128)}, f32[320,512]{1,0:T(8,128)}, u32[]{:S(2)}, u32[]{:S(2)}) collective-permute-start(f32[320,512]{1,0:T(8,128)} %get-tuple-element.7), channel_id=1, source_target_pairs={{1,5},{9,1},{17,9},{25,17},{29,25},{21,29},{13,21},{5,13}} | collective-permute-start | bytes 1966088 | tf_op jit(solution)/shard_map/ppermute | solution.py:381
  61.3 62.9 %collective-permute-start.22 = (f32[320,512]{1,0:T(8,128)}, f32[320,512]{1,0:T(8,128)}, u32[]{:S(2)}, u32[]{:S(2)}) collective-permute-start(f32[320,512]{1,0:T(8,128)} %get-tuple-element.8), channel_id=1, source_target_pairs={{1,9},{9,17},{17,25},{25,29},{29,21},{21,13},{13,5},{5,1}} | collective-permute-start | bytes 1966088 | tf_op jit(solution)/shard_map/ppermute | solution.py:381
  71.8 53.7 %collective-permute-start.25 = (f32[320,512]{1,0:T(8,128)}, f32[320,512]{1,0:T(8,128)}, u32[]{:S(2)}, u32[]{:S(2)}) collective-permute-start(f32[320,512]{1,0:T(8,128)} %get-tuple-element.8), channel_id=1, source_target_pairs={{1,5},{9,1},{17,9},{25,17},{29,25},{21,29},{13,21},{5,13}} | collective-permute-start | bytes 1966088 | tf_op jit(solution)/shard_map/ppermute | solution.py:381
  73.4 53.7 %collective-permute-start.16 = (f32[320,512]{1,0:T(8,128)}, f32[320,512]{1,0:T(8,128)}, u32[]{:S(2)}, u32[]{:S(2)}) collective-permute-start(f32[320,512]{1,0:T(8,128)} %collective-permute-done.15.refs_11_), channel_id=1, source_target_pairs={{1,9},{9,17},{17,25},{25,29},{29,21},{21,13},{13,5},{5,1}} | collective-permute-start | bytes 1966088 | tf_op jit(solution)/shard_map/ppermute | solution.py:381
  90.4 44.7 %collective-permute-start.33 = (f32[512,512]{1,0:T(8,128)}, f32[512,512]{1,0:T(8,128)S(1)}, u32[]{:S(2)}, u32[]{:S(2)}) collective-permute-start(f32[512,512]{1,0:T(8,128)} %shard_map.40.refs_25_.refs_17_), channel_id=1, source_target_pairs={{0,2},{4,6},{8,10},{12,14},{16,18},{20,22},{24,26},{28,30}} | collective-permute-start | bytes 3145736 | tf_op jit(solution)/shard_map/ppermute | solution.py:404
  124.2 22.1 %collective-permute-start.30 = (f32[512,512]{1,0:T(8,128)S(1)}, f32[512,512]{1,0:T(8,128)S(1)}, u32[]{:S(2)}, u32[]{:S(2)}) collective-permute-start(f32[512,512]{1,0:T(8,128)S(1)} %copy-done.1), channel_id=1, source_target_pairs={{0,2},{4,6},{8,10},{12,14},{16,18},{20,22},{24,26},{28,30}} | collective-permute-start | bytes 3145736 | tf_op jit(solution)/shard_map/ppermute | solution.py:404
  127.1 21.4 %collective-permute-start.32 = (f32[512,512]{1,0:T(8,128)}, f32[512,512]{1,0:T(8,128)S(1)}, u32[]{:S(2)}, u32[]{:S(2)}) collective-permute-start(f32[512,512]{1,0:T(8,128)} %shard_map.40.refs_25_.refs_17_), channel_id=1, source_target_pairs={{0,1},{4,5},{8,9},{12,13},{16,17},{20,21},{24,25},{28,29}} | collective-permute-start | bytes 3145736 | tf_op jit(solution)/shard_map/ppermute | solution.py:404
  128.4 18.5 %collective-permute-start.26 = (f32[320,512]{1,0:T(8,128)}, f32[320,512]{1,0:T(8,128)S(1)}, u32[]{:S(2)}, u32[]{:S(2)}) collective-permute-start(f32[320,512]{1,0:T(8,128)} %collective-permute-done.25.refs_17_), channel_id=1, source_target_pairs={{1,5},{9,1},{17,9},{25,17},{29,25},{21,29},{13,21},{5,13}} | collective-permute-start | bytes 1966088 | tf_op jit(solution)/shard_map/ppermute | solution.py:381
  129.2 20.9 %collective-permute-start.29 = (f32[512,512]{1,0:T(8,128)S(1)}, f32[512,512]{1,0:T(8,128)S(1)}, u32[]{:S(2)}, u32[]{:S(2)}) collective-permute-start(f32[512,512]{1,0:T(8,128)S(1)} %copy-done.1), channel_id=1, source_target_pairs={{0,1},{4,5},{8,9},{12,13},{16,17},{20,21},{24,25},{28,29}} | collective-permute-start | bytes 3145736 | tf_op jit(solution)/shard_map/ppermute | solution.py:404
  135.1 17.8 %collective-permute-start.34 = (f32[512,512]{1,0:T(8,128)S(1)}, f32[512,512]{1,0:T(8,128)S(1)}, u32[]{:S(2)}, u32[]{:S(2)}) collective-permute-start(f32[512,512]{1,0:T(8,128)S(1)} %collective-permute-done.33.refs_27_.refs_19_), channel_id=1, source_target_pairs={{2,3},{6,7},{10,11},{14,15},{18,19},{22,23},{26,27},{30,31}} | collective-permute-start | bytes 3145736 | tf_op jit(solution)/shard_map/ppermute | solution.py:404
  150.0 19.1 %collective-permute-start.20 = (f32[320,512]{1,0:T(8,128)}, f32[320,512]{1,0:T(8,128)S(1)}, u32[]{:S(2)}, u32[]{:S(2)}) collective-permute-start(f32[320,512]{1,0:T(8,128)} %collective-permute-done.19.refs_14_), channel_id=1, source_target_pairs={{1,5},{9,1},{17,9},{25,17},{29,25},{21,29},{13,21},{5,13}} | collective-permute-start | bytes 1966088 | tf_op jit(solution)/shard_map/ppermute | solution.py:381
  150.7 18.4 %collective-permute-start.24 = (f32[320,512]{1,0:T(8,128)}, f32[320,512]{1,0:T(8,128)S(1)}, u32[]{:S(2)}, u32[]{:S(2)}) collective-permute-start(f32[320,512]{1,0:T(8,128)} %collective-permute-done.23.refs_18_), channel_id=1, source_target_pairs={{1,9},{9,17},{17,25},{25,29},{29,21},{21,13},{13,5},{5,1}} | collective-permute-start | bytes 1966088 | tf_op jit(solution)/shard_map/ppermute | solution.py:381
  151.5 17.7 %collective-permute-start.21 = (f32[320,512]{1,0:T(8,128)}, f32[320,512]{1,0:T(8,128)}, u32[]{:S(2)}, u32[]{:S(2)}) collective-permute-start(f32[320,512]{1,0:T(8,128)} %collective-permute-done.17.refs_6_), channel_id=1, source_target_pairs={{1,9},{9,17},{17,25},{25,29},{29,21},{21,13},{13,5},{5,1}} | collective-permute-start | bytes 1966088 | tf_op jit(solution)/shard_map/ppermute | solution.py:381
  154.0 15.2 %collective-permute-start.28 = (f32[320,512]{1,0:T(8,128)}, f32[320,512]{1,0:T(8,128)}, u32[]{:S(2)}, u32[]{:S(2)}) collective-permute-start(f32[320,512]{1,0:T(8,128)} %collective-permute-done.27.refs_10_), channel_id=1, source_target_pairs={{1,5},{9,1},{17,9},{25,17},{29,25},{21,29},{13,21},{5,13}} | collective-permute-start | bytes 1966088 | tf_op jit(solution)/shard_map/ppermute | solution.py:381
  (32 other events, 644.3 us)

commit v2 on v0

--- a/solution.py
+++ b/solution.py
@@ -8,7 +8,7 @@
 from jax.experimental.pallas import tpu as pltpu
 from jax.sharding import PartitionSpec as P
 
-VMEM_BYTES = 40 * 1024 * 1024
+VMEM_BYTES = 52 * 1024 * 1024
 LANES = 128
 RING_LIMIT = 16
 
@@ -63,8 +63,11 @@
     return inverses
 
 
-def prepare_kernel(rows, block, depth, me, place, factor, out):
+def prepare_kernel(rows, block, depth, me, place, source, out, factor, sem):
     width = depth // 2
+    load = pltpu.make_async_copy(source, factor, sem)
+    load.start()
+    load.wait()
     out[...] = factor[:, width:]
     first = me[0] * rows
 
@@ -94,9 +97,10 @@
     return pl.pallas_call(
         functools.partial(prepare_kernel, rows, block, depth),
         out_shape=jax.ShapeDtypeStruct((rows, depth // 2), jnp.float32),
-        in_specs=[SCALARS] * 2 + [WHOLE],
+        in_specs=[SCALARS] * 2 + [ANY],
         out_specs=WHOLE,
-        compiler_params=pltpu.CompilerParams(vmem_limit_bytes=VMEM_BYTES // 2),
+        scratch_shapes=[pltpu.VMEM((rows, depth), jnp.float32), pltpu.SemaphoreType.DMA],
+        compiler_params=pltpu.CompilerParams(vmem_limit_bytes=VMEM_BYTES),
         cost_estimate=pl.CostEstimate(
             flops=24 * rows * block * block, bytes_accessed=6 * rows * depth, transcendentals=0
         ),
@@ -212,7 +216,7 @@
             pltpu.SemaphoreType.DMA((2, pieces)),
             pltpu.SemaphoreType.DMA,
         ],
-        compiler_params=pltpu.CompilerParams(vmem_limit_bytes=VMEM_BYTES // 2),
+        compiler_params=pltpu.CompilerParams(vmem_limit_bytes=VMEM_BYTES),
         cost_estimate=pl.CostEstimate(
             flops=6 * (panel + 1) * width * width * columns,
             bytes_accessed=12 * width * columns,
@@ -327,6 +331,21 @@
     )(ids, place, *held, current, *solved)
 
 
+def gate_kernel(block, token, out):
+    pass
+
+
+def gate(block, token):
+    return pl.pallas_call(
+        gate_kernel,
+        out_shape=jax.ShapeDtypeStruct(block.shape, block.dtype),
+        in_specs=[ANY] * 2,
+        out_specs=ANY,
+        input_output_aliases={0: 0},
+        compiler_params=pltpu.CompilerParams(vmem_limit_bytes=VMEM_BYTES),
+    )(block, token)
+
+
 def gather_pieces(panels, count):
     me = lax.axis_index("src")
     if count % 2 or count > RING_LIMIT:
@@ -356,13 +375,23 @@
     return held, ids
 
 
-def spread_rows(block, count):
+def spread_far(block, count):
     found = {0: block}
     stride = count // 2
-    while stride:
+    while stride > 1:
         for r in list(found):
             found[r + stride] = lax.ppermute(found[r], "row", [(r, r + stride)])
         stride //= 2
+    return found
+
+
+def spread_near(found, count, token=None):
+    found = dict(found)
+    for r in sorted(found):
+        if r and token is not None:
+            found[r] = gate(found[r], token)
+        if r + 1 < count:
+            found[r + 1] = lax.ppermute(found[r], "row", [(r, r + 1)])
     return [found[r] for r in range(count)]
 
 
@@ -380,8 +409,10 @@
         ids = jnp.stack(ids).astype(jnp.int32)
         first = solve_panel(0, ids, place, held, right_side, [], width, block)
         second = solve_panel(1, ids, place, held, right_side, [first], width, block)
-        current = update(0, ids, place, held[0], right_side, spread_rows(first, places), width)
-        return update(1, ids, place, held[1], current, spread_rows(second, places), width)
+        near = spread_near(spread_far(first, places), places)
+        far = spread_far(second, places)
+        current = update(0, ids, place, held[0], right_side, near, width)
+        return update(1, ids, place, held[1], current, spread_near(far, places, current), width)
 
     placed = (P(("row", "src"), None), P("row", "src"))
     return jax.shard_map(

time: 159 us -> 163 us (1.025); the launches traced: 158 us -> 160 us
  Pallas kernels: 29.5 us -> 34.2 us
  local copies, waits for them, and re-layouts: 9.77 us -> 7.45 us
    pallas_call x2, Pallas kernels: 8.94 us -> 13.4 us  [solve_panel(): pl.pallas_call(functools.partial(solve_kernel, pieces, rows, width, chunk...]
    unnamed x22 -> x34, local copies, waits for them, and re-layouts: 9.65 us -> 7.31 us
    ppermute x6, waiting for transfers between devices: 13.2 us -> 11.2 us  [the longest x2 11.2 us: spread_far(): found[r + stride] = lax.ppermute(found[r], 'row', [(r, r + stride)])]
    ppermute x14, waiting for transfers between devices: 83.1 us -> 84.8 us  [gather_pieces(): going[k][way] = lax.ppermute(going[k][way], 'src', pairs)]
  transfers between devices with their start and end apart: 20 -> 20, of which waited for: 13 -> 12; matrix products, arithmetic and copies ran while one was open for 0% -> 0% of each run, Pallas kernels for 9% -> 11%
where the time goes in v2:
time: 163 us; the launch traced here: 160 us
  waiting for transfers between devices  96 us (59%)
  Pallas kernels  34.2 us (21%)
  starting transfers between devices  22.3 us (14%)
  local copies, waits for them, and re-layouts  7.45 us (5%)
    ppermute x14, waiting for transfers between devices, gather_pieces(): going[k][way] = lax.ppermute(going[k][way], 'src', pairs)  84.8 us
    pallas_call x2, Pallas kernels, update(): pl.pallas_call(functools.partial(update_kernel, pieces, rows, width, tile...  18.1 us
    ppermute x14, starting transfers between devices, gather_pieces(): going[k][way] = lax.ppermute(going[k][way], 'src', pairs)  15.3 us
    pallas_call x2, Pallas kernels, solve_panel(): pl.pallas_call(functools.partial(solve_kernel, pieces, rows, width, chunk...  13.4 us
    ppermute x2, waiting for transfers between devices, spread_far(): found[r + stride] = lax.ppermute(found[r], 'row', [(r, r + stride)])  11.2 us
    unnamed x34, local copies, waits for them, and re-layouts  7.31 us
    ppermute x4, starting transfers between devices, spread_near(): found[r + 1] = lax.ppermute(found[r], 'row', [(r, r + 1)])  4.29 us
  transfers between devices with their start and end apart: 20, of which 12 were waited for; matrix products, arithmetic and copies ran while one was open for 0% of the time, Pallas kernels for 11%

profile of v2, /device:TPU:0, one launch (start us, length us, event | category | flops | bytes accessed | tf_op | source)
XLA Modules:
  0.0 160.2 jit_solution(16439918218619759996)
XLA Ops:
  1.3 2.7 %shard_map.28.refs_8_.refs_0_ = f32[320,512]{1,0:T(8,128)S(1)} custom-call(s32[1]{0:T(128)} %bitcast.me, s32[1]{0:T(128)} %bitcast.8.place, f32[320,1024]{1,0:T(8,128)S(1)} %copy-done.9), custom_call_target="tpu_custom_call" | custom-call | flops 31457280 | bytes 1966080 | tf_op jit(solution)/shard_map/pallas_call | solution.py:97
  4.0 3.0 %collective-permute-start.1 = (f32[320,512]{1,0:T(8,128)S(1)}, f32[320,512]{1,0:T(8,128)S(1)}, u32[]{:S(2)}, u32[]{:S(2)}) collective-permute-start(f32[320,512]{1,0:T(8,128)S(1)} %shard_map.28.refs_8_.refs_0_), channel_id=1, source_target_pairs={{8,0},{16,8},{24,16},{28,24},{20,28},{12,20},{4,12},{0,4},{9,1},{1... | collective-permute-start | bytes 1966088 | tf_op jit(solution)/shard_map/ppermute | solution.py:372
  7.2 2.0 %collective-permute-start = (f32[320,512]{1,0:T(8,128)S(1)}, f32[320,512]{1,0:T(8,128)S(1)}, u32[]{:S(2)}, u32[]{:S(2)}) collective-permute-start(f32[320,512]{1,0:T(8,128)S(1)} %shard_map.28.refs_8_.refs_0_), channel_id=1, source_target_pairs={{0,8},{8,16},{16,24},{24,28},{28,20},{20,12},{12,4},{4,0},{1,9},{9... | collective-permute-start | bytes 1966088 | tf_op jit(solution)/shard_map/ppermute | solution.py:372
  9.2 13.5 %collective-permute-done.1.refs_10_.refs_2_ = f32[320,512]{1,0:T(8,128)S(1)} collective-permute-done((f32[320,512]{1,0:T(8,128)S(1)}, f32[320,512]{1,0:T(8,128)S(1)}, u32[]{:S(2)}, u32[]{:S(2)}) %collective-permute-start.1) | collective-permute-done | bytes 655392 | tf_op jit(solution)/shard_map/ppermute | solution.py:372
  22.7 1.9 %collective-permute-start.3 = (f32[320,512]{1,0:T(8,128)S(1)}, f32[320,512]{1,0:T(8,128)S(1)}, u32[]{:S(2)}, u32[]{:S(2)}) collective-permute-start(f32[320,512]{1,0:T(8,128)S(1)} %collective-permute-done.1.refs_10_.refs_2_), channel_id=1, source_target_pairs={{8,0},{16,8},{24,16},{28,24},{20,28},{12,20},{4,12},{0,4},{9,1},{1... | collective-permute-start | bytes 1966088 | tf_op jit(solution)/shard_map/ppermute | solution.py:372
  24.9 13.9 %collective-permute-done.refs_9_.refs_1_ = f32[320,512]{1,0:T(8,128)S(1)} collective-permute-done((f32[320,512]{1,0:T(8,128)S(1)}, f32[320,512]{1,0:T(8,128)S(1)}, u32[]{:S(2)}, u32[]{:S(2)}) %collective-permute-start) | collective-permute-done | bytes 655392 | tf_op jit(solution)/shard_map/ppermute | solution.py:372
  38.9 1.9 %collective-permute-start.10 = (f32[320,512]{1,0:T(8,128)S(1)}, f32[320,512]{1,0:T(8,128)}, u32[]{:S(2)}, u32[]{:S(2)}) collective-permute-start(f32[320,512]{1,0:T(8,128)S(1)} %collective-permute-done.8.refs_2_), channel_id=1, source_target_pairs={{8,0},{16,8},{24,16},{28,24},{20,28},{12,20},{4,12},{0,4},{9,1},{1... | collective-permute-start | bytes 1966088 | tf_op jit(solution)/shard_map/ppermute | solution.py:372
  41.7 9.1 %collective-permute-done.3.refs_12_.refs_4_ = f32[320,512]{1,0:T(8,128)S(1)} collective-permute-done((f32[320,512]{1,0:T(8,128)S(1)}, f32[320,512]{1,0:T(8,128)S(1)}, u32[]{:S(2)}, u32[]{:S(2)}) %collective-permute-start.3) | collective-permute-done | bytes 655392 | tf_op jit(solution)/shard_map/ppermute | solution.py:372
  50.8 1.9 %collective-permute-start.5 = (f32[320,512]{1,0:T(8,128)S(1)}, f32[320,512]{1,0:T(8,128)}, u32[]{:S(2)}, u32[]{:S(2)}) collective-permute-start(f32[320,512]{1,0:T(8,128)S(1)} %collective-permute-done.3.refs_12_.refs_4_), channel_id=1, source_target_pairs={{8,0},{16,8},{24,16},{28,24},{20,28},{12,20},{4,12},{0,4},{9,1},{1... | collective-permute-start | bytes 1966088 | tf_op jit(solution)/shard_map/ppermute | solution.py:372
  53.0 14.0 %collective-permute-done.2.refs_11_.refs_3_ = f32[320,512]{1,0:T(8,128)} collective-permute-done((f32[320,512]{1,0:T(8,128)S(1)}, f32[320,512]{1,0:T(8,128)}, u32[]{:S(2)}, u32[]{:S(2)}) %collective-permute-start.2) | collective-permute-done | bytes 655392 | tf_op jit(solution)/shard_map/ppermute | solution.py:372
  67.1 1.9 %collective-permute-start.12 = (f32[320,512]{1,0:T(8,128)}, f32[320,512]{1,0:T(8,128)}, u32[]{:S(2)}, u32[]{:S(2)}) collective-permute-start(f32[320,512]{1,0:T(8,128)} %collective-permute-done.10.refs_4_), channel_id=1, source_target_pairs={{8,0},{16,8},{24,16},{28,24},{20,28},{12,20},{4,12},{0,4},{9,1},{1... | collective-permute-start | bytes 1966088 | tf_op jit(solution)/shard_map/ppermute | solution.py:372
  69.0 10.0 %collective-permute-done.5.refs_14_.refs_6_ = f32[320,512]{1,0:T(8,128)} collective-permute-done((f32[320,512]{1,0:T(8,128)S(1)}, f32[320,512]{1,0:T(8,128)}, u32[]{:S(2)}, u32[]{:S(2)}) %collective-permute-start.5) | collective-permute-done | bytes 655392 | tf_op jit(solution)/shard_map/ppermute | solution.py:372
  79.0 1.9 %collective-permute-start.6 = (f32[320,512]{1,0:T(8,128)}, f32[320,512]{1,0:T(8,128)}, u32[]{:S(2)}, u32[]{:S(2)}) collective-permute-start(f32[320,512]{1,0:T(8,128)} %collective-permute-done.5.refs_14_.refs_6_), channel_id=1, source_target_pairs={{8,0},{16,8},{24,16},{28,24},{20,28},{12,20},{4,12},{0,4},{9,1},{1... | collective-permute-start | bytes 1966088 | tf_op jit(solution)/shard_map/ppermute | solution.py:372
  81.2 13.9 %collective-permute-done.4.refs_13_.refs_5_ = f32[320,512]{1,0:T(8,128)} collective-permute-done((f32[320,512]{1,0:T(8,128)}, f32[320,512]{1,0:T(8,128)}, u32[]{:S(2)}, u32[]{:S(2)}) %collective-permute-start.4) | collective-permute-done | bytes 655392 | tf_op jit(solution)/shard_map/ppermute | solution.py:372
  95.1 8.5 %collective-permute-done.6.refs_15_.refs_7_ = f32[320,512]{1,0:T(8,128)} collective-permute-done((f32[320,512]{1,0:T(8,128)}, f32[320,512]{1,0:T(8,128)}, u32[]{:S(2)}, u32[]{:S(2)}) %collective-permute-start.6) | collective-permute-done | bytes 655392 | tf_op jit(solution)/shard_map/ppermute | solution.py:372
  103.7 1.5 collective-permute-done.13.refs_7_
  106.2 5.6 %shard_map.29.refs_9_.refs_17_ = f32[512,512]{1,0:T(8,128)} custom-call(s32[8]{0:T(128)S(1)} %stack.35.ids, s32[1]{0:T(128)} %bitcast.8.place, f32[320,512]{1,0:T(8,128)S(1)} %slice.3.refs_0_, f32[320,512]{1,0:T(8,128)S(1)} %collective-permute-done.7.refs_1_, f32[320,512]{1,0:T(8,128)S(1)} %copy-done.7, f32[320,512]{1,0:T(8,128)} %copy-done.11, ...), custom_call_target="tpu_custom_call" | custom-call | flops 805306368 | bytes 3145728 | tf_op jit(solution)/shard_map/pallas_call | solution.py:209
  111.8 1.4 collective-permute-start.15
  113.2 1.4 collective-permute-start.14
  114.6 11.2 %collective-permute-done.15.refs_11_ = f32[512,512]{1,0:T(8,128)S(1)} collective-permute-done((f32[512,512]{1,0:T(8,128)}, f32[512,512]{1,0:T(8,128)S(1)}, u32[]{:S(2)}, u32[]{:S(2)}) %collective-permute-start.15) | collective-permute-done | bytes 1048608 | tf_op jit(solution)/shard_map/ppermute | solution.py:383
  126.5 7.8 %shard_map.31.refs_9_ = f32[512,512]{1,0:T(8,128)} custom-call(s32[8]{0:T(128)S(1)} %stack.35.ids, s32[1]{0:T(128)} %bitcast.8.place, f32[320,512]{1,0:T(8,128)S(1)} %slice.3.refs_0_, f32[320,512]{1,0:T(8,128)S(1)} %collective-permute-done.7.refs_1_, f32[320,512]{1,0:T(8,128)S(1)} %copy-done.7, f32[320,512]{1,0:T(8,128)} %copy-done.11, ...), custom_call_target="tpu_custom_call" | custom-call | flops 1610612736 | bytes 3145728 | tf_op jit(solution)/shard_map/pallas_call | solution.py:209
  135.7 1.4 collective-permute-start.17
  139.2 9.0 %shard_map.30.token.refs_8_ = f32[2560,512]{1,0:T(8,128)} custom-call(s32[8]{0:T(128)S(1)} %stack.35.ids, s32[1]{0:T(128)} %bitcast.8.place, f32[320,512]{1,0:T(8,128)S(1)} %slice.3.refs_0_, f32[320,512]{1,0:T(8,128)S(1)} %collective-permute-done.7.refs_1_, f32[320,512]{1,0:T(8,128)S(1)} %copy-done.7, f32[320,512]{1,0:T(8,128)} %copy-done.11, ...), custom_call_target="tpu_custom_call" | custom-call | flops 4026531840 | bytes 15728640 | tf_op jit(solution)/shard_map/pallas_call | solution.py:308
  151.2 9.1 %shard_map.33 = f32[2560,512]{1,0:T(8,128)} custom-call(s32[8]{0:T(128)S(1)} %stack.35.ids, s32[1]{0:T(128)} %bitcast.8.place, f32[320,512]{1,0:T(8,128)S(1)} %copy-done.1, f32[320,512]{1,0:T(8,128)S(1)} %copy-done.5, f32[320,512]{1,0:T(8,128)S(1)} %copy-done.3, f32[320,512]{1,0:T(8,128)} %collective-permute-done.2.refs_11_.refs_3_, f32[320,512]{1,0:T(8,128)} %copy-done.10, ...), custom_call_target="tpu_custom_call" | custom-call | flops 4026531840 | bytes 15728640 | tf_op jit(solution)/shard_map/pallas_call | solution.py:308
  (58 shorter events, 11.4 us)
Async XLA Ops:
  4.0 101.1 %copy-start = (f32[320,512]{1,0:T(8,128)}, f32[320,512]{1,0:T(8,128)S(1)}, u32[]{:S(2)}) copy-start(f32[320,512]{1,0:T(8,128)S(1)} %shard_map.28.refs_8_.refs_0_) | copy-start | bytes 1966084
  4.0 18.7 %collective-permute-start.1 = (f32[320,512]{1,0:T(8,128)S(1)}, f32[320,512]{1,0:T(8,128)S(1)}, u32[]{:S(2)}, u32[]{:S(2)}) collective-permute-start(f32[320,512]{1,0:T(8,128)S(1)} %shard_map.28.refs_8_.refs_0_), channel_id=1, source_target_pairs={{8,0},{16,8},{24,16},{28,24},{20,28},{12,20},{4,12},{0,4},{9,1},{1... | collective-permute-start | bytes 1966088 | tf_op jit(solution)/shard_map/ppermute | solution.py:372
  7.1 17.7 %collective-permute-start.7 = (f32[320,512]{1,0:T(8,128)S(1)}, f32[320,512]{1,0:T(8,128)S(1)}, u32[]{:S(2)}, u32[]{:S(2)}) collective-permute-start(f32[320,512]{1,0:T(8,128)S(1)} %slice.3.refs_0_), channel_id=1, source_target_pairs={{0,8},{8,16},{16,24},{24,28},{28,20},{20,12},{12,4},{4,0},{1,9},{9... | collective-permute-start | bytes 1966088 | tf_op jit(solution)/shard_map/ppermute | solution.py:372
  7.2 31.6 %collective-permute-start = (f32[320,512]{1,0:T(8,128)S(1)}, f32[320,512]{1,0:T(8,128)S(1)}, u32[]{:S(2)}, u32[]{:S(2)}) collective-permute-start(f32[320,512]{1,0:T(8,128)S(1)} %shard_map.28.refs_8_.refs_0_), channel_id=1, source_target_pairs={{0,8},{8,16},{16,24},{24,28},{28,20},{20,12},{12,4},{4,0},{1,9},{9... | collective-permute-start | bytes 1966088 | tf_op jit(solution)/shard_map/ppermute | solution.py:372
  9.2 29.7 %collective-permute-start.8 = (f32[320,512]{1,0:T(8,128)S(1)}, f32[320,512]{1,0:T(8,128)S(1)}, u32[]{:S(2)}, u32[]{:S(2)}) collective-permute-start(f32[320,512]{1,0:T(8,128)S(1)} %slice.3.refs_0_), channel_id=1, source_target_pairs={{8,0},{16,8},{24,16},{28,24},{20,28},{12,20},{4,12},{0,4},{9,1},{1... | collective-permute-start | bytes 1966088 | tf_op jit(solution)/shard_map/ppermute | solution.py:372
  22.7 82.4 %copy-start.2 = (f32[320,512]{1,0:T(8,128)}, f32[320,512]{1,0:T(8,128)S(1)}, u32[]{:S(2)}) copy-start(f32[320,512]{1,0:T(8,128)S(1)} %collective-permute-done.1.refs_10_.refs_2_) | copy-start | bytes 1966084
  22.7 28.1 %collective-permute-start.3 = (f32[320,512]{1,0:T(8,128)S(1)}, f32[320,512]{1,0:T(8,128)S(1)}, u32[]{:S(2)}, u32[]{:S(2)}) collective-permute-start(f32[320,512]{1,0:T(8,128)S(1)} %collective-permute-done.1.refs_10_.refs_2_), channel_id=1, source_target_pairs={{8,0},{16,8},{24,16},{28,24},{20,28},{12,20},{4,12},{0,4},{9,1},{1... | collective-permute-start | bytes 1966088 | tf_op jit(solution)/shard_map/ppermute | solution.py:372
  24.8 28.1 %collective-permute-start.9 = (f32[320,512]{1,0:T(8,128)S(1)}, f32[320,512]{1,0:T(8,128)S(1)}, u32[]{:S(2)}, u32[]{:S(2)}) collective-permute-start(f32[320,512]{1,0:T(8,128)S(1)} %collective-permute-done.7.refs_1_), channel_id=1, source_target_pairs={{0,8},{8,16},{16,24},{24,28},{28,20},{20,12},{12,4},{4,0},{1,9},{9... | collective-permute-start | bytes 1966088 | tf_op jit(solution)/shard_map/ppermute | solution.py:372
  38.8 66.3 %copy-start.4 = (f32[320,512]{1,0:T(8,128)}, f32[320,512]{1,0:T(8,128)S(1)}, u32[]{:S(2)}) copy-start(f32[320,512]{1,0:T(8,128)S(1)} %collective-permute-done.refs_9_.refs_1_) | copy-start | bytes 1966084
  38.8 28.2 %collective-permute-start.2 = (f32[320,512]{1,0:T(8,128)S(1)}, f32[320,512]{1,0:T(8,128)}, u32[]{:S(2)}, u32[]{:S(2)}) collective-permute-start(f32[320,512]{1,0:T(8,128)S(1)} %collective-permute-done.refs_9_.refs_1_), channel_id=1, source_target_pairs={{0,8},{8,16},{16,24},{24,28},{28,20},{20,12},{12,4},{4,0},{1,9},{9... | collective-permute-start | bytes 1966088 | tf_op jit(solution)/shard_map/ppermute | solution.py:372
  38.9 28.2 %collective-permute-start.10 = (f32[320,512]{1,0:T(8,128)S(1)}, f32[320,512]{1,0:T(8,128)}, u32[]{:S(2)}, u32[]{:S(2)}) collective-permute-start(f32[320,512]{1,0:T(8,128)S(1)} %collective-permute-done.8.refs_2_), channel_id=1, source_target_pairs={{8,0},{16,8},{24,16},{28,24},{20,28},{12,20},{4,12},{0,4},{9,1},{1... | collective-permute-start | bytes 1966088 | tf_op jit(solution)/shard_map/ppermute | solution.py:372
  50.8 28.2 %collective-permute-start.5 = (f32[320,512]{1,0:T(8,128)S(1)}, f32[320,512]{1,0:T(8,128)}, u32[]{:S(2)}, u32[]{:S(2)}) collective-permute-start(f32[320,512]{1,0:T(8,128)S(1)} %collective-permute-done.3.refs_12_.refs_4_), channel_id=1, source_target_pairs={{8,0},{16,8},{24,16},{28,24},{20,28},{12,20},{4,12},{0,4},{9,1},{1... | collective-permute-start | bytes 1966088 | tf_op jit(solution)/shard_map/ppermute | solution.py:372
  52.9 26.2 %copy-start.11 = (f32[320,512]{1,0:T(8,128)}, f32[320,512]{1,0:T(8,128)S(1)}, u32[]{:S(2)}) copy-start(f32[320,512]{1,0:T(8,128)S(1)} %collective-permute-done.9.refs_3_) | copy-start | bytes 1966084
  52.9 28.2 %collective-permute-start.11 = (f32[320,512]{1,0:T(8,128)S(1)}, f32[320,512]{1,0:T(8,128)}, u32[]{:S(2)}, u32[]{:S(2)}) collective-permute-start(f32[320,512]{1,0:T(8,128)S(1)} %collective-permute-done.9.refs_3_), channel_id=1, source_target_pairs={{0,8},{8,16},{16,24},{24,28},{28,20},{20,12},{12,4},{4,0},{1,9},{9... | collective-permute-start | bytes 1966088 | tf_op jit(solution)/shard_map/ppermute | solution.py:372
  67.0 28.1 %collective-permute-start.4 = (f32[320,512]{1,0:T(8,128)}, f32[320,512]{1,0:T(8,128)}, u32[]{:S(2)}, u32[]{:S(2)}) collective-permute-start(f32[320,512]{1,0:T(8,128)} %collective-permute-done.2.refs_11_.refs_3_), channel_id=1, source_target_pairs={{0,8},{8,16},{16,24},{24,28},{28,20},{20,12},{12,4},{4,0},{1,9},{9... | collective-permute-start | bytes 1966088 | tf_op jit(solution)/shard_map/ppermute | solution.py:372
  67.1 28.0 %collective-permute-start.12 = (f32[320,512]{1,0:T(8,128)}, f32[320,512]{1,0:T(8,128)}, u32[]{:S(2)}, u32[]{:S(2)}) collective-permute-start(f32[320,512]{1,0:T(8,128)} %collective-permute-done.10.refs_4_), channel_id=1, source_target_pairs={{8,0},{16,8},{24,16},{28,24},{20,28},{12,20},{4,12},{0,4},{9,1},{1... | collective-permute-start | bytes 1966088 | tf_op jit(solution)/shard_map/ppermute | solution.py:372
  79.0 24.6 %collective-permute-start.6 = (f32[320,512]{1,0:T(8,128)}, f32[320,512]{1,0:T(8,128)}, u32[]{:S(2)}, u32[]{:S(2)}) collective-permute-start(f32[320,512]{1,0:T(8,128)} %collective-permute-done.5.refs_14_.refs_6_), channel_id=1, source_target_pairs={{8,0},{16,8},{24,16},{28,24},{20,28},{12,20},{4,12},{0,4},{9,1},{1... | collective-permute-start | bytes 1966088 | tf_op jit(solution)/shard_map/ppermute | solution.py:372
  81.1 24.1 %collective-permute-start.13 = (f32[320,512]{1,0:T(8,128)}, f32[320,512]{1,0:T(8,128)}, u32[]{:S(2)}, u32[]{:S(2)}) collective-permute-start(f32[320,512]{1,0:T(8,128)} %collective-permute-done.11.refs_5_), channel_id=1, source_target_pairs={{0,8},{8,16},{16,24},{24,28},{28,20},{20,12},{12,4},{4,0},{1,9},{9... | collective-permute-start | bytes 1966088 | tf_op jit(solution)/shard_map/ppermute | solution.py:372
  111.8 13.9 %collective-permute-start.15 = (f32[512,512]{1,0:T(8,128)}, f32[512,512]{1,0:T(8,128)S(1)}, u32[]{:S(2)}, u32[]{:S(2)}) collective-permute-start(f32[512,512]{1,0:T(8,128)} %shard_map.29.refs_9_.refs_17_), channel_id=1, source_target_pairs={{0,2},{4,6},{8,10},{12,14},{16,18},{20,22},{24,26},{28,30}} | collective-permute-start | bytes 3145736 | tf_op jit(solution)/shard_map/ppermute | solution.py:383
  113.2 23.9 %collective-permute-start.14 = (f32[512,512]{1,0:T(8,128)}, f32[512,512]{1,0:T(8,128)S(1)}, u32[]{:S(2)}, u32[]{:S(2)}) collective-permute-start(f32[512,512]{1,0:T(8,128)} %shard_map.29.refs_9_.refs_17_), channel_id=1, source_target_pairs={{0,1},{4,5},{8,9},{12,13},{16,17},{20,21},{24,25},{28,29}} | collective-permute-start | bytes 3145736 | tf_op jit(solution)/shard_map/ppermute | solution.py:394
  125.8 11.3 %collective-permute-start.16 = (f32[512,512]{1,0:T(8,128)S(1)}, f32[512,512]{1,0:T(8,128)S(1)}, u32[]{:S(2)}, u32[]{:S(2)}) collective-permute-start(f32[512,512]{1,0:T(8,128)S(1)} %collective-permute-done.15.refs_11_), channel_id=1, source_target_pairs={{2,3},{6,7},{10,11},{14,15},{18,19},{22,23},{26,27},{30,31}} | collective-permute-start | bytes 3145736 | tf_op jit(solution)/shard_map/ppermute | solution.py:394
  134.4 13.9 %collective-permute-start.18 = (f32[512,512]{1,0:T(8,128)}, f32[512,512]{1,0:T(8,128)S(1)}, u32[]{:S(2)}, u32[]{:S(2)}) collective-permute-start(f32[512,512]{1,0:T(8,128)} %shard_map.31.refs_9_), channel_id=1, source_target_pairs={{0,2},{4,6},{8,10},{12,14},{16,18},{20,22},{24,26},{28,30}} | collective-permute-start | bytes 3145736 | tf_op jit(solution)/shard_map/ppermute | solution.py:383
  135.7 13.4 %collective-permute-start.17 = (f32[512,512]{1,0:T(8,128)}, f32[512,512]{1,0:T(8,128)S(1)}, u32[]{:S(2)}, u32[]{:S(2)}) collective-permute-start(f32[512,512]{1,0:T(8,128)} %shard_map.31.refs_9_), channel_id=1, source_target_pairs={{0,1},{4,5},{8,9},{12,13},{16,17},{20,21},{24,25},{28,29}} | collective-permute-start | bytes 3145736 | tf_op jit(solution)/shard_map/ppermute | solution.py:394
  148.3 0.9 collective-permute-start.19
  (13 other events, 42.0 us)

commit v3 on v1

--- a/solution.py
+++ b/solution.py
@@ -8,10 +8,10 @@
 from jax.experimental.pallas import tpu as pltpu
 from jax.sharding import PartitionSpec as P
 
-VMEM_BYTES = 60 * 1024 * 1024
+VMEM_BYTES = 52 * 1024 * 1024
 LANES = 128
+SHORT = pl.CostEstimate(flops=1000, bytes_accessed=1000, transcendentals=0)
 RING_LIMIT = 16
-TOKEN_STEP = 2
 
 ANY = pl.BlockSpec(memory_space=pltpu.HBM)
 SCALARS = pl.BlockSpec(memory_space=pltpu.SMEM)
@@ -64,12 +64,12 @@
     return inverses
 
 
-def prepare_kernel(rows, block, depth, me, place, source, out, factor, sem):
-    width = depth // 2
-    load = pltpu.make_async_copy(source, factor, sem)
+def prepare_kernel(rows, block, depth, cuts, movers, me, place, source, *refs):
+    *outs, factor, load_sem, store_sem = refs
+    width, part = depth // 2, rows // cuts
+    load = pltpu.make_async_copy(source, factor, load_sem)
     load.start()
     load.wait()
-    out[...] = factor[:, width:]
     first = me[0] * rows
 
     @pl.when((place[0] == 0) & (first < depth))
@@ -90,21 +90,40 @@
 
             @pl.when(first + i * block < depth)
             def _(i=i, inverse=inverse):
-                out[i * block : (i + 1) * block, width - block :] = inverse
-
-
-def prepare(me, place, factor, block):
+                factor[i * block : (i + 1) * block, depth - block :] = inverse
+
+    moves = me[0] < movers
+    copies = []
+    for k in range(2):
+        panel = pl.ds(k * width, width)
+        for cut in range(cuts):
+            at = pl.ds(cut * part, part)
+            copies.append((factor.at[at, panel], outs[2 * cut + k], store_sem.at[2 * cut + k]))
+        if cuts > 1:
+            sent = pl.ds(pl.multiple_of(jnp.where(moves, part, 0), 8), part)
+            copies.append((factor.at[sent, panel], outs[4 + k], store_sem.at[4 + k]))
+    copies = [pltpu.make_async_copy(*copy) for copy in copies]
+    for copy in copies:
+        copy.start()
+    for copy in copies:
+        copy.wait()
+
+
+def prepare(me, place, factor, block, cuts, movers):
     rows, depth = factor.shape
+    count = 2 * cuts + (2 if cuts > 1 else 0)
     return pl.pallas_call(
-        functools.partial(prepare_kernel, rows, block, depth),
-        out_shape=jax.ShapeDtypeStruct((rows, depth // 2), jnp.float32),
+        functools.partial(prepare_kernel, rows, block, depth, cuts, movers),
+        out_shape=[jax.ShapeDtypeStruct((rows // cuts, depth // 2), jnp.float32)] * count,
         in_specs=[SCALARS] * 2 + [ANY],
-        out_specs=WHOLE,
-        scratch_shapes=[pltpu.VMEM((rows, depth), jnp.float32), pltpu.SemaphoreType.DMA],
+        out_specs=[ANY] * count,
+        scratch_shapes=[
+            pltpu.VMEM((rows, depth), jnp.float32),
+            pltpu.SemaphoreType.DMA,
+            pltpu.SemaphoreType.DMA((count,)),
+        ],
         compiler_params=pltpu.CompilerParams(vmem_limit_bytes=VMEM_BYTES),
-        cost_estimate=pl.CostEstimate(
-            flops=24 * rows * block * block, bytes_accessed=6 * rows * depth, transcendentals=0
-        ),
+        cost_estimate=SHORT,
     )(me, place, factor)
 
 
@@ -218,16 +237,12 @@
             pltpu.SemaphoreType.DMA,
         ],
         compiler_params=pltpu.CompilerParams(vmem_limit_bytes=VMEM_BYTES),
-        cost_estimate=pl.CostEstimate(
-            flops=6 * (panel + 1) * width * width * columns,
-            bytes_accessed=12 * width * columns,
-            transcendentals=0,
-        ),
+        cost_estimate=SHORT,
     )(ids, place, *held[0], *held[1], rhs, *earlier)
 
 
-def update_kernel(pieces, rows, width, tile, step, places, behind, ids, place, *refs):
-    held, refs = refs[: 4 * pieces], refs[4 * pieces :]
+def update_kernel(pieces, rows, width, tile, step, places, ids, place, *refs):
+    held, refs = refs[: 2 * pieces], refs[2 * pieces :]
     rhs, refs = refs[0], refs[1:]
     solved, refs = refs[: 2 * places], refs[2 * places :]
     refs = refs[len(refs) - 11 :]
@@ -261,15 +276,9 @@
             for k in range(2):
                 fetch(k, r).start()
 
-    for group in range(2):
-
-        @pl.when((place[0] == behind) == (group == 1))
-        def _(group=group):
-            for i in range(pieces):
-                for k in range(2):
-                    load(k, i, (2 * group + k) * pieces + i).start()
-
     for i in range(pieces):
+        for k in range(2):
+            load(k, i, k * pieces + i).start()
         load_block(i).start()
     for k in range(2):
         fetch(k, 0).wait()
@@ -316,7 +325,7 @@
         store(i).wait()
 
 
-def update(ids, place, held, rhs, solved, width, behind, written=None):
+def update(ids, place, held, rhs, solved, width, written=None):
     pieces, places = len(held[0]), len(solved[0])
     rows, columns = held[0][0].shape[0], rhs.shape[1]
     step = math.gcd(rows, 2 * width)
@@ -324,7 +333,7 @@
     operands = [ids, place, *[piece for group in held for piece in group], rhs, *solved[0], *solved[1]]
     extra = [] if written is None else [written]
     return pl.pallas_call(
-        functools.partial(update_kernel, pieces, rows, width, tile, step, places, behind),
+        functools.partial(update_kernel, pieces, rows, width, tile, step, places),
         out_shape=jax.ShapeDtypeStruct(rhs.shape, jnp.float32),
         in_specs=[SCALARS] * 2 + [ANY] * (len(operands) - 2 + len(extra)),
         out_specs=ANY,
@@ -342,112 +351,151 @@
             pltpu.SemaphoreType.DMA((pieces,)),
         ],
         compiler_params=pltpu.CompilerParams(vmem_limit_bytes=VMEM_BYTES),
-        cost_estimate=pl.CostEstimate(
-            flops=12 * pieces * rows * width * columns,
-            bytes_accessed=8 * pieces * rows * (width + columns),
-            transcendentals=0,
-        ),
+        cost_estimate=SHORT,
     )(*operands, *extra)
 
 
-def gate_kernel(first, second, token, first_out, second_out):
+def gate_kernel(count, *refs):
     pass
 
 
-def gate(panels, token):
+def gate(blocks, token):
+    count = len(blocks)
     return pl.pallas_call(
-        gate_kernel,
-        out_shape=[jax.ShapeDtypeStruct(panel.shape, panel.dtype) for panel in panels],
-        in_specs=[ANY] * 3,
-        out_specs=[ANY] * 2,
-        input_output_aliases={0: 0, 1: 1},
+        functools.partial(gate_kernel, count),
+        out_shape=[jax.ShapeDtypeStruct(block.shape, block.dtype) for block in blocks],
+        in_specs=[ANY] * (count + 1),
+        out_specs=[ANY] * count,
+        input_output_aliases={i: i for i in range(count)},
         compiler_params=pltpu.CompilerParams(vmem_limit_bytes=VMEM_BYTES),
-    )(*panels, token)
-
-
-def ring_steps(panels, ring, members, number):
+    )(*blocks, token)
+
+
+def ring_pass(panels, ring, cut):
     count = len(ring)
-    ways = [
-        [(number(ring[i], r), number(ring[(i + way) % count], r)) for i in range(count) for r in members]
-        for way in (1, -1)
-    ]
+    onward = [(ring[i], ring[(i + 1) % count]) for i in range(count)]
+    back = [(b, a) for a, b in onward]
+    held = [[panel] for panel in panels]
     going = [[panel, panel] for panel in panels]
     for step in range(1, count // 2 + 1):
-        arrived = [[], []]
         for k in range(2):
-            for way in range(2):
+            for way, pairs in enumerate((onward, back)):
                 if step == count // 2 and way != k:
                     continue
-                going[k][way] = lax.ppermute(going[k][way], number.axes, ways[way])
-                arrived[k].append(going[k][way])
-        yield arrived
-
-
-class Number:
-    def __init__(self, mesh):
-        self.axes = tuple(mesh.axis_names)
-        self.shape = dict(mesh.shape)
-
-    def __call__(self, source, row):
-        at = {"src": source, "row": row}
-        place = 0
-        for axis in self.axes:
-            place = place * self.shape[axis] + at[axis]
-        return place
-
-
-def spread_rows(block, count):
+                going[k][way] = lax.ppermute(going[k][way], "src", pairs)
+                held[k].append(going[k][way])
+        if step == cut:
+            token = going[0][1]
+    return held, token
+
+
+def spread_far(block, count):
     found = {0: block}
     stride = count // 2
-    while stride:
+    while stride > 1:
         for r in list(found):
             found[r + stride] = lax.ppermute(found[r], "row", [(r, r + stride)])
         stride //= 2
+    return found
+
+
+def spread_near(found, count, token=None):
+    found = dict(found)
+    for r in sorted(found):
+        if r and token is not None:
+            (found[r],) = gate([found[r]], token)
+        if r + 1 < count:
+            found[r + 1] = lax.ppermute(found[r], "row", [(r, r + 1)])
     return [found[r] for r in range(count)]
+
+
+def swap_partners(count, tops):
+    free = [s for s in range(count) if 2 * s >= tops]
+    partners = []
+    for s in range(count):
+        if 2 * s + 1 < tops:
+            pool = [f for f in free if f % 2 == s % 2] or free
+            if not pool:
+                return None
+            partners.append(pool[-1])
+            free.remove(pool[-1])
+    return partners
+
+
+def lookup(table, index):
+    hit = index[:, None] == jnp.arange(len(table), dtype=jnp.int32)[None, :]
+    return jnp.sum(jnp.where(hit, jnp.array(table, jnp.int32)[None, :], 0), axis=1)
 
 
 def solution(mesh):
     count, places = mesh.shape["src"], mesh.shape["row"]
-    number = Number(mesh)
-    behind = 1
+    axes = tuple(mesh.axis_names)
+
+    def number(source, row):
+        at, place = {"src": source, "row": row}, 0
+        for axis in axes:
+            place = place * mesh.shape[axis] + at[axis]
+        return place
 
     def local(factor, right_side):
         rows, depth = factor.shape
-        width = depth // 2
+        width, part = depth // 2, rows // 2
         block = math.gcd(math.gcd(rows, width), LANES)
         me = lax.axis_index("src").reshape(1).astype(jnp.int32)
         place = lax.axis_index("row").reshape(1).astype(jnp.int32)
-        panels = [factor[:, :width], prepare(me, place, factor, block)]
-        if count % 2 or count > RING_LIMIT or places < 2:
-            held = [[lax.all_gather(panel, "src", axis=0, tiled=True)] for panel in panels]
-            late, ids, cut = held, jnp.zeros_like(me), 1
+        partners = swap_partners(count, -(-depth // part))
+        ringed = count % 2 == 0 and count <= RING_LIMIT and part % 8 == 0 and partners is not None
+        if not ringed:
+            held = [
+                [lax.all_gather(panel, "src", axis=0, tiled=True)]
+                for panel in prepare(me, place, factor, block, 1, 0)
+            ]
+            top, top_spots = held, jnp.zeros_like(me)
+            groups = [(held, top_spots)]
         else:
+            movers = len(partners)
+            *halves, sent_first, sent_second = prepare(me, place, factor, block, 2, movers)
+            pairs = [(s, f) for s, f in enumerate(partners)]
+            swap = [(number(a, 0), number(b, 0)) for s, f in pairs for a, b in ((s, f), (f, s))]
+            got = [lax.ppermute(sent, axes, swap) for sent in (sent_first, sent_second)]
+            source = me[0]
+            paired = functools.reduce(jnp.logical_or, [source == f for f in partners])
+            takes = [(place[0] == 0) & paired, (place[0] == 0) & (source < movers)]
+            own = [
+                [jnp.where(takes[h], got[k], halves[2 * h + k]) for k in range(2)] for h in range(2)
+            ]
             ring = list(range(0, count, 2)) + list(range(count - 1, 0, -2))
-            spot = jnp.where(me % 2 == 0, me // 2, count - 1 - me // 2)
+            position = jnp.where(source % 2 == 0, source // 2, count - 1 - source // 2)
             half = count // 2
             away = [0] + [d for step in range(1, half) for d in (-step, step)] + [half]
-            spot = (spot + jnp.array(away, jnp.int32) + count) % count
-            ids = jnp.where(spot < half, 2 * spot, 2 * (count - 1 - spot) + 1)
-            held = [[panel] for panel in panels]
-            ahead = [r for r in range(places) if r != behind]
-            for step, arrived in enumerate(ring_steps(panels, ring, ahead, number)):
-                for k in range(2):
-                    held[k] += arrived[k]
-                if step == TOKEN_STEP:
-                    token = lax.ppermute(arrived[0][0][:8, :LANES], "row", [(0, behind)])
-            late = [[panel] for panel in panels]
-            for arrived in ring_steps(gate(panels, token), ring, [behind], number):
-                for k in range(2):
-                    late[k] += arrived[k]
-            cut = 5
-        first = solve_panel(0, ids, place, held, right_side, [], width, block)
-        second = solve_panel(1, ids, place, held, right_side, [first], width, block)
-        solved = [spread_rows(first, places), spread_rows(second, places)]
+            position = (position + jnp.array(away, jnp.int32) + count) % count
+            ids = jnp.where(position < half, 2 * position, 2 * (count - 1 - position) + 1)
+            tables = [[2 * s + h for s in range(count)] for h in range(2)]
+            for s, f in pairs:
+                tables[0][f], tables[1][s] = 2 * s + 1, 2 * f
+            spots = [
+                jnp.where(place[0] == 0, lookup(tables[h], ids), 2 * ids + h).astype(jnp.int32)
+                for h in range(2)
+            ]
+            top, token = ring_pass(own[0], ring, half - 1)
+            rest, _ = ring_pass(gate(own[1], token), ring, half - 1)
+            top_spots, cut = spots[0], 2 * half - 3
+            groups = [
+                (
+                    [top[k] + rest[k][:cut] for k in range(2)],
+                    jnp.concatenate([spots[0], spots[1][:cut]]),
+                ),
+                ([rest[k][cut:] for k in range(2)], spots[1][cut:]),
+            ]
+        first = solve_panel(0, top_spots, place, top, right_side, [], width, block)
+        second = solve_panel(1, top_spots, place, top, right_side, [first], width, block)
+        solved = [
+            spread_near(spread_far(first, places), places, second),
+            spread_near(spread_far(second, places), places),
+        ]
         result = None
-        for part in (slice(0, cut), slice(cut, None)):
-            group = [pieces[part] for pieces in held + late]
-            if group[0]:
-                result = update(ids[part], place, group, right_side, solved, width, behind, result)
+        for held, spots in groups:
+            result = update(spots, place, held, right_side, solved, width, result)
         return result
 
     placed = (P(("row", "src"), None), P("row", "src"))

time: 180 us -> 167 us (0.928)
  starting transfers between devices: 99.6 us -> 59.5 us
  waiting for transfers between devices: 30.2 us -> 65 us
  local copies, waits for them, and re-layouts: 8.36 us -> 2.65 us
  Pallas kernels: 39.2 us -> 36.1 us
  other arithmetic: 0.6 us -> 2.46 us
    ppermute x35 -> x36, starting transfers between devices: 99.6 us -> 59.5 us  [the longest x28 45 us: ring_pass(): going[k][way] = lax.ppermute(going[k][way], 'src', pairs)]
    ppermute x35 -> x36, waiting for transfers between devices: 30.2 us -> 65 us  [the longest x28 54.3 us: ring_pass(): going[k][way] = lax.ppermute(going[k][way], 'src', pairs)]
    unnamed x44 -> x46, local copies, waits for them, and re-layouts: 6.56 us -> 2.58 us
    pallas_call x2 -> x3, Pallas kernels: 4.78 us -> 4.05 us  [the longest x1 4.05 us: prepare(): pl.pallas_call(functools.partial(prepare_kernel, rows, block, depth, cuts...]
  transfers between devices with their start and end apart: 35 -> 36, of which waited for: 10 -> 16; matrix products, arithmetic and copies ran while one was open for 2% -> 2% of each run, Pallas kernels for 17% -> 8%
where the time goes in v3:
time: 167 us; the launch traced here: 166 us
  waiting for transfers between devices  65 us (39%)
  starting transfers between devices  59.5 us (36%)
  Pallas kernels  36.1 us (22%)
  local copies, waits for them, and re-layouts  2.65 us (2%)
  other arithmetic  2.46 us (1%)
    ppermute x28, waiting for transfers between devices, ring_pass(): going[k][way] = lax.ppermute(going[k][way], 'src', pairs)  54.3 us
    ppermute x28, starting transfers between devices, ring_pass(): going[k][way] = lax.ppermute(going[k][way], 'src', pairs)  45 us
    pallas_call x2, Pallas kernels, update(): pl.pallas_call(functools.partial(update_kernel, pieces, rows, width, tile...  18.7 us
    pallas_call x2, Pallas kernels, solve_panel(): pl.pallas_call(functools.partial(solve_kernel, pieces, rows, width, chunk...  13.4 us
    ppermute x2, waiting for transfers between devices, local(): got = [lax.ppermute(sent, axes, swap) for sent in (sent_first, sent_second)]  10.6 us
    ppermute x2, starting transfers between devices, local(): got = [lax.ppermute(sent, axes, swap) for sent in (sent_first, sent_second)]  7.64 us
    ppermute x4, starting transfers between devices, spread_near(): found[r + 1] = lax.ppermute(found[r], 'row', [(r, r + 1)])  4.13 us
    pallas_call x1, Pallas kernels, prepare(): pl.pallas_call(functools.partial(prepare_kernel, rows, block, depth, cuts...  4.05 us
  transfers between devices with their start and end apart: 36, of which 16 were waited for; matrix products, arithmetic and copies ran while one was open for 2% of the time, Pallas kernels for 8%

profile of v3, /device:TPU:0, one launch (start us, length us, event | category | flops | bytes accessed | tf_op | source)
XLA Modules:
  0.0 166.3 jit_solution(3544281280256241768)
XLA Ops:
  0.0 4.0 %shard_map.55 = (f32[160,512]{1,0:T(8,128)S(1)}, f32[160,512]{1,0:T(8,128)S(1)}, f32[160,512]{1,0:T(8,128)S(1)}, f32[160,512]{1,0:T(8,128)S(1)}, f32[160,512]{1,0:T(8,128)S(1)}, /*index=5*/f32[160,512]{1,0:T(8,128)S(1)}) custom-call(s32[1]{0:T(128)} %bitcast.1.me, s32[1]{0:T(128)} %bitcast.place, f32[320,1024]{1,0:T(8,128)} %source.1), custom_call_target="tpu_custom_call" | custom-call | flops 1000 | bytes 1000 | tf_op jit(solution)/shard_map/pallas_call | solution.py:115
  4.1 4.4 %collective-permute-start.1 = (f32[160,512]{1,0:T(8,128)S(1)}, f32[160,512]{1,0:T(8,128)S(1)}, u32[]{:S(2)}, u32[]{:S(2)}) collective-permute-start(f32[160,512]{1,0:T(8,128)S(1)} %get-tuple-element.15), channel_id=1, source_target_pairs={{0,24},{24,0},{4,28},{28,4},{8,16},{16,8}} | collective-permute-start | bytes 983048 | tf_op jit(solution)/shard_map/ppermute | solution.py:460
  8.5 3.2 %collective-permute-start = (f32[160,512]{1,0:T(8,128)S(1)}, f32[160,512]{1,0:T(8,128)S(1)}, u32[]{:S(2)}, u32[]{:S(2)}) collective-permute-start(f32[160,512]{1,0:T(8,128)S(1)} %get-tuple-element.13), channel_id=1, source_target_pairs={{0,24},{24,0},{4,28},{28,4},{8,16},{16,8}} | collective-permute-start | bytes 983048 | tf_op jit(solution)/shard_map/ppermute | solution.py:460
  11.7 6.7 %collective-permute-done.1 = f32[160,512]{1,0:T(8,128)S(1)} collective-permute-done((f32[160,512]{1,0:T(8,128)S(1)}, f32[160,512]{1,0:T(8,128)S(1)}, u32[]{:S(2)}, u32[]{:S(2)}) %collective-permute-start.1) | collective-permute-done | bytes 327712 | tf_op jit(solution)/shard_map/ppermute | solution.py:460
  18.5 3.0 %collective-permute-start.24 = (f32[160,512]{1,0:T(8,128)S(1)}, f32[160,512]{1,0:T(8,128)S(1)}, u32[]{:S(2)}, u32[]{:S(2)}) collective-permute-start(f32[160,512]{1,0:T(8,128)S(1)} %get-tuple-element.23.refs_8_.refs_13_), channel_id=1, source_target_pairs={{8,0},{16,8},{24,16},{28,24},{20,28},{12,20},{4,12},{0,4},{9,1},{1... | collective-permute-start | bytes 983048 | tf_op jit(solution)/shard_map/ppermute | solution.py:385
  21.5 3.9 %collective-permute-done = f32[160,512]{1,0:T(8,128)S(1)} collective-permute-done((f32[160,512]{1,0:T(8,128)S(1)}, f32[160,512]{1,0:T(8,128)S(1)}, u32[]{:S(2)}, u32[]{:S(2)}) %collective-permute-start) | collective-permute-done | bytes 327712 | tf_op jit(solution)/shard_map/ppermute | solution.py:460
  25.5 8.0 %collective-permute-start.19 = (f32[160,512]{1,0:T(8,128)S(1)}, f32[160,512]{1,0:T(8,128)S(1)}, u32[]{:S(2)}, u32[]{:S(2)}) collective-permute-start(f32[160,512]{1,0:T(8,128)S(1)} %get-tuple-element.25.refs_0_), channel_id=1, source_target_pairs={{0,8},{8,16},{16,24},{24,28},{28,20},{20,12},{12,4},{4,0},{1,9},{9... | collective-permute-start | bytes 983048 | tf_op jit(solution)/shard_map/ppermute | solution.py:385
  35.5 4.6 %collective-permute-done.19.refs_1_ = f32[160,512]{1,0:T(8,128)S(1)} collective-permute-done((f32[160,512]{1,0:T(8,128)S(1)}, f32[160,512]{1,0:T(8,128)S(1)}, u32[]{:S(2)}, u32[]{:S(2)}) %collective-permute-start.19) | collective-permute-done | bytes 327712 | tf_op jit(solution)/shard_map/ppermute | solution.py:385
  43.8 3.1 %collective-permute-done.23.refs_9_.refs_14_ = f32[160,512]{1,0:T(8,128)} collective-permute-done((f32[160,512]{1,0:T(8,128)S(1)}, f32[160,512]{1,0:T(8,128)}, u32[]{:S(2)}, u32[]{:S(2)}) %collective-permute-start.23) | collective-permute-done | bytes 327712 | tf_op jit(solution)/shard_map/ppermute | solution.py:385
  46.9 2.6 %collective-permute-start.25 = (f32[160,512]{1,0:T(8,128)}, f32[160,512]{1,0:T(8,128)}, u32[]{:S(2)}, u32[]{:S(2)}) collective-permute-start(f32[160,512]{1,0:T(8,128)} %collective-permute-done.23.refs_9_.refs_14_), channel_id=1, source_target_pairs={{0,8},{8,16},{16,24},{24,28},{28,20},{20,12},{12,4},{4,0},{1,9},{9... | collective-permute-start | bytes 983048 | tf_op jit(solution)/shard_map/ppermute | solution.py:385
  50.5 3.4 %collective-permute-done.20.refs_3_ = f32[160,512]{1,0:T(8,128)S(1)} collective-permute-done((f32[160,512]{1,0:T(8,128)S(1)}, f32[160,512]{1,0:T(8,128)S(1)}, u32[]{:S(2)}, u32[]{:S(2)}) %collective-permute-start.20) | collective-permute-done | bytes 327712 | tf_op jit(solution)/shard_map/ppermute | solution.py:385
  57.8 3.4 %collective-permute-start.27 = (f32[160,512]{1,0:T(8,128)}, f32[160,512]{1,0:T(8,128)S(1)}, u32[]{:S(2)}, u32[]{:S(2)}) collective-permute-start(f32[160,512]{1,0:T(8,128)} %collective-permute-done.25.refs_11_.refs_16_), channel_id=1, source_target_pairs={{0,8},{8,16},{16,24},{24,28},{28,20},{20,12},{12,4},{4,0},{1,9},{9... | collective-permute-start | bytes 983048 | tf_op jit(solution)/shard_map/ppermute | solution.py:385
  61.2 3.6 %collective-permute-start.22 = (f32[160,512]{1,0:T(8,128)S(1)}, f32[160,512]{1,0:T(8,128)S(1)}, u32[]{:S(2)}, u32[]{:S(2)}) collective-permute-start(f32[160,512]{1,0:T(8,128)S(1)} %collective-permute-done.21.refs_5_), channel_id=1, source_target_pairs={{0,8},{8,16},{16,24},{24,28},{28,20},{20,12},{12,4},{4,0},{1,9},{9... | collective-permute-start | bytes 983048 | tf_op jit(solution)/shard_map/ppermute | solution.py:385
  66.4 3.7 %collective-permute-done.29.refs_15_.refs_20_ = f32[160,512]{1,0:T(8,128)S(1)} collective-permute-done((f32[160,512]{1,0:T(8,128)}, f32[160,512]{1,0:T(8,128)S(1)}, u32[]{:S(2)}, u32[]{:S(2)}) %collective-permute-start.29) | collective-permute-done | bytes 327712 | tf_op jit(solution)/shard_map/ppermute | solution.py:385
  70.1 3.0 %collective-permute-done.22.refs_7_ = f32[160,512]{1,0:T(8,128)S(1)} collective-permute-done((f32[160,512]{1,0:T(8,128)S(1)}, f32[160,512]{1,0:T(8,128)S(1)}, u32[]{:S(2)}, u32[]{:S(2)}) %collective-permute-start.22) | collective-permute-done | bytes 327712 | tf_op jit(solution)/shard_map/ppermute | solution.py:385
  73.8 5.8 %shard_map.57.refs_17_.refs_27_.refs_7_ = f32[512,512]{1,0:T(8,128)} custom-call(s32[8]{0:T(128)S(1)} %get-tuple-element.27.ids, s32[1]{0:T(128)} %bitcast.place, f32[160,512]{1,0:T(8,128)S(1)} %get-tuple-element.25.refs_0_, f32[160,512]{1,0:T(8,128)S(1)} %collective-permute-done.19.refs_1_, f32[160,512]{1,0:T(8,128)S(1)} %collective-permute-done.2.refs_2_, ...), custom_call_target="tpu_custom_call" | custom-call | flops 1000 | bytes 1000 | tf_op jit(solution)/shard_map/pallas_call | solution.py:229
  79.7 7.6 %shard_map.58.refs_1_.refs_31_.refs_11_ = f32[512,512]{1,0:T(8,128)} custom-call(s32[8]{0:T(128)S(1)} %get-tuple-element.27.ids, s32[1]{0:T(128)} %bitcast.place, f32[160,512]{1,0:T(8,128)S(1)} %get-tuple-element.25.refs_0_, f32[160,512]{1,0:T(8,128)S(1)} %collective-permute-done.19.refs_1_, f32[160,512]{1,0:T(8,128)S(1)} %collective-permute-done.2.refs_2_, ...), custom_call_target="tpu_custom_call" | custom-call | flops 1000 | bytes 1000 | tf_op jit(solution)/shard_map/pallas_call | solution.py:229
  94.2 6.0 %collective-permute-done.12.refs_22_ = f32[160,512]{1,0:T(8,128)S(1)} collective-permute-done((f32[160,512]{1,0:T(8,128)S(1)}, f32[160,512]{1,0:T(8,128)S(1)}, u32[]{:S(2)}, u32[]{:S(2)}) %collective-permute-start.12) | collective-permute-done | bytes 327712 | tf_op jit(solution)/shard_map/ppermute | solution.py:385
  104.2 6.5 %collective-permute-done.8.refs_10_ = f32[160,512]{1,0:T(8,128)S(1)} collective-permute-done((f32[160,512]{1,0:T(8,128)S(1)}, f32[160,512]{1,0:T(8,128)S(1)}, u32[]{:S(2)}, u32[]{:S(2)}) %collective-permute-start.8) | collective-permute-done | bytes 327712 | tf_op jit(solution)/shard_map/ppermute | solution.py:385
  118.5 6.7 %collective-permute-done.9.refs_12_ = f32[160,512]{1,0:T(8,128)} collective-permute-done((f32[160,512]{1,0:T(8,128)S(1)}, f32[160,512]{1,0:T(8,128)}, u32[]{:S(2)}, u32[]{:S(2)}) %collective-permute-start.9) | collective-permute-done | bytes 327712 | tf_op jit(solution)/shard_map/ppermute | solution.py:385
  127.6 4.7 %collective-permute-done.7.refs_0_ = f32[160,512]{1,0:T(8,128)S(1)} collective-permute-done((f32[160,512]{1,0:T(8,128)S(1)}, f32[160,512]{1,0:T(8,128)S(1)}, u32[]{:S(2)}, u32[]{:S(2)}) %collective-permute-start.7) | collective-permute-done | bytes 327712 | tf_op jit(solution)/shard_map/ppermute | solution.py:385
  132.3 8.5 %collective-permute-done.17.refs_4_ = f32[160,512]{1,0:T(8,128)S(1)} collective-permute-done((f32[160,512]{1,0:T(8,128)S(1)}, f32[160,512]{1,0:T(8,128)S(1)}, u32[]{:S(2)}, u32[]{:S(2)}) %collective-permute-start.17) | collective-permute-done | bytes 327712 | tf_op jit(solution)/shard_map/ppermute | solution.py:385
  147.4 13.3 %shard_map.60.refs_15_ = f32[2560,512]{1,0:T(8,128)} custom-call(s32[13]{0:T(128)S(1)} %pad_add_fusion.ids, s32[1]{0:T(128)} %bitcast.place, f32[160,512]{1,0:T(8,128)S(1)} %get-tuple-element.25.refs_0_, f32[160,512]{1,0:T(8,128)S(1)} %collective-permute-done.19.refs_1_, f32[160,512]{1,0:T(8,128)S(1)} %collective-permute-done.2.refs_2_, ...), custom_call_target="tpu_custom_call" | custom-call | flops 1000 | bytes 1000 | tf_op jit(solution)/shard_map/pallas_call | solution.py:335
  160.8 5.4 %shard_map.61 = f32[2560,512]{1,0:T(8,128)} custom-call(s32[3]{0:T(128)S(1)} %slice.6.ids, s32[1]{0:T(128)} %bitcast.place, f32[160,512]{1,0:T(8,128)S(1)} %collective-permute-done.7.refs_0_, f32[160,512]{1,0:T(8,128)S(1)} %collective-permute-done.10.refs_1_, f32[160,512]{1,0:T(8,128)S(1)} %collective-permute-done.11.refs_2_, ...), custom_call_target="tpu_custom_call", output_to_operand_aliasing={{}: (17, {})} | custom-call | flops 1000 | bytes 1000 | tf_op jit(solution)/shard_map/pallas_call | solution.py:335
  (108 shorter events, 40.6 us)
Async XLA Ops:
  4.1 14.3 %collective-permute-start.1 = (f32[160,512]{1,0:T(8,128)S(1)}, f32[160,512]{1,0:T(8,128)S(1)}, u32[]{:S(2)}, u32[]{:S(2)}) collective-permute-start(f32[160,512]{1,0:T(8,128)S(1)} %get-tuple-element.15), channel_id=1, source_target_pairs={{0,24},{24,0},{4,28},{28,4},{8,16},{16,8}} | collective-permute-start | bytes 983048 | tf_op jit(solution)/shard_map/ppermute | solution.py:460
  8.5 16.9 %collective-permute-start = (f32[160,512]{1,0:T(8,128)S(1)}, f32[160,512]{1,0:T(8,128)S(1)}, u32[]{:S(2)}, u32[]{:S(2)}) collective-permute-start(f32[160,512]{1,0:T(8,128)S(1)} %get-tuple-element.13), channel_id=1, source_target_pairs={{0,24},{24,0},{4,28},{28,4},{8,16},{16,8}} | collective-permute-start | bytes 983048 | tf_op jit(solution)/shard_map/ppermute | solution.py:460
  18.5 17.0 %collective-permute-start.24 = (f32[160,512]{1,0:T(8,128)S(1)}, f32[160,512]{1,0:T(8,128)S(1)}, u32[]{:S(2)}, u32[]{:S(2)}) collective-permute-start(f32[160,512]{1,0:T(8,128)S(1)} %get-tuple-element.23.refs_8_.refs_13_), channel_id=1, source_target_pairs={{8,0},{16,8},{24,16},{28,24},{20,28},{12,20},{4,12},{0,4},{9,1},{1... | collective-permute-start | bytes 983048 | tf_op jit(solution)/shard_map/ppermute | solution.py:385
  25.5 14.6 %collective-permute-start.19 = (f32[160,512]{1,0:T(8,128)S(1)}, f32[160,512]{1,0:T(8,128)S(1)}, u32[]{:S(2)}, u32[]{:S(2)}) collective-permute-start(f32[160,512]{1,0:T(8,128)S(1)} %get-tuple-element.25.refs_0_), channel_id=1, source_target_pairs={{0,8},{8,16},{16,24},{24,28},{28,20},{20,12},{12,4},{4,0},{1,9},{9... | collective-permute-start | bytes 983048 | tf_op jit(solution)/shard_map/ppermute | solution.py:385
  33.5 13.4 %collective-permute-start.23 = (f32[160,512]{1,0:T(8,128)S(1)}, f32[160,512]{1,0:T(8,128)}, u32[]{:S(2)}, u32[]{:S(2)}) collective-permute-start(f32[160,512]{1,0:T(8,128)S(1)} %get-tuple-element.23.refs_8_.refs_13_), channel_id=1, source_target_pairs={{0,8},{8,16},{16,24},{24,28},{28,20},{20,12},{12,4},{4,0},{1,9},{9... | collective-permute-start | bytes 983048 | tf_op jit(solution)/shard_map/ppermute | solution.py:385
  35.5 13.9 %collective-permute-start.26 = (f32[160,512]{1,0:T(8,128)S(1)}, f32[160,512]{1,0:T(8,128)}, u32[]{:S(2)}, u32[]{:S(2)}) collective-permute-start(f32[160,512]{1,0:T(8,128)S(1)} %collective-permute-done.24.refs_10_.refs_15_), channel_id=1, source_target_pairs={{8,0},{16,8},{24,16},{28,24},{20,28},{12,20},{4,12},{0,4},{9,1},{1... | collective-permute-start | bytes 983048 | tf_op jit(solution)/shard_map/ppermute | solution.py:385
  40.1 13.8 %collective-permute-start.20 = (f32[160,512]{1,0:T(8,128)S(1)}, f32[160,512]{1,0:T(8,128)S(1)}, u32[]{:S(2)}, u32[]{:S(2)}) collective-permute-start(f32[160,512]{1,0:T(8,128)S(1)} %collective-permute-done.19.refs_1_), channel_id=1, source_target_pairs={{0,8},{8,16},{16,24},{24,28},{28,20},{20,12},{12,4},{4,0},{1,9},{9... | collective-permute-start | bytes 983048 | tf_op jit(solution)/shard_map/ppermute | solution.py:385
  42.6 14.4 %collective-permute-start.3 = (f32[160,512]{1,0:T(8,128)S(1)}, f32[160,512]{1,0:T(8,128)S(1)}, u32[]{:S(2)}, u32[]{:S(2)}) collective-permute-start(f32[160,512]{1,0:T(8,128)S(1)} %collective-permute-done.2.refs_2_), channel_id=1, source_target_pairs={{8,0},{16,8},{24,16},{28,24},{20,28},{12,20},{4,12},{0,4},{9,1},{1... | collective-permute-start | bytes 983048 | tf_op jit(solution)/shard_map/ppermute | solution.py:385
  46.9 10.9 %collective-permute-start.25 = (f32[160,512]{1,0:T(8,128)}, f32[160,512]{1,0:T(8,128)}, u32[]{:S(2)}, u32[]{:S(2)}) collective-permute-start(f32[160,512]{1,0:T(8,128)} %collective-permute-done.23.refs_9_.refs_14_), channel_id=1, source_target_pairs={{0,8},{8,16},{16,24},{24,28},{28,20},{20,12},{12,4},{4,0},{1,9},{9... | collective-permute-start | bytes 983048 | tf_op jit(solution)/shard_map/ppermute | solution.py:385
  49.5 11.8 %collective-permute-start.28 = (f32[160,512]{1,0:T(8,128)}, f32[160,512]{1,0:T(8,128)}, u32[]{:S(2)}, u32[]{:S(2)}) collective-permute-start(f32[160,512]{1,0:T(8,128)} %collective-permute-done.26.refs_12_.refs_17_), channel_id=1, source_target_pairs={{8,0},{16,8},{24,16},{28,24},{20,28},{12,20},{4,12},{0,4},{9,1},{1... | collective-permute-start | bytes 983048 | tf_op jit(solution)/shard_map/ppermute | solution.py:385
  61.2 11.9 %collective-permute-start.22 = (f32[160,512]{1,0:T(8,128)S(1)}, f32[160,512]{1,0:T(8,128)S(1)}, u32[]{:S(2)}, u32[]{:S(2)}) collective-permute-start(f32[160,512]{1,0:T(8,128)S(1)} %collective-permute-done.21.refs_5_), channel_id=1, source_target_pairs={{0,8},{8,16},{16,24},{24,28},{28,20},{20,12},{12,4},{4,0},{1,9},{9... | collective-permute-start | bytes 983048 | tf_op jit(solution)/shard_map/ppermute | solution.py:385
  87.2 28.8 %collective-permute-start.34 = (f32[512,512]{1,0:T(8,128)}, f32[512,512]{1,0:T(8,128)S(1)}, u32[]{:S(2)}, u32[]{:S(2)}) collective-permute-start(f32[512,512]{1,0:T(8,128)} %shard_map.58.refs_1_.refs_31_.refs_11_), channel_id=1, source_target_pairs={{0,2},{4,6},{8,10},{12,14},{16,18},{20,22},{24,26},{28,30}} | collective-permute-start | bytes 3145736 | tf_op jit(solution)/shard_map/ppermute | solution.py:397
  88.6 28.2 %collective-permute-start.31 = (f32[512,512]{1,0:T(8,128)S(1)}, f32[512,512]{1,0:T(8,128)S(1)}, u32[]{:S(2)}, u32[]{:S(2)}) collective-permute-start(f32[512,512]{1,0:T(8,128)S(1)} %copy-done.5), channel_id=1, source_target_pairs={{0,2},{4,6},{8,10},{12,14},{16,18},{20,22},{24,26},{28,30}} | collective-permute-start | bytes 3145736 | tf_op jit(solution)/shard_map/ppermute | solution.py:397
  92.1 12.1 %collective-permute-start.5 = (f32[160,512]{1,0:T(8,128)S(1)}, f32[160,512]{1,0:T(8,128)S(1)}, u32[]{:S(2)}, u32[]{:S(2)}) collective-permute-start(f32[160,512]{1,0:T(8,128)S(1)} %get-tuple-element.18.refs_8_), channel_id=1, source_target_pairs={{0,8},{8,16},{16,24},{24,28},{28,20},{20,12},{12,4},{4,0},{1,9},{9... | collective-permute-start | bytes 983048 | tf_op jit(solution)/shard_map/ppermute | solution.py:385
  100.2 12.4 %collective-permute-start.13 = (f32[160,512]{1,0:T(8,128)S(1)}, f32[160,512]{1,0:T(8,128)S(1)}, u32[]{:S(2)}, u32[]{:S(2)}) collective-permute-start(f32[160,512]{1,0:T(8,128)S(1)} %collective-permute-done.12.refs_22_), channel_id=1, source_target_pairs={{0,8},{8,16},{16,24},{24,28},{28,20},{20,12},{12,4},{4,0},{1,9},{9... | collective-permute-start | bytes 983048 | tf_op jit(solution)/shard_map/ppermute | solution.py:385
  104.2 10.5 %collective-permute-start.16 = (f32[160,512]{1,0:T(8,128)S(1)}, f32[160,512]{1,0:T(8,128)S(1)}, u32[]{:S(2)}, u32[]{:S(2)}) collective-permute-start(f32[160,512]{1,0:T(8,128)S(1)} %collective-permute-done.15.refs_23_), channel_id=1, source_target_pairs={{8,0},{16,8},{24,16},{28,24},{20,28},{12,20},{4,12},{0,4},{9,1},{1... | collective-permute-start | bytes 983048 | tf_op jit(solution)/shard_map/ppermute | solution.py:385
  112.6 28.2 %collective-permute-start.33 = (f32[512,512]{1,0:T(8,128)}, f32[512,512]{1,0:T(8,128)S(1)}, u32[]{:S(2)}, u32[]{:S(2)}) collective-permute-start(f32[512,512]{1,0:T(8,128)} %shard_map.58.refs_1_.refs_31_.refs_11_), channel_id=1, source_target_pairs={{0,1},{4,5},{8,9},{12,13},{16,17},{20,21},{24,25},{28,29}} | collective-permute-start | bytes 3145736 | tf_op jit(solution)/shard_map/ppermute | solution.py:408
  114.7 28.6 %collective-permute-start.30 = (f32[512,512]{1,0:T(8,128)S(1)}, f32[512,512]{1,0:T(8,128)S(1)}, u32[]{:S(2)}, u32[]{:S(2)}) collective-permute-start(f32[512,512]{1,0:T(8,128)S(1)} %copy-done.5), channel_id=1, source_target_pairs={{0,1},{4,5},{8,9},{12,13},{16,17},{20,21},{24,25},{28,29}} | collective-permute-start | bytes 3145736 | tf_op jit(solution)/shard_map/ppermute | solution.py:408
  116.1 29.3 %collective-permute-start.35 = (f32[512,512]{1,0:T(8,128)S(1)}, f32[512,512]{1,0:T(8,128)S(1)}, u32[]{:S(2)}, u32[]{:S(2)}) collective-permute-start(f32[512,512]{1,0:T(8,128)S(1)} %collective-permute-done.34.refs_33_.refs_13_), channel_id=1, source_target_pairs={{2,3},{6,7},{10,11},{14,15},{18,19},{22,23},{26,27},{30,31}} | collective-permute-start | bytes 3145736 | tf_op jit(solution)/shard_map/ppermute | solution.py:408
  117.8 27.8 %collective-permute-start.32 = (f32[512,512]{1,0:T(8,128)S(1)}, f32[512,512]{1,0:T(8,128)S(1)}, u32[]{:S(2)}, u32[]{:S(2)}) collective-permute-start(f32[512,512]{1,0:T(8,128)S(1)} %shard_map.59.refs_29_.refs_9_), channel_id=1, source_target_pairs={{2,3},{6,7},{10,11},{14,15},{18,19},{22,23},{26,27},{30,31}} | collective-permute-start | bytes 3145736 | tf_op jit(solution)/shard_map/ppermute | solution.py:408
  140.8 20.0 %collective-permute-start.10 = (f32[160,512]{1,0:T(8,128)}, f32[160,512]{1,0:T(8,128)S(1)}, u32[]{:S(2)}, u32[]{:S(2)}) collective-permute-start(f32[160,512]{1,0:T(8,128)} %collective-permute-done.9.refs_12_), channel_id=1, source_target_pairs={{8,0},{16,8},{24,16},{28,24},{20,28},{12,20},{4,12},{0,4},{9,1},{1... | collective-permute-start | bytes 983048 | tf_op jit(solution)/shard_map/ppermute | solution.py:385
  140.8 19.9 %collective-permute-start.14 = (f32[160,512]{1,0:T(8,128)}, f32[160,512]{1,0:T(8,128)S(1)}, u32[]{:S(2)}, u32[]{:S(2)}) collective-permute-start(f32[160,512]{1,0:T(8,128)} %copy-done.19), channel_id=1, source_target_pairs={{0,8},{8,16},{16,24},{24,28},{28,20},{20,12},{12,4},{4,0},{1,9},{9... | collective-permute-start | bytes 983048 | tf_op jit(solution)/shard_map/ppermute | solution.py:385
  143.3 17.4 %collective-permute-start.11 = (f32[160,512]{1,0:T(8,128)S(1)}, f32[160,512]{1,0:T(8,128)S(1)}, u32[]{:S(2)}, u32[]{:S(2)}) collective-permute-start(f32[160,512]{1,0:T(8,128)S(1)} %collective-permute-done.7.refs_0_), channel_id=1, source_target_pairs={{0,8},{8,16},{16,24},{24,28},{28,20},{20,12},{12,4},{4,0},{1,9},{9... | collective-permute-start | bytes 983048 | tf_op jit(solution)/shard_map/ppermute | solution.py:385
  145.4 15.4 %collective-permute-start.18 = (f32[160,512]{1,0:T(8,128)S(1)}, f32[160,512]{1,0:T(8,128)S(1)}, u32[]{:S(2)}, u32[]{:S(2)}) collective-permute-start(f32[160,512]{1,0:T(8,128)S(1)} %collective-permute-done.17.refs_4_), channel_id=1, source_target_pairs={{8,0},{16,8},{24,16},{28,24},{20,28},{12,20},{4,12},{0,4},{9,1},{1... | collective-permute-start | bytes 983048 | tf_op jit(solution)/shard_map/ppermute | solution.py:385
  (35 other events, 581.9 us)

commit v4 on v3

--- a/solution.py
+++ b/solution.py
@@ -130,8 +130,8 @@
 def solve_kernel(pieces, rows, width, chunk, block, panel, ids, place, *refs):
     held, refs = refs[: 2 * pieces], refs[2 * pieces :]
     rhs, refs = refs[0], refs[1:]
-    earlier, refs = refs[:panel], refs[panel:]
-    solved, lower, piece_sem, rhs_sem = refs
+    earlier = refs[:panel]
+    solved, lower, piece_sem, rhs_sem = refs[len(refs) - 4 :]
     first, last = panel * width, (panel + 1) * width
     side = lower.shape[1] - LANES
 
@@ -220,7 +220,7 @@
             solved[j : j + chunk] = dot_split(split16(inverses[j // chunk]), split16(value))
 
 
-def solve_panel(panel, ids, place, held, rhs, earlier, width, block):
+def solve_panel(panel, ids, place, held, rhs, earlier, after, width, block):
     pieces = len(held[0])
     rows = held[0][0].shape[0]
     columns = rhs.shape[1]
@@ -229,7 +229,10 @@
     return pl.pallas_call(
         functools.partial(solve_kernel, pieces, rows, width, chunk, block, panel),
         out_shape=jax.ShapeDtypeStruct((width, columns), jnp.float32),
-        in_specs=[SCALARS] * 2 + [ANY] * (2 * pieces + 1) + [WHOLE] * panel,
+        in_specs=[SCALARS] * 2
+        + [ANY] * (2 * pieces + 1)
+        + [WHOLE] * panel
+        + [ANY] * len(after),
         out_specs=WHOLE,
         scratch_shapes=[
             pltpu.VMEM((tall, 2 * width if panel else width + LANES), jnp.float32),
@@ -237,8 +240,12 @@
             pltpu.SemaphoreType.DMA,
         ],
         compiler_params=pltpu.CompilerParams(vmem_limit_bytes=VMEM_BYTES),
-        cost_estimate=SHORT,
-    )(ids, place, *held[0], *held[1], rhs, *earlier)
+        cost_estimate=pl.CostEstimate(
+            flops=24 * (panel + 1) * width * width * columns,
+            bytes_accessed=12 * width * columns,
+            transcendentals=0,
+        ),
+    )(ids, place, *held[0], *held[1], rhs, *earlier, *after)
 
 
 def update_kernel(pieces, rows, width, tile, step, places, ids, place, *refs):
@@ -351,7 +358,11 @@
             pltpu.SemaphoreType.DMA((pieces,)),
         ],
         compiler_params=pltpu.CompilerParams(vmem_limit_bytes=VMEM_BYTES),
-        cost_estimate=SHORT,
+        cost_estimate=pl.CostEstimate(
+            flops=12 * pieces * rows * width * columns,
+            bytes_accessed=8 * pieces * rows * (width + columns),
+            transcendentals=0,
+        ),
     )(*operands, *extra)
 
 
@@ -359,24 +370,25 @@
     pass
 
 
-def gate(blocks, token):
+def gate(blocks, tokens):
     count = len(blocks)
     return pl.pallas_call(
         functools.partial(gate_kernel, count),
         out_shape=[jax.ShapeDtypeStruct(block.shape, block.dtype) for block in blocks],
-        in_specs=[ANY] * (count + 1),
+        in_specs=[ANY] * (count + len(tokens)),
         out_specs=[ANY] * count,
         input_output_aliases={i: i for i in range(count)},
         compiler_params=pltpu.CompilerParams(vmem_limit_bytes=VMEM_BYTES),
-    )(*blocks, token)
-
-
-def ring_pass(panels, ring, cut):
+    )(*blocks, *tokens)
+
+
+def ring_pass(starts, ring):
     count = len(ring)
     onward = [(ring[i], ring[(i + 1) % count]) for i in range(count)]
     back = [(b, a) for a, b in onward]
-    held = [[panel] for panel in panels]
-    going = [[panel, panel] for panel in panels]
+    held = [[starts[k][k]] for k in range(2)]
+    going = [list(ways) for ways in starts]
+    steps = []
     for step in range(1, count // 2 + 1):
         for k in range(2):
             for way, pairs in enumerate((onward, back)):
@@ -384,9 +396,8 @@
                     continue
                 going[k][way] = lax.ppermute(going[k][way], "src", pairs)
                 held[k].append(going[k][way])
-        if step == cut:
-            token = going[0][1]
-    return held, token
+        steps.append([list(ways) for ways in going])
+    return held, steps
 
 
 def spread_far(block, count):
@@ -399,11 +410,11 @@
     return found
 
 
-def spread_near(found, count, token=None):
+def spread_near(found, count, tokens):
     found = dict(found)
     for r in sorted(found):
-        if r and token is not None:
-            (found[r],) = gate([found[r]], token)
+        if r and tokens:
+            (found[r],) = gate([found[r]], tokens)
         if r + 1 < count:
             found[r + 1] = lax.ppermute(found[r], "row", [(r, r + 1)])
     return [found[r] for r in range(count)]
@@ -452,6 +463,7 @@
             ]
             top, top_spots = held, jnp.zeros_like(me)
             groups = [(held, top_spots)]
+            after, near = [[], []], [[], []]
         else:
             movers = len(partners)
             *halves, sent_first, sent_second = prepare(me, place, factor, block, 2, movers)
@@ -477,8 +489,12 @@
                 jnp.where(place[0] == 0, lookup(tables[h], ids), 2 * ids + h).astype(jnp.int32)
                 for h in range(2)
             ]
-            top, token = ring_pass(own[0], ring, half - 1)
-            rest, _ = ring_pass(gate(own[1], token), ring, half - 1)
+            top, steps = ring_pass([[piece] * 2 for piece in own[0]], ring)
+            free = gate(own[1], [steps[-2][0][0]])
+            full = gate(free, [steps[-1][0][0]])
+            rest, steps = ring_pass([[full[0], free[0]], [free[1], full[1]]], ring)
+            after = [[steps[0][0][1], steps[0][1][0]], [steps[0][0][0], steps[0][1][1]]]
+            near = [steps[i][0] + steps[i][1] for i in (1, -2)]
             top_spots, cut = spots[0], 2 * half - 3
             groups = [
                 (
@@ -487,11 +503,11 @@
                 ),
                 ([rest[k][cut:] for k in range(2)], spots[1][cut:]),
             ]
-        first = solve_panel(0, top_spots, place, top, right_side, [], width, block)
-        second = solve_panel(1, top_spots, place, top, right_side, [first], width, block)
+        first = solve_panel(0, top_spots, place, top, right_side, [], after[0], width, block)
+        second = solve_panel(1, top_spots, place, top, right_side, [first], after[1], width, block)
         solved = [
-            spread_near(spread_far(first, places), places, second),
-            spread_near(spread_far(second, places), places),
+            spread_near(spread_far(first, places), places, near[0]),
+            spread_near(spread_far(second, places), places, near[1]),
         ]
         result = None
         for held, spots in groups:

time: 167 us -> 151 us (0.904)
  waiting for transfers between devices: 65 us -> 52.5 us
  starting transfers between devices: 59.5 us -> 55.6 us
  local copies, waits for them, and re-layouts: 2.65 us -> 5.94 us
  other arithmetic: 2.46 us -> 0.44 us
    ppermute x28, waiting for transfers between devices: 54.3 us -> 46.7 us  [ring_pass(): going[k][way] = lax.ppermute(going[k][way], 'src', pairs)]
    ppermute x2, waiting for transfers between devices: 10.6 us -> 5.76 us  [local(): got = [lax.ppermute(sent, axes, swap) for sent in (sent_first, sent_second)]]
    ppermute x28, starting transfers between devices: 45 us -> 41 us  [ring_pass(): going[k][way] = lax.ppermute(going[k][way], 'src', pairs)]
    unnamed x46 -> x52, local copies, waits for them, and re-layouts: 2.58 us -> 5.87 us
  transfers between devices with their start and end apart: 36 -> 36, of which waited for: 16 -> 17; matrix products, arithmetic and copies ran while one was open for 2% -> 0% of each run, Pallas kernels for 8% -> 18%
where the time goes in v4:
time: 151 us
  starting transfers between devices  55.6 us (37%)
  waiting for transfers between devices  52.5 us (35%)
  Pallas kernels  36.1 us (24%)
  local copies, waits for them, and re-layouts  5.94 us (4%)
    ppermute x28, waiting for transfers between devices, ring_pass(): going[k][way] = lax.ppermute(going[k][way], 'src', pairs)  46.7 us
    ppermute x28, starting transfers between devices, ring_pass(): going[k][way] = lax.ppermute(going[k][way], 'src', pairs)  41 us
    pallas_call x2, Pallas kernels, update(): pl.pallas_call(functools.partial(update_kernel, pieces, rows, width, tile...  18.7 us
    pallas_call x2, Pallas kernels, solve_panel(): pl.pallas_call(functools.partial(solve_kernel, pieces, rows, width, chunk...  13.3 us
    ppermute x2, starting transfers between devices, local(): got = [lax.ppermute(sent, axes, swap) for sent in (sent_first, sent_second)]  7.64 us
    unnamed x52, local copies, waits for them, and re-layouts  5.87 us
    ppermute x2, waiting for transfers between devices, local(): got = [lax.ppermute(sent, axes, swap) for sent in (sent_first, sent_second)]  5.76 us
    ppermute x4, starting transfers between devices, spread_near(): found[r + 1] = lax.ppermute(found[r], 'row', [(r, r + 1)])  4.13 us
  transfers between devices with their start and end apart: 36, of which 17 were waited for; matrix products, arithmetic and copies ran while one was open for 0% of the time, Pallas kernels for 18%

profile of v4, /device:TPU:0, one launch (start us, length us, event | category | flops | bytes accessed | tf_op | source)
XLA Modules:
  0.0 151.1 jit_solution(12813306552851874419)
XLA Ops:
  0.0 4.1 %shard_map.55 = (f32[160,512]{1,0:T(8,128)S(1)}, f32[160,512]{1,0:T(8,128)S(1)}, f32[160,512]{1,0:T(8,128)S(1)}, f32[160,512]{1,0:T(8,128)S(1)}, f32[160,512]{1,0:T(8,128)S(1)}, /*index=5*/f32[160,512]{1,0:T(8,128)S(1)}) custom-call(s32[1]{0:T(128)} %bitcast.1.me, s32[1]{0:T(128)} %bitcast.place, f32[320,1024]{1,0:T(8,128)} %source.1), custom_call_target="tpu_custom_call" | custom-call | flops 1000 | bytes 1000 | tf_op jit(solution)/shard_map/pallas_call | solution.py:115
  4.1 4.4 %collective-permute-start = (f32[160,512]{1,0:T(8,128)S(1)}, f32[160,512]{1,0:T(8,128)S(1)}, u32[]{:S(2)}, u32[]{:S(2)}) collective-permute-start(f32[160,512]{1,0:T(8,128)S(1)} %get-tuple-element.15), channel_id=1, source_target_pairs={{0,24},{24,0},{4,28},{28,4},{8,16},{16,8}} | collective-permute-start | bytes 983048 | tf_op jit(solution)/shard_map/ppermute | solution.py:472
  8.5 3.2 %collective-permute-start.1 = (f32[160,512]{1,0:T(8,128)S(1)}, f32[160,512]{1,0:T(8,128)S(1)}, u32[]{:S(2)}, u32[]{:S(2)}) collective-permute-start(f32[160,512]{1,0:T(8,128)S(1)} %get-tuple-element.17), channel_id=1, source_target_pairs={{0,24},{24,0},{4,28},{28,4},{8,16},{16,8}} | collective-permute-start | bytes 983048 | tf_op jit(solution)/shard_map/ppermute | solution.py:472
  11.8 5.8 %collective-permute-done = f32[160,512]{1,0:T(8,128)S(1)} collective-permute-done((f32[160,512]{1,0:T(8,128)S(1)}, f32[160,512]{1,0:T(8,128)S(1)}, u32[]{:S(2)}, u32[]{:S(2)}) %collective-permute-start) | collective-permute-done | bytes 327712 | tf_op jit(solution)/shard_map/ppermute | solution.py:472
  17.6 6.6 %collective-permute-start.2 = (f32[160,512]{1,0:T(8,128)S(1)}, f32[160,512]{1,0:T(8,128)S(1)}, u32[]{:S(2)}, u32[]{:S(2)}) collective-permute-start(f32[160,512]{1,0:T(8,128)S(1)} %get-tuple-element.29.refs_0_), channel_id=1, source_target_pairs={{0,8},{8,16},{16,24},{24,28},{28,20},{20,12},{12,4},{4,0},{1,9},{9... | collective-permute-start | bytes 983048 | tf_op jit(solution)/shard_map/ppermute | solution.py:397
  26.2 4.4 %collective-permute-done.2.refs_1_ = f32[160,512]{1,0:T(8,128)S(1)} collective-permute-done((f32[160,512]{1,0:T(8,128)S(1)}, f32[160,512]{1,0:T(8,128)S(1)}, u32[]{:S(2)}, u32[]{:S(2)}) %collective-permute-start.2) | collective-permute-done | bytes 327712 | tf_op jit(solution)/shard_map/ppermute | solution.py:397
  30.6 4.9 %collective-permute-start.3 = (f32[160,512]{1,0:T(8,128)S(1)}, f32[160,512]{1,0:T(8,128)S(1)}, u32[]{:S(2)}, u32[]{:S(2)}) collective-permute-start(f32[160,512]{1,0:T(8,128)S(1)} %collective-permute-done.2.refs_1_), channel_id=1, source_target_pairs={{0,8},{8,16},{16,24},{24,28},{28,20},{20,12},{12,4},{4,0},{1,9},{9... | collective-permute-start | bytes 983048 | tf_op jit(solution)/shard_map/ppermute | solution.py:397
  35.5 2.5 %collective-permute-start.23 = (f32[160,512]{1,0:T(8,128)S(1)}, f32[160,512]{1,0:T(8,128)}, u32[]{:S(2)}, u32[]{:S(2)}) collective-permute-start(f32[160,512]{1,0:T(8,128)S(1)} %get-tuple-element.27.refs_8_.refs_13_), channel_id=1, source_target_pairs={{0,8},{8,16},{16,24},{24,28},{28,20},{20,12},{12,4},{4,0},{1,9},{9... | collective-permute-start | bytes 983048 | tf_op jit(solution)/shard_map/ppermute | solution.py:397
  38.1 5.5 %collective-permute-done.3.refs_3_ = f32[160,512]{1,0:T(8,128)S(1)} collective-permute-done((f32[160,512]{1,0:T(8,128)S(1)}, f32[160,512]{1,0:T(8,128)S(1)}, u32[]{:S(2)}, u32[]{:S(2)}) %collective-permute-start.3) | collective-permute-done | bytes 327712 | tf_op jit(solution)/shard_map/ppermute | solution.py:397
  43.5 2.6 %collective-permute-start.4 = (f32[160,512]{1,0:T(8,128)S(1)}, f32[160,512]{1,0:T(8,128)S(1)}, u32[]{:S(2)}, u32[]{:S(2)}) collective-permute-start(f32[160,512]{1,0:T(8,128)S(1)} %collective-permute-done.3.refs_3_), channel_id=1, source_target_pairs={{0,8},{8,16},{16,24},{24,28},{28,20},{20,12},{12,4},{4,0},{1,9},{9... | collective-permute-start | bytes 983048 | tf_op jit(solution)/shard_map/ppermute | solution.py:397
  46.1 4.4 %collective-permute-done.23.refs_9_.refs_14_ = f32[160,512]{1,0:T(8,128)} collective-permute-done((f32[160,512]{1,0:T(8,128)S(1)}, f32[160,512]{1,0:T(8,128)}, u32[]{:S(2)}, u32[]{:S(2)}) %collective-permute-start.23) | collective-permute-done | bytes 327712 | tf_op jit(solution)/shard_map/ppermute | solution.py:397
  50.6 2.6 %collective-permute-start.25 = (f32[160,512]{1,0:T(8,128)}, f32[160,512]{1,0:T(8,128)}, u32[]{:S(2)}, u32[]{:S(2)}) collective-permute-start(f32[160,512]{1,0:T(8,128)} %collective-permute-done.23.refs_9_.refs_14_), channel_id=1, source_target_pairs={{0,8},{8,16},{16,24},{24,28},{28,20},{20,12},{12,4},{4,0},{1,9},{9... | collective-permute-start | bytes 983048 | tf_op jit(solution)/shard_map/ppermute | solution.py:397
  53.2 2.6 %collective-permute-done.26.refs_12_.refs_17_ = f32[160,512]{1,0:T(8,128)} collective-permute-done((f32[160,512]{1,0:T(8,128)S(1)}, f32[160,512]{1,0:T(8,128)}, u32[]{:S(2)}, u32[]{:S(2)}) %collective-permute-start.26) | collective-permute-done | bytes 327712 | tf_op jit(solution)/shard_map/ppermute | solution.py:397
  57.6 2.6 %collective-permute-start.13 = (f32[160,512]{1,0:T(8,128)S(1)}, f32[160,512]{1,0:T(8,128)}, u32[]{:S(2)}, u32[]{:S(2)}) collective-permute-start(f32[160,512]{1,0:T(8,128)S(1)} %get-tuple-element.21.refs_1_), channel_id=1, source_target_pairs={{0,8},{8,16},{16,24},{24,28},{28,20},{20,12},{12,4},{4,0},{1,9},{9... | collective-permute-start | bytes 983048 | tf_op jit(solution)/shard_map/ppermute | solution.py:397
  60.2 4.5 %collective-permute-done.25.refs_11_.refs_16_ = f32[160,512]{1,0:T(8,128)} collective-permute-done((f32[160,512]{1,0:T(8,128)}, f32[160,512]{1,0:T(8,128)}, u32[]{:S(2)}, u32[]{:S(2)}) %collective-permute-start.25) | collective-permute-done | bytes 327712 | tf_op jit(solution)/shard_map/ppermute | solution.py:397
  64.7 2.6 %collective-permute-start.5 = (f32[160,512]{1,0:T(8,128)S(1)}, f32[160,512]{1,0:T(8,128)S(1)}, u32[]{:S(2)}, u32[]{:S(2)}) collective-permute-start(f32[160,512]{1,0:T(8,128)S(1)} %collective-permute-done.4.refs_2_.refs_5_), channel_id=1, source_target_pairs={{0,8},{8,16},{16,24},{24,28},{28,20},{20,12},{12,4},{4,0},{1,9},{9... | collective-permute-start | bytes 983048 | tf_op jit(solution)/shard_map/ppermute | solution.py:397
  67.3 2.5 %collective-permute-start.27 = (f32[160,512]{1,0:T(8,128)}, f32[160,512]{1,0:T(8,128)S(1)}, u32[]{:S(2)}, u32[]{:S(2)}) collective-permute-start(f32[160,512]{1,0:T(8,128)} %collective-permute-done.25.refs_11_.refs_16_), channel_id=1, source_target_pairs={{0,8},{8,16},{16,24},{24,28},{28,20},{20,12},{12,4},{4,0},{1,9},{9... | collective-permute-start | bytes 983048 | tf_op jit(solution)/shard_map/ppermute | solution.py:397
  71.7 5.8 %collective-permute-done.9.refs_17_.refs_10_ = f32[160,512]{1,0:T(8,128)S(1)} collective-permute-done((f32[160,512]{1,0:T(8,128)S(1)}, f32[160,512]{1,0:T(8,128)S(1)}, u32[]{:S(2)}, u32[]{:S(2)}) %collective-permute-start.9) | collective-permute-done | bytes 327712 | tf_op jit(solution)/shard_map/ppermute | solution.py:397
  81.0 4.0 %collective-permute-done.29.refs_15_.refs_20_ = f32[160,512]{1,0:T(8,128)S(1)} collective-permute-done((f32[160,512]{1,0:T(8,128)}, f32[160,512]{1,0:T(8,128)S(1)}, u32[]{:S(2)}, u32[]{:S(2)}) %collective-permute-start.29) | collective-permute-done | bytes 327712 | tf_op jit(solution)/shard_map/ppermute | solution.py:397
  85.8 5.8 %shard_map.58.refs_17_.refs_27_.refs_7_ = f32[512,512]{1,0:T(8,128)} custom-call(s32[8]{0:T(128)S(1)} %get-tuple-element.31.ids, s32[1]{0:T(128)} %bitcast.place, f32[160,512]{1,0:T(8,128)S(1)} %get-tuple-element.29.refs_0_, f32[160,512]{1,0:T(8,128)S(1)} %collective-permute-done.2.refs_1_, f32[160,512]{1,0:T(8,128)S(1)} %collective-permute-done.20.refs_2_, ...), custom_call_target="tpu_custom_call" | custom-call | flops 3221225472 | bytes 3145728 | tf_op jit(solution)/shard_map/pallas_call | solution.py:229
  94.6 7.5 %shard_map.60.refs_31_.refs_11_ = f32[512,512]{1,0:T(8,128)} custom-call(s32[8]{0:T(128)S(1)} %get-tuple-element.31.ids, s32[1]{0:T(128)} %bitcast.place, f32[160,512]{1,0:T(8,128)S(1)} %get-tuple-element.29.refs_0_, f32[160,512]{1,0:T(8,128)S(1)} %collective-permute-done.2.refs_1_, f32[160,512]{1,0:T(8,128)S(1)} %collective-permute-done.20.refs_2_, ...), custom_call_target="tpu_custom_call" | custom-call | flops 6442450944 | bytes 3145728 | tf_op jit(solution)/shard_map/pallas_call | solution.py:229
  105.6 5.0 %collective-permute-done.10.refs_2_.refs_12_ = f32[160,512]{1,0:T(8,128)S(1)} collective-permute-done((f32[160,512]{1,0:T(8,128)S(1)}, f32[160,512]{1,0:T(8,128)S(1)}, u32[]{:S(2)}, u32[]{:S(2)}) %collective-permute-start.10) | collective-permute-done | bytes 327712 | tf_op jit(solution)/shard_map/ppermute | solution.py:397
  132.3 13.3 %shard_map.62.refs_15_ = f32[2560,512]{1,0:T(8,128)} custom-call(s32[13]{0:T(128)S(1)} %pad_add_fusion.ids, s32[1]{0:T(128)} %bitcast.place, f32[160,512]{1,0:T(8,128)S(1)} %get-tuple-element.29.refs_0_, f32[160,512]{1,0:T(8,128)S(1)} %collective-permute-done.2.refs_1_, f32[160,512]{1,0:T(8,128)S(1)} %collective-permute-done.20.refs_2_, ...), custom_call_target="tpu_custom_call" | custom-call | flops 6543114240 | bytes 17039360 | tf_op jit(solution)/shard_map/pallas_call | solution.py:342
  145.7 5.4 %shard_map.63 = f32[2560,512]{1,0:T(8,128)} custom-call(s32[3]{0:T(128)S(1)} %slice.6.ids, s32[1]{0:T(128)} %bitcast.place, f32[160,512]{1,0:T(8,128)S(1)} %collective-permute-done.8.refs_1_.refs_0_, f32[160,512]{1,0:T(8,128)S(1)} %collective-permute-done.11.refs_2_.refs_1_, ...), custom_call_target="tpu_custom_call", output_to_operand_aliasing={{}: (17, {})} | custom-call | flops 1509949440 | bytes 3932160 | tf_op jit(solution)/shard_map/pallas_call | solution.py:342
  (116 shorter events, 38.1 us)
Async XLA Ops:
  4.1 13.4 %collective-permute-start = (f32[160,512]{1,0:T(8,128)S(1)}, f32[160,512]{1,0:T(8,128)S(1)}, u32[]{:S(2)}, u32[]{:S(2)}) collective-permute-start(f32[160,512]{1,0:T(8,128)S(1)} %get-tuple-element.15), channel_id=1, source_target_pairs={{0,24},{24,0},{4,28},{28,4},{8,16},{16,8}} | collective-permute-start | bytes 983048 | tf_op jit(solution)/shard_map/ppermute | solution.py:472
  8.5 15.7 %collective-permute-start.1 = (f32[160,512]{1,0:T(8,128)S(1)}, f32[160,512]{1,0:T(8,128)S(1)}, u32[]{:S(2)}, u32[]{:S(2)}) collective-permute-start(f32[160,512]{1,0:T(8,128)S(1)} %get-tuple-element.17), channel_id=1, source_target_pairs={{0,24},{24,0},{4,28},{28,4},{8,16},{16,8}} | collective-permute-start | bytes 983048 | tf_op jit(solution)/shard_map/ppermute | solution.py:472
  17.6 13.0 %collective-permute-start.2 = (f32[160,512]{1,0:T(8,128)S(1)}, f32[160,512]{1,0:T(8,128)S(1)}, u32[]{:S(2)}, u32[]{:S(2)}) collective-permute-start(f32[160,512]{1,0:T(8,128)S(1)} %get-tuple-element.29.refs_0_), channel_id=1, source_target_pairs={{0,8},{8,16},{16,24},{24,28},{28,20},{20,12},{12,4},{4,0},{1,9},{9... | collective-permute-start | bytes 983048 | tf_op jit(solution)/shard_map/ppermute | solution.py:397
  24.3 13.7 %collective-permute-start.24 = (f32[160,512]{1,0:T(8,128)S(1)}, f32[160,512]{1,0:T(8,128)S(1)}, u32[]{:S(2)}, u32[]{:S(2)}) collective-permute-start(f32[160,512]{1,0:T(8,128)S(1)} %get-tuple-element.27.refs_8_.refs_13_), channel_id=1, source_target_pairs={{8,0},{16,8},{24,16},{28,24},{20,28},{12,20},{4,12},{0,4},{9,1},{1... | collective-permute-start | bytes 983048 | tf_op jit(solution)/shard_map/ppermute | solution.py:397
  30.6 12.9 %collective-permute-start.3 = (f32[160,512]{1,0:T(8,128)S(1)}, f32[160,512]{1,0:T(8,128)S(1)}, u32[]{:S(2)}, u32[]{:S(2)}) collective-permute-start(f32[160,512]{1,0:T(8,128)S(1)} %collective-permute-done.2.refs_1_), channel_id=1, source_target_pairs={{0,8},{8,16},{16,24},{24,28},{28,20},{20,12},{12,4},{4,0},{1,9},{9... | collective-permute-start | bytes 983048 | tf_op jit(solution)/shard_map/ppermute | solution.py:397
  35.5 15.0 %collective-permute-start.23 = (f32[160,512]{1,0:T(8,128)S(1)}, f32[160,512]{1,0:T(8,128)}, u32[]{:S(2)}, u32[]{:S(2)}) collective-permute-start(f32[160,512]{1,0:T(8,128)S(1)} %get-tuple-element.27.refs_8_.refs_13_), channel_id=1, source_target_pairs={{0,8},{8,16},{16,24},{24,28},{28,20},{20,12},{12,4},{4,0},{1,9},{9... | collective-permute-start | bytes 983048 | tf_op jit(solution)/shard_map/ppermute | solution.py:397
  38.0 15.2 %collective-permute-start.20 = (f32[160,512]{1,0:T(8,128)S(1)}, f32[160,512]{1,0:T(8,128)S(1)}, u32[]{:S(2)}, u32[]{:S(2)}) collective-permute-start(f32[160,512]{1,0:T(8,128)S(1)} %get-tuple-element.29.refs_0_), channel_id=1, source_target_pairs={{8,0},{16,8},{24,16},{28,24},{20,28},{12,20},{4,12},{0,4},{9,1},{1... | collective-permute-start | bytes 983048 | tf_op jit(solution)/shard_map/ppermute | solution.py:397
  38.0 17.8 %collective-permute-start.26 = (f32[160,512]{1,0:T(8,128)S(1)}, f32[160,512]{1,0:T(8,128)}, u32[]{:S(2)}, u32[]{:S(2)}) collective-permute-start(f32[160,512]{1,0:T(8,128)S(1)} %collective-permute-done.24.refs_10_.refs_15_), channel_id=1, source_target_pairs={{8,0},{16,8},{24,16},{28,24},{20,28},{12,20},{4,12},{0,4},{9,1},{1... | collective-permute-start | bytes 983048 | tf_op jit(solution)/shard_map/ppermute | solution.py:397
  43.5 14.0 %collective-permute-start.4 = (f32[160,512]{1,0:T(8,128)S(1)}, f32[160,512]{1,0:T(8,128)S(1)}, u32[]{:S(2)}, u32[]{:S(2)}) collective-permute-start(f32[160,512]{1,0:T(8,128)S(1)} %collective-permute-done.3.refs_3_), channel_id=1, source_target_pairs={{0,8},{8,16},{16,24},{24,28},{28,20},{20,12},{12,4},{4,0},{1,9},{9... | collective-permute-start | bytes 983048 | tf_op jit(solution)/shard_map/ppermute | solution.py:397
  50.6 14.1 %collective-permute-start.25 = (f32[160,512]{1,0:T(8,128)}, f32[160,512]{1,0:T(8,128)}, u32[]{:S(2)}, u32[]{:S(2)}) collective-permute-start(f32[160,512]{1,0:T(8,128)} %collective-permute-done.23.refs_9_.refs_14_), channel_id=1, source_target_pairs={{0,8},{8,16},{16,24},{24,28},{28,20},{20,12},{12,4},{4,0},{1,9},{9... | collective-permute-start | bytes 983048 | tf_op jit(solution)/shard_map/ppermute | solution.py:397
  53.2 14.2 %collective-permute-start.21 = (f32[160,512]{1,0:T(8,128)S(1)}, f32[160,512]{1,0:T(8,128)S(1)}, u32[]{:S(2)}, u32[]{:S(2)}) collective-permute-start(f32[160,512]{1,0:T(8,128)S(1)} %collective-permute-done.20.refs_2_), channel_id=1, source_target_pairs={{8,0},{16,8},{24,16},{28,24},{20,28},{12,20},{4,12},{0,4},{9,1},{1... | collective-permute-start | bytes 983048 | tf_op jit(solution)/shard_map/ppermute | solution.py:397
  55.8 15.8 %collective-permute-start.28 = (f32[160,512]{1,0:T(8,128)}, f32[160,512]{1,0:T(8,128)}, u32[]{:S(2)}, u32[]{:S(2)}) collective-permute-start(f32[160,512]{1,0:T(8,128)} %collective-permute-done.26.refs_12_.refs_17_), channel_id=1, source_target_pairs={{8,0},{16,8},{24,16},{28,24},{20,28},{12,20},{4,12},{0,4},{9,1},{1... | collective-permute-start | bytes 983048 | tf_op jit(solution)/shard_map/ppermute | solution.py:397
  57.6 13.9 %collective-permute-start.13 = (f32[160,512]{1,0:T(8,128)S(1)}, f32[160,512]{1,0:T(8,128)}, u32[]{:S(2)}, u32[]{:S(2)}) collective-permute-start(f32[160,512]{1,0:T(8,128)S(1)} %get-tuple-element.21.refs_1_), channel_id=1, source_target_pairs={{0,8},{8,16},{16,24},{24,28},{28,20},{20,12},{12,4},{4,0},{1,9},{9... | collective-permute-start | bytes 983048 | tf_op jit(solution)/shard_map/ppermute | solution.py:397
  60.2 17.3 %collective-permute-start.9 = (f32[160,512]{1,0:T(8,128)S(1)}, f32[160,512]{1,0:T(8,128)S(1)}, u32[]{:S(2)}, u32[]{:S(2)}) collective-permute-start(f32[160,512]{1,0:T(8,128)S(1)} %get-tuple-element.20.refs_0_), channel_id=1, source_target_pairs={{8,0},{16,8},{24,16},{28,24},{20,28},{12,20},{4,12},{0,4},{9,1},{1... | collective-permute-start | bytes 983048 | tf_op jit(solution)/shard_map/ppermute | solution.py:397
  64.7 12.8 %collective-permute-start.5 = (f32[160,512]{1,0:T(8,128)S(1)}, f32[160,512]{1,0:T(8,128)S(1)}, u32[]{:S(2)}, u32[]{:S(2)}) collective-permute-start(f32[160,512]{1,0:T(8,128)S(1)} %collective-permute-done.4.refs_2_.refs_5_), channel_id=1, source_target_pairs={{0,8},{8,16},{16,24},{24,28},{28,20},{20,12},{12,4},{4,0},{1,9},{9... | collective-permute-start | bytes 983048 | tf_op jit(solution)/shard_map/ppermute | solution.py:397
  67.3 12.3 %collective-permute-start.27 = (f32[160,512]{1,0:T(8,128)}, f32[160,512]{1,0:T(8,128)S(1)}, u32[]{:S(2)}, u32[]{:S(2)}) collective-permute-start(f32[160,512]{1,0:T(8,128)} %collective-permute-done.25.refs_11_.refs_16_), channel_id=1, source_target_pairs={{0,8},{8,16},{16,24},{24,28},{28,20},{20,12},{12,4},{4,0},{1,9},{9... | collective-permute-start | bytes 983048 | tf_op jit(solution)/shard_map/ppermute | solution.py:397
  71.5 9.5 %collective-permute-start.22 = (f32[160,512]{1,0:T(8,128)S(1)}, f32[160,512]{1,0:T(8,128)S(1)}, u32[]{:S(2)}, u32[]{:S(2)}) collective-permute-start(f32[160,512]{1,0:T(8,128)S(1)} %collective-permute-done.21.refs_4_), channel_id=1, source_target_pairs={{8,0},{16,8},{24,16},{28,24},{20,28},{12,20},{4,12},{0,4},{9,1},{1... | collective-permute-start | bytes 983048 | tf_op jit(solution)/shard_map/ppermute | solution.py:397
  71.5 13.5 %collective-permute-start.29 = (f32[160,512]{1,0:T(8,128)}, f32[160,512]{1,0:T(8,128)S(1)}, u32[]{:S(2)}, u32[]{:S(2)}) collective-permute-start(f32[160,512]{1,0:T(8,128)} %collective-permute-done.28.refs_14_.refs_19_), channel_id=1, source_target_pairs={{8,0},{16,8},{24,16},{28,24},{20,28},{12,20},{4,12},{0,4},{9,1},{1... | collective-permute-start | bytes 983048 | tf_op jit(solution)/shard_map/ppermute | solution.py:397
  77.5 15.6 %collective-permute-start.16 = (f32[160,512]{1,0:T(8,128)S(1)}, f32[160,512]{1,0:T(8,128)S(1)}, u32[]{:S(2)}, u32[]{:S(2)}) collective-permute-start(f32[160,512]{1,0:T(8,128)S(1)} %get-tuple-element.23.refs_21_), channel_id=1, source_target_pairs={{8,0},{16,8},{24,16},{28,24},{20,28},{12,20},{4,12},{0,4},{9,1},{1... | collective-permute-start | bytes 983048 | tf_op jit(solution)/shard_map/ppermute | solution.py:397
  77.6 15.6 %collective-permute-start.6 = (f32[160,512]{1,0:T(8,128)S(1)}, f32[160,512]{1,0:T(8,128)S(1)}, u32[]{:S(2)}, u32[]{:S(2)}) collective-permute-start(f32[160,512]{1,0:T(8,128)S(1)} %get-tuple-element.22.refs_8_), channel_id=1, source_target_pairs={{0,8},{8,16},{16,24},{24,28},{28,20},{20,12},{12,4},{4,0},{1,9},{9... | collective-permute-start | bytes 983048 | tf_op jit(solution)/shard_map/ppermute | solution.py:397
  91.7 26.3 %collective-permute-start.31 = (f32[512,512]{1,0:T(8,128)}, f32[512,512]{1,0:T(8,128)S(1)}, u32[]{:S(2)}, u32[]{:S(2)}) collective-permute-start(f32[512,512]{1,0:T(8,128)} %shard_map.58.refs_17_.refs_27_.refs_7_), channel_id=1, source_target_pairs={{0,2},{4,6},{8,10},{12,14},{16,18},{20,22},{24,26},{28,30}} | collective-permute-start | bytes 3145736 | tf_op jit(solution)/shard_map/ppermute | solution.py:408
  102.1 23.6 %collective-permute-start.34 = (f32[512,512]{1,0:T(8,128)}, f32[512,512]{1,0:T(8,128)S(1)}, u32[]{:S(2)}, u32[]{:S(2)}) collective-permute-start(f32[512,512]{1,0:T(8,128)} %shard_map.60.refs_31_.refs_11_), channel_id=1, source_target_pairs={{0,2},{4,6},{8,10},{12,14},{16,18},{20,22},{24,26},{28,30}} | collective-permute-start | bytes 3145736 | tf_op jit(solution)/shard_map/ppermute | solution.py:408
  127.7 18.0 %collective-permute-start.12 = (f32[160,512]{1,0:T(8,128)S(1)}, f32[160,512]{1,0:T(8,128)S(1)}, u32[]{:S(2)}, u32[]{:S(2)}) collective-permute-start(f32[160,512]{1,0:T(8,128)S(1)} %collective-permute-done.8.refs_1_.refs_0_), channel_id=1, source_target_pairs={{0,8},{8,16},{16,24},{24,28},{28,20},{20,12},{12,4},{4,0},{1,9},{9... | collective-permute-start | bytes 983048 | tf_op jit(solution)/shard_map/ppermute | solution.py:397
  129.6 16.1 %collective-permute-start.19 = (f32[160,512]{1,0:T(8,128)S(1)}, f32[160,512]{1,0:T(8,128)S(1)}, u32[]{:S(2)}, u32[]{:S(2)}) collective-permute-start(f32[160,512]{1,0:T(8,128)S(1)} %collective-permute-done.18.refs_4_), channel_id=1, source_target_pairs={{8,0},{16,8},{24,16},{28,24},{20,28},{12,20},{4,12},{0,4},{9,1},{1... | collective-permute-start | bytes 983048 | tf_op jit(solution)/shard_map/ppermute | solution.py:397
  (38 other events, 572.8 us)

commit v5 on v4

--- a/solution.py
+++ b/solution.py
@@ -127,56 +127,44 @@
     )(me, place, factor)
 
 
-def solve_kernel(pieces, rows, width, chunk, block, panel, ids, place, *refs):
-    held, refs = refs[: 2 * pieces], refs[2 * pieces :]
-    rhs, refs = refs[0], refs[1:]
-    earlier = refs[:panel]
-    solved, lower, piece_sem, rhs_sem = refs[len(refs) - 4 :]
-    first, last = panel * width, (panel + 1) * width
-    side = lower.shape[1] - LANES
+def solve_kernel(pieces, rows, width, chunk, block, ids, place, *refs):
+    held, rhs = refs[: 2 * pieces], refs[2 * pieces]
+    *outs, lower, solved, piece_sem, rhs_sem, out_sem = refs[len(refs) - 7 :]
+    depth = 2 * width
 
     @pl.when(place[0] == 0)
     def _():
         def copies(i):
             at = pl.ds(pl.multiple_of(ids[i] * rows, 8), rows)
-            cut = 0 if panel else width - LANES
             return [
                 pltpu.make_async_copy(
-                    held[i], lower.at[at, pl.ds(0, width)], piece_sem.at[0, i]
-                ),
-                pltpu.make_async_copy(
-                    held[pieces + i].at[:, pl.ds(cut, width - cut)],
-                    lower.at[at, pl.ds(width, width - cut)],
-                    piece_sem.at[1, i],
-                ),
-            ]
-
-        def needed(i):
-            return (ids[i] * rows < last) & ((ids[i] + 1) * rows > first)
+                    held[k * pieces + i], lower.at[at, pl.ds(k * width, width)], piece_sem.at[k, i]
+                )
+                for k in range(2)
+            ]
 
         for i in range(pieces):
 
-            @pl.when(needed(i))
+            @pl.when(ids[i] * rows < depth)
             def _(i=i):
                 for copy in copies(i):
                     copy.start()
 
-        load = pltpu.make_async_copy(rhs.at[pl.ds(first, width)], solved, rhs_sem)
+        load = pltpu.make_async_copy(rhs.at[pl.ds(0, depth)], solved, rhs_sem)
         load.start()
         for i in range(pieces):
 
-            @pl.when(needed(i))
+            @pl.when(ids[i] * rows < depth)
             def _(i=i):
                 for copy in copies(i):
                     copy.wait()
 
-        load.wait()
         row, col = grid_ids(chunk)
         lane = lax.broadcasted_iota(jnp.int32, (chunk, LANES), 1)
-        starts = range(0, width, chunk)
+        starts = range(0, depth, chunk)
         inverses = []
         for j in starts:
-            value = lower[first + j : first + j + chunk, side:]
+            value = lower[j : j + chunk, depth - LANES :]
             value = jnp.where(lane >= LANES - block, value, 0.0)
             shift = block
             while shift < LANES:
@@ -190,14 +178,7 @@
             parts = [split16(inverse) for inverse in inverses]
             inner = [
                 dot_split(
-                    split16(
-                        jnp.where(
-                            below,
-                            lower[first + j : first + j + chunk, first + j : first + j + chunk],
-                            0.0,
-                        )
-                    ),
-                    part,
+                    split16(jnp.where(below, lower[j : j + chunk, j : j + chunk], 0.0)), part
                 )
                 for j, part in zip(starts, parts)
             ]
@@ -206,46 +187,49 @@
                 for inverse, part, value in zip(inverses, parts, inner)
             ]
             half *= 2
-        for k in range(panel):
-            solved[...] = solved[...] - dot_split(
-                split16(lower[first:last, k * width : (k + 1) * width]), split16(earlier[k][...])
-            )
+        load.wait()
+        stores = [
+            pltpu.make_async_copy(solved.at[pl.ds(k * width, width)], outs[k], out_sem.at[k])
+            for k in range(2)
+        ]
         for j in starts:
             value = solved[j : j + chunk]
             if j:
-                at = slice(first + j, first + j + chunk)
                 value = value - dot_split(
-                    split16(lower[at, first : first + j]), split16(solved[:j])
+                    split16(lower[j : j + chunk, :j]), split16(solved[:j])
                 )
             solved[j : j + chunk] = dot_split(split16(inverses[j // chunk]), split16(value))
-
-
-def solve_panel(panel, ids, place, held, rhs, earlier, after, width, block):
+            if (j + chunk) % width == 0:
+                stores[j // width].start()
+        for store in stores:
+            store.wait()
+
+
+def solve_panels(ids, place, held, rhs, after, width, block):
     pieces = len(held[0])
     rows = held[0][0].shape[0]
-    columns = rhs.shape[1]
-    tall = -(-(panel + 1) * width // rows) * rows
+    columns, depth = rhs.shape[1], 2 * width
+    tall = -(-depth // rows) * rows
     chunk = math.gcd(width, 2 * LANES)
     return pl.pallas_call(
-        functools.partial(solve_kernel, pieces, rows, width, chunk, block, panel),
-        out_shape=jax.ShapeDtypeStruct((width, columns), jnp.float32),
-        in_specs=[SCALARS] * 2
-        + [ANY] * (2 * pieces + 1)
-        + [WHOLE] * panel
-        + [ANY] * len(after),
-        out_specs=WHOLE,
+        functools.partial(solve_kernel, pieces, rows, width, chunk, block),
+        out_shape=[jax.ShapeDtypeStruct((width, columns), jnp.float32)] * 2,
+        in_specs=[SCALARS] * 2 + [ANY] * (2 * pieces + 1 + len(after)),
+        out_specs=[ANY] * 2,
         scratch_shapes=[
-            pltpu.VMEM((tall, 2 * width if panel else width + LANES), jnp.float32),
+            pltpu.VMEM((tall, depth), jnp.float32),
+            pltpu.VMEM((depth, columns), jnp.float32),
             pltpu.SemaphoreType.DMA((2, pieces)),
             pltpu.SemaphoreType.DMA,
+            pltpu.SemaphoreType.DMA((2,)),
         ],
         compiler_params=pltpu.CompilerParams(vmem_limit_bytes=VMEM_BYTES),
         cost_estimate=pl.CostEstimate(
-            flops=24 * (panel + 1) * width * width * columns,
-            bytes_accessed=12 * width * columns,
+            flops=72 * width * width * columns,
+            bytes_accessed=24 * width * columns,
             transcendentals=0,
         ),
-    )(ids, place, *held[0], *held[1], rhs, *earlier, *after)
+    )(ids, place, *held[0], *held[1], rhs, *after)
 
 
 def update_kernel(pieces, rows, width, tile, step, places, ids, place, *refs):
@@ -301,9 +285,12 @@
         def _(t):
             inside = pl.multiple_of(t * tile, 8)
             top = start + ids[i] * rows + inside
-            product[...] = dot_split(
-                split16(lower[i, pl.ds(inside, tile)]), (high[...], low[...])
-            )
+
+            @pl.when(top + tile > depth)
+            def _():
+                product[...] = dot_split(
+                    split16(lower[i, pl.ds(inside, tile)]), (high[...], low[...])
+                )
 
             @pl.when(top >= depth)
             def _():
@@ -463,7 +450,7 @@
             ]
             top, top_spots = held, jnp.zeros_like(me)
             groups = [(held, top_spots)]
-            after, near = [[], []], [[], []]
+            after, near = [], [[], []]
         else:
             movers = len(partners)
             *halves, sent_first, sent_second = prepare(me, place, factor, block, 2, movers)
@@ -493,9 +480,9 @@
             free = gate(own[1], [steps[-2][0][0]])
             full = gate(free, [steps[-1][0][0]])
             rest, steps = ring_pass([[full[0], free[0]], [free[1], full[1]]], ring)
-            after = [[steps[0][0][1], steps[0][1][0]], [steps[0][0][0], steps[0][1][1]]]
+            after = [steps[0][0][1], steps[0][1][0]]
             near = [steps[i][0] + steps[i][1] for i in (1, -2)]
-            top_spots, cut = spots[0], 2 * half - 3
+            top_spots, cut = spots[0], 2 * half - 1
             groups = [
                 (
                     [top[k] + rest[k][:cut] for k in range(2)],
@@ -503,12 +490,10 @@
                 ),
                 ([rest[k][cut:] for k in range(2)], spots[1][cut:]),
             ]
-        first = solve_panel(0, top_spots, place, top, right_side, [], after[0], width, block)
-        second = solve_panel(1, top_spots, place, top, right_side, [first], after[1], width, block)
-        solved = [
-            spread_near(spread_far(first, places), places, near[0]),
-            spread_near(spread_far(second, places), places, near[1]),
-        ]
+        first, second = solve_panels(top_spots, place, top, right_side, after, width, block)
+        first = spread_near(spread_far(first, places), places, near[0])
+        second = spread_near(spread_far(second, places), places, near[1] + first[1:2])
+        solved = [first, second]
         result = None
         for held, spots in groups:
             result = update(spots, place, held, right_side, solved, width, result)

time: 151 us -> 154 us (1.020)
  waiting for transfers between devices: 52.5 us -> 61.3 us
  Pallas kernels: 36.1 us -> 28.6 us
    ppermute x28, waiting for transfers between devices: 46.7 us -> 55.6 us  [ring_pass(): going[k][way] = lax.ppermute(going[k][way], 'src', pairs)]
    pallas_call x2 -> x1, Pallas kernels: 13.3 us -> 9.03 us  [solve_panels(): pl.pallas_call(functools.partial(solve_kernel, pieces, rows, width, chunk...]
    pallas_call x2, Pallas kernels: 18.7 us -> 15.5 us  [update(): pl.pallas_call(functools.partial(update_kernel, pieces, rows, width, tile...]
    unnamed x52 -> x58, local copies, waits for them, and re-layouts: 5.87 us -> 6.03 us
  transfers between devices with their start and end apart: 36 -> 36, of which waited for: 17 -> 13; matrix products, arithmetic and copies ran while one was open for 0% -> 1% of each run, Pallas kernels for 18% -> 14%
where the time goes in v5:
time: 154 us; the launch traced here: 153 us
  waiting for transfers between devices  61.3 us (40%)
  starting transfers between devices  56 us (36%)
  Pallas kernels  28.6 us (19%)
  local copies, waits for them, and re-layouts  6.59 us (4%)
    ppermute x28, waiting for transfers between devices, ring_pass(): going[k][way] = lax.ppermute(going[k][way], 'src', pairs)  55.6 us
    ppermute x28, starting transfers between devices, ring_pass(): going[k][way] = lax.ppermute(going[k][way], 'src', pairs)  41.5 us
    pallas_call x2, Pallas kernels, update(): pl.pallas_call(functools.partial(update_kernel, pieces, rows, width, tile...  15.5 us
    pallas_call x1, Pallas kernels, solve_panels(): pl.pallas_call(functools.partial(solve_kernel, pieces, rows, width, chunk...  9.03 us
    ppermute x2, starting transfers between devices, local(): got = [lax.ppermute(sent, axes, swap) for sent in (sent_first, sent_second)]  7.64 us
    unnamed x58, local copies, waits for them, and re-layouts  6.03 us
    ppermute x2, waiting for transfers between devices, local(): got = [lax.ppermute(sent, axes, swap) for sent in (sent_first, sent_second)]  5.76 us
    ppermute x4, starting transfers between devices, spread_near(): found[r + 1] = lax.ppermute(found[r], 'row', [(r, r + 1)])  4.13 us
  transfers between devices with their start and end apart: 36, of which 13 were waited for; matrix products, arithmetic and copies ran while one was open for 1% of the time, Pallas kernels for 14%

profile of v5, /device:TPU:0, one launch (start us, length us, event | category | flops | bytes accessed | tf_op | source)
XLA Modules:
  0.0 153.5 jit_solution(6504798885590349031)
XLA Ops:
  0.0 4.1 %shard_map.55 = (f32[160,512]{1,0:T(8,128)S(1)}, f32[160,512]{1,0:T(8,128)S(1)}, f32[160,512]{1,0:T(8,128)S(1)}, f32[160,512]{1,0:T(8,128)S(1)}, f32[160,512]{1,0:T(8,128)S(1)}, /*index=5*/f32[160,512]{1,0:T(8,128)S(1)}) custom-call(s32[1]{0:T(128)} %bitcast.1.me, s32[1]{0:T(128)} %bitcast.place, f32[320,1024]{1,0:T(8,128)} %source.1), custom_call_target="tpu_custom_call" | custom-call | flops 1000 | bytes 1000 | tf_op jit(solution)/shard_map/pallas_call | solution.py:115
  4.1 4.4 %collective-permute-start = (f32[160,512]{1,0:T(8,128)S(1)}, f32[160,512]{1,0:T(8,128)S(1)}, u32[]{:S(2)}, u32[]{:S(2)}) collective-permute-start(f32[160,512]{1,0:T(8,128)S(1)} %get-tuple-element.17), channel_id=1, source_target_pairs={{0,24},{24,0},{4,28},{28,4},{8,16},{16,8}} | collective-permute-start | bytes 983048 | tf_op jit(solution)/shard_map/ppermute | solution.py:459
  8.5 3.2 %collective-permute-start.1 = (f32[160,512]{1,0:T(8,128)S(1)}, f32[160,512]{1,0:T(8,128)S(1)}, u32[]{:S(2)}, u32[]{:S(2)}) collective-permute-start(f32[160,512]{1,0:T(8,128)S(1)} %get-tuple-element.19), channel_id=1, source_target_pairs={{0,24},{24,0},{4,28},{28,4},{8,16},{16,8}} | collective-permute-start | bytes 983048 | tf_op jit(solution)/shard_map/ppermute | solution.py:459
  11.8 5.8 %collective-permute-done = f32[160,512]{1,0:T(8,128)S(1)} collective-permute-done((f32[160,512]{1,0:T(8,128)S(1)}, f32[160,512]{1,0:T(8,128)S(1)}, u32[]{:S(2)}, u32[]{:S(2)}) %collective-permute-start) | collective-permute-done | bytes 327712 | tf_op jit(solution)/shard_map/ppermute | solution.py:459
  17.6 6.6 %collective-permute-start.2 = (f32[160,512]{1,0:T(8,128)S(1)}, f32[160,512]{1,0:T(8,128)S(1)}, u32[]{:S(2)}, u32[]{:S(2)}) collective-permute-start(f32[160,512]{1,0:T(8,128)S(1)} %get-tuple-element.33.refs_0_), channel_id=1, source_target_pairs={{0,8},{8,16},{16,24},{24,28},{28,20},{20,12},{12,4},{4,0},{1,9},{9... | collective-permute-start | bytes 983048 | tf_op jit(solution)/shard_map/ppermute | solution.py:384
  26.2 4.4 %collective-permute-done.2.refs_1_ = f32[160,512]{1,0:T(8,128)S(1)} collective-permute-done((f32[160,512]{1,0:T(8,128)S(1)}, f32[160,512]{1,0:T(8,128)S(1)}, u32[]{:S(2)}, u32[]{:S(2)}) %collective-permute-start.2) | collective-permute-done | bytes 327712 | tf_op jit(solution)/shard_map/ppermute | solution.py:384
  30.6 4.9 %collective-permute-start.3 = (f32[160,512]{1,0:T(8,128)S(1)}, f32[160,512]{1,0:T(8,128)S(1)}, u32[]{:S(2)}, u32[]{:S(2)}) collective-permute-start(f32[160,512]{1,0:T(8,128)S(1)} %collective-permute-done.2.refs_1_), channel_id=1, source_target_pairs={{0,8},{8,16},{16,24},{24,28},{28,20},{20,12},{12,4},{4,0},{1,9},{9... | collective-permute-start | bytes 983048 | tf_op jit(solution)/shard_map/ppermute | solution.py:384
  38.1 5.2 %collective-permute-done.3.refs_3_ = f32[160,512]{1,0:T(8,128)S(1)} collective-permute-done((f32[160,512]{1,0:T(8,128)S(1)}, f32[160,512]{1,0:T(8,128)S(1)}, u32[]{:S(2)}, u32[]{:S(2)}) %collective-permute-start.3) | collective-permute-done | bytes 327712 | tf_op jit(solution)/shard_map/ppermute | solution.py:384
  43.2 2.9 %collective-permute-start.4 = (f32[160,512]{1,0:T(8,128)S(1)}, f32[160,512]{1,0:T(8,128)S(1)}, u32[]{:S(2)}, u32[]{:S(2)}) collective-permute-start(f32[160,512]{1,0:T(8,128)S(1)} %collective-permute-done.3.refs_3_), channel_id=1, source_target_pairs={{0,8},{8,16},{16,24},{24,28},{28,20},{20,12},{12,4},{4,0},{1,9},{9... | collective-permute-start | bytes 983048 | tf_op jit(solution)/shard_map/ppermute | solution.py:384
  46.7 3.3 %collective-permute-start.19 = (f32[160,512]{1,0:T(8,128)}, f32[160,512]{1,0:T(8,128)}, u32[]{:S(2)}, u32[]{:S(2)}) collective-permute-start(f32[160,512]{1,0:T(8,128)} %collective-permute-done.17.refs_9_.refs_16_), channel_id=1, source_target_pairs={{0,8},{8,16},{16,24},{24,28},{28,20},{20,12},{12,4},{4,0},{1,9},{9... | collective-permute-start | bytes 983048 | tf_op jit(solution)/shard_map/ppermute | solution.py:384
  50.1 5.7 %collective-permute-done.20.refs_12_.refs_19_ = f32[160,512]{1,0:T(8,128)} collective-permute-done((f32[160,512]{1,0:T(8,128)S(1)}, f32[160,512]{1,0:T(8,128)}, u32[]{:S(2)}, u32[]{:S(2)}) %collective-permute-start.20) | collective-permute-done | bytes 327712 | tf_op jit(solution)/shard_map/ppermute | solution.py:384
  55.9 5.5 %collective-permute-done.19.refs_11_.refs_18_ = f32[160,512]{1,0:T(8,128)} collective-permute-done((f32[160,512]{1,0:T(8,128)}, f32[160,512]{1,0:T(8,128)}, u32[]{:S(2)}, u32[]{:S(2)}) %collective-permute-start.19) | collective-permute-done | bytes 327712 | tf_op jit(solution)/shard_map/ppermute | solution.py:384
  61.4 2.9 %collective-permute-start.21 = (f32[160,512]{1,0:T(8,128)}, f32[160,512]{1,0:T(8,128)S(1)}, u32[]{:S(2)}, u32[]{:S(2)}) collective-permute-start(f32[160,512]{1,0:T(8,128)} %collective-permute-done.19.refs_11_.refs_18_), channel_id=1, source_target_pairs={{0,8},{8,16},{16,24},{24,28},{28,20},{20,12},{12,4},{4,0},{1,9},{9... | collective-permute-start | bytes 983048 | tf_op jit(solution)/shard_map/ppermute | solution.py:384
  66.7 3.1 %collective-permute-done.22.refs_14_.refs_21_ = f32[160,512]{1,0:T(8,128)} collective-permute-done((f32[160,512]{1,0:T(8,128)}, f32[160,512]{1,0:T(8,128)}, u32[]{:S(2)}, u32[]{:S(2)}) %collective-permute-start.22) | collective-permute-done | bytes 327712 | tf_op jit(solution)/shard_map/ppermute | solution.py:384
  70.4 6.4 %collective-permute-done.24.refs_17_.refs_10_ = f32[160,512]{1,0:T(8,128)} collective-permute-done((f32[160,512]{1,0:T(8,128)S(1)}, f32[160,512]{1,0:T(8,128)}, u32[]{:S(2)}, u32[]{:S(2)}) %collective-permute-start.24) | collective-permute-done | bytes 327712 | tf_op jit(solution)/shard_map/ppermute | solution.py:384
  77.4 5.7 %collective-permute-done.5.refs_2_.refs_7_ = f32[160,512]{1,0:T(8,128)S(1)} collective-permute-done((f32[160,512]{1,0:T(8,128)S(1)}, f32[160,512]{1,0:T(8,128)S(1)}, u32[]{:S(2)}, u32[]{:S(2)}) %collective-permute-start.5) | collective-permute-done | bytes 327712 | tf_op jit(solution)/shard_map/ppermute | solution.py:384
  83.1 2.6 %collective-permute-start.6 = (f32[160,512]{1,0:T(8,128)S(1)}, f32[160,512]{1,0:T(8,128)S(1)}, u32[]{:S(2)}, u32[]{:S(2)}) collective-permute-start(f32[160,512]{1,0:T(8,128)S(1)} %get-tuple-element.24.refs_8_), channel_id=1, source_target_pairs={{0,8},{8,16},{16,24},{24,28},{28,20},{20,12},{12,4},{4,0},{1,9},{9... | collective-permute-start | bytes 983048 | tf_op jit(solution)/shard_map/ppermute | solution.py:384
  85.7 2.5 %collective-permute-start.29 = (f32[160,512]{1,0:T(8,128)S(1)}, f32[160,512]{1,0:T(8,128)S(1)}, u32[]{:S(2)}, u32[]{:S(2)}) collective-permute-start(f32[160,512]{1,0:T(8,128)S(1)} %collective-permute-done.25.refs_18_.refs_24_), channel_id=1, source_target_pairs={{0,8},{8,16},{16,24},{24,28},{28,20},{20,12},{12,4},{4,0},{1,9},{9... | collective-permute-start | bytes 983048 | tf_op jit(solution)/shard_map/ppermute | solution.py:384
  89.0 9.0 %shard_map.58 = (f32[512,512]{1,0:T(8,128)}, f32[512,512]{1,0:T(8,128)}) custom-call(s32[8]{0:T(128)S(1)} %get-tuple-element.35.ids, s32[1]{0:T(128)} %bitcast.place, f32[160,512]{1,0:T(8,128)S(1)} %get-tuple-element.33.refs_0_, f32[160,512]{1,0:T(8,128)S(1)} %collective-permute-done.2.refs_1_, f32[160,512]{1,0:T(8,128)S(1)} %collective-permute-done.14.refs_2_, ...), custom_call_target="tpu_custom_call" | custom-call | flops 9663676416 | bytes 6291456 | tf_op jit(solution)/shard_map/pallas_call | solution.py:214
  104.3 7.6 %collective-permute-done.11.refs_4_.refs_27_ = f32[160,512]{1,0:T(8,128)S(1)} collective-permute-done((f32[160,512]{1,0:T(8,128)S(1)}, f32[160,512]{1,0:T(8,128)S(1)}, u32[]{:S(2)}, u32[]{:S(2)}) %collective-permute-start.11) | collective-permute-done | bytes 327712 | tf_op jit(solution)/shard_map/ppermute | solution.py:384
  113.9 5.0 %collective-permute-done.33.refs_2_.refs_14_ = f32[160,512]{1,0:T(8,128)S(1)} collective-permute-done((f32[160,512]{1,0:T(8,128)S(1)}, f32[160,512]{1,0:T(8,128)S(1)}, u32[]{:S(2)}, u32[]{:S(2)}) %collective-permute-start.33) | collective-permute-done | bytes 327712 | tf_op jit(solution)/shard_map/ppermute | solution.py:384
  120.9 6.1 %collective-permute-done.12.refs_4_.refs_29_ = f32[160,512]{1,0:T(8,128)S(1)} collective-permute-done((f32[160,512]{1,0:T(8,128)S(1)}, f32[160,512]{1,0:T(8,128)S(1)}, u32[]{:S(2)}, u32[]{:S(2)}) %collective-permute-start.12) | collective-permute-done | bytes 327712 | tf_op jit(solution)/shard_map/ppermute | solution.py:384
  138.0 11.8 %shard_map.61.refs_11_ = f32[2560,512]{1,0:T(8,128)} custom-call(s32[15]{0:T(128)S(1)} %pad_add_fusion.ids, s32[1]{0:T(128)} %bitcast.place, f32[160,512]{1,0:T(8,128)S(1)} %get-tuple-element.33.refs_0_, f32[160,512]{1,0:T(8,128)S(1)} %collective-permute-done.2.refs_1_, f32[160,512]{1,0:T(8,128)S(1)} %collective-permute-done.14.refs_2_, ...), custom_call_target="tpu_custom_call" | custom-call | flops 7549747200 | bytes 19660800 | tf_op jit(solution)/shard_map/pallas_call | solution.py:329
  149.8 3.7 %shard_map.62 = f32[2560,512]{1,0:T(8,128)} custom-call(s32[1]{0:T(128)} %slice.6.ids, s32[1]{0:T(128)} %bitcast.place, f32[160,512]{1,0:T(8,128)S(1)} %collective-permute-done.9.refs_0_, f32[160,512]{1,0:T(8,128)S(1)} %collective-permute-done.13.refs_1_, f32[2560,512]{1,0:T(8,128)} %refs_2_.1, ...), custom_call_target="tpu_custom_call", output_to_operand_aliasing={{}: (13, {})} | custom-call | flops 503316480 | bytes 1310720 | tf_op jit(solution)/shard_map/pallas_call | solution.py:329
  (121 shorter events, 30.7 us)
Async XLA Ops:
  4.1 13.4 %collective-permute-start = (f32[160,512]{1,0:T(8,128)S(1)}, f32[160,512]{1,0:T(8,128)S(1)}, u32[]{:S(2)}, u32[]{:S(2)}) collective-permute-start(f32[160,512]{1,0:T(8,128)S(1)} %get-tuple-element.17), channel_id=1, source_target_pairs={{0,24},{24,0},{4,28},{28,4},{8,16},{16,8}} | collective-permute-start | bytes 983048 | tf_op jit(solution)/shard_map/ppermute | solution.py:459
  8.5 15.7 %collective-permute-start.1 = (f32[160,512]{1,0:T(8,128)S(1)}, f32[160,512]{1,0:T(8,128)S(1)}, u32[]{:S(2)}, u32[]{:S(2)}) collective-permute-start(f32[160,512]{1,0:T(8,128)S(1)} %get-tuple-element.19), channel_id=1, source_target_pairs={{0,24},{24,0},{4,28},{28,4},{8,16},{16,8}} | collective-permute-start | bytes 983048 | tf_op jit(solution)/shard_map/ppermute | solution.py:459
  17.6 13.0 %collective-permute-start.2 = (f32[160,512]{1,0:T(8,128)S(1)}, f32[160,512]{1,0:T(8,128)S(1)}, u32[]{:S(2)}, u32[]{:S(2)}) collective-permute-start(f32[160,512]{1,0:T(8,128)S(1)} %get-tuple-element.33.refs_0_), channel_id=1, source_target_pairs={{0,8},{8,16},{16,24},{24,28},{28,20},{20,12},{12,4},{4,0},{1,9},{9... | collective-permute-start | bytes 983048 | tf_op jit(solution)/shard_map/ppermute | solution.py:384
  24.3 13.7 %collective-permute-start.18 = (f32[160,512]{1,0:T(8,128)S(1)}, f32[160,512]{1,0:T(8,128)S(1)}, u32[]{:S(2)}, u32[]{:S(2)}) collective-permute-start(f32[160,512]{1,0:T(8,128)S(1)} %get-tuple-element.31.refs_8_.refs_15_), channel_id=1, source_target_pairs={{8,0},{16,8},{24,16},{28,24},{20,28},{12,20},{4,12},{0,4},{9,1},{1... | collective-permute-start | bytes 983048 | tf_op jit(solution)/shard_map/ppermute | solution.py:384
  30.6 12.6 %collective-permute-start.3 = (f32[160,512]{1,0:T(8,128)S(1)}, f32[160,512]{1,0:T(8,128)S(1)}, u32[]{:S(2)}, u32[]{:S(2)}) collective-permute-start(f32[160,512]{1,0:T(8,128)S(1)} %collective-permute-done.2.refs_1_), channel_id=1, source_target_pairs={{0,8},{8,16},{16,24},{24,28},{28,20},{20,12},{12,4},{4,0},{1,9},{9... | collective-permute-start | bytes 983048 | tf_op jit(solution)/shard_map/ppermute | solution.py:384
  38.0 17.8 %collective-permute-start.20 = (f32[160,512]{1,0:T(8,128)S(1)}, f32[160,512]{1,0:T(8,128)}, u32[]{:S(2)}, u32[]{:S(2)}) collective-permute-start(f32[160,512]{1,0:T(8,128)S(1)} %collective-permute-done.18.refs_10_.refs_17_), channel_id=1, source_target_pairs={{8,0},{16,8},{24,16},{28,24},{20,28},{12,20},{4,12},{0,4},{9,1},{1... | collective-permute-start | bytes 983048 | tf_op jit(solution)/shard_map/ppermute | solution.py:384
  43.2 12.5 %collective-permute-start.4 = (f32[160,512]{1,0:T(8,128)S(1)}, f32[160,512]{1,0:T(8,128)S(1)}, u32[]{:S(2)}, u32[]{:S(2)}) collective-permute-start(f32[160,512]{1,0:T(8,128)S(1)} %collective-permute-done.3.refs_3_), channel_id=1, source_target_pairs={{0,8},{8,16},{16,24},{24,28},{28,20},{20,12},{12,4},{4,0},{1,9},{9... | collective-permute-start | bytes 983048 | tf_op jit(solution)/shard_map/ppermute | solution.py:384
  46.7 14.6 %collective-permute-start.19 = (f32[160,512]{1,0:T(8,128)}, f32[160,512]{1,0:T(8,128)}, u32[]{:S(2)}, u32[]{:S(2)}) collective-permute-start(f32[160,512]{1,0:T(8,128)} %collective-permute-done.17.refs_9_.refs_16_), channel_id=1, source_target_pairs={{0,8},{8,16},{16,24},{24,28},{28,20},{20,12},{12,4},{4,0},{1,9},{9... | collective-permute-start | bytes 983048 | tf_op jit(solution)/shard_map/ppermute | solution.py:384
  50.1 14.1 %collective-permute-start.15 = (f32[160,512]{1,0:T(8,128)S(1)}, f32[160,512]{1,0:T(8,128)S(1)}, u32[]{:S(2)}, u32[]{:S(2)}) collective-permute-start(f32[160,512]{1,0:T(8,128)S(1)} %collective-permute-done.14.refs_2_), channel_id=1, source_target_pairs={{8,0},{16,8},{24,16},{28,24},{20,28},{12,20},{4,12},{0,4},{9,1},{1... | collective-permute-start | bytes 983048 | tf_op jit(solution)/shard_map/ppermute | solution.py:384
  55.8 14.0 %collective-permute-start.22 = (f32[160,512]{1,0:T(8,128)}, f32[160,512]{1,0:T(8,128)}, u32[]{:S(2)}, u32[]{:S(2)}) collective-permute-start(f32[160,512]{1,0:T(8,128)} %collective-permute-done.20.refs_12_.refs_19_), channel_id=1, source_target_pairs={{8,0},{16,8},{24,16},{28,24},{20,28},{12,20},{4,12},{0,4},{9,1},{1... | collective-permute-start | bytes 983048 | tf_op jit(solution)/shard_map/ppermute | solution.py:384
  55.8 21.1 %collective-permute-start.24 = (f32[160,512]{1,0:T(8,128)S(1)}, f32[160,512]{1,0:T(8,128)}, u32[]{:S(2)}, u32[]{:S(2)}) collective-permute-start(f32[160,512]{1,0:T(8,128)S(1)} %get-tuple-element.22.refs_0_), channel_id=1, source_target_pairs={{8,0},{16,8},{24,16},{28,24},{20,28},{12,20},{4,12},{0,4},{9,1},{1... | collective-permute-start | bytes 983048 | tf_op jit(solution)/shard_map/ppermute | solution.py:384
  61.4 24.3 %collective-permute-start.21 = (f32[160,512]{1,0:T(8,128)}, f32[160,512]{1,0:T(8,128)S(1)}, u32[]{:S(2)}, u32[]{:S(2)}) collective-permute-start(f32[160,512]{1,0:T(8,128)} %collective-permute-done.19.refs_11_.refs_18_), channel_id=1, source_target_pairs={{0,8},{8,16},{16,24},{24,28},{28,20},{20,12},{12,4},{4,0},{1,9},{9... | collective-permute-start | bytes 983048 | tf_op jit(solution)/shard_map/ppermute | solution.py:384
  64.2 21.5 %collective-permute-start.16 = (f32[160,512]{1,0:T(8,128)S(1)}, f32[160,512]{1,0:T(8,128)S(1)}, u32[]{:S(2)}, u32[]{:S(2)}) collective-permute-start(f32[160,512]{1,0:T(8,128)S(1)} %collective-permute-done.15.refs_4_), channel_id=1, source_target_pairs={{8,0},{16,8},{24,16},{28,24},{20,28},{12,20},{4,12},{0,4},{9,1},{1... | collective-permute-start | bytes 983048 | tf_op jit(solution)/shard_map/ppermute | solution.py:384
  64.2 13.1 %collective-permute-start.25 = (f32[160,512]{1,0:T(8,128)S(1)}, f32[160,512]{1,0:T(8,128)S(1)}, u32[]{:S(2)}, u32[]{:S(2)}) collective-permute-start(f32[160,512]{1,0:T(8,128)S(1)} %get-tuple-element.23.refs_1_), channel_id=1, source_target_pairs={{0,8},{8,16},{16,24},{24,28},{28,20},{20,12},{12,4},{4,0},{1,9},{9... | collective-permute-start | bytes 983048 | tf_op jit(solution)/shard_map/ppermute | solution.py:384
  69.8 13.3 %collective-permute-start.5 = (f32[160,512]{1,0:T(8,128)S(1)}, f32[160,512]{1,0:T(8,128)S(1)}, u32[]{:S(2)}, u32[]{:S(2)}) collective-permute-start(f32[160,512]{1,0:T(8,128)S(1)} %collective-permute-done.4.refs_2_.refs_5_), channel_id=1, source_target_pairs={{0,8},{8,16},{16,24},{24,28},{28,20},{20,12},{12,4},{4,0},{1,9},{9... | collective-permute-start | bytes 983048 | tf_op jit(solution)/shard_map/ppermute | solution.py:384
  83.1 16.3 %collective-permute-start.10 = (f32[160,512]{1,0:T(8,128)S(1)}, f32[160,512]{1,0:T(8,128)S(1)}, u32[]{:S(2)}, u32[]{:S(2)}) collective-permute-start(f32[160,512]{1,0:T(8,128)S(1)} %get-tuple-element.25.refs_23_), channel_id=1, source_target_pairs={{8,0},{16,8},{24,16},{28,24},{20,28},{12,20},{4,12},{0,4},{9,1},{1... | collective-permute-start | bytes 983048 | tf_op jit(solution)/shard_map/ppermute | solution.py:384
  83.1 17.7 %collective-permute-start.6 = (f32[160,512]{1,0:T(8,128)S(1)}, f32[160,512]{1,0:T(8,128)S(1)}, u32[]{:S(2)}, u32[]{:S(2)}) collective-permute-start(f32[160,512]{1,0:T(8,128)S(1)} %get-tuple-element.24.refs_8_), channel_id=1, source_target_pairs={{0,8},{8,16},{16,24},{24,28},{28,20},{20,12},{12,4},{4,0},{1,9},{9... | collective-permute-start | bytes 983048 | tf_op jit(solution)/shard_map/ppermute | solution.py:384
  85.7 16.5 %collective-permute-start.28 = (f32[160,512]{1,0:T(8,128)}, f32[160,512]{1,0:T(8,128)S(1)}, u32[]{:S(2)}, u32[]{:S(2)}) collective-permute-start(f32[160,512]{1,0:T(8,128)} %collective-permute-done.24.refs_17_.refs_10_), channel_id=1, source_target_pairs={{8,0},{16,8},{24,16},{28,24},{20,28},{12,20},{4,12},{0,4},{9,1},{1... | collective-permute-start | bytes 983048 | tf_op jit(solution)/shard_map/ppermute | solution.py:384
  85.7 16.5 %collective-permute-start.29 = (f32[160,512]{1,0:T(8,128)S(1)}, f32[160,512]{1,0:T(8,128)S(1)}, u32[]{:S(2)}, u32[]{:S(2)}) collective-permute-start(f32[160,512]{1,0:T(8,128)S(1)} %collective-permute-done.25.refs_18_.refs_24_), channel_id=1, source_target_pairs={{0,8},{8,16},{16,24},{24,28},{28,20},{20,12},{12,4},{4,0},{1,9},{9... | collective-permute-start | bytes 983048 | tf_op jit(solution)/shard_map/ppermute | solution.py:384
  98.0 30.4 %collective-permute-start.26 = (f32[512,512]{1,0:T(8,128)}, f32[512,512]{1,0:T(8,128)S(1)}, u32[]{:S(2)}, u32[]{:S(2)}) collective-permute-start(f32[512,512]{1,0:T(8,128)} %get-tuple-element.27.refs_31_.refs_3_), channel_id=1, source_target_pairs={{0,1},{4,5},{8,9},{12,13},{16,17},{20,21},{24,25},{28,29}} | collective-permute-start | bytes 3145736 | tf_op jit(solution)/shard_map/ppermute | solution.py:406
  99.4 29.0 %collective-permute-start.32 = (f32[512,512]{1,0:T(8,128)}, f32[512,512]{1,0:T(8,128)S(1)}, u32[]{:S(2)}, u32[]{:S(2)}) collective-permute-start(f32[512,512]{1,0:T(8,128)} %get-tuple-element.28.refs_35_.refs_7_), channel_id=1, source_target_pairs={{0,2},{4,6},{8,10},{12,14},{16,18},{20,22},{24,26},{28,30}} | collective-permute-start | bytes 3145736 | tf_op jit(solution)/shard_map/ppermute | solution.py:395
  100.8 30.4 %collective-permute-start.27 = (f32[512,512]{1,0:T(8,128)}, f32[512,512]{1,0:T(8,128)S(1)}, u32[]{:S(2)}, u32[]{:S(2)}) collective-permute-start(f32[512,512]{1,0:T(8,128)} %get-tuple-element.27.refs_31_.refs_3_), channel_id=1, source_target_pairs={{0,2},{4,6},{8,10},{12,14},{16,18},{20,22},{24,26},{28,30}} | collective-permute-start | bytes 3145736 | tf_op jit(solution)/shard_map/ppermute | solution.py:395
  133.6 16.2 %collective-permute-start.13 = (f32[160,512]{1,0:T(8,128)S(1)}, f32[160,512]{1,0:T(8,128)S(1)}, u32[]{:S(2)}, u32[]{:S(2)}) collective-permute-start(f32[160,512]{1,0:T(8,128)S(1)} %collective-permute-done.12.refs_4_.refs_29_), channel_id=1, source_target_pairs={{8,0},{16,8},{24,16},{28,24},{20,28},{12,20},{4,12},{0,4},{9,1},{1... | collective-permute-start | bytes 983048 | tf_op jit(solution)/shard_map/ppermute | solution.py:384
  134.2 15.6 %collective-permute-start.9 = (f32[160,512]{1,0:T(8,128)S(1)}, f32[160,512]{1,0:T(8,128)S(1)}, u32[]{:S(2)}, u32[]{:S(2)}) collective-permute-start(f32[160,512]{1,0:T(8,128)S(1)} %collective-permute-done.8.refs_1_.refs_13_), channel_id=1, source_target_pairs={{0,8},{8,16},{16,24},{24,28},{28,20},{20,12},{12,4},{4,0},{1,9},{9... | collective-permute-start | bytes 983048 | tf_op jit(solution)/shard_map/ppermute | solution.py:384
  (41 other events, 682.6 us)

commit v6 on v4

--- a/solution.py
+++ b/solution.py
@@ -278,7 +278,7 @@
 
     for r in range(places):
 
-        @pl.when(place[0] == r)
+        @pl.when(place[0] % places == r)
         def _(r=r):
             for k in range(2):
                 fetch(k, r).start()
@@ -301,9 +301,12 @@
         def _(t):
             inside = pl.multiple_of(t * tile, 8)
             top = start + ids[i] * rows + inside
-            product[...] = dot_split(
-                split16(lower[i, pl.ds(inside, tile)]), (high[...], low[...])
-            )
+
+            @pl.when(top + tile > depth)
+            def _():
+                product[...] = dot_split(
+                    split16(lower[i, pl.ds(inside, tile)]), (high[...], low[...])
+                )
 
             @pl.when(top >= depth)
             def _():
@@ -400,24 +403,23 @@
     return held, steps
 
 
-def spread_far(block, count):
+def spread_far(block, count, place):
     found = {0: block}
     stride = count // 2
     while stride > 1:
         for r in list(found):
             found[r + stride] = lax.ppermute(found[r], "row", [(r, r + stride)])
         stride //= 2
-    return found
-
-
-def spread_near(found, count, tokens):
-    found = dict(found)
-    for r in sorted(found):
-        if r and tokens:
-            (found[r],) = gate([found[r]], tokens)
-        if r + 1 < count:
-            found[r + 1] = lax.ppermute(found[r], "row", [(r, r + 1)])
-    return [found[r] for r in range(count)]
+    for r in found:
+        if r:
+            block = jnp.where(place[0] == r, found[r], block)
+    return block
+
+
+def spread_near(block, count, tokens):
+    if tokens:
+        (block,) = gate([block], tokens)
+    return [block, lax.ppermute(block, "row", [(r, r + 1) for r in range(0, count - 1, 2)])]
 
 
 def swap_partners(count, tops):
@@ -495,7 +497,7 @@
             rest, steps = ring_pass([[full[0], free[0]], [free[1], full[1]]], ring)
             after = [[steps[0][0][1], steps[0][1][0]], [steps[0][0][0], steps[0][1][1]]]
             near = [steps[i][0] + steps[i][1] for i in (1, -2)]
-            top_spots, cut = spots[0], 2 * half - 3
+            top_spots, cut = spots[0], 2 * half - 1
             groups = [
                 (
                     [top[k] + rest[k][:cut] for k in range(2)],
@@ -506,8 +508,8 @@
         first = solve_panel(0, top_spots, place, top, right_side, [], after[0], width, block)
         second = solve_panel(1, top_spots, place, top, right_side, [first], after[1], width, block)
         solved = [
-            spread_near(spread_far(first, places), places, near[0]),
-            spread_near(spread_far(second, places), places, near[1]),
+            spread_near(spread_far(first, places, place), places, near[0]),
+            spread_near(spread_far(second, places, place), places, near[1]),
         ]
         result = None
         for held, spots in groups:

time: 151 us -> 154 us (1.020); the launches traced: 151 us -> 151 us
  other arithmetic: 0.44 us -> 4.05 us
  Pallas kernels: 36.1 us -> 32.8 us
    select_n x0 -> x2, other arithmetic: none -> 3.61 us  [spread_far(): block = jnp.where(place[0] == r, found[r], block)]
    pallas_call x2, Pallas kernels: 18.7 us -> 15.5 us  [update(): pl.pallas_call(functools.partial(update_kernel, pieces, rows, width, tile...]
    ppermute x2, starting transfers between devices: 2.84 us -> 4.59 us  [spread_far(): found[r + stride] = lax.ppermute(found[r], 'row', [(r, r + stride)])]
    unnamed x52 -> x50, local copies, waits for them, and re-layouts: 5.87 us -> 4.22 us
    ppermute x4 -> x2, starting transfers between devices: 4.13 us -> 2.7 us  [spread_near(): lax.ppermute(block, 'row', [(r, r + 1) for r in range(0, count - 1, 2)])]
  transfers between devices with their start and end apart: 36 -> 34, of which waited for: 17 -> 15; matrix products, arithmetic and copies ran while one was open for 0% -> 3% of each run, Pallas kernels for 18% -> 17%
where the time goes in v6:
time: 154 us; the launch traced here: 151 us
  starting transfers between devices  55.8 us (36%)
  waiting for transfers between devices  53.7 us (35%)
  Pallas kernels  32.8 us (21%)
  local copies, waits for them, and re-layouts  4.79 us (3%)
  other arithmetic  4.05 us (3%)
    ppermute x28, waiting for transfers between devices, ring_pass(): going[k][way] = lax.ppermute(going[k][way], 'src', pairs)  47.9 us
    ppermute x28, starting transfers between devices, ring_pass(): going[k][way] = lax.ppermute(going[k][way], 'src', pairs)  40.8 us
    pallas_call x2, Pallas kernels, update(): pl.pallas_call(functools.partial(update_kernel, pieces, rows, width, tile...  15.5 us
    pallas_call x2, Pallas kernels, solve_panel(): pl.pallas_call(functools.partial(solve_kernel, pieces, rows, width, chunk...  13.2 us
    ppermute x2, starting transfers between devices, local(): got = [lax.ppermute(sent, axes, swap) for sent in (sent_first, sent_second)]  7.64 us
    ppermute x2, waiting for transfers between devices, local(): got = [lax.ppermute(sent, axes, swap) for sent in (sent_first, sent_second)]  5.76 us
    ppermute x2, starting transfers between devices, spread_far(): found[r + stride] = lax.ppermute(found[r], 'row', [(r, r + stride)])  4.59 us
    unnamed x50, local copies, waits for them, and re-layouts  4.22 us
  transfers between devices with their start and end apart: 34, of which 15 were waited for; matrix products, arithmetic and copies ran while one was open for 3% of the time, Pallas kernels for 17%

profile of v6, /device:TPU:0, one launch (start us, length us, event | category | flops | bytes accessed | tf_op | source)
XLA Modules:
  0.0 151.4 jit_solution(7000265267358578854)
XLA Ops:
  0.0 4.1 %shard_map.55 = (f32[160,512]{1,0:T(8,128)S(1)}, f32[160,512]{1,0:T(8,128)S(1)}, f32[160,512]{1,0:T(8,128)S(1)}, f32[160,512]{1,0:T(8,128)S(1)}, f32[160,512]{1,0:T(8,128)S(1)}, /*index=5*/f32[160,512]{1,0:T(8,128)S(1)}) custom-call(s32[1]{0:T(128)} %bitcast.1.me, s32[1]{0:T(128)} %bitcast.place, f32[320,1024]{1,0:T(8,128)} %source.1), custom_call_target="tpu_custom_call" | custom-call | flops 1000 | bytes 1000 | tf_op jit(solution)/shard_map/pallas_call | solution.py:115
  4.1 4.4 %collective-permute-start = (f32[160,512]{1,0:T(8,128)S(1)}, f32[160,512]{1,0:T(8,128)S(1)}, u32[]{:S(2)}, u32[]{:S(2)}) collective-permute-start(f32[160,512]{1,0:T(8,128)S(1)} %get-tuple-element.15), channel_id=1, source_target_pairs={{0,24},{24,0},{4,28},{28,4},{8,16},{16,8}} | collective-permute-start | bytes 983048 | tf_op jit(solution)/shard_map/ppermute | solution.py:474
  8.5 3.2 %collective-permute-start.1 = (f32[160,512]{1,0:T(8,128)S(1)}, f32[160,512]{1,0:T(8,128)S(1)}, u32[]{:S(2)}, u32[]{:S(2)}) collective-permute-start(f32[160,512]{1,0:T(8,128)S(1)} %get-tuple-element.17), channel_id=1, source_target_pairs={{0,24},{24,0},{4,28},{28,4},{8,16},{16,8}} | collective-permute-start | bytes 983048 | tf_op jit(solution)/shard_map/ppermute | solution.py:474
  11.8 5.8 %collective-permute-done = f32[160,512]{1,0:T(8,128)S(1)} collective-permute-done((f32[160,512]{1,0:T(8,128)S(1)}, f32[160,512]{1,0:T(8,128)S(1)}, u32[]{:S(2)}, u32[]{:S(2)}) %collective-permute-start) | collective-permute-done | bytes 327712 | tf_op jit(solution)/shard_map/ppermute | solution.py:474
  17.6 6.6 %collective-permute-start.2 = (f32[160,512]{1,0:T(8,128)S(1)}, f32[160,512]{1,0:T(8,128)S(1)}, u32[]{:S(2)}, u32[]{:S(2)}) collective-permute-start(f32[160,512]{1,0:T(8,128)S(1)} %get-tuple-element.29.refs_0_), channel_id=1, source_target_pairs={{0,8},{8,16},{16,24},{24,28},{28,20},{20,12},{12,4},{4,0},{1,9},{9... | collective-permute-start | bytes 983048 | tf_op jit(solution)/shard_map/ppermute | solution.py:400
  26.2 4.4 %collective-permute-done.2.refs_1_ = f32[160,512]{1,0:T(8,128)S(1)} collective-permute-done((f32[160,512]{1,0:T(8,128)S(1)}, f32[160,512]{1,0:T(8,128)S(1)}, u32[]{:S(2)}, u32[]{:S(2)}) %collective-permute-start.2) | collective-permute-done | bytes 327712 | tf_op jit(solution)/shard_map/ppermute | solution.py:400
  30.6 4.9 %collective-permute-start.3 = (f32[160,512]{1,0:T(8,128)S(1)}, f32[160,512]{1,0:T(8,128)S(1)}, u32[]{:S(2)}, u32[]{:S(2)}) collective-permute-start(f32[160,512]{1,0:T(8,128)S(1)} %collective-permute-done.2.refs_1_), channel_id=1, source_target_pairs={{0,8},{8,16},{16,24},{24,28},{28,20},{20,12},{12,4},{4,0},{1,9},{9... | collective-permute-start | bytes 983048 | tf_op jit(solution)/shard_map/ppermute | solution.py:400
  38.1 5.5 %collective-permute-done.3.refs_3_ = f32[160,512]{1,0:T(8,128)S(1)} collective-permute-done((f32[160,512]{1,0:T(8,128)S(1)}, f32[160,512]{1,0:T(8,128)S(1)}, u32[]{:S(2)}, u32[]{:S(2)}) %collective-permute-start.3) | collective-permute-done | bytes 327712 | tf_op jit(solution)/shard_map/ppermute | solution.py:400
  43.5 2.6 %collective-permute-start.4 = (f32[160,512]{1,0:T(8,128)S(1)}, f32[160,512]{1,0:T(8,128)S(1)}, u32[]{:S(2)}, u32[]{:S(2)}) collective-permute-start(f32[160,512]{1,0:T(8,128)S(1)} %collective-permute-done.3.refs_3_), channel_id=1, source_target_pairs={{0,8},{8,16},{16,24},{24,28},{28,20},{20,12},{12,4},{4,0},{1,9},{9... | collective-permute-start | bytes 983048 | tf_op jit(solution)/shard_map/ppermute | solution.py:400
  46.1 4.4 %collective-permute-done.17.refs_9_.refs_16_ = f32[160,512]{1,0:T(8,128)} collective-permute-done((f32[160,512]{1,0:T(8,128)S(1)}, f32[160,512]{1,0:T(8,128)}, u32[]{:S(2)}, u32[]{:S(2)}) %collective-permute-start.17) | collective-permute-done | bytes 327712 | tf_op jit(solution)/shard_map/ppermute | solution.py:400
  50.6 2.6 %collective-permute-start.19 = (f32[160,512]{1,0:T(8,128)}, f32[160,512]{1,0:T(8,128)}, u32[]{:S(2)}, u32[]{:S(2)}) collective-permute-start(f32[160,512]{1,0:T(8,128)} %collective-permute-done.17.refs_9_.refs_16_), channel_id=1, source_target_pairs={{0,8},{8,16},{16,24},{24,28},{28,20},{20,12},{12,4},{4,0},{1,9},{9... | collective-permute-start | bytes 983048 | tf_op jit(solution)/shard_map/ppermute | solution.py:400
  53.2 2.6 %collective-permute-done.20.refs_12_.refs_19_ = f32[160,512]{1,0:T(8,128)} collective-permute-done((f32[160,512]{1,0:T(8,128)S(1)}, f32[160,512]{1,0:T(8,128)}, u32[]{:S(2)}, u32[]{:S(2)}) %collective-permute-start.20) | collective-permute-done | bytes 327712 | tf_op jit(solution)/shard_map/ppermute | solution.py:400
  57.6 2.6 %collective-permute-start.25 = (f32[160,512]{1,0:T(8,128)S(1)}, f32[160,512]{1,0:T(8,128)}, u32[]{:S(2)}, u32[]{:S(2)}) collective-permute-start(f32[160,512]{1,0:T(8,128)S(1)} %get-tuple-element.21.refs_1_), channel_id=1, source_target_pairs={{0,8},{8,16},{16,24},{24,28},{28,20},{20,12},{12,4},{4,0},{1,9},{9... | collective-permute-start | bytes 983048 | tf_op jit(solution)/shard_map/ppermute | solution.py:400
  60.2 4.5 %collective-permute-done.19.refs_11_.refs_18_ = f32[160,512]{1,0:T(8,128)} collective-permute-done((f32[160,512]{1,0:T(8,128)}, f32[160,512]{1,0:T(8,128)}, u32[]{:S(2)}, u32[]{:S(2)}) %collective-permute-start.19) | collective-permute-done | bytes 327712 | tf_op jit(solution)/shard_map/ppermute | solution.py:400
  64.7 2.6 %collective-permute-start.5 = (f32[160,512]{1,0:T(8,128)S(1)}, f32[160,512]{1,0:T(8,128)S(1)}, u32[]{:S(2)}, u32[]{:S(2)}) collective-permute-start(f32[160,512]{1,0:T(8,128)S(1)} %collective-permute-done.4.refs_2_.refs_5_), channel_id=1, source_target_pairs={{0,8},{8,16},{16,24},{24,28},{28,20},{20,12},{12,4},{4,0},{1,9},{9... | collective-permute-start | bytes 983048 | tf_op jit(solution)/shard_map/ppermute | solution.py:400
  67.3 2.5 %collective-permute-start.21 = (f32[160,512]{1,0:T(8,128)}, f32[160,512]{1,0:T(8,128)S(1)}, u32[]{:S(2)}, u32[]{:S(2)}) collective-permute-start(f32[160,512]{1,0:T(8,128)} %collective-permute-done.19.refs_11_.refs_18_), channel_id=1, source_target_pairs={{0,8},{8,16},{16,24},{24,28},{28,20},{20,12},{12,4},{4,0},{1,9},{9... | collective-permute-start | bytes 983048 | tf_op jit(solution)/shard_map/ppermute | solution.py:400
  71.5 6.1 %collective-permute-done.24.refs_17_.refs_10_ = f32[160,512]{1,0:T(8,128)} collective-permute-done((f32[160,512]{1,0:T(8,128)S(1)}, f32[160,512]{1,0:T(8,128)}, u32[]{:S(2)}, u32[]{:S(2)}) %collective-permute-start.24) | collective-permute-done | bytes 327712 | tf_op jit(solution)/shard_map/ppermute | solution.py:400
  81.0 3.9 %collective-permute-done.23.refs_15_.refs_22_ = f32[160,512]{1,0:T(8,128)S(1)} collective-permute-done((f32[160,512]{1,0:T(8,128)}, f32[160,512]{1,0:T(8,128)S(1)}, u32[]{:S(2)}, u32[]{:S(2)}) %collective-permute-start.23) | collective-permute-done | bytes 327712 | tf_op jit(solution)/shard_map/ppermute | solution.py:400
  85.6 5.7 %shard_map.58.refs_17_ = f32[512,512]{1,0:T(8,128)} custom-call(s32[8]{0:T(128)S(1)} %get-tuple-element.31.ids, s32[1]{0:T(128)} %bitcast.place, f32[160,512]{1,0:T(8,128)S(1)} %get-tuple-element.29.refs_0_, f32[160,512]{1,0:T(8,128)S(1)} %collective-permute-done.2.refs_1_, f32[160,512]{1,0:T(8,128)S(1)} %collective-permute-done.14.refs_2_, ...), custom_call_target="tpu_custom_call" | custom-call | flops 3221225472 | bytes 3145728 | tf_op jit(solution)/shard_map/pallas_call | solution.py:229
  95.2 7.5 %shard_map.60 = f32[512,512]{1,0:T(8,128)} custom-call(s32[8]{0:T(128)S(1)} %get-tuple-element.31.ids, s32[1]{0:T(128)} %bitcast.place, f32[160,512]{1,0:T(8,128)S(1)} %get-tuple-element.29.refs_0_, f32[160,512]{1,0:T(8,128)S(1)} %collective-permute-done.2.refs_1_, f32[160,512]{1,0:T(8,128)S(1)} %collective-permute-done.14.refs_2_, ...), custom_call_target="tpu_custom_call" | custom-call | flops 6442450944 | bytes 3145728 | tf_op jit(solution)/shard_map/pallas_call | solution.py:229
  107.0 7.7 %collective-permute-done.27.refs_2_.refs_12_ = f32[160,512]{1,0:T(8,128)S(1)} collective-permute-done((f32[160,512]{1,0:T(8,128)}, f32[160,512]{1,0:T(8,128)S(1)}, u32[]{:S(2)}, u32[]{:S(2)}) %collective-permute-start.27) | collective-permute-done | bytes 327712 | tf_op jit(solution)/shard_map/ppermute | solution.py:400
  116.7 2.5 %collective-permute-done.11.refs_4_.refs_27_ = f32[160,512]{1,0:T(8,128)S(1)} collective-permute-done((f32[160,512]{1,0:T(8,128)}, f32[160,512]{1,0:T(8,128)S(1)}, u32[]{:S(2)}, u32[]{:S(2)}) %collective-permute-start.11) | collective-permute-done | bytes 327712 | tf_op jit(solution)/shard_map/ppermute | solution.py:400
  135.9 11.8 %shard_map.62.refs_7_ = f32[2560,512]{1,0:T(8,128)} custom-call(s32[15]{0:T(128)S(1)} %pad_add_fusion.ids, s32[1]{0:T(128)} %bitcast.place, f32[160,512]{1,0:T(8,128)S(1)} %get-tuple-element.29.refs_0_, f32[160,512]{1,0:T(8,128)S(1)} %collective-permute-done.2.refs_1_, f32[160,512]{1,0:T(8,128)S(1)} %collective-permute-done.14.refs_2_, ...), custom_call_target="tpu_custom_call" | custom-call | flops 7549747200 | bytes 19660800 | tf_op jit(solution)/shard_map/pallas_call | solution.py:345
  147.8 3.7 %shard_map.63 = f32[2560,512]{1,0:T(8,128)} custom-call(s32[1]{0:T(128)} %slice.6.ids, s32[1]{0:T(128)} %bitcast.place, f32[160,512]{1,0:T(8,128)S(1)} %collective-permute-done.9.refs_0_, f32[160,512]{1,0:T(8,128)S(1)} %collective-permute-done.13.refs_1_, f32[2560,512]{1,0:T(8,128)} %refs_2_.1, ...), custom_call_target="tpu_custom_call", output_to_operand_aliasing={{}: (9, {})} | custom-call | flops 503316480 | bytes 1310720 | tf_op jit(solution)/shard_map/pallas_call | solution.py:345
  (112 shorter events, 38.9 us)
Async XLA Ops:
  4.1 13.4 %collective-permute-start = (f32[160,512]{1,0:T(8,128)S(1)}, f32[160,512]{1,0:T(8,128)S(1)}, u32[]{:S(2)}, u32[]{:S(2)}) collective-permute-start(f32[160,512]{1,0:T(8,128)S(1)} %get-tuple-element.15), channel_id=1, source_target_pairs={{0,24},{24,0},{4,28},{28,4},{8,16},{16,8}} | collective-permute-start | bytes 983048 | tf_op jit(solution)/shard_map/ppermute | solution.py:474
  8.5 15.7 %collective-permute-start.1 = (f32[160,512]{1,0:T(8,128)S(1)}, f32[160,512]{1,0:T(8,128)S(1)}, u32[]{:S(2)}, u32[]{:S(2)}) collective-permute-start(f32[160,512]{1,0:T(8,128)S(1)} %get-tuple-element.17), channel_id=1, source_target_pairs={{0,24},{24,0},{4,28},{28,4},{8,16},{16,8}} | collective-permute-start | bytes 983048 | tf_op jit(solution)/shard_map/ppermute | solution.py:474
  17.6 13.0 %collective-permute-start.2 = (f32[160,512]{1,0:T(8,128)S(1)}, f32[160,512]{1,0:T(8,128)S(1)}, u32[]{:S(2)}, u32[]{:S(2)}) collective-permute-start(f32[160,512]{1,0:T(8,128)S(1)} %get-tuple-element.29.refs_0_), channel_id=1, source_target_pairs={{0,8},{8,16},{16,24},{24,28},{28,20},{20,12},{12,4},{4,0},{1,9},{9... | collective-permute-start | bytes 983048 | tf_op jit(solution)/shard_map/ppermute | solution.py:400
  24.3 13.7 %collective-permute-start.18 = (f32[160,512]{1,0:T(8,128)S(1)}, f32[160,512]{1,0:T(8,128)S(1)}, u32[]{:S(2)}, u32[]{:S(2)}) collective-permute-start(f32[160,512]{1,0:T(8,128)S(1)} %get-tuple-element.27.refs_8_.refs_15_), channel_id=1, source_target_pairs={{8,0},{16,8},{24,16},{28,24},{20,28},{12,20},{4,12},{0,4},{9,1},{1... | collective-permute-start | bytes 983048 | tf_op jit(solution)/shard_map/ppermute | solution.py:400
  30.6 12.9 %collective-permute-start.3 = (f32[160,512]{1,0:T(8,128)S(1)}, f32[160,512]{1,0:T(8,128)S(1)}, u32[]{:S(2)}, u32[]{:S(2)}) collective-permute-start(f32[160,512]{1,0:T(8,128)S(1)} %collective-permute-done.2.refs_1_), channel_id=1, source_target_pairs={{0,8},{8,16},{16,24},{24,28},{28,20},{20,12},{12,4},{4,0},{1,9},{9... | collective-permute-start | bytes 983048 | tf_op jit(solution)/shard_map/ppermute | solution.py:400
  35.5 15.0 %collective-permute-start.17 = (f32[160,512]{1,0:T(8,128)S(1)}, f32[160,512]{1,0:T(8,128)}, u32[]{:S(2)}, u32[]{:S(2)}) collective-permute-start(f32[160,512]{1,0:T(8,128)S(1)} %get-tuple-element.27.refs_8_.refs_15_), channel_id=1, source_target_pairs={{0,8},{8,16},{16,24},{24,28},{28,20},{20,12},{12,4},{4,0},{1,9},{9... | collective-permute-start | bytes 983048 | tf_op jit(solution)/shard_map/ppermute | solution.py:400
  38.0 15.2 %collective-permute-start.14 = (f32[160,512]{1,0:T(8,128)S(1)}, f32[160,512]{1,0:T(8,128)S(1)}, u32[]{:S(2)}, u32[]{:S(2)}) collective-permute-start(f32[160,512]{1,0:T(8,128)S(1)} %get-tuple-element.29.refs_0_), channel_id=1, source_target_pairs={{8,0},{16,8},{24,16},{28,24},{20,28},{12,20},{4,12},{0,4},{9,1},{1... | collective-permute-start | bytes 983048 | tf_op jit(solution)/shard_map/ppermute | solution.py:400
  38.0 17.8 %collective-permute-start.20 = (f32[160,512]{1,0:T(8,128)S(1)}, f32[160,512]{1,0:T(8,128)}, u32[]{:S(2)}, u32[]{:S(2)}) collective-permute-start(f32[160,512]{1,0:T(8,128)S(1)} %collective-permute-done.18.refs_10_.refs_17_), channel_id=1, source_target_pairs={{8,0},{16,8},{24,16},{28,24},{20,28},{12,20},{4,12},{0,4},{9,1},{1... | collective-permute-start | bytes 983048 | tf_op jit(solution)/shard_map/ppermute | solution.py:400
  43.5 14.0 %collective-permute-start.4 = (f32[160,512]{1,0:T(8,128)S(1)}, f32[160,512]{1,0:T(8,128)S(1)}, u32[]{:S(2)}, u32[]{:S(2)}) collective-permute-start(f32[160,512]{1,0:T(8,128)S(1)} %collective-permute-done.3.refs_3_), channel_id=1, source_target_pairs={{0,8},{8,16},{16,24},{24,28},{28,20},{20,12},{12,4},{4,0},{1,9},{9... | collective-permute-start | bytes 983048 | tf_op jit(solution)/shard_map/ppermute | solution.py:400
  50.6 14.1 %collective-permute-start.19 = (f32[160,512]{1,0:T(8,128)}, f32[160,512]{1,0:T(8,128)}, u32[]{:S(2)}, u32[]{:S(2)}) collective-permute-start(f32[160,512]{1,0:T(8,128)} %collective-permute-done.17.refs_9_.refs_16_), channel_id=1, source_target_pairs={{0,8},{8,16},{16,24},{24,28},{28,20},{20,12},{12,4},{4,0},{1,9},{9... | collective-permute-start | bytes 983048 | tf_op jit(solution)/shard_map/ppermute | solution.py:400
  53.2 14.2 %collective-permute-start.15 = (f32[160,512]{1,0:T(8,128)S(1)}, f32[160,512]{1,0:T(8,128)S(1)}, u32[]{:S(2)}, u32[]{:S(2)}) collective-permute-start(f32[160,512]{1,0:T(8,128)S(1)} %collective-permute-done.14.refs_2_), channel_id=1, source_target_pairs={{8,0},{16,8},{24,16},{28,24},{20,28},{12,20},{4,12},{0,4},{9,1},{1... | collective-permute-start | bytes 983048 | tf_op jit(solution)/shard_map/ppermute | solution.py:400
  55.8 15.8 %collective-permute-start.22 = (f32[160,512]{1,0:T(8,128)}, f32[160,512]{1,0:T(8,128)}, u32[]{:S(2)}, u32[]{:S(2)}) collective-permute-start(f32[160,512]{1,0:T(8,128)} %collective-permute-done.20.refs_12_.refs_19_), channel_id=1, source_target_pairs={{8,0},{16,8},{24,16},{28,24},{20,28},{12,20},{4,12},{0,4},{9,1},{1... | collective-permute-start | bytes 983048 | tf_op jit(solution)/shard_map/ppermute | solution.py:400
  57.6 20.0 %collective-permute-start.24 = (f32[160,512]{1,0:T(8,128)S(1)}, f32[160,512]{1,0:T(8,128)}, u32[]{:S(2)}, u32[]{:S(2)}) collective-permute-start(f32[160,512]{1,0:T(8,128)S(1)} %get-tuple-element.20.refs_0_), channel_id=1, source_target_pairs={{8,0},{16,8},{24,16},{28,24},{20,28},{12,20},{4,12},{0,4},{9,1},{1... | collective-permute-start | bytes 983048 | tf_op jit(solution)/shard_map/ppermute | solution.py:400
  57.6 20.2 %collective-permute-start.25 = (f32[160,512]{1,0:T(8,128)S(1)}, f32[160,512]{1,0:T(8,128)}, u32[]{:S(2)}, u32[]{:S(2)}) collective-permute-start(f32[160,512]{1,0:T(8,128)S(1)} %get-tuple-element.21.refs_1_), channel_id=1, source_target_pairs={{0,8},{8,16},{16,24},{24,28},{28,20},{20,12},{12,4},{4,0},{1,9},{9... | collective-permute-start | bytes 983048 | tf_op jit(solution)/shard_map/ppermute | solution.py:400
  64.7 13.1 %collective-permute-start.5 = (f32[160,512]{1,0:T(8,128)S(1)}, f32[160,512]{1,0:T(8,128)S(1)}, u32[]{:S(2)}, u32[]{:S(2)}) collective-permute-start(f32[160,512]{1,0:T(8,128)S(1)} %collective-permute-done.4.refs_2_.refs_5_), channel_id=1, source_target_pairs={{0,8},{8,16},{16,24},{24,28},{28,20},{20,12},{12,4},{4,0},{1,9},{9... | collective-permute-start | bytes 983048 | tf_op jit(solution)/shard_map/ppermute | solution.py:400
  67.3 12.7 %collective-permute-start.21 = (f32[160,512]{1,0:T(8,128)}, f32[160,512]{1,0:T(8,128)S(1)}, u32[]{:S(2)}, u32[]{:S(2)}) collective-permute-start(f32[160,512]{1,0:T(8,128)} %collective-permute-done.19.refs_11_.refs_18_), channel_id=1, source_target_pairs={{0,8},{8,16},{16,24},{24,28},{28,20},{20,12},{12,4},{4,0},{1,9},{9... | collective-permute-start | bytes 983048 | tf_op jit(solution)/shard_map/ppermute | solution.py:400
  77.8 15.9 %collective-permute-start.10 = (f32[160,512]{1,0:T(8,128)S(1)}, f32[160,512]{1,0:T(8,128)S(1)}, u32[]{:S(2)}, u32[]{:S(2)}) collective-permute-start(f32[160,512]{1,0:T(8,128)S(1)} %get-tuple-element.23.refs_23_), channel_id=1, source_target_pairs={{8,0},{16,8},{24,16},{28,24},{20,28},{12,20},{4,12},{0,4},{9,1},{1... | collective-permute-start | bytes 983048 | tf_op jit(solution)/shard_map/ppermute | solution.py:400
  77.9 15.8 %collective-permute-start.6 = (f32[160,512]{1,0:T(8,128)S(1)}, f32[160,512]{1,0:T(8,128)S(1)}, u32[]{:S(2)}, u32[]{:S(2)}) collective-permute-start(f32[160,512]{1,0:T(8,128)S(1)} %get-tuple-element.22.refs_8_), channel_id=1, source_target_pairs={{0,8},{8,16},{16,24},{24,28},{28,20},{20,12},{12,4},{4,0},{1,9},{9... | collective-permute-start | bytes 983048 | tf_op jit(solution)/shard_map/ppermute | solution.py:400
  91.4 30.6 %collective-permute-start.26 = (f32[512,512]{1,0:T(8,128)}, f32[512,512]{1,0:T(8,128)}, u32[]{:S(2)}, u32[]{:S(2)}) collective-permute-start(f32[512,512]{1,0:T(8,128)} %shard_map.58.refs_17_), channel_id=1, source_target_pairs={{0,2},{4,6},{8,10},{12,14},{16,18},{20,22},{24,26},{28,30}} | collective-permute-start | bytes 3145736 | tf_op jit(solution)/shard_map/ppermute | solution.py:411
  102.6 23.8 %collective-permute-start.30 = (f32[512,512]{1,0:T(8,128)}, f32[512,512]{1,0:T(8,128)}, u32[]{:S(2)}, u32[]{:S(2)}) collective-permute-start(f32[512,512]{1,0:T(8,128)} %shard_map.60), channel_id=1, source_target_pairs={{0,2},{4,6},{8,10},{12,14},{16,18},{20,22},{24,26},{28,30}} | collective-permute-start | bytes 3145736 | tf_op jit(solution)/shard_map/ppermute | solution.py:411
  107.0 12.3 %collective-permute-start.11 = (f32[160,512]{1,0:T(8,128)}, f32[160,512]{1,0:T(8,128)S(1)}, u32[]{:S(2)}, u32[]{:S(2)}) collective-permute-start(f32[160,512]{1,0:T(8,128)} %copy-done.23), channel_id=1, source_target_pairs={{8,0},{16,8},{24,16},{28,24},{20,28},{12,20},{4,12},{0,4},{9,1},{1... | collective-permute-start | bytes 983048 | tf_op jit(solution)/shard_map/ppermute | solution.py:400
  116.2 12.8 %collective-permute-start.31 = (f32[160,512]{1,0:T(8,128)S(1)}, f32[160,512]{1,0:T(8,128)S(1)}, u32[]{:S(2)}, u32[]{:S(2)}) collective-permute-start(f32[160,512]{1,0:T(8,128)S(1)} %collective-permute-done.27.refs_2_.refs_12_), channel_id=1, source_target_pairs={{8,0},{16,8},{24,16},{28,24},{20,28},{12,20},{4,12},{0,4},{9,1},{1... | collective-permute-start | bytes 983048 | tf_op jit(solution)/shard_map/ppermute | solution.py:400
  131.9 15.9 %collective-permute-start.13 = (f32[160,512]{1,0:T(8,128)S(1)}, f32[160,512]{1,0:T(8,128)S(1)}, u32[]{:S(2)}, u32[]{:S(2)}) collective-permute-start(f32[160,512]{1,0:T(8,128)S(1)} %collective-permute-done.12.refs_4_.refs_29_), channel_id=1, source_target_pairs={{8,0},{16,8},{24,16},{28,24},{20,28},{12,20},{4,12},{0,4},{9,1},{1... | collective-permute-start | bytes 983048 | tf_op jit(solution)/shard_map/ppermute | solution.py:400
  131.9 15.9 %collective-permute-start.9 = (f32[160,512]{1,0:T(8,128)S(1)}, f32[160,512]{1,0:T(8,128)S(1)}, u32[]{:S(2)}, u32[]{:S(2)}) collective-permute-start(f32[160,512]{1,0:T(8,128)S(1)} %collective-permute-done.8.refs_1_.refs_13_), channel_id=1, source_target_pairs={{0,8},{8,16},{16,24},{24,28},{28,20},{20,12},{12,4},{4,0},{1,9},{9... | collective-permute-start | bytes 983048 | tf_op jit(solution)/shard_map/ppermute | solution.py:400
  (35 other events, 527.3 us)

commit v7 on v6

--- a/solution.py
+++ b/solution.py
@@ -248,7 +248,7 @@
     )(ids, place, *held[0], *held[1], rhs, *earlier, *after)
 
 
-def update_kernel(pieces, rows, width, tile, step, places, ids, place, *refs):
+def update_kernel(pieces, rows, width, group, tile, step, places, ids, place, *refs):
     held, refs = refs[: 2 * pieces], refs[2 * pieces :]
     rhs, refs = refs[0], refs[1:]
     solved, refs = refs[: 2 * places], refs[2 * places :]
@@ -267,7 +267,9 @@
 
     def load(k, i, source):
         return pltpu.make_async_copy(
-            held[source], lower.at[i, :, pl.ds(k * width, width)], piece_sem.at[k, i]
+            held[source],
+            lower.at[pl.ds(pl.multiple_of(i * rows, 8), rows), pl.ds(k * width, width)],
+            piece_sem.at[k, i],
         )
 
     def load_block(i):
@@ -291,44 +293,52 @@
         fetch(k, 0).wait()
     high[...], low[...] = split16(found[...])
 
-    @pl.loop(0, pieces)
-    def _(i):
-        for k in range(2):
-            load(k, i, 0).wait()
-        load_block(i).wait()
+    @pl.loop(0, pieces // group)
+    def _(g):
+        members = [g * group + u for u in range(group)]
+        for i in members:
+            for k in range(2):
+                load(k, i, 0).wait()
+            load_block(i).wait()
 
         @pl.loop(0, rows // tile)
         def _(t):
             inside = pl.multiple_of(t * tile, 8)
-            top = start + ids[i] * rows + inside
-
-            @pl.when(top + tile > depth)
+            tops = [start + ids[i] * rows + inside for i in members]
+            highest = functools.reduce(jnp.maximum, tops)
+
+            @pl.when(highest + tile > depth)
             def _():
-                product[...] = dot_split(
-                    split16(lower[i, pl.ds(inside, tile)]), (high[...], low[...])
-                )
-
-            @pl.when(top >= depth)
-            def _():
-                block[i, pl.ds(inside, tile)] = block[i, pl.ds(inside, tile)] - product[...]
-
-            @pl.when(top < depth)
-            def _():
-                @pl.loop(0, tile // step)
-                def _(u):
-                    part = pl.multiple_of(u * step, 8)
-                    row = top + part
-                    here = pl.ds(inside + part, step)
-
-                    @pl.when(row < depth)
-                    def _():
-                        block[i, here] = found[pl.ds(pl.multiple_of(row, 8), step)]
-
-                    @pl.when(row >= depth)
-                    def _():
-                        block[i, here] = block[i, here] - product[pl.ds(part, step)]
-
-        store(i).start()
+                here = pl.ds(pl.multiple_of(g * group * rows + inside, 8), group * tile)
+                product[...] = dot_split(split16(lower[here]), (high[...], low[...]))
+
+            for u, (i, top) in enumerate(zip(members, tops)):
+
+                @pl.when(top >= depth)
+                def _(i=i, u=u):
+                    here = pl.ds(inside, tile)
+                    block[i, here] = block[i, here] - product[u * tile : (u + 1) * tile]
+
+                @pl.when(top < depth)
+                def _(i=i, u=u, top=top):
+                    @pl.loop(0, tile // step)
+                    def _(v):
+                        part = pl.multiple_of(v * step, 8)
+                        row = top + part
+                        here = pl.ds(inside + part, step)
+
+                        @pl.when(row < depth)
+                        def _():
+                            block[i, here] = found[pl.ds(pl.multiple_of(row, 8), step)]
+
+                        @pl.when(row >= depth)
+                        def _():
+                            block[i, here] = (
+                                block[i, here] - product[pl.ds(u * tile + part, step)]
+                            )
+
+        for i in members:
+            store(i).start()
 
     @pl.loop(0, pieces)
     def _(i):
@@ -340,21 +350,22 @@
     rows, columns = held[0][0].shape[0], rhs.shape[1]
     step = math.gcd(rows, 2 * width)
     tile = step * max(m for m in range(1, rows // step + 1) if rows // step % m == 0 and step * m <= 512)
+    group = 2 if pieces % 2 == 0 and tile == rows else 1
     operands = [ids, place, *[piece for group in held for piece in group], rhs, *solved[0], *solved[1]]
     extra = [] if written is None else [written]
     return pl.pallas_call(
-        functools.partial(update_kernel, pieces, rows, width, tile, step, places),
+        functools.partial(update_kernel, pieces, rows, width, group, tile, step, places),
         out_shape=jax.ShapeDtypeStruct(rhs.shape, jnp.float32),
         in_specs=[SCALARS] * 2 + [ANY] * (len(operands) - 2 + len(extra)),
         out_specs=ANY,
         input_output_aliases={len(operands): 0} if extra else {},
         scratch_shapes=[
-            pltpu.VMEM((pieces, rows, 2 * width), jnp.float32),
+            pltpu.VMEM((pieces * rows, 2 * width), jnp.float32),
             pltpu.VMEM((pieces, rows, columns), jnp.float32),
             pltpu.VMEM((2 * width, columns), jnp.float32),
             pltpu.VMEM((2 * width, columns), jnp.bfloat16),
             pltpu.VMEM((2 * width, columns), jnp.bfloat16),
-            pltpu.VMEM((tile, columns), jnp.float32),
+            pltpu.VMEM((group * tile, columns), jnp.float32),
             pltpu.SemaphoreType.DMA((2, pieces)),
             pltpu.SemaphoreType.DMA((pieces,)),
             pltpu.SemaphoreType.DMA((2,)),
@@ -496,8 +507,8 @@
             full = gate(free, [steps[-1][0][0]])
             rest, steps = ring_pass([[full[0], free[0]], [free[1], full[1]]], ring)
             after = [[steps[0][0][1], steps[0][1][0]], [steps[0][0][0], steps[0][1][1]]]
-            near = [steps[i][0] + steps[i][1] for i in (1, -2)]
-            top_spots, cut = spots[0], 2 * half - 1
+            near = [steps[i][0] + steps[i][1] for i in (0, -2)]
+            top_spots, cut = spots[0], 2 * half - 2
             groups = [
                 (
                     [top[k] + rest[k][:cut] for k in range(2)],

time: 154 us -> 154 us (level)
    unnamed x50 -> x54, local copies, waits for them, and re-layouts: 4.22 us -> 5.99 us
  transfers between devices with their start and end apart: 34 -> 34, of which waited for: 15 -> 16; matrix products, arithmetic and copies ran while one was open for 3% -> 3% of each run, Pallas kernels for 17% -> 16%
where the time goes in v7:
time: 154 us; the launch traced here: 152 us
  starting transfers between devices  55.8 us (36%)
  waiting for transfers between devices  52.9 us (34%)
  Pallas kernels  33 us (21%)
  local copies, waits for them, and re-layouts  6.06 us (4%)
  other arithmetic  4.05 us (3%)
    ppermute x28, waiting for transfers between devices, ring_pass(): going[k][way] = lax.ppermute(going[k][way], 'src', pairs)  46.9 us
    ppermute x28, starting transfers between devices, ring_pass(): going[k][way] = lax.ppermute(going[k][way], 'src', pairs)  40.7 us
    pallas_call x2, Pallas kernels, update(): pl.pallas_call(functools.partial(update_kernel, pieces, rows, width, grou...  15.7 us
    pallas_call x2, Pallas kernels, solve_panel(): pl.pallas_call(functools.partial(solve_kernel, pieces, rows, width, chunk...  13.2 us
    ppermute x2, starting transfers between devices, local(): got = [lax.ppermute(sent, axes, swap) for sent in (sent_first, sent_second)]  7.64 us
    unnamed x54, local copies, waits for them, and re-layouts  5.99 us
    ppermute x2, waiting for transfers between devices, local(): got = [lax.ppermute(sent, axes, swap) for sent in (sent_first, sent_second)]  5.76 us
    ppermute x2, starting transfers between devices, spread_far(): found[r + stride] = lax.ppermute(found[r], 'row', [(r, r + stride)])  4.76 us
  transfers between devices with their start and end apart: 34, of which 16 were waited for; matrix products, arithmetic and copies ran while one was open for 3% of the time, Pallas kernels for 16%

profile of v7, /device:TPU:0, one launch (start us, length us, event | category | flops | bytes accessed | tf_op | source)
XLA Modules:
  0.0 152.3 jit_solution(16963145267735651984)
XLA Ops:
  0.0 4.1 %shard_map.55 = (f32[160,512]{1,0:T(8,128)S(1)}, f32[160,512]{1,0:T(8,128)S(1)}, f32[160,512]{1,0:T(8,128)S(1)}, f32[160,512]{1,0:T(8,128)S(1)}, f32[160,512]{1,0:T(8,128)S(1)}, /*index=5*/f32[160,512]{1,0:T(8,128)S(1)}) custom-call(s32[1]{0:T(128)} %bitcast.1.me, s32[1]{0:T(128)} %bitcast.place, f32[320,1024]{1,0:T(8,128)} %source.1), custom_call_target="tpu_custom_call" | custom-call | flops 1000 | bytes 1000 | tf_op jit(solution)/shard_map/pallas_call | solution.py:115
  4.1 4.4 %collective-permute-start = (f32[160,512]{1,0:T(8,128)S(1)}, f32[160,512]{1,0:T(8,128)S(1)}, u32[]{:S(2)}, u32[]{:S(2)}) collective-permute-start(f32[160,512]{1,0:T(8,128)S(1)} %get-tuple-element.15), channel_id=1, source_target_pairs={{0,24},{24,0},{4,28},{28,4},{8,16},{16,8}} | collective-permute-start | bytes 983048 | tf_op jit(solution)/shard_map/ppermute | solution.py:485
  8.5 3.2 %collective-permute-start.1 = (f32[160,512]{1,0:T(8,128)S(1)}, f32[160,512]{1,0:T(8,128)S(1)}, u32[]{:S(2)}, u32[]{:S(2)}) collective-permute-start(f32[160,512]{1,0:T(8,128)S(1)} %get-tuple-element.17), channel_id=1, source_target_pairs={{0,24},{24,0},{4,28},{28,4},{8,16},{16,8}} | collective-permute-start | bytes 983048 | tf_op jit(solution)/shard_map/ppermute | solution.py:485
  11.8 5.8 %collective-permute-done = f32[160,512]{1,0:T(8,128)S(1)} collective-permute-done((f32[160,512]{1,0:T(8,128)S(1)}, f32[160,512]{1,0:T(8,128)S(1)}, u32[]{:S(2)}, u32[]{:S(2)}) %collective-permute-start) | collective-permute-done | bytes 327712 | tf_op jit(solution)/shard_map/ppermute | solution.py:485
  17.6 6.6 %collective-permute-start.2 = (f32[160,512]{1,0:T(8,128)S(1)}, f32[160,512]{1,0:T(8,128)S(1)}, u32[]{:S(2)}, u32[]{:S(2)}) collective-permute-start(f32[160,512]{1,0:T(8,128)S(1)} %get-tuple-element.29.refs_0_), channel_id=1, source_target_pairs={{0,8},{8,16},{16,24},{24,28},{28,20},{20,12},{12,4},{4,0},{1,9},{9... | collective-permute-start | bytes 983048 | tf_op jit(solution)/shard_map/ppermute | solution.py:411
  26.2 4.4 %collective-permute-done.2.refs_1_ = f32[160,512]{1,0:T(8,128)S(1)} collective-permute-done((f32[160,512]{1,0:T(8,128)S(1)}, f32[160,512]{1,0:T(8,128)S(1)}, u32[]{:S(2)}, u32[]{:S(2)}) %collective-permute-start.2) | collective-permute-done | bytes 327712 | tf_op jit(solution)/shard_map/ppermute | solution.py:411
  30.6 4.9 %collective-permute-start.3 = (f32[160,512]{1,0:T(8,128)S(1)}, f32[160,512]{1,0:T(8,128)S(1)}, u32[]{:S(2)}, u32[]{:S(2)}) collective-permute-start(f32[160,512]{1,0:T(8,128)S(1)} %collective-permute-done.2.refs_1_), channel_id=1, source_target_pairs={{0,8},{8,16},{16,24},{24,28},{28,20},{20,12},{12,4},{4,0},{1,9},{9... | collective-permute-start | bytes 983048 | tf_op jit(solution)/shard_map/ppermute | solution.py:411
  38.1 5.5 %collective-permute-done.3.refs_3_ = f32[160,512]{1,0:T(8,128)S(1)} collective-permute-done((f32[160,512]{1,0:T(8,128)S(1)}, f32[160,512]{1,0:T(8,128)S(1)}, u32[]{:S(2)}, u32[]{:S(2)}) %collective-permute-start.3) | collective-permute-done | bytes 327712 | tf_op jit(solution)/shard_map/ppermute | solution.py:411
  43.5 2.6 %collective-permute-start.4 = (f32[160,512]{1,0:T(8,128)S(1)}, f32[160,512]{1,0:T(8,128)S(1)}, u32[]{:S(2)}, u32[]{:S(2)}) collective-permute-start(f32[160,512]{1,0:T(8,128)S(1)} %collective-permute-done.3.refs_3_), channel_id=1, source_target_pairs={{0,8},{8,16},{16,24},{24,28},{28,20},{20,12},{12,4},{4,0},{1,9},{9... | collective-permute-start | bytes 983048 | tf_op jit(solution)/shard_map/ppermute | solution.py:411
  46.2 4.4 %collective-permute-done.20.refs_9_.refs_15_ = f32[160,512]{1,0:T(8,128)} collective-permute-done((f32[160,512]{1,0:T(8,128)S(1)}, f32[160,512]{1,0:T(8,128)}, u32[]{:S(2)}, u32[]{:S(2)}) %collective-permute-start.20) | collective-permute-done | bytes 327712 | tf_op jit(solution)/shard_map/ppermute | solution.py:411
  50.6 2.6 %collective-permute-start.22 = (f32[160,512]{1,0:T(8,128)}, f32[160,512]{1,0:T(8,128)}, u32[]{:S(2)}, u32[]{:S(2)}) collective-permute-start(f32[160,512]{1,0:T(8,128)} %collective-permute-done.20.refs_9_.refs_15_), channel_id=1, source_target_pairs={{0,8},{8,16},{16,24},{24,28},{28,20},{20,12},{12,4},{4,0},{1,9},{9... | collective-permute-start | bytes 983048 | tf_op jit(solution)/shard_map/ppermute | solution.py:411
  53.2 2.6 %collective-permute-done.23.refs_12_.refs_18_ = f32[160,512]{1,0:T(8,128)} collective-permute-done((f32[160,512]{1,0:T(8,128)S(1)}, f32[160,512]{1,0:T(8,128)}, u32[]{:S(2)}, u32[]{:S(2)}) %collective-permute-start.23) | collective-permute-done | bytes 327712 | tf_op jit(solution)/shard_map/ppermute | solution.py:411
  57.6 2.6 %collective-permute-start.27 = (f32[160,512]{1,0:T(8,128)S(1)}, f32[160,512]{1,0:T(8,128)S(1)}, u32[]{:S(2)}, u32[]{:S(2)}) collective-permute-start(f32[160,512]{1,0:T(8,128)S(1)} %get-tuple-element.21.refs_1_), channel_id=1, source_target_pairs={{0,8},{8,16},{16,24},{24,28},{28,20},{20,12},{12,4},{4,0},{1,9},{9... | collective-permute-start | bytes 983048 | tf_op jit(solution)/shard_map/ppermute | solution.py:411
  60.2 4.5 %collective-permute-done.22.refs_11_.refs_17_ = f32[160,512]{1,0:T(8,128)} collective-permute-done((f32[160,512]{1,0:T(8,128)}, f32[160,512]{1,0:T(8,128)}, u32[]{:S(2)}, u32[]{:S(2)}) %collective-permute-start.22) | collective-permute-done | bytes 327712 | tf_op jit(solution)/shard_map/ppermute | solution.py:411
  64.7 2.6 %collective-permute-start.8 = (f32[160,512]{1,0:T(8,128)S(1)}, f32[160,512]{1,0:T(8,128)S(1)}, u32[]{:S(2)}, u32[]{:S(2)}) collective-permute-start(f32[160,512]{1,0:T(8,128)S(1)} %collective-permute-done.4.refs_2_.refs_5_), channel_id=1, source_target_pairs={{0,8},{8,16},{16,24},{24,28},{28,20},{20,12},{12,4},{4,0},{1,9},{9... | collective-permute-start | bytes 983048 | tf_op jit(solution)/shard_map/ppermute | solution.py:411
  67.3 2.5 %collective-permute-start.24 = (f32[160,512]{1,0:T(8,128)}, f32[160,512]{1,0:T(8,128)S(1)}, u32[]{:S(2)}, u32[]{:S(2)}) collective-permute-start(f32[160,512]{1,0:T(8,128)} %collective-permute-done.22.refs_11_.refs_17_), channel_id=1, source_target_pairs={{0,8},{8,16},{16,24},{24,28},{28,20},{20,12},{12,4},{4,0},{1,9},{9... | collective-permute-start | bytes 983048 | tf_op jit(solution)/shard_map/ppermute | solution.py:411
  71.8 5.7 %collective-permute-done.5.refs_17_.refs_2_.refs_10_ = f32[160,512]{1,0:T(8,128)S(1)} collective-permute-done((f32[160,512]{1,0:T(8,128)S(1)}, f32[160,512]{1,0:T(8,128)S(1)}, u32[]{:S(2)}, u32[]{:S(2)}) %collective-permute-start.5) | collective-permute-done | bytes 327712 | tf_op jit(solution)/shard_map/ppermute | solution.py:411
  81.0 3.5 %collective-permute-done.26.refs_15_.refs_21_ = f32[160,512]{1,0:T(8,128)S(1)} collective-permute-done((f32[160,512]{1,0:T(8,128)}, f32[160,512]{1,0:T(8,128)S(1)}, u32[]{:S(2)}, u32[]{:S(2)}) %collective-permute-start.26) | collective-permute-done | bytes 327712 | tf_op jit(solution)/shard_map/ppermute | solution.py:411
  85.3 5.7 %shard_map.58.refs_17_ = f32[512,512]{1,0:T(8,128)} custom-call(s32[8]{0:T(128)S(1)} %get-tuple-element.31.ids, s32[1]{0:T(128)} %bitcast.place, f32[160,512]{1,0:T(8,128)S(1)} %get-tuple-element.29.refs_0_, f32[160,512]{1,0:T(8,128)S(1)} %collective-permute-done.2.refs_1_, f32[160,512]{1,0:T(8,128)S(1)} %collective-permute-done.17.refs_2_, ...), custom_call_target="tpu_custom_call" | custom-call | flops 3221225472 | bytes 3145728 | tf_op jit(solution)/shard_map/pallas_call | solution.py:229
  94.9 7.5 %shard_map.60 = f32[512,512]{1,0:T(8,128)} custom-call(s32[8]{0:T(128)S(1)} %get-tuple-element.31.ids, s32[1]{0:T(128)} %bitcast.place, f32[160,512]{1,0:T(8,128)S(1)} %get-tuple-element.29.refs_0_, f32[160,512]{1,0:T(8,128)S(1)} %collective-permute-done.2.refs_1_, f32[160,512]{1,0:T(8,128)S(1)} %collective-permute-done.17.refs_2_, ...), custom_call_target="tpu_custom_call" | custom-call | flops 6442450944 | bytes 3145728 | tf_op jit(solution)/shard_map/pallas_call | solution.py:229
  108.5 6.0 %collective-permute-done.31.refs_25_ = f32[160,512]{1,0:T(8,128)S(1)} collective-permute-done((f32[160,512]{1,0:T(8,128)S(1)}, f32[160,512]{1,0:T(8,128)S(1)}, u32[]{:S(2)}, u32[]{:S(2)}) %collective-permute-start.31) | collective-permute-done | bytes 327712 | tf_op jit(solution)/shard_map/ppermute | solution.py:411
  118.3 3.6 %collective-permute-done.14.refs_26_ = f32[160,512]{1,0:T(8,128)} collective-permute-done((f32[160,512]{1,0:T(8,128)}, f32[160,512]{1,0:T(8,128)}, u32[]{:S(2)}, u32[]{:S(2)}) %collective-permute-start.14) | collective-permute-done | bytes 327712 | tf_op jit(solution)/shard_map/ppermute | solution.py:411
  136.5 11.1 %shard_map.62.refs_9_ = f32[2560,512]{1,0:T(8,128)} custom-call(s32[14]{0:T(128)S(1)} %pad_add_fusion.ids, s32[1]{0:T(128)} %bitcast.place, f32[160,512]{1,0:T(8,128)S(1)} %get-tuple-element.29.refs_0_, f32[160,512]{1,0:T(8,128)S(1)} %collective-permute-done.2.refs_1_, f32[160,512]{1,0:T(8,128)S(1)} %collective-permute-done.17.refs_2_, ...), custom_call_target="tpu_custom_call" | custom-call | flops 7046430720 | bytes 18350080 | tf_op jit(solution)/shard_map/pallas_call | solution.py:356
  147.6 4.6 %shard_map.63 = f32[2560,512]{1,0:T(8,128)} custom-call(s32[2]{0:T(128)S(1)} %slice.6.ids, s32[1]{0:T(128)} %bitcast.place, f32[160,512]{1,0:T(8,128)S(1)} %collective-permute-done.7.refs_2_.refs_0_, f32[160,512]{1,0:T(8,128)S(1)} %collective-permute-done.12.refs_1_, ...), custom_call_target="tpu_custom_call", output_to_operand_aliasing={{}: (11, {})} | custom-call | flops 1006632960 | bytes 2621440 | tf_op jit(solution)/shard_map/pallas_call | solution.py:356
  (116 shorter events, 40.8 us)
Async XLA Ops:
  4.1 13.4 %collective-permute-start = (f32[160,512]{1,0:T(8,128)S(1)}, f32[160,512]{1,0:T(8,128)S(1)}, u32[]{:S(2)}, u32[]{:S(2)}) collective-permute-start(f32[160,512]{1,0:T(8,128)S(1)} %get-tuple-element.15), channel_id=1, source_target_pairs={{0,24},{24,0},{4,28},{28,4},{8,16},{16,8}} | collective-permute-start | bytes 983048 | tf_op jit(solution)/shard_map/ppermute | solution.py:485
  8.5 15.7 %collective-permute-start.1 = (f32[160,512]{1,0:T(8,128)S(1)}, f32[160,512]{1,0:T(8,128)S(1)}, u32[]{:S(2)}, u32[]{:S(2)}) collective-permute-start(f32[160,512]{1,0:T(8,128)S(1)} %get-tuple-element.17), channel_id=1, source_target_pairs={{0,24},{24,0},{4,28},{28,4},{8,16},{16,8}} | collective-permute-start | bytes 983048 | tf_op jit(solution)/shard_map/ppermute | solution.py:485
  17.6 13.0 %collective-permute-start.2 = (f32[160,512]{1,0:T(8,128)S(1)}, f32[160,512]{1,0:T(8,128)S(1)}, u32[]{:S(2)}, u32[]{:S(2)}) collective-permute-start(f32[160,512]{1,0:T(8,128)S(1)} %get-tuple-element.29.refs_0_), channel_id=1, source_target_pairs={{0,8},{8,16},{16,24},{24,28},{28,20},{20,12},{12,4},{4,0},{1,9},{9... | collective-permute-start | bytes 983048 | tf_op jit(solution)/shard_map/ppermute | solution.py:411
  24.3 13.7 %collective-permute-start.21 = (f32[160,512]{1,0:T(8,128)S(1)}, f32[160,512]{1,0:T(8,128)S(1)}, u32[]{:S(2)}, u32[]{:S(2)}) collective-permute-start(f32[160,512]{1,0:T(8,128)S(1)} %get-tuple-element.27.refs_8_.refs_14_), channel_id=1, source_target_pairs={{8,0},{16,8},{24,16},{28,24},{20,28},{12,20},{4,12},{0,4},{9,1},{1... | collective-permute-start | bytes 983048 | tf_op jit(solution)/shard_map/ppermute | solution.py:411
  30.6 12.9 %collective-permute-start.3 = (f32[160,512]{1,0:T(8,128)S(1)}, f32[160,512]{1,0:T(8,128)S(1)}, u32[]{:S(2)}, u32[]{:S(2)}) collective-permute-start(f32[160,512]{1,0:T(8,128)S(1)} %collective-permute-done.2.refs_1_), channel_id=1, source_target_pairs={{0,8},{8,16},{16,24},{24,28},{28,20},{20,12},{12,4},{4,0},{1,9},{9... | collective-permute-start | bytes 983048 | tf_op jit(solution)/shard_map/ppermute | solution.py:411
  35.5 15.0 %collective-permute-start.20 = (f32[160,512]{1,0:T(8,128)S(1)}, f32[160,512]{1,0:T(8,128)}, u32[]{:S(2)}, u32[]{:S(2)}) collective-permute-start(f32[160,512]{1,0:T(8,128)S(1)} %get-tuple-element.27.refs_8_.refs_14_), channel_id=1, source_target_pairs={{0,8},{8,16},{16,24},{24,28},{28,20},{20,12},{12,4},{4,0},{1,9},{9... | collective-permute-start | bytes 983048 | tf_op jit(solution)/shard_map/ppermute | solution.py:411
  38.0 15.2 %collective-permute-start.17 = (f32[160,512]{1,0:T(8,128)S(1)}, f32[160,512]{1,0:T(8,128)S(1)}, u32[]{:S(2)}, u32[]{:S(2)}) collective-permute-start(f32[160,512]{1,0:T(8,128)S(1)} %get-tuple-element.29.refs_0_), channel_id=1, source_target_pairs={{8,0},{16,8},{24,16},{28,24},{20,28},{12,20},{4,12},{0,4},{9,1},{1... | collective-permute-start | bytes 983048 | tf_op jit(solution)/shard_map/ppermute | solution.py:411
  38.0 17.8 %collective-permute-start.23 = (f32[160,512]{1,0:T(8,128)S(1)}, f32[160,512]{1,0:T(8,128)}, u32[]{:S(2)}, u32[]{:S(2)}) collective-permute-start(f32[160,512]{1,0:T(8,128)S(1)} %collective-permute-done.21.refs_10_.refs_16_), channel_id=1, source_target_pairs={{8,0},{16,8},{24,16},{28,24},{20,28},{12,20},{4,12},{0,4},{9,1},{1... | collective-permute-start | bytes 983048 | tf_op jit(solution)/shard_map/ppermute | solution.py:411
  43.5 14.0 %collective-permute-start.4 = (f32[160,512]{1,0:T(8,128)S(1)}, f32[160,512]{1,0:T(8,128)S(1)}, u32[]{:S(2)}, u32[]{:S(2)}) collective-permute-start(f32[160,512]{1,0:T(8,128)S(1)} %collective-permute-done.3.refs_3_), channel_id=1, source_target_pairs={{0,8},{8,16},{16,24},{24,28},{28,20},{20,12},{12,4},{4,0},{1,9},{9... | collective-permute-start | bytes 983048 | tf_op jit(solution)/shard_map/ppermute | solution.py:411
  50.6 14.1 %collective-permute-start.22 = (f32[160,512]{1,0:T(8,128)}, f32[160,512]{1,0:T(8,128)}, u32[]{:S(2)}, u32[]{:S(2)}) collective-permute-start(f32[160,512]{1,0:T(8,128)} %collective-permute-done.20.refs_9_.refs_15_), channel_id=1, source_target_pairs={{0,8},{8,16},{16,24},{24,28},{28,20},{20,12},{12,4},{4,0},{1,9},{9... | collective-permute-start | bytes 983048 | tf_op jit(solution)/shard_map/ppermute | solution.py:411
  53.2 14.2 %collective-permute-start.18 = (f32[160,512]{1,0:T(8,128)S(1)}, f32[160,512]{1,0:T(8,128)}, u32[]{:S(2)}, u32[]{:S(2)}) collective-permute-start(f32[160,512]{1,0:T(8,128)S(1)} %collective-permute-done.17.refs_2_), channel_id=1, source_target_pairs={{8,0},{16,8},{24,16},{28,24},{20,28},{12,20},{4,12},{0,4},{9,1},{1... | collective-permute-start | bytes 983048 | tf_op jit(solution)/shard_map/ppermute | solution.py:411
  55.8 15.8 %collective-permute-start.25 = (f32[160,512]{1,0:T(8,128)}, f32[160,512]{1,0:T(8,128)}, u32[]{:S(2)}, u32[]{:S(2)}) collective-permute-start(f32[160,512]{1,0:T(8,128)} %collective-permute-done.23.refs_12_.refs_18_), channel_id=1, source_target_pairs={{8,0},{16,8},{24,16},{28,24},{20,28},{12,20},{4,12},{0,4},{9,1},{1... | collective-permute-start | bytes 983048 | tf_op jit(solution)/shard_map/ppermute | solution.py:411
  57.6 13.9 %collective-permute-start.27 = (f32[160,512]{1,0:T(8,128)S(1)}, f32[160,512]{1,0:T(8,128)S(1)}, u32[]{:S(2)}, u32[]{:S(2)}) collective-permute-start(f32[160,512]{1,0:T(8,128)S(1)} %get-tuple-element.21.refs_1_), channel_id=1, source_target_pairs={{0,8},{8,16},{16,24},{24,28},{28,20},{20,12},{12,4},{4,0},{1,9},{9... | collective-permute-start | bytes 983048 | tf_op jit(solution)/shard_map/ppermute | solution.py:411
  60.2 17.3 %collective-permute-start.5 = (f32[160,512]{1,0:T(8,128)S(1)}, f32[160,512]{1,0:T(8,128)S(1)}, u32[]{:S(2)}, u32[]{:S(2)}) collective-permute-start(f32[160,512]{1,0:T(8,128)S(1)} %get-tuple-element.20.refs_0_), channel_id=1, source_target_pairs={{8,0},{16,8},{24,16},{28,24},{20,28},{12,20},{4,12},{0,4},{9,1},{1... | collective-permute-start | bytes 983048 | tf_op jit(solution)/shard_map/ppermute | solution.py:411
  64.7 12.8 %collective-permute-start.8 = (f32[160,512]{1,0:T(8,128)S(1)}, f32[160,512]{1,0:T(8,128)S(1)}, u32[]{:S(2)}, u32[]{:S(2)}) collective-permute-start(f32[160,512]{1,0:T(8,128)S(1)} %collective-permute-done.4.refs_2_.refs_5_), channel_id=1, source_target_pairs={{0,8},{8,16},{16,24},{24,28},{28,20},{20,12},{12,4},{4,0},{1,9},{9... | collective-permute-start | bytes 983048 | tf_op jit(solution)/shard_map/ppermute | solution.py:411
  71.5 13.0 %collective-permute-start.26 = (f32[160,512]{1,0:T(8,128)}, f32[160,512]{1,0:T(8,128)S(1)}, u32[]{:S(2)}, u32[]{:S(2)}) collective-permute-start(f32[160,512]{1,0:T(8,128)} %collective-permute-done.25.refs_14_.refs_20_), channel_id=1, source_target_pairs={{8,0},{16,8},{24,16},{28,24},{20,28},{12,20},{4,12},{0,4},{9,1},{1... | collective-permute-start | bytes 983048 | tf_op jit(solution)/shard_map/ppermute | solution.py:411
  77.5 15.9 %collective-permute-start.13 = (f32[160,512]{1,0:T(8,128)S(1)}, f32[160,512]{1,0:T(8,128)S(1)}, u32[]{:S(2)}, u32[]{:S(2)}) collective-permute-start(f32[160,512]{1,0:T(8,128)S(1)} %get-tuple-element.23.refs_22_), channel_id=1, source_target_pairs={{8,0},{16,8},{24,16},{28,24},{20,28},{12,20},{4,12},{0,4},{9,1},{1... | collective-permute-start | bytes 983048 | tf_op jit(solution)/shard_map/ppermute | solution.py:411
  77.6 15.8 %collective-permute-start.9 = (f32[160,512]{1,0:T(8,128)S(1)}, f32[160,512]{1,0:T(8,128)S(1)}, u32[]{:S(2)}, u32[]{:S(2)}) collective-permute-start(f32[160,512]{1,0:T(8,128)S(1)} %get-tuple-element.22.refs_8_), channel_id=1, source_target_pairs={{0,8},{8,16},{16,24},{24,28},{28,20},{20,12},{12,4},{4,0},{1,9},{9... | collective-permute-start | bytes 983048 | tf_op jit(solution)/shard_map/ppermute | solution.py:411
  91.0 32.6 %collective-permute-start.28 = (f32[512,512]{1,0:T(8,128)}, f32[512,512]{1,0:T(8,128)}, u32[]{:S(2)}, u32[]{:S(2)}) collective-permute-start(f32[512,512]{1,0:T(8,128)} %shard_map.58.refs_17_), channel_id=1, source_target_pairs={{0,2},{4,6},{8,10},{12,14},{16,18},{20,22},{24,26},{28,30}} | collective-permute-start | bytes 3145736 | tf_op jit(solution)/shard_map/ppermute | solution.py:422
  102.5 25.8 %collective-permute-start.30 = (f32[512,512]{1,0:T(8,128)}, f32[512,512]{1,0:T(8,128)}, u32[]{:S(2)}, u32[]{:S(2)}) collective-permute-start(f32[512,512]{1,0:T(8,128)} %shard_map.60), channel_id=1, source_target_pairs={{0,2},{4,6},{8,10},{12,14},{16,18},{20,22},{24,26},{28,30}} | collective-permute-start | bytes 3145736 | tf_op jit(solution)/shard_map/ppermute | solution.py:422
  115.9 14.9 %collective-permute-start.32 = (f32[160,512]{1,0:T(8,128)S(1)}, f32[160,512]{1,0:T(8,128)S(1)}, u32[]{:S(2)}, u32[]{:S(2)}) collective-permute-start(f32[160,512]{1,0:T(8,128)S(1)} %collective-permute-done.31.refs_25_), channel_id=1, source_target_pairs={{0,8},{8,16},{16,24},{24,28},{28,20},{20,12},{12,4},{4,0},{1,9},{9... | collective-permute-start | bytes 983048 | tf_op jit(solution)/shard_map/ppermute | solution.py:411
  118.0 12.8 %collective-permute-start.7 = (f32[160,512]{1,0:T(8,128)S(1)}, f32[160,512]{1,0:T(8,128)S(1)}, u32[]{:S(2)}, u32[]{:S(2)}) collective-permute-start(f32[160,512]{1,0:T(8,128)S(1)} %collective-permute-done.6.refs_12_), channel_id=1, source_target_pairs={{8,0},{16,8},{24,16},{28,24},{20,28},{12,20},{4,12},{0,4},{9,1},{1... | collective-permute-start | bytes 983048 | tf_op jit(solution)/shard_map/ppermute | solution.py:411
  132.4 15.2 %collective-permute-start.12 = (f32[160,512]{1,0:T(8,128)S(1)}, f32[160,512]{1,0:T(8,128)S(1)}, u32[]{:S(2)}, u32[]{:S(2)}) collective-permute-start(f32[160,512]{1,0:T(8,128)S(1)} %collective-permute-done.11.refs_1_.refs_13_), channel_id=1, source_target_pairs={{0,8},{8,16},{16,24},{24,28},{28,20},{20,12},{12,4},{4,0},{1,9},{9... | collective-permute-start | bytes 983048 | tf_op jit(solution)/shard_map/ppermute | solution.py:411
  134.1 13.5 %collective-permute-start.16 = (f32[160,512]{1,0:T(8,128)S(1)}, f32[160,512]{1,0:T(8,128)S(1)}, u32[]{:S(2)}, u32[]{:S(2)}) collective-permute-start(f32[160,512]{1,0:T(8,128)S(1)} %collective-permute-done.15.refs_4_.refs_2_), channel_id=1, source_target_pairs={{8,0},{16,8},{24,16},{28,24},{20,28},{12,20},{4,12},{0,4},{9,1},{1... | collective-permute-start | bytes 983048 | tf_op jit(solution)/shard_map/ppermute | solution.py:411
  (37 other events, 567.8 us)

commit v8 on v7

--- a/solution.py
+++ b/solution.py
@@ -93,15 +93,14 @@
                 factor[i * block : (i + 1) * block, depth - block :] = inverse
 
     moves = me[0] < movers
-    copies = []
-    for k in range(2):
-        panel = pl.ds(k * width, width)
-        for cut in range(cuts):
-            at = pl.ds(cut * part, part)
-            copies.append((factor.at[at, panel], outs[2 * cut + k], store_sem.at[2 * cut + k]))
-        if cuts > 1:
-            sent = pl.ds(pl.multiple_of(jnp.where(moves, part, 0), 8), part)
-            copies.append((factor.at[sent, panel], outs[4 + k], store_sem.at[4 + k]))
+    panel = pl.ds(width, width)
+    copies = [
+        (factor.at[pl.ds(cut * part, part), panel], outs[cut], store_sem.at[cut])
+        for cut in range(cuts)
+    ]
+    if cuts > 1:
+        sent = pl.ds(pl.multiple_of(jnp.where(moves, part, 0), 8), part)
+        copies.append((factor.at[sent, panel], outs[cuts], store_sem.at[cuts]))
     copies = [pltpu.make_async_copy(*copy) for copy in copies]
     for copy in copies:
         copy.start()
@@ -111,7 +110,7 @@
 
 def prepare(me, place, factor, block, cuts, movers):
     rows, depth = factor.shape
-    count = 2 * cuts + (2 if cuts > 1 else 0)
+    count = cuts + (1 if cuts > 1 else 0)
     return pl.pallas_call(
         functools.partial(prepare_kernel, rows, block, depth, cuts, movers),
         out_shape=[jax.ShapeDtypeStruct((rows // cuts, depth // 2), jnp.float32)] * count,
@@ -127,56 +126,44 @@
     )(me, place, factor)
 
 
-def solve_kernel(pieces, rows, width, chunk, block, panel, ids, place, *refs):
-    held, refs = refs[: 2 * pieces], refs[2 * pieces :]
-    rhs, refs = refs[0], refs[1:]
-    earlier = refs[:panel]
-    solved, lower, piece_sem, rhs_sem = refs[len(refs) - 4 :]
-    first, last = panel * width, (panel + 1) * width
-    side = lower.shape[1] - LANES
+def solve_kernel(pieces, rows, width, chunk, block, ids, place, *refs):
+    held, rhs = refs[: 2 * pieces], refs[2 * pieces]
+    *outs, lower, solved, piece_sem, rhs_sem, out_sem = refs[len(refs) - 7 :]
+    depth = 2 * width
 
     @pl.when(place[0] == 0)
     def _():
         def copies(i):
             at = pl.ds(pl.multiple_of(ids[i] * rows, 8), rows)
-            cut = 0 if panel else width - LANES
             return [
                 pltpu.make_async_copy(
-                    held[i], lower.at[at, pl.ds(0, width)], piece_sem.at[0, i]
-                ),
-                pltpu.make_async_copy(
-                    held[pieces + i].at[:, pl.ds(cut, width - cut)],
-                    lower.at[at, pl.ds(width, width - cut)],
-                    piece_sem.at[1, i],
-                ),
-            ]
-
-        def needed(i):
-            return (ids[i] * rows < last) & ((ids[i] + 1) * rows > first)
+                    held[k * pieces + i], lower.at[at, pl.ds(k * width, width)], piece_sem.at[k, i]
+                )
+                for k in range(2)
+            ]
 
         for i in range(pieces):
 
-            @pl.when(needed(i))
+            @pl.when(ids[i] * rows < depth)
             def _(i=i):
                 for copy in copies(i):
                     copy.start()
 
-        load = pltpu.make_async_copy(rhs.at[pl.ds(first, width)], solved, rhs_sem)
+        load = pltpu.make_async_copy(rhs.at[pl.ds(0, depth)], solved, rhs_sem)
         load.start()
         for i in range(pieces):
 
-            @pl.when(needed(i))
+            @pl.when(ids[i] * rows < depth)
             def _(i=i):
                 for copy in copies(i):
                     copy.wait()
 
-        load.wait()
         row, col = grid_ids(chunk)
         lane = lax.broadcasted_iota(jnp.int32, (chunk, LANES), 1)
-        starts = range(0, width, chunk)
+        starts = range(0, depth, chunk)
         inverses = []
         for j in starts:
-            value = lower[first + j : first + j + chunk, side:]
+            value = lower[j : j + chunk, depth - LANES :]
             value = jnp.where(lane >= LANES - block, value, 0.0)
             shift = block
             while shift < LANES:
@@ -190,14 +177,7 @@
             parts = [split16(inverse) for inverse in inverses]
             inner = [
                 dot_split(
-                    split16(
-                        jnp.where(
-                            below,
-                            lower[first + j : first + j + chunk, first + j : first + j + chunk],
-                            0.0,
-                        )
-                    ),
-                    part,
+                    split16(jnp.where(below, lower[j : j + chunk, j : j + chunk], 0.0)), part
                 )
                 for j, part in zip(starts, parts)
             ]
@@ -206,46 +186,49 @@
                 for inverse, part, value in zip(inverses, parts, inner)
             ]
             half *= 2
-        for k in range(panel):
-            solved[...] = solved[...] - dot_split(
-                split16(lower[first:last, k * width : (k + 1) * width]), split16(earlier[k][...])
-            )
+        load.wait()
+        stores = [
+            pltpu.make_async_copy(solved.at[pl.ds(k * width, width)], outs[k], out_sem.at[k])
+            for k in range(2)
+        ]
         for j in starts:
             value = solved[j : j + chunk]
             if j:
-                at = slice(first + j, first + j + chunk)
                 value = value - dot_split(
-                    split16(lower[at, first : first + j]), split16(solved[:j])
+                    split16(lower[j : j + chunk, :j]), split16(solved[:j])
                 )
             solved[j : j + chunk] = dot_split(split16(inverses[j // chunk]), split16(value))
-
-
-def solve_panel(panel, ids, place, held, rhs, earlier, after, width, block):
+            if (j + chunk) % width == 0:
+                stores[j // width].start()
+        for store in stores:
+            store.wait()
+
+
+def solve_panels(ids, place, held, rhs, after, width, block):
     pieces = len(held[0])
     rows = held[0][0].shape[0]
-    columns = rhs.shape[1]
-    tall = -(-(panel + 1) * width // rows) * rows
+    columns, depth = rhs.shape[1], 2 * width
+    tall = -(-depth // rows) * rows
     chunk = math.gcd(width, 2 * LANES)
     return pl.pallas_call(
-        functools.partial(solve_kernel, pieces, rows, width, chunk, block, panel),
-        out_shape=jax.ShapeDtypeStruct((width, columns), jnp.float32),
-        in_specs=[SCALARS] * 2
-        + [ANY] * (2 * pieces + 1)
-        + [WHOLE] * panel
-        + [ANY] * len(after),
-        out_specs=WHOLE,
+        functools.partial(solve_kernel, pieces, rows, width, chunk, block),
+        out_shape=[jax.ShapeDtypeStruct((width, columns), jnp.float32)] * 2,
+        in_specs=[SCALARS] * 2 + [ANY] * (2 * pieces + 1 + len(after)),
+        out_specs=[ANY] * 2,
         scratch_shapes=[
-            pltpu.VMEM((tall, 2 * width if panel else width + LANES), jnp.float32),
+            pltpu.VMEM((tall, depth), jnp.float32),
+            pltpu.VMEM((depth, columns), jnp.float32),
             pltpu.SemaphoreType.DMA((2, pieces)),
             pltpu.SemaphoreType.DMA,
+            pltpu.SemaphoreType.DMA((2,)),
         ],
         compiler_params=pltpu.CompilerParams(vmem_limit_bytes=VMEM_BYTES),
         cost_estimate=pl.CostEstimate(
-            flops=24 * (panel + 1) * width * width * columns,
-            bytes_accessed=12 * width * columns,
+            flops=72 * width * width * columns,
+            bytes_accessed=24 * width * columns,
             transcendentals=0,
         ),
-    )(ids, place, *held[0], *held[1], rhs, *earlier, *after)
+    )(ids, place, *held[0], *held[1], rhs, *after)
 
 
 def update_kernel(pieces, rows, width, group, tile, step, places, ids, place, *refs):
@@ -472,14 +455,17 @@
         if not ringed:
             held = [
                 [lax.all_gather(panel, "src", axis=0, tiled=True)]
-                for panel in prepare(me, place, factor, block, 1, 0)
+                for panel in (factor[:, :width], *prepare(me, place, factor, block, 1, 0))
             ]
             top, top_spots = held, jnp.zeros_like(me)
             groups = [(held, top_spots)]
-            after, near = [[], []], [[], []]
+            after, near = [], [[], []]
         else:
             movers = len(partners)
-            *halves, sent_first, sent_second = prepare(me, place, factor, block, 2, movers)
+            left = factor[:, :width]
+            sent_first = jnp.where(me[0] < movers, left[part:], left[:part])
+            *right, sent_second = prepare(me, place, factor, block, 2, movers)
+            halves = [left[:part], right[0], left[part:], right[1]]
             pairs = [(s, f) for s, f in enumerate(partners)]
             swap = [(number(a, 0), number(b, 0)) for s, f in pairs for a, b in ((s, f), (f, s))]
             got = [lax.ppermute(sent, axes, swap) for sent in (sent_first, sent_second)]
@@ -506,7 +492,7 @@
             free = gate(own[1], [steps[-2][0][0]])
             full = gate(free, [steps[-1][0][0]])
             rest, steps = ring_pass([[full[0], free[0]], [free[1], full[1]]], ring)
-            after = [[steps[0][0][1], steps[0][1][0]], [steps[0][0][0], steps[0][1][1]]]
+            after = [steps[0][0][1], steps[0][1][0]]
             near = [steps[i][0] + steps[i][1] for i in (0, -2)]
             top_spots, cut = spots[0], 2 * half - 2
             groups = [
@@ -516,8 +502,7 @@
                 ),
                 ([rest[k][cut:] for k in range(2)], spots[1][cut:]),
             ]
-        first = solve_panel(0, top_spots, place, top, right_side, [], after[0], width, block)
-        second = solve_panel(1, top_spots, place, top, right_side, [first], after[1], width, block)
+        first, second = solve_panels(top_spots, place, top, right_side, after, width, block)
         solved = [
             spread_near(spread_far(first, places, place), places, near[0]),
             spread_near(spread_far(second, places, place), places, near[1]),

time: 154 us -> 151 us (0.981)
  starting transfers between devices: 55.8 us -> 68.8 us
  waiting for transfers between devices: 52.9 us -> 41.7 us
  Pallas kernels: 33 us -> 28.8 us
  other arithmetic: 4.05 us -> 6.37 us
  local copies, waits for them, and re-layouts: 6.06 us -> 3.74 us
    ppermute x28, starting transfers between devices: 40.7 us -> 52.6 us  [ring_pass(): going[k][way] = lax.ppermute(going[k][way], 'src', pairs)]
    ppermute x28, waiting for transfers between devices: 46.9 us -> 36.1 us  [ring_pass(): going[k][way] = lax.ppermute(going[k][way], 'src', pairs)]
    pallas_call x2 -> x1, Pallas kernels: 13.2 us -> 9.1 us  [solve_panels(): pl.pallas_call(functools.partial(solve_kernel, pieces, rows, width, chunk...]
    unnamed x54 -> x56, local copies, waits for them, and re-layouts: 5.99 us -> 3.67 us
  transfers between devices with their start and end apart: 34 -> 34, of which waited for: 16 -> 23; matrix products, arithmetic and copies ran while one was open for 3% -> 4% of each run, Pallas kernels for 16% -> 10%
where the time goes in v8:
time: 151 us; the launch traced here: 150 us
  starting transfers between devices  68.8 us (46%)
  waiting for transfers between devices  41.7 us (28%)
  Pallas kernels  28.8 us (19%)
  other arithmetic  6.37 us (4%)
  local copies, waits for them, and re-layouts  3.74 us (2%)
    ppermute x28, starting transfers between devices, ring_pass(): going[k][way] = lax.ppermute(going[k][way], 'src', pairs)  52.6 us
    ppermute x28, waiting for transfers between devices, ring_pass(): going[k][way] = lax.ppermute(going[k][way], 'src', pairs)  36.1 us
    pallas_call x2, Pallas kernels, update(): pl.pallas_call(functools.partial(update_kernel, pieces, rows, width, grou...  15.7 us
    pallas_call x1, Pallas kernels, solve_panels(): pl.pallas_call(functools.partial(solve_kernel, pieces, rows, width, chunk...  9.1 us
    ppermute x2, starting transfers between devices, local(): got = [lax.ppermute(sent, axes, swap) for sent in (sent_first, sent_second)]  8.88 us
    ppermute x2, waiting for transfers between devices, local(): got = [lax.ppermute(sent, axes, swap) for sent in (sent_first, sent_second)]  5.36 us
    ppermute x2, starting transfers between devices, spread_far(): found[r + stride] = lax.ppermute(found[r], 'row', [(r, r + stride)])  4.6 us
    pallas_call x1, Pallas kernels, prepare(): pl.pallas_call(functools.partial(prepare_kernel, rows, block, depth, cuts...  3.96 us
  transfers between devices with their start and end apart: 34, of which 23 were waited for; matrix products, arithmetic and copies ran while one was open for 4% of the time, Pallas kernels for 10%

profile of v8, /device:TPU:0, one launch (start us, length us, event | category | flops | bytes accessed | tf_op | source)
XLA Modules:
  0.0 149.9 jit_solution(11870026341013643137)
XLA Ops:
  1.2 7.0 %collective-permute-start = (f32[160,512]{1,0:T(8,128)S(1)}, f32[160,512]{1,0:T(8,128)S(1)}, u32[]{:S(2)}, u32[]{:S(2)}) collective-permute-start(f32[160,512]{1,0:T(8,128)S(1)} %slice_select_fusion.1), channel_id=1, source_target_pairs={{0,24},{24,0},{4,28},{28,4},{8,16},{16,8}} | collective-permute-start | bytes 983048 | tf_op jit(solution)/shard_map/ppermute | solution.py:471
  8.1 4.0 %shard_map.55 = (f32[160,512]{1,0:T(8,128)S(1)}, f32[160,512]{1,0:T(8,128)S(1)}, f32[160,512]{1,0:T(8,128)S(1)}) custom-call(s32[1]{0:T(128)} %bitcast.1.me, s32[1]{0:T(128)} %bitcast.place, f32[320,1024]{1,0:T(8,128)} %source.1), custom_call_target="tpu_custom_call" | custom-call | flops 1000 | bytes 1000 | tf_op jit(solution)/shard_map/pallas_call | solution.py:114
  17.4 3.3 %collective-permute-start.2 = (f32[160,512]{1,0:T(8,128)S(1)}, f32[160,512]{1,0:T(8,128)S(1)}, u32[]{:S(2)}, u32[]{:S(2)}) collective-permute-start(f32[160,512]{1,0:T(8,128)S(1)} %get-tuple-element.25.refs_0_), channel_id=1, source_target_pairs={{0,8},{8,16},{16,24},{24,28},{28,20},{20,12},{12,4},{4,0},{1,9},{9... | collective-permute-start | bytes 983048 | tf_op jit(solution)/shard_map/ppermute | solution.py:394
  20.6 3.2 %collective-permute-done.1 = f32[160,512]{1,0:T(8,128)S(1)} collective-permute-done((f32[160,512]{1,0:T(8,128)S(1)}, f32[160,512]{1,0:T(8,128)S(1)}, u32[]{:S(2)}, u32[]{:S(2)}) %collective-permute-start.1) | collective-permute-done | bytes 327712 | tf_op jit(solution)/shard_map/ppermute | solution.py:471
  23.9 4.1 %collective-permute-start.21 = (f32[160,512]{1,0:T(8,128)S(1)}, f32[160,512]{1,0:T(8,128)S(1)}, u32[]{:S(2)}, u32[]{:S(2)}) collective-permute-start(f32[160,512]{1,0:T(8,128)S(1)} %get-tuple-element.27.refs_8_.refs_14_), channel_id=1, source_target_pairs={{8,0},{16,8},{24,16},{28,24},{20,28},{12,20},{4,12},{0,4},{9,1},{1... | collective-permute-start | bytes 983048 | tf_op jit(solution)/shard_map/ppermute | solution.py:394
  30.2 5.6 %collective-permute-start.3 = (f32[160,512]{1,0:T(8,128)S(1)}, f32[160,512]{1,0:T(8,128)S(1)}, u32[]{:S(2)}, u32[]{:S(2)}) collective-permute-start(f32[160,512]{1,0:T(8,128)S(1)} %collective-permute-done.2.refs_1_), channel_id=1, source_target_pairs={{0,8},{8,16},{16,24},{24,28},{28,20},{20,12},{12,4},{4,0},{1,9},{9... | collective-permute-start | bytes 983048 | tf_op jit(solution)/shard_map/ppermute | solution.py:394
  38.1 4.7 %collective-permute-start.22 = (f32[160,512]{1,0:T(8,128)S(1)}, f32[160,512]{1,0:T(8,128)}, u32[]{:S(2)}, u32[]{:S(2)}) collective-permute-start(f32[160,512]{1,0:T(8,128)S(1)} %collective-permute-done.20.refs_9_.refs_15_), channel_id=1, source_target_pairs={{0,8},{8,16},{16,24},{24,28},{28,20},{20,12},{12,4},{4,0},{1,9},{9... | collective-permute-start | bytes 983048 | tf_op jit(solution)/shard_map/ppermute | solution.py:394
  45.0 4.8 %collective-permute-start.4 = (f32[160,512]{1,0:T(8,128)S(1)}, f32[160,512]{1,0:T(8,128)S(1)}, u32[]{:S(2)}, u32[]{:S(2)}) collective-permute-start(f32[160,512]{1,0:T(8,128)S(1)} %collective-permute-done.3.refs_3_), channel_id=1, source_target_pairs={{0,8},{8,16},{16,24},{24,28},{28,20},{20,12},{12,4},{4,0},{1,9},{9... | collective-permute-start | bytes 983048 | tf_op jit(solution)/shard_map/ppermute | solution.py:394
  51.9 5.0 %collective-permute-start.24 = (f32[160,512]{1,0:T(8,128)}, f32[160,512]{1,0:T(8,128)}, u32[]{:S(2)}, u32[]{:S(2)}) collective-permute-start(f32[160,512]{1,0:T(8,128)} %collective-permute-done.22.refs_11_.refs_17_), channel_id=1, source_target_pairs={{0,8},{8,16},{16,24},{24,28},{28,20},{20,12},{12,4},{4,0},{1,9},{9... | collective-permute-start | bytes 983048 | tf_op jit(solution)/shard_map/ppermute | solution.py:394
  58.9 5.0 %collective-permute-start.27 = (f32[160,512]{1,0:T(8,128)S(1)}, f32[160,512]{1,0:T(8,128)S(1)}, u32[]{:S(2)}, u32[]{:S(2)}) collective-permute-start(f32[160,512]{1,0:T(8,128)S(1)} %get-tuple-element.17.refs_1_), channel_id=1, source_target_pairs={{0,8},{8,16},{16,24},{24,28},{28,20},{20,12},{12,4},{4,0},{1,9},{9... | collective-permute-start | bytes 983048 | tf_op jit(solution)/shard_map/ppermute | solution.py:394
  64.2 3.4 %collective-permute-start.8 = (f32[160,512]{1,0:T(8,128)S(1)}, f32[160,512]{1,0:T(8,128)S(1)}, u32[]{:S(2)}, u32[]{:S(2)}) collective-permute-start(f32[160,512]{1,0:T(8,128)S(1)} %collective-permute-done.4.refs_2_.refs_5_), channel_id=1, source_target_pairs={{0,8},{8,16},{16,24},{24,28},{28,20},{20,12},{12,4},{4,0},{1,9},{9... | collective-permute-start | bytes 983048 | tf_op jit(solution)/shard_map/ppermute | solution.py:394
  67.8 2.5 %collective-permute-done.19.refs_6_ = f32[160,512]{1,0:T(8,128)S(1)} collective-permute-done((f32[160,512]{1,0:T(8,128)}, f32[160,512]{1,0:T(8,128)S(1)}, u32[]{:S(2)}, u32[]{:S(2)}) %collective-permute-start.19) | collective-permute-done | bytes 327712 | tf_op jit(solution)/shard_map/ppermute | solution.py:394
  70.3 3.5 %collective-permute-done.5.refs_17_.refs_2_.refs_10_ = f32[160,512]{1,0:T(8,128)S(1)} collective-permute-done((f32[160,512]{1,0:T(8,128)S(1)}, f32[160,512]{1,0:T(8,128)S(1)}, u32[]{:S(2)}, u32[]{:S(2)}) %collective-permute-start.5) | collective-permute-done | bytes 327712 | tf_op jit(solution)/shard_map/ppermute | solution.py:394
  73.8 3.5 %collective-permute-done.26.refs_15_.refs_21_ = f32[160,512]{1,0:T(8,128)S(1)} collective-permute-done((f32[160,512]{1,0:T(8,128)}, f32[160,512]{1,0:T(8,128)S(1)}, u32[]{:S(2)}, u32[]{:S(2)}) %collective-permute-start.26) | collective-permute-done | bytes 327712 | tf_op jit(solution)/shard_map/ppermute | solution.py:394
  78.2 9.1 %shard_map.58 = (f32[512,512]{1,0:T(8,128)}, f32[512,512]{1,0:T(8,128)}) custom-call(s32[8]{0:T(128)S(1)} %get-tuple-element.29.ids, s32[1]{0:T(128)} %bitcast.place, f32[160,512]{1,0:T(8,128)S(1)} %get-tuple-element.25.refs_0_, f32[160,512]{1,0:T(8,128)S(1)} %collective-permute-done.2.refs_1_, f32[160,512]{1,0:T(8,128)S(1)} %collective-permute-done.17.refs_2_, ...), custom_call_target="tpu_custom_call" | custom-call | flops 9663676416 | bytes 6291456 | tf_op jit(solution)/shard_map/pallas_call | solution.py:213
  89.6 2.3 %collective-permute-start.28 = (f32[512,512]{1,0:T(8,128)}, f32[512,512]{1,0:T(8,128)}, u32[]{:S(2)}, u32[]{:S(2)}) collective-permute-start(f32[512,512]{1,0:T(8,128)} %get-tuple-element.21), channel_id=1, source_target_pairs={{0,2},{4,6},{8,10},{12,14},{16,18},{20,22},{24,26},{28,30}} | collective-permute-start | bytes 3145736 | tf_op jit(solution)/shard_map/ppermute | solution.py:405
  92.9 2.5 %collective-permute-start.9 = (f32[160,512]{1,0:T(8,128)S(1)}, f32[160,512]{1,0:T(8,128)S(1)}, u32[]{:S(2)}, u32[]{:S(2)}) collective-permute-start(f32[160,512]{1,0:T(8,128)S(1)} %get-tuple-element.18.refs_8_), channel_id=1, source_target_pairs={{0,8},{8,16},{16,24},{24,28},{28,20},{20,12},{12,4},{4,0},{1,9},{9... | collective-permute-start | bytes 983048 | tf_op jit(solution)/shard_map/ppermute | solution.py:394
  97.4 5.6 %collective-permute-done.9.refs_1_.refs_9_ = f32[160,512]{1,0:T(8,128)S(1)} collective-permute-done((f32[160,512]{1,0:T(8,128)S(1)}, f32[160,512]{1,0:T(8,128)S(1)}, u32[]{:S(2)}, u32[]{:S(2)}) %collective-permute-start.9) | collective-permute-done | bytes 327712 | tf_op jit(solution)/shard_map/ppermute | solution.py:394
  106.9 3.6 %collective-permute-done.6.refs_12_ = f32[160,512]{1,0:T(8,128)} collective-permute-done((f32[160,512]{1,0:T(8,128)}, f32[160,512]{1,0:T(8,128)}, u32[]{:S(2)}, u32[]{:S(2)}) %collective-permute-start.6) | collective-permute-done | bytes 327712 | tf_op jit(solution)/shard_map/ppermute | solution.py:394
  115.4 2.3 %collective-permute-start.11 = (f32[160,512]{1,0:T(8,128)}, f32[160,512]{1,0:T(8,128)}, u32[]{:S(2)}, u32[]{:S(2)}) collective-permute-start(f32[160,512]{1,0:T(8,128)} %collective-permute-done.10.refs_11_), channel_id=1, source_target_pairs={{0,8},{8,16},{16,24},{24,28},{28,20},{20,12},{12,4},{4,0},{1,9},{9... | collective-permute-start | bytes 983048 | tf_op jit(solution)/shard_map/ppermute | solution.py:394
  117.7 2.5 %broadcast_select_fusion.refs_0_ = f32[512,512]{1,0:T(8,128)} fusion(f32[512,512]{1,0:T(8,128)} %collective-permute-done.30, f32[512,512]{1,0:T(8,128)} %get-tuple-element.22, pred[]{:T(512)S(6)} %eq.54), kind=kLoop, calls=%fused_computation | loop fusion | flops 262144 | bytes 3145729 | tf_op jit(solution)/shard_map/jit(_where)/select_n | solution.py:409
  122.7 3.0 %collective-permute-done.15.refs_4_.refs_2_ = f32[160,512]{1,0:T(8,128)S(1)} collective-permute-done((f32[160,512]{1,0:T(8,128)}, f32[160,512]{1,0:T(8,128)S(1)}, u32[]{:S(2)}, u32[]{:S(2)}) %collective-permute-start.15) | collective-permute-done | bytes 327712 | tf_op jit(solution)/shard_map/ppermute | solution.py:394
  134.0 11.2 %shard_map.61.refs_9_ = f32[2560,512]{1,0:T(8,128)} custom-call(s32[14]{0:T(128)S(1)} %pad_add_fusion.ids, s32[1]{0:T(128)} %bitcast.place, f32[160,512]{1,0:T(8,128)S(1)} %get-tuple-element.25.refs_0_, f32[160,512]{1,0:T(8,128)S(1)} %copy-done.11, f32[160,512]{1,0:T(8,128)S(1)} %copy-done.13, f32[160,512]{1,0:T(8,128)S(1)} %copy-done.15, ...), custom_call_target="tpu_custom_call" | custom-call | flops 7046430720 | bytes 18350080 | tf_op jit(solution)/shard_map/pallas_call | solution.py:339
  145.1 4.6 %shard_map.62 = f32[2560,512]{1,0:T(8,128)} custom-call(s32[2]{0:T(128)S(1)} %slice.17.ids, s32[1]{0:T(128)} %bitcast.place, f32[160,512]{1,0:T(8,128)S(1)} %collective-permute-done.7.refs_2_.refs_0_, f32[160,512]{1,0:T(8,128)S(1)} %collective-permute-done.12.refs_1_, ...), custom_call_target="tpu_custom_call", output_to_operand_aliasing={{}: (11, {})} | custom-call | flops 1006632960 | bytes 2621440 | tf_op jit(solution)/shard_map/pallas_call | solution.py:339
  (118 shorter events, 43.2 us)
Async XLA Ops:
  1.2 15.0 %collective-permute-start = (f32[160,512]{1,0:T(8,128)S(1)}, f32[160,512]{1,0:T(8,128)S(1)}, u32[]{:S(2)}, u32[]{:S(2)}) collective-permute-start(f32[160,512]{1,0:T(8,128)S(1)} %slice_select_fusion.1), channel_id=1, source_target_pairs={{0,24},{24,0},{4,28},{28,4},{8,16},{16,8}} | collective-permute-start | bytes 983048 | tf_op jit(solution)/shard_map/ppermute | solution.py:471
  12.1 11.8 %collective-permute-start.1 = (f32[160,512]{1,0:T(8,128)S(1)}, f32[160,512]{1,0:T(8,128)S(1)}, u32[]{:S(2)}, u32[]{:S(2)}) collective-permute-start(f32[160,512]{1,0:T(8,128)S(1)} %get-tuple-element.14), channel_id=1, source_target_pairs={{0,24},{24,0},{4,28},{28,4},{8,16},{16,8}} | collective-permute-start | bytes 983048 | tf_op jit(solution)/shard_map/ppermute | solution.py:471
  17.4 12.8 %collective-permute-start.2 = (f32[160,512]{1,0:T(8,128)S(1)}, f32[160,512]{1,0:T(8,128)S(1)}, u32[]{:S(2)}, u32[]{:S(2)}) collective-permute-start(f32[160,512]{1,0:T(8,128)S(1)} %get-tuple-element.25.refs_0_), channel_id=1, source_target_pairs={{0,8},{8,16},{16,24},{24,28},{28,20},{20,12},{12,4},{4,0},{1,9},{9... | collective-permute-start | bytes 983048 | tf_op jit(solution)/shard_map/ppermute | solution.py:394
  23.9 12.3 %collective-permute-start.21 = (f32[160,512]{1,0:T(8,128)S(1)}, f32[160,512]{1,0:T(8,128)S(1)}, u32[]{:S(2)}, u32[]{:S(2)}) collective-permute-start(f32[160,512]{1,0:T(8,128)S(1)} %get-tuple-element.27.refs_8_.refs_14_), channel_id=1, source_target_pairs={{8,0},{16,8},{24,16},{28,24},{20,28},{12,20},{4,12},{0,4},{9,1},{1... | collective-permute-start | bytes 983048 | tf_op jit(solution)/shard_map/ppermute | solution.py:394
  28.1 10.0 %collective-permute-start.20 = (f32[160,512]{1,0:T(8,128)S(1)}, f32[160,512]{1,0:T(8,128)S(1)}, u32[]{:S(2)}, u32[]{:S(2)}) collective-permute-start(f32[160,512]{1,0:T(8,128)S(1)} %get-tuple-element.27.refs_8_.refs_14_), channel_id=1, source_target_pairs={{0,8},{8,16},{16,24},{24,28},{28,20},{20,12},{12,4},{4,0},{1,9},{9... | collective-permute-start | bytes 983048 | tf_op jit(solution)/shard_map/ppermute | solution.py:394
  30.2 13.1 %collective-permute-start.17 = (f32[160,512]{1,0:T(8,128)S(1)}, f32[160,512]{1,0:T(8,128)S(1)}, u32[]{:S(2)}, u32[]{:S(2)}) collective-permute-start(f32[160,512]{1,0:T(8,128)S(1)} %get-tuple-element.25.refs_0_), channel_id=1, source_target_pairs={{8,0},{16,8},{24,16},{28,24},{20,28},{12,20},{4,12},{0,4},{9,1},{1... | collective-permute-start | bytes 983048 | tf_op jit(solution)/shard_map/ppermute | solution.py:394
  30.2 14.9 %collective-permute-start.3 = (f32[160,512]{1,0:T(8,128)S(1)}, f32[160,512]{1,0:T(8,128)S(1)}, u32[]{:S(2)}, u32[]{:S(2)}) collective-permute-start(f32[160,512]{1,0:T(8,128)S(1)} %collective-permute-done.2.refs_1_), channel_id=1, source_target_pairs={{0,8},{8,16},{16,24},{24,28},{28,20},{20,12},{12,4},{4,0},{1,9},{9... | collective-permute-start | bytes 983048 | tf_op jit(solution)/shard_map/ppermute | solution.py:394
  36.3 13.8 %collective-permute-start.23 = (f32[160,512]{1,0:T(8,128)S(1)}, f32[160,512]{1,0:T(8,128)S(1)}, u32[]{:S(2)}, u32[]{:S(2)}) collective-permute-start(f32[160,512]{1,0:T(8,128)S(1)} %collective-permute-done.21.refs_10_.refs_16_), channel_id=1, source_target_pairs={{8,0},{16,8},{24,16},{28,24},{20,28},{12,20},{4,12},{0,4},{9,1},{1... | collective-permute-start | bytes 983048 | tf_op jit(solution)/shard_map/ppermute | solution.py:394
  38.1 13.8 %collective-permute-start.22 = (f32[160,512]{1,0:T(8,128)S(1)}, f32[160,512]{1,0:T(8,128)}, u32[]{:S(2)}, u32[]{:S(2)}) collective-permute-start(f32[160,512]{1,0:T(8,128)S(1)} %collective-permute-done.20.refs_9_.refs_15_), channel_id=1, source_target_pairs={{0,8},{8,16},{16,24},{24,28},{28,20},{20,12},{12,4},{4,0},{1,9},{9... | collective-permute-start | bytes 983048 | tf_op jit(solution)/shard_map/ppermute | solution.py:394
  43.3 13.9 %collective-permute-start.18 = (f32[160,512]{1,0:T(8,128)S(1)}, f32[160,512]{1,0:T(8,128)}, u32[]{:S(2)}, u32[]{:S(2)}) collective-permute-start(f32[160,512]{1,0:T(8,128)S(1)} %collective-permute-done.17.refs_2_), channel_id=1, source_target_pairs={{8,0},{16,8},{24,16},{28,24},{20,28},{12,20},{4,12},{0,4},{9,1},{1... | collective-permute-start | bytes 983048 | tf_op jit(solution)/shard_map/ppermute | solution.py:394
  45.0 13.8 %collective-permute-start.4 = (f32[160,512]{1,0:T(8,128)S(1)}, f32[160,512]{1,0:T(8,128)S(1)}, u32[]{:S(2)}, u32[]{:S(2)}) collective-permute-start(f32[160,512]{1,0:T(8,128)S(1)} %collective-permute-done.3.refs_3_), channel_id=1, source_target_pairs={{0,8},{8,16},{16,24},{24,28},{28,20},{20,12},{12,4},{4,0},{1,9},{9... | collective-permute-start | bytes 983048 | tf_op jit(solution)/shard_map/ppermute | solution.py:394
  50.0 14.1 %collective-permute-start.25 = (f32[160,512]{1,0:T(8,128)S(1)}, f32[160,512]{1,0:T(8,128)}, u32[]{:S(2)}, u32[]{:S(2)}) collective-permute-start(f32[160,512]{1,0:T(8,128)S(1)} %collective-permute-done.23.refs_12_.refs_18_), channel_id=1, source_target_pairs={{8,0},{16,8},{24,16},{28,24},{20,28},{12,20},{4,12},{0,4},{9,1},{1... | collective-permute-start | bytes 983048 | tf_op jit(solution)/shard_map/ppermute | solution.py:394
  51.9 15.7 %collective-permute-start.24 = (f32[160,512]{1,0:T(8,128)}, f32[160,512]{1,0:T(8,128)}, u32[]{:S(2)}, u32[]{:S(2)}) collective-permute-start(f32[160,512]{1,0:T(8,128)} %collective-permute-done.22.refs_11_.refs_17_), channel_id=1, source_target_pairs={{0,8},{8,16},{16,24},{24,28},{28,20},{20,12},{12,4},{4,0},{1,9},{9... | collective-permute-start | bytes 983048 | tf_op jit(solution)/shard_map/ppermute | solution.py:394
  57.1 13.1 %collective-permute-start.19 = (f32[160,512]{1,0:T(8,128)}, f32[160,512]{1,0:T(8,128)S(1)}, u32[]{:S(2)}, u32[]{:S(2)}) collective-permute-start(f32[160,512]{1,0:T(8,128)} %collective-permute-done.18.refs_4_), channel_id=1, source_target_pairs={{8,0},{16,8},{24,16},{28,24},{20,28},{12,20},{4,12},{0,4},{9,1},{1... | collective-permute-start | bytes 983048 | tf_op jit(solution)/shard_map/ppermute | solution.py:394
  58.9 11.4 %collective-permute-start.27 = (f32[160,512]{1,0:T(8,128)S(1)}, f32[160,512]{1,0:T(8,128)S(1)}, u32[]{:S(2)}, u32[]{:S(2)}) collective-permute-start(f32[160,512]{1,0:T(8,128)S(1)} %get-tuple-element.17.refs_1_), channel_id=1, source_target_pairs={{0,8},{8,16},{16,24},{24,28},{28,20},{20,12},{12,4},{4,0},{1,9},{9... | collective-permute-start | bytes 983048 | tf_op jit(solution)/shard_map/ppermute | solution.py:394
  63.9 9.9 %collective-permute-start.5 = (f32[160,512]{1,0:T(8,128)S(1)}, f32[160,512]{1,0:T(8,128)S(1)}, u32[]{:S(2)}, u32[]{:S(2)}) collective-permute-start(f32[160,512]{1,0:T(8,128)S(1)} %get-tuple-element.16.refs_0_), channel_id=1, source_target_pairs={{8,0},{16,8},{24,16},{28,24},{20,28},{12,20},{4,12},{0,4},{9,1},{1... | collective-permute-start | bytes 983048 | tf_op jit(solution)/shard_map/ppermute | solution.py:394
  64.2 13.1 %collective-permute-start.8 = (f32[160,512]{1,0:T(8,128)S(1)}, f32[160,512]{1,0:T(8,128)S(1)}, u32[]{:S(2)}, u32[]{:S(2)}) collective-permute-start(f32[160,512]{1,0:T(8,128)S(1)} %collective-permute-done.4.refs_2_.refs_5_), channel_id=1, source_target_pairs={{0,8},{8,16},{16,24},{24,28},{28,20},{20,12},{12,4},{4,0},{1,9},{9... | collective-permute-start | bytes 983048 | tf_op jit(solution)/shard_map/ppermute | solution.py:394
  67.6 9.7 %collective-permute-start.26 = (f32[160,512]{1,0:T(8,128)}, f32[160,512]{1,0:T(8,128)S(1)}, u32[]{:S(2)}, u32[]{:S(2)}) collective-permute-start(f32[160,512]{1,0:T(8,128)} %collective-permute-done.25.refs_14_.refs_20_), channel_id=1, source_target_pairs={{8,0},{16,8},{24,16},{28,24},{20,28},{12,20},{4,12},{0,4},{9,1},{1... | collective-permute-start | bytes 983048 | tf_op jit(solution)/shard_map/ppermute | solution.py:394
  87.3 30.4 %collective-permute-start.30 = (f32[512,512]{1,0:T(8,128)}, f32[512,512]{1,0:T(8,128)}, u32[]{:S(2)}, u32[]{:S(2)}) collective-permute-start(f32[512,512]{1,0:T(8,128)} %get-tuple-element.22), channel_id=1, source_target_pairs={{0,2},{4,6},{8,10},{12,14},{16,18},{20,22},{24,26},{28,30}} | collective-permute-start | bytes 3145736 | tf_op jit(solution)/shard_map/ppermute | solution.py:405
  89.6 37.5 %collective-permute-start.28 = (f32[512,512]{1,0:T(8,128)}, f32[512,512]{1,0:T(8,128)}, u32[]{:S(2)}, u32[]{:S(2)}) collective-permute-start(f32[512,512]{1,0:T(8,128)} %get-tuple-element.21), channel_id=1, source_target_pairs={{0,2},{4,6},{8,10},{12,14},{16,18},{20,22},{24,26},{28,30}} | collective-permute-start | bytes 3145736 | tf_op jit(solution)/shard_map/ppermute | solution.py:405
  92.9 10.1 %collective-permute-start.9 = (f32[160,512]{1,0:T(8,128)S(1)}, f32[160,512]{1,0:T(8,128)S(1)}, u32[]{:S(2)}, u32[]{:S(2)}) collective-permute-start(f32[160,512]{1,0:T(8,128)S(1)} %get-tuple-element.18.refs_8_), channel_id=1, source_target_pairs={{0,8},{8,16},{16,24},{24,28},{28,20},{20,12},{12,4},{4,0},{1,9},{9... | collective-permute-start | bytes 983048 | tf_op jit(solution)/shard_map/ppermute | solution.py:394
  95.4 11.2 %collective-permute-start.31 = (f32[160,512]{1,0:T(8,128)}, f32[160,512]{1,0:T(8,128)}, u32[]{:S(2)}, u32[]{:S(2)}) collective-permute-start(f32[160,512]{1,0:T(8,128)} %copy-done.4), channel_id=1, source_target_pairs={{0,8},{8,16},{16,24},{24,28},{28,20},{20,12},{12,4},{4,0},{1,9},{9... | collective-permute-start | bytes 983048 | tf_op jit(solution)/shard_map/ppermute | solution.py:394
  129.9 15.2 %collective-permute-start.12 = (f32[160,512]{1,0:T(8,128)}, f32[160,512]{1,0:T(8,128)S(1)}, u32[]{:S(2)}, u32[]{:S(2)}) collective-permute-start(f32[160,512]{1,0:T(8,128)} %collective-permute-done.11.refs_1_.refs_13_), channel_id=1, source_target_pairs={{0,8},{8,16},{16,24},{24,28},{28,20},{20,12},{12,4},{4,0},{1,9},{9... | collective-permute-start | bytes 983048 | tf_op jit(solution)/shard_map/ppermute | solution.py:394
  131.9 13.2 %collective-permute-start.16 = (f32[160,512]{1,0:T(8,128)S(1)}, f32[160,512]{1,0:T(8,128)S(1)}, u32[]{:S(2)}, u32[]{:S(2)}) collective-permute-start(f32[160,512]{1,0:T(8,128)S(1)} %collective-permute-done.15.refs_4_.refs_2_), channel_id=1, source_target_pairs={{8,0},{16,8},{24,16},{28,24},{20,28},{12,20},{4,12},{0,4},{9,1},{1... | collective-permute-start | bytes 983048 | tf_op jit(solution)/shard_map/ppermute | solution.py:394
  (38 other events, 800.0 us)

commit v9 on v8

--- a/solution.py
+++ b/solution.py
@@ -459,7 +459,7 @@
             ]
             top, top_spots = held, jnp.zeros_like(me)
             groups = [(held, top_spots)]
-            after, near = [], [[], []]
+            after, sends, near = [], [], [[], []]
         else:
             movers = len(partners)
             left = factor[:, :width]
@@ -492,7 +492,7 @@
             free = gate(own[1], [steps[-2][0][0]])
             full = gate(free, [steps[-1][0][0]])
             rest, steps = ring_pass([[full[0], free[0]], [free[1], full[1]]], ring)
-            after = [steps[0][0][1], steps[0][1][0]]
+            after, sends = [steps[0][0][1], steps[0][1][0]], [steps[0][0][0], steps[0][1][1]]
             near = [steps[i][0] + steps[i][1] for i in (0, -2)]
             top_spots, cut = spots[0], 2 * half - 2
             groups = [
@@ -503,6 +503,8 @@
                 ([rest[k][cut:] for k in range(2)], spots[1][cut:]),
             ]
         first, second = solve_panels(top_spots, place, top, right_side, after, width, block)
+        if sends:
+            first, second = gate([first, second], sends)
         solved = [
             spread_near(spread_far(first, places, place), places, near[0]),
             spread_near(spread_far(second, places, place), places, near[1]),

time: 151 us -> 154 us (1.020)
  waiting for transfers between devices: 41.7 us -> 55.9 us
  starting transfers between devices: 68.8 us -> 55.8 us
    ppermute x28, waiting for transfers between devices: 36.1 us -> 54.4 us  [ring_pass(): going[k][way] = lax.ppermute(going[k][way], 'src', pairs)]
    ppermute x28, starting transfers between devices: 52.6 us -> 39.5 us  [ring_pass(): going[k][way] = lax.ppermute(going[k][way], 'src', pairs)]
    ppermute x2, waiting for transfers between devices: 5.36 us -> 1.18 us  [local(): got = [lax.ppermute(sent, axes, swap) for sent in (sent_first, sent_second)]]
    unnamed x56 -> x60, local copies, waits for them, and re-layouts: 3.67 us -> 4.53 us
  transfers between devices with their start and end apart: 34 -> 34, of which waited for: 23 -> 19; matrix products, arithmetic and copies ran while one was open for 4% -> 4% of each run, Pallas kernels for 10% -> 16%
where the time goes in v9:
time: 154 us; the launch traced here: 153 us
  waiting for transfers between devices  55.9 us (36%)
  starting transfers between devices  55.8 us (36%)
  Pallas kernels  28.8 us (19%)
  other arithmetic  7.51 us (5%)
  local copies, waits for them, and re-layouts  4.6 us (3%)
    ppermute x28, waiting for transfers between devices, ring_pass(): going[k][way] = lax.ppermute(going[k][way], 'src', pairs)  54.4 us
    ppermute x28, starting transfers between devices, ring_pass(): going[k][way] = lax.ppermute(going[k][way], 'src', pairs)  39.5 us
    pallas_call x2, Pallas kernels, update(): pl.pallas_call(functools.partial(update_kernel, pieces, rows, width, grou...  15.7 us
    pallas_call x1, Pallas kernels, solve_panels(): pl.pallas_call(functools.partial(solve_kernel, pieces, rows, width, chunk...  9.07 us
    ppermute x2, starting transfers between devices, local(): got = [lax.ppermute(sent, axes, swap) for sent in (sent_first, sent_second)]  8.88 us
    select_n x2, other arithmetic, spread_far(): block = jnp.where(place[0] == r, found[r], block)  4.84 us
    ppermute x2, starting transfers between devices, spread_far(): found[r + stride] = lax.ppermute(found[r], 'row', [(r, r + stride)])  4.73 us
    unnamed x60, local copies, waits for them, and re-layouts  4.53 us
  transfers between devices with their start and end apart: 34, of which 19 were waited for; matrix products, arithmetic and copies ran while one was open for 4% of the time, Pallas kernels for 16%

profile of v9, /device:TPU:0, one launch (start us, length us, event | category | flops | bytes accessed | tf_op | source)
XLA Modules:
  0.0 153.1 jit_solution(2455447610730406922)
XLA Ops:
  1.2 7.0 %collective-permute-start = (f32[160,512]{1,0:T(8,128)S(1)}, f32[160,512]{1,0:T(8,128)S(1)}, u32[]{:S(2)}, u32[]{:S(2)}) collective-permute-start(f32[160,512]{1,0:T(8,128)S(1)} %slice_select_fusion.1), channel_id=1, source_target_pairs={{0,24},{24,0},{4,28},{28,4},{8,16},{16,8}} | collective-permute-start | bytes 983048 | tf_op jit(solution)/shard_map/ppermute | solution.py:471
  8.1 4.0 %shard_map.55 = (f32[160,512]{1,0:T(8,128)S(1)}, f32[160,512]{1,0:T(8,128)S(1)}, f32[160,512]{1,0:T(8,128)S(1)}) custom-call(s32[1]{0:T(128)} %bitcast.1.me, s32[1]{0:T(128)} %bitcast.place, f32[320,1024]{1,0:T(8,128)} %source.1), custom_call_target="tpu_custom_call" | custom-call | flops 1000 | bytes 1000 | tf_op jit(solution)/shard_map/pallas_call | solution.py:114
  16.4 6.6 %collective-permute-start.2 = (f32[160,512]{1,0:T(8,128)S(1)}, f32[160,512]{1,0:T(8,128)S(1)}, u32[]{:S(2)}, u32[]{:S(2)}) collective-permute-start(f32[160,512]{1,0:T(8,128)S(1)} %get-tuple-element.29.refs_0_), channel_id=1, source_target_pairs={{0,8},{8,16},{16,24},{24,28},{28,20},{20,12},{12,4},{4,0},{1,9},{9... | collective-permute-start | bytes 983048 | tf_op jit(solution)/shard_map/ppermute | solution.py:394
  23.1 3.5 %collective-permute-start.21 = (f32[160,512]{1,0:T(8,128)S(1)}, f32[160,512]{1,0:T(8,128)S(1)}, u32[]{:S(2)}, u32[]{:S(2)}) collective-permute-start(f32[160,512]{1,0:T(8,128)S(1)} %get-tuple-element.31.refs_8_.refs_14_), channel_id=1, source_target_pairs={{8,0},{16,8},{24,16},{28,24},{20,28},{12,20},{4,12},{0,4},{9,1},{1... | collective-permute-start | bytes 983048 | tf_op jit(solution)/shard_map/ppermute | solution.py:394
  26.5 4.5 %collective-permute-done.2.refs_1_ = f32[160,512]{1,0:T(8,128)S(1)} collective-permute-done((f32[160,512]{1,0:T(8,128)S(1)}, f32[160,512]{1,0:T(8,128)S(1)}, u32[]{:S(2)}, u32[]{:S(2)}) %collective-permute-start.2) | collective-permute-done | bytes 327712 | tf_op jit(solution)/shard_map/ppermute | solution.py:394
  31.1 2.5 %collective-permute-start.3 = (f32[160,512]{1,0:T(8,128)S(1)}, f32[160,512]{1,0:T(8,128)S(1)}, u32[]{:S(2)}, u32[]{:S(2)}) collective-permute-start(f32[160,512]{1,0:T(8,128)S(1)} %collective-permute-done.2.refs_1_), channel_id=1, source_target_pairs={{0,8},{8,16},{16,24},{24,28},{28,20},{20,12},{12,4},{4,0},{1,9},{9... | collective-permute-start | bytes 983048 | tf_op jit(solution)/shard_map/ppermute | solution.py:394
  33.5 2.5 %collective-permute-start.20 = (f32[160,512]{1,0:T(8,128)S(1)}, f32[160,512]{1,0:T(8,128)S(1)}, u32[]{:S(2)}, u32[]{:S(2)}) collective-permute-start(f32[160,512]{1,0:T(8,128)S(1)} %get-tuple-element.31.refs_8_.refs_14_), channel_id=1, source_target_pairs={{0,8},{8,16},{16,24},{24,28},{28,20},{20,12},{12,4},{4,0},{1,9},{9... | collective-permute-start | bytes 983048 | tf_op jit(solution)/shard_map/ppermute | solution.py:394
  37.2 4.6 %collective-permute-done.3.refs_3_ = f32[160,512]{1,0:T(8,128)S(1)} collective-permute-done((f32[160,512]{1,0:T(8,128)S(1)}, f32[160,512]{1,0:T(8,128)S(1)}, u32[]{:S(2)}, u32[]{:S(2)}) %collective-permute-start.3) | collective-permute-done | bytes 327712 | tf_op jit(solution)/shard_map/ppermute | solution.py:394
  41.7 2.5 %collective-permute-start.4 = (f32[160,512]{1,0:T(8,128)S(1)}, f32[160,512]{1,0:T(8,128)S(1)}, u32[]{:S(2)}, u32[]{:S(2)}) collective-permute-start(f32[160,512]{1,0:T(8,128)S(1)} %collective-permute-done.3.refs_3_), channel_id=1, source_target_pairs={{0,8},{8,16},{16,24},{24,28},{28,20},{20,12},{12,4},{4,0},{1,9},{9... | collective-permute-start | bytes 983048 | tf_op jit(solution)/shard_map/ppermute | solution.py:394
  44.2 4.5 %collective-permute-done.20.refs_9_.refs_15_ = f32[160,512]{1,0:T(8,128)S(1)} collective-permute-done((f32[160,512]{1,0:T(8,128)S(1)}, f32[160,512]{1,0:T(8,128)S(1)}, u32[]{:S(2)}, u32[]{:S(2)}) %collective-permute-start.20) | collective-permute-done | bytes 327712 | tf_op jit(solution)/shard_map/ppermute | solution.py:394
  48.7 2.5 %collective-permute-start.22 = (f32[160,512]{1,0:T(8,128)S(1)}, f32[160,512]{1,0:T(8,128)}, u32[]{:S(2)}, u32[]{:S(2)}) collective-permute-start(f32[160,512]{1,0:T(8,128)S(1)} %collective-permute-done.20.refs_9_.refs_15_), channel_id=1, source_target_pairs={{0,8},{8,16},{16,24},{24,28},{28,20},{20,12},{12,4},{4,0},{1,9},{9... | collective-permute-start | bytes 983048 | tf_op jit(solution)/shard_map/ppermute | solution.py:394
  55.8 2.5 %collective-permute-start.27 = (f32[160,512]{1,0:T(8,128)S(1)}, f32[160,512]{1,0:T(8,128)S(1)}, u32[]{:S(2)}, u32[]{:S(2)}) collective-permute-start(f32[160,512]{1,0:T(8,128)S(1)} %get-tuple-element.19.refs_1_), channel_id=1, source_target_pairs={{0,8},{8,16},{16,24},{24,28},{28,20},{20,12},{12,4},{4,0},{1,9},{9... | collective-permute-start | bytes 983048 | tf_op jit(solution)/shard_map/ppermute | solution.py:394
  58.3 4.5 %collective-permute-done.22.refs_11_.refs_17_ = f32[160,512]{1,0:T(8,128)} collective-permute-done((f32[160,512]{1,0:T(8,128)S(1)}, f32[160,512]{1,0:T(8,128)}, u32[]{:S(2)}, u32[]{:S(2)}) %collective-permute-start.22) | collective-permute-done | bytes 327712 | tf_op jit(solution)/shard_map/ppermute | solution.py:394
  62.8 2.6 %collective-permute-start.24 = (f32[160,512]{1,0:T(8,128)}, f32[160,512]{1,0:T(8,128)S(1)}, u32[]{:S(2)}, u32[]{:S(2)}) collective-permute-start(f32[160,512]{1,0:T(8,128)} %collective-permute-done.22.refs_11_.refs_17_), channel_id=1, source_target_pairs={{0,8},{8,16},{16,24},{24,28},{28,20},{20,12},{12,4},{4,0},{1,9},{9... | collective-permute-start | bytes 983048 | tf_op jit(solution)/shard_map/ppermute | solution.py:394
  65.4 4.0 %collective-permute-done.25.refs_14_.refs_20_ = f32[160,512]{1,0:T(8,128)} collective-permute-done((f32[160,512]{1,0:T(8,128)}, f32[160,512]{1,0:T(8,128)}, u32[]{:S(2)}, u32[]{:S(2)}) %collective-permute-start.25) | collective-permute-done | bytes 327712 | tf_op jit(solution)/shard_map/ppermute | solution.py:394
  71.7 10.8 %collective-permute-done.5.refs_17_.refs_2_.refs_10_ = f32[160,512]{1,0:T(8,128)S(1)} collective-permute-done((f32[160,512]{1,0:T(8,128)S(1)}, f32[160,512]{1,0:T(8,128)S(1)}, u32[]{:S(2)}, u32[]{:S(2)}) %collective-permute-start.5) | collective-permute-done | bytes 327712 | tf_op jit(solution)/shard_map/ppermute | solution.py:394
  88.7 9.1 %shard_map.58 = (f32[512,512]{1,0:T(8,128)}, f32[512,512]{1,0:T(8,128)}) custom-call(s32[8]{0:T(128)S(1)} %get-tuple-element.33.ids, s32[1]{0:T(128)} %bitcast.place, f32[160,512]{1,0:T(8,128)S(1)} %get-tuple-element.29.refs_0_, f32[160,512]{1,0:T(8,128)S(1)} %collective-permute-done.2.refs_1_, f32[160,512]{1,0:T(8,128)S(1)} %copy-done.17, ...), custom_call_target="tpu_custom_call" | custom-call | flops 9663676416 | bytes 6291456 | tf_op jit(solution)/shard_map/pallas_call | solution.py:213
  97.9 2.4 %collective-permute-start.30 = (f32[512,512]{1,0:T(8,128)}, f32[512,512]{1,0:T(8,128)}, u32[]{:S(2)}, u32[]{:S(2)}) collective-permute-start(f32[512,512]{1,0:T(8,128)} %get-tuple-element.26), channel_id=1, source_target_pairs={{0,2},{4,6},{8,10},{12,14},{16,18},{20,22},{24,26},{28,30}} | collective-permute-start | bytes 3145736 | tf_op jit(solution)/shard_map/ppermute | solution.py:405
  106.3 3.7 %collective-permute-done.31.refs_25_ = f32[160,512]{1,0:T(8,128)} collective-permute-done((f32[160,512]{1,0:T(8,128)}, f32[160,512]{1,0:T(8,128)}, u32[]{:S(2)}, u32[]{:S(2)}) %collective-permute-start.31) | collective-permute-done | bytes 327712 | tf_op jit(solution)/shard_map/ppermute | solution.py:394
  113.7 3.5 %collective-permute-done.14.refs_26_ = f32[160,512]{1,0:T(8,128)} collective-permute-done((f32[160,512]{1,0:T(8,128)S(1)}, f32[160,512]{1,0:T(8,128)}, u32[]{:S(2)}, u32[]{:S(2)}) %collective-permute-start.14) | collective-permute-done | bytes 327712 | tf_op jit(solution)/shard_map/ppermute | solution.py:394
  119.2 2.4 %broadcast_select_fusion.refs_0_ = f32[512,512]{1,0:T(8,128)} fusion(f32[512,512]{1,0:T(8,128)} %collective-permute-done.30, f32[512,512]{1,0:T(8,128)} %get-tuple-element.26, pred[]{:T(512)S(6)} %eq.54), kind=kLoop, calls=%fused_computation | loop fusion | flops 262144 | bytes 3145729 | tf_op jit(solution)/shard_map/jit(_where)/select_n | solution.py:409
  129.2 2.4 %broadcast_select_fusion.1.refs_0_ = f32[512,512]{1,0:T(8,128)} fusion(f32[512,512]{1,0:T(8,128)} %collective-permute-done.28, f32[512,512]{1,0:T(8,128)} %get-tuple-element.25, pred[]{:T(512)S(6)} %eq.54), kind=kLoop, calls=%fused_computation.1 | loop fusion | flops 262144 | bytes 3145729 | tf_op jit(solution)/shard_map/jit(_where)/select_n | solution.py:409
  137.2 11.2 %shard_map.62.refs_9_ = f32[2560,512]{1,0:T(8,128)} custom-call(s32[14]{0:T(128)S(1)} %pad_add_fusion.ids, s32[1]{0:T(128)} %bitcast.place, f32[160,512]{1,0:T(8,128)S(1)} %get-tuple-element.29.refs_0_, f32[160,512]{1,0:T(8,128)S(1)} %copy-done.12, f32[160,512]{1,0:T(8,128)S(1)} %copy-done.18, f32[160,512]{1,0:T(8,128)S(1)} %copy-done.15, ...), custom_call_target="tpu_custom_call" | custom-call | flops 7046430720 | bytes 18350080 | tf_op jit(solution)/shard_map/pallas_call | solution.py:339
  148.4 4.6 %shard_map.63 = f32[2560,512]{1,0:T(8,128)} custom-call(s32[2]{0:T(128)S(1)} %slice.17.ids, s32[1]{0:T(128)} %bitcast.place, f32[160,512]{1,0:T(8,128)S(1)} %collective-permute-done.7.refs_2_.refs_0_, f32[160,512]{1,0:T(8,128)S(1)} %collective-permute-done.12.refs_1_, ...), custom_call_target="tpu_custom_call", output_to_operand_aliasing={{}: (11, {})} | custom-call | flops 1006632960 | bytes 2621440 | tf_op jit(solution)/shard_map/pallas_call | solution.py:339
  (123 shorter events, 44.4 us)
Async XLA Ops:
  1.2 14.1 %collective-permute-start = (f32[160,512]{1,0:T(8,128)S(1)}, f32[160,512]{1,0:T(8,128)S(1)}, u32[]{:S(2)}, u32[]{:S(2)}) collective-permute-start(f32[160,512]{1,0:T(8,128)S(1)} %slice_select_fusion.1), channel_id=1, source_target_pairs={{0,24},{24,0},{4,28},{28,4},{8,16},{16,8}} | collective-permute-start | bytes 983048 | tf_op jit(solution)/shard_map/ppermute | solution.py:471
  12.1 10.9 %collective-permute-start.1 = (f32[160,512]{1,0:T(8,128)S(1)}, f32[160,512]{1,0:T(8,128)S(1)}, u32[]{:S(2)}, u32[]{:S(2)}) collective-permute-start(f32[160,512]{1,0:T(8,128)S(1)} %get-tuple-element.16), channel_id=1, source_target_pairs={{0,24},{24,0},{4,28},{28,4},{8,16},{16,8}} | collective-permute-start | bytes 983048 | tf_op jit(solution)/shard_map/ppermute | solution.py:471
  16.4 14.7 %collective-permute-start.2 = (f32[160,512]{1,0:T(8,128)S(1)}, f32[160,512]{1,0:T(8,128)S(1)}, u32[]{:S(2)}, u32[]{:S(2)}) collective-permute-start(f32[160,512]{1,0:T(8,128)S(1)} %get-tuple-element.29.refs_0_), channel_id=1, source_target_pairs={{0,8},{8,16},{16,24},{24,28},{28,20},{20,12},{12,4},{4,0},{1,9},{9... | collective-permute-start | bytes 983048 | tf_op jit(solution)/shard_map/ppermute | solution.py:394
  23.1 13.0 %collective-permute-start.21 = (f32[160,512]{1,0:T(8,128)S(1)}, f32[160,512]{1,0:T(8,128)S(1)}, u32[]{:S(2)}, u32[]{:S(2)}) collective-permute-start(f32[160,512]{1,0:T(8,128)S(1)} %get-tuple-element.31.refs_8_.refs_14_), channel_id=1, source_target_pairs={{8,0},{16,8},{24,16},{28,24},{20,28},{12,20},{4,12},{0,4},{9,1},{1... | collective-permute-start | bytes 983048 | tf_op jit(solution)/shard_map/ppermute | solution.py:394
  31.1 10.7 %collective-permute-start.3 = (f32[160,512]{1,0:T(8,128)S(1)}, f32[160,512]{1,0:T(8,128)S(1)}, u32[]{:S(2)}, u32[]{:S(2)}) collective-permute-start(f32[160,512]{1,0:T(8,128)S(1)} %collective-permute-done.2.refs_1_), channel_id=1, source_target_pairs={{0,8},{8,16},{16,24},{24,28},{28,20},{20,12},{12,4},{4,0},{1,9},{9... | collective-permute-start | bytes 983048 | tf_op jit(solution)/shard_map/ppermute | solution.py:394
  33.5 15.2 %collective-permute-start.20 = (f32[160,512]{1,0:T(8,128)S(1)}, f32[160,512]{1,0:T(8,128)S(1)}, u32[]{:S(2)}, u32[]{:S(2)}) collective-permute-start(f32[160,512]{1,0:T(8,128)S(1)} %get-tuple-element.31.refs_8_.refs_14_), channel_id=1, source_target_pairs={{0,8},{8,16},{16,24},{24,28},{28,20},{20,12},{12,4},{4,0},{1,9},{9... | collective-permute-start | bytes 983048 | tf_op jit(solution)/shard_map/ppermute | solution.py:394
  36.0 15.2 %collective-permute-start.17 = (f32[160,512]{1,0:T(8,128)S(1)}, f32[160,512]{1,0:T(8,128)S(1)}, u32[]{:S(2)}, u32[]{:S(2)}) collective-permute-start(f32[160,512]{1,0:T(8,128)S(1)} %get-tuple-element.29.refs_0_), channel_id=1, source_target_pairs={{8,0},{16,8},{24,16},{28,24},{20,28},{12,20},{4,12},{0,4},{9,1},{1... | collective-permute-start | bytes 983048 | tf_op jit(solution)/shard_map/ppermute | solution.py:394
  36.0 17.1 %collective-permute-start.23 = (f32[160,512]{1,0:T(8,128)S(1)}, f32[160,512]{1,0:T(8,128)}, u32[]{:S(2)}, u32[]{:S(2)}) collective-permute-start(f32[160,512]{1,0:T(8,128)S(1)} %collective-permute-done.21.refs_10_.refs_16_), channel_id=1, source_target_pairs={{8,0},{16,8},{24,16},{28,24},{20,28},{12,20},{4,12},{0,4},{9,1},{1... | collective-permute-start | bytes 983048 | tf_op jit(solution)/shard_map/ppermute | solution.py:394
  41.7 14.0 %collective-permute-start.4 = (f32[160,512]{1,0:T(8,128)S(1)}, f32[160,512]{1,0:T(8,128)S(1)}, u32[]{:S(2)}, u32[]{:S(2)}) collective-permute-start(f32[160,512]{1,0:T(8,128)S(1)} %collective-permute-done.3.refs_3_), channel_id=1, source_target_pairs={{0,8},{8,16},{16,24},{24,28},{28,20},{20,12},{12,4},{4,0},{1,9},{9... | collective-permute-start | bytes 983048 | tf_op jit(solution)/shard_map/ppermute | solution.py:394
  48.7 14.1 %collective-permute-start.22 = (f32[160,512]{1,0:T(8,128)S(1)}, f32[160,512]{1,0:T(8,128)}, u32[]{:S(2)}, u32[]{:S(2)}) collective-permute-start(f32[160,512]{1,0:T(8,128)S(1)} %collective-permute-done.20.refs_9_.refs_15_), channel_id=1, source_target_pairs={{0,8},{8,16},{16,24},{24,28},{28,20},{20,12},{12,4},{4,0},{1,9},{9... | collective-permute-start | bytes 983048 | tf_op jit(solution)/shard_map/ppermute | solution.py:394
  51.2 14.1 %collective-permute-start.18 = (f32[160,512]{1,0:T(8,128)S(1)}, f32[160,512]{1,0:T(8,128)}, u32[]{:S(2)}, u32[]{:S(2)}) collective-permute-start(f32[160,512]{1,0:T(8,128)S(1)} %collective-permute-done.17.refs_2_), channel_id=1, source_target_pairs={{8,0},{16,8},{24,16},{28,24},{20,28},{12,20},{4,12},{0,4},{9,1},{1... | collective-permute-start | bytes 983048 | tf_op jit(solution)/shard_map/ppermute | solution.py:394
  53.1 16.2 %collective-permute-start.25 = (f32[160,512]{1,0:T(8,128)}, f32[160,512]{1,0:T(8,128)}, u32[]{:S(2)}, u32[]{:S(2)}) collective-permute-start(f32[160,512]{1,0:T(8,128)} %collective-permute-done.23.refs_12_.refs_18_), channel_id=1, source_target_pairs={{8,0},{16,8},{24,16},{28,24},{20,28},{12,20},{4,12},{0,4},{9,1},{1... | collective-permute-start | bytes 983048 | tf_op jit(solution)/shard_map/ppermute | solution.py:394
  55.8 15.7 %collective-permute-start.27 = (f32[160,512]{1,0:T(8,128)S(1)}, f32[160,512]{1,0:T(8,128)S(1)}, u32[]{:S(2)}, u32[]{:S(2)}) collective-permute-start(f32[160,512]{1,0:T(8,128)S(1)} %get-tuple-element.19.refs_1_), channel_id=1, source_target_pairs={{0,8},{8,16},{16,24},{24,28},{28,20},{20,12},{12,4},{4,0},{1,9},{9... | collective-permute-start | bytes 983048 | tf_op jit(solution)/shard_map/ppermute | solution.py:394
  62.8 21.8 %collective-permute-start.24 = (f32[160,512]{1,0:T(8,128)}, f32[160,512]{1,0:T(8,128)S(1)}, u32[]{:S(2)}, u32[]{:S(2)}) collective-permute-start(f32[160,512]{1,0:T(8,128)} %collective-permute-done.22.refs_11_.refs_17_), channel_id=1, source_target_pairs={{0,8},{8,16},{16,24},{24,28},{28,20},{20,12},{12,4},{4,0},{1,9},{9... | collective-permute-start | bytes 983048 | tf_op jit(solution)/shard_map/ppermute | solution.py:394
  65.4 19.2 %collective-permute-start.19 = (f32[160,512]{1,0:T(8,128)}, f32[160,512]{1,0:T(8,128)S(1)}, u32[]{:S(2)}, u32[]{:S(2)}) collective-permute-start(f32[160,512]{1,0:T(8,128)} %collective-permute-done.18.refs_4_), channel_id=1, source_target_pairs={{8,0},{16,8},{24,16},{28,24},{20,28},{12,20},{4,12},{0,4},{9,1},{1... | collective-permute-start | bytes 983048 | tf_op jit(solution)/shard_map/ppermute | solution.py:394
  65.4 17.1 %collective-permute-start.5 = (f32[160,512]{1,0:T(8,128)S(1)}, f32[160,512]{1,0:T(8,128)S(1)}, u32[]{:S(2)}, u32[]{:S(2)}) collective-permute-start(f32[160,512]{1,0:T(8,128)S(1)} %get-tuple-element.18.refs_0_), channel_id=1, source_target_pairs={{8,0},{16,8},{24,16},{28,24},{20,28},{12,20},{4,12},{0,4},{9,1},{1... | collective-permute-start | bytes 983048 | tf_op jit(solution)/shard_map/ppermute | solution.py:394
  69.4 13.1 %collective-permute-start.8 = (f32[160,512]{1,0:T(8,128)S(1)}, f32[160,512]{1,0:T(8,128)S(1)}, u32[]{:S(2)}, u32[]{:S(2)}) collective-permute-start(f32[160,512]{1,0:T(8,128)S(1)} %collective-permute-done.4.refs_2_.refs_5_), channel_id=1, source_target_pairs={{0,8},{8,16},{16,24},{24,28},{28,20},{20,12},{12,4},{4,0},{1,9},{9... | collective-permute-start | bytes 983048 | tf_op jit(solution)/shard_map/ppermute | solution.py:394
  71.4 14.5 %collective-permute-start.26 = (f32[160,512]{1,0:T(8,128)}, f32[160,512]{1,0:T(8,128)S(1)}, u32[]{:S(2)}, u32[]{:S(2)}) collective-permute-start(f32[160,512]{1,0:T(8,128)} %collective-permute-done.25.refs_14_.refs_20_), channel_id=1, source_target_pairs={{8,0},{16,8},{24,16},{28,24},{20,28},{12,20},{4,12},{0,4},{9,1},{1... | collective-permute-start | bytes 983048 | tf_op jit(solution)/shard_map/ppermute | solution.py:394
  82.5 15.3 %collective-permute-start.13 = (f32[160,512]{1,0:T(8,128)S(1)}, f32[160,512]{1,0:T(8,128)S(1)}, u32[]{:S(2)}, u32[]{:S(2)}) collective-permute-start(f32[160,512]{1,0:T(8,128)S(1)} %get-tuple-element.21.refs_22_), channel_id=1, source_target_pairs={{8,0},{16,8},{24,16},{28,24},{20,28},{12,20},{4,12},{0,4},{9,1},{1... | collective-permute-start | bytes 983048 | tf_op jit(solution)/shard_map/ppermute | solution.py:394
  82.6 15.2 %collective-permute-start.9 = (f32[160,512]{1,0:T(8,128)S(1)}, f32[160,512]{1,0:T(8,128)S(1)}, u32[]{:S(2)}, u32[]{:S(2)}) collective-permute-start(f32[160,512]{1,0:T(8,128)S(1)} %get-tuple-element.20.refs_8_), channel_id=1, source_target_pairs={{0,8},{8,16},{16,24},{24,28},{28,20},{20,12},{12,4},{4,0},{1,9},{9... | collective-permute-start | bytes 983048 | tf_op jit(solution)/shard_map/ppermute | solution.py:394
  97.9 21.0 %collective-permute-start.30 = (f32[512,512]{1,0:T(8,128)}, f32[512,512]{1,0:T(8,128)}, u32[]{:S(2)}, u32[]{:S(2)}) collective-permute-start(f32[512,512]{1,0:T(8,128)} %get-tuple-element.26), channel_id=1, source_target_pairs={{0,2},{4,6},{8,10},{12,14},{16,18},{20,22},{24,26},{28,30}} | collective-permute-start | bytes 3145736 | tf_op jit(solution)/shard_map/ppermute | solution.py:405
  100.3 28.9 %collective-permute-start.28 = (f32[512,512]{1,0:T(8,128)}, f32[512,512]{1,0:T(8,128)}, u32[]{:S(2)}, u32[]{:S(2)}) collective-permute-start(f32[512,512]{1,0:T(8,128)} %get-tuple-element.25), channel_id=1, source_target_pairs={{0,2},{4,6},{8,10},{12,14},{16,18},{20,22},{24,26},{28,30}} | collective-permute-start | bytes 3145736 | tf_op jit(solution)/shard_map/ppermute | solution.py:405
  133.1 15.2 %collective-permute-start.12 = (f32[160,512]{1,0:T(8,128)S(1)}, f32[160,512]{1,0:T(8,128)S(1)}, u32[]{:S(2)}, u32[]{:S(2)}) collective-permute-start(f32[160,512]{1,0:T(8,128)S(1)} %collective-permute-done.11.refs_1_.refs_13_), channel_id=1, source_target_pairs={{0,8},{8,16},{16,24},{24,28},{28,20},{20,12},{12,4},{4,0},{1,9},{9... | collective-permute-start | bytes 983048 | tf_op jit(solution)/shard_map/ppermute | solution.py:394
  134.8 13.6 %collective-permute-start.16 = (f32[160,512]{1,0:T(8,128)S(1)}, f32[160,512]{1,0:T(8,128)S(1)}, u32[]{:S(2)}, u32[]{:S(2)}) collective-permute-start(f32[160,512]{1,0:T(8,128)S(1)} %collective-permute-done.15.refs_4_.refs_2_), channel_id=1, source_target_pairs={{8,0},{16,8},{24,16},{28,24},{20,28},{12,20},{4,12},{0,4},{9,1},{1... | collective-permute-start | bytes 983048 | tf_op jit(solution)/shard_map/ppermute | solution.py:394
  (40 other events, 790.0 us)

commit v10 on v7

--- a/solution.py
+++ b/solution.py
@@ -93,15 +93,14 @@
                 factor[i * block : (i + 1) * block, depth - block :] = inverse
 
     moves = me[0] < movers
-    copies = []
-    for k in range(2):
-        panel = pl.ds(k * width, width)
-        for cut in range(cuts):
-            at = pl.ds(cut * part, part)
-            copies.append((factor.at[at, panel], outs[2 * cut + k], store_sem.at[2 * cut + k]))
-        if cuts > 1:
-            sent = pl.ds(pl.multiple_of(jnp.where(moves, part, 0), 8), part)
-            copies.append((factor.at[sent, panel], outs[4 + k], store_sem.at[4 + k]))
+    panel = pl.ds(width, width)
+    copies = [
+        (factor.at[pl.ds(cut * part, part), panel], outs[cut], store_sem.at[cut])
+        for cut in range(cuts)
+    ]
+    if cuts > 1:
+        sent = pl.ds(pl.multiple_of(jnp.where(moves, part, 0), 8), part)
+        copies.append((factor.at[sent, panel], outs[cuts], store_sem.at[cuts]))
     copies = [pltpu.make_async_copy(*copy) for copy in copies]
     for copy in copies:
         copy.start()
@@ -111,7 +110,7 @@
 
 def prepare(me, place, factor, block, cuts, movers):
     rows, depth = factor.shape
-    count = 2 * cuts + (2 if cuts > 1 else 0)
+    count = cuts + (1 if cuts > 1 else 0)
     return pl.pallas_call(
         functools.partial(prepare_kernel, rows, block, depth, cuts, movers),
         out_shape=[jax.ShapeDtypeStruct((rows // cuts, depth // 2), jnp.float32)] * count,
@@ -414,23 +413,24 @@
     return held, steps
 
 
-def spread_far(block, count, place):
+def spread_far(block, count):
     found = {0: block}
     stride = count // 2
     while stride > 1:
         for r in list(found):
             found[r + stride] = lax.ppermute(found[r], "row", [(r, r + stride)])
         stride //= 2
-    for r in found:
-        if r:
-            block = jnp.where(place[0] == r, found[r], block)
-    return block
-
-
-def spread_near(block, count, tokens):
-    if tokens:
-        (block,) = gate([block], tokens)
-    return [block, lax.ppermute(block, "row", [(r, r + 1) for r in range(0, count - 1, 2)])]
+    return found
+
+
+def spread_near(found, count, tokens):
+    found = dict(found)
+    for r in sorted(found):
+        if r and tokens:
+            (found[r],) = gate([found[r]], tokens)
+        if r + 1 < count:
+            found[r + 1] = lax.ppermute(found[r], "row", [(r, r + 1)])
+    return [found[r] for r in range(count)]
 
 
 def swap_partners(count, tops):
@@ -472,14 +472,17 @@
         if not ringed:
             held = [
                 [lax.all_gather(panel, "src", axis=0, tiled=True)]
-                for panel in prepare(me, place, factor, block, 1, 0)
+                for panel in (factor[:, :width], *prepare(me, place, factor, block, 1, 0))
             ]
             top, top_spots = held, jnp.zeros_like(me)
             groups = [(held, top_spots)]
             after, near = [[], []], [[], []]
         else:
             movers = len(partners)
-            *halves, sent_first, sent_second = prepare(me, place, factor, block, 2, movers)
+            left = factor[:, :width]
+            sent_first = jnp.where(me[0] < movers, left[part:], left[:part])
+            *right, sent_second = prepare(me, place, factor, block, 2, movers)
+            halves = [left[:part], right[0], left[part:], right[1]]
             pairs = [(s, f) for s, f in enumerate(partners)]
             swap = [(number(a, 0), number(b, 0)) for s, f in pairs for a, b in ((s, f), (f, s))]
             got = [lax.ppermute(sent, axes, swap) for sent in (sent_first, sent_second)]
@@ -507,7 +510,7 @@
             full = gate(free, [steps[-1][0][0]])
             rest, steps = ring_pass([[full[0], free[0]], [free[1], full[1]]], ring)
             after = [[steps[0][0][1], steps[0][1][0]], [steps[0][0][0], steps[0][1][1]]]
-            near = [steps[i][0] + steps[i][1] for i in (0, -2)]
+            near = [steps[i][0] + steps[i][1] for i in (1, -2)]
             top_spots, cut = spots[0], 2 * half - 2
             groups = [
                 (
@@ -519,8 +522,8 @@
         first = solve_panel(0, top_spots, place, top, right_side, [], after[0], width, block)
         second = solve_panel(1, top_spots, place, top, right_side, [first], after[1], width, block)
         solved = [
-            spread_near(spread_far(first, places, place), places, near[0]),
-            spread_near(spread_far(second, places, place), places, near[1]),
+            spread_near(spread_far(first, places), places, near[0]),
+            spread_near(spread_far(second, places), places, near[1]),
         ]
         result = None
         for held, spots in groups:

time: 154 us -> 151 us (0.981)
    ppermute x28, waiting for transfers between devices: 46.9 us -> 51.6 us  [ring_pass(): going[k][way] = lax.ppermute(going[k][way], 'src', pairs)]
    ppermute x2, waiting for transfers between devices: 5.76 us -> 1.18 us  [local(): got = [lax.ppermute(sent, axes, swap) for sent in (sent_first, sent_second)]]
    select_n x2 -> x1, other arithmetic: 3.61 us -> 1.16 us  [local(): sent_first = jnp.where(me[0] < movers, left[part:], left[:part])]
    ppermute x2, starting transfers between devices: 4.76 us -> 2.84 us  [spread_far(): found[r + stride] = lax.ppermute(found[r], 'row', [(r, r + stride)])]
    ppermute x2 -> x4, starting transfers between devices: 2.7 us -> 4.13 us  [spread_near(): found[r + 1] = lax.ppermute(found[r], 'row', [(r, r + 1)])]
    unnamed x54 -> x56, local copies, waits for them, and re-layouts: 5.99 us -> 5.49 us
  transfers between devices with their start and end apart: 34 -> 36, of which waited for: 16 -> 20; matrix products, arithmetic and copies ran while one was open for 3% -> 1% of each run, Pallas kernels for 16% -> 19%
where the time goes in v10:
time: 151 us
  starting transfers between devices  56.2 us (37%)
  waiting for transfers between devices  52.8 us (35%)
  Pallas kernels  32.8 us (22%)
  local copies, waits for them, and re-layouts  5.57 us (4%)
  other arithmetic  2.67 us (2%)
    ppermute x28, waiting for transfers between devices, ring_pass(): going[k][way] = lax.ppermute(going[k][way], 'src', pairs)  51.6 us
    ppermute x28, starting transfers between devices, ring_pass(): going[k][way] = lax.ppermute(going[k][way], 'src', pairs)  40.4 us
    pallas_call x2, Pallas kernels, update(): pl.pallas_call(functools.partial(update_kernel, pieces, rows, width, grou...  15.6 us
    pallas_call x2, Pallas kernels, solve_panel(): pl.pallas_call(functools.partial(solve_kernel, pieces, rows, width, chunk...  13.3 us
    ppermute x2, starting transfers between devices, local(): got = [lax.ppermute(sent, axes, swap) for sent in (sent_first, sent_second)]  8.88 us
    unnamed x56, local copies, waits for them, and re-layouts  5.49 us
    ppermute x4, starting transfers between devices, spread_near(): found[r + 1] = lax.ppermute(found[r], 'row', [(r, r + 1)])  4.13 us
    pallas_call x1, Pallas kernels, prepare(): pl.pallas_call(functools.partial(prepare_kernel, rows, block, depth, cuts...  3.96 us
  transfers between devices with their start and end apart: 36, of which 20 were waited for; matrix products, arithmetic and copies ran while one was open for 1% of the time, Pallas kernels for 19%

profile of v10, /device:TPU:0, one launch (start us, length us, event | category | flops | bytes accessed | tf_op | source)
XLA Modules:
  0.0 150.6 jit_solution(4348897970764161268)
XLA Ops:
  1.2 7.0 %collective-permute-start = (f32[160,512]{1,0:T(8,128)S(1)}, f32[160,512]{1,0:T(8,128)S(1)}, u32[]{:S(2)}, u32[]{:S(2)}) collective-permute-start(f32[160,512]{1,0:T(8,128)S(1)} %slice_select_fusion.1), channel_id=1, source_target_pairs={{0,24},{24,0},{4,28},{28,4},{8,16},{16,8}} | collective-permute-start | bytes 983048 | tf_op jit(solution)/shard_map/ppermute | solution.py:488
  8.1 4.0 %shard_map.55 = (f32[160,512]{1,0:T(8,128)S(1)}, f32[160,512]{1,0:T(8,128)S(1)}, f32[160,512]{1,0:T(8,128)S(1)}) custom-call(s32[1]{0:T(128)} %bitcast.1.me, s32[1]{0:T(128)} %bitcast.place, f32[320,1024]{1,0:T(8,128)} %source.1), custom_call_target="tpu_custom_call" | custom-call | flops 1000 | bytes 1000 | tf_op jit(solution)/shard_map/pallas_call | solution.py:114
  16.4 6.6 %collective-permute-start.2 = (f32[160,512]{1,0:T(8,128)S(1)}, f32[160,512]{1,0:T(8,128)S(1)}, u32[]{:S(2)}, u32[]{:S(2)}) collective-permute-start(f32[160,512]{1,0:T(8,128)S(1)} %get-tuple-element.21.refs_0_), channel_id=1, source_target_pairs={{0,8},{8,16},{16,24},{24,28},{28,20},{20,12},{12,4},{4,0},{1,9},{9... | collective-permute-start | bytes 983048 | tf_op jit(solution)/shard_map/ppermute | solution.py:410
  23.1 3.5 %collective-permute-start.21 = (f32[160,512]{1,0:T(8,128)S(1)}, f32[160,512]{1,0:T(8,128)S(1)}, u32[]{:S(2)}, u32[]{:S(2)}) collective-permute-start(f32[160,512]{1,0:T(8,128)S(1)} %get-tuple-element.23.refs_8_.refs_14_), channel_id=1, source_target_pairs={{8,0},{16,8},{24,16},{28,24},{20,28},{12,20},{4,12},{0,4},{9,1},{1... | collective-permute-start | bytes 983048 | tf_op jit(solution)/shard_map/ppermute | solution.py:410
  26.5 4.5 %collective-permute-done.2.refs_1_ = f32[160,512]{1,0:T(8,128)S(1)} collective-permute-done((f32[160,512]{1,0:T(8,128)S(1)}, f32[160,512]{1,0:T(8,128)S(1)}, u32[]{:S(2)}, u32[]{:S(2)}) %collective-permute-start.2) | collective-permute-done | bytes 327712 | tf_op jit(solution)/shard_map/ppermute | solution.py:410
  31.1 2.5 %collective-permute-start.3 = (f32[160,512]{1,0:T(8,128)S(1)}, f32[160,512]{1,0:T(8,128)S(1)}, u32[]{:S(2)}, u32[]{:S(2)}) collective-permute-start(f32[160,512]{1,0:T(8,128)S(1)} %collective-permute-done.2.refs_1_), channel_id=1, source_target_pairs={{0,8},{8,16},{16,24},{24,28},{28,20},{20,12},{12,4},{4,0},{1,9},{9... | collective-permute-start | bytes 983048 | tf_op jit(solution)/shard_map/ppermute | solution.py:410
  33.5 2.5 %collective-permute-start.20 = (f32[160,512]{1,0:T(8,128)S(1)}, f32[160,512]{1,0:T(8,128)}, u32[]{:S(2)}, u32[]{:S(2)}) collective-permute-start(f32[160,512]{1,0:T(8,128)S(1)} %get-tuple-element.23.refs_8_.refs_14_), channel_id=1, source_target_pairs={{0,8},{8,16},{16,24},{24,28},{28,20},{20,12},{12,4},{4,0},{1,9},{9... | collective-permute-start | bytes 983048 | tf_op jit(solution)/shard_map/ppermute | solution.py:410
  37.1 4.6 %collective-permute-done.3.refs_3_ = f32[160,512]{1,0:T(8,128)S(1)} collective-permute-done((f32[160,512]{1,0:T(8,128)S(1)}, f32[160,512]{1,0:T(8,128)S(1)}, u32[]{:S(2)}, u32[]{:S(2)}) %collective-permute-start.3) | collective-permute-done | bytes 327712 | tf_op jit(solution)/shard_map/ppermute | solution.py:410
  41.7 2.5 %collective-permute-start.4 = (f32[160,512]{1,0:T(8,128)S(1)}, f32[160,512]{1,0:T(8,128)S(1)}, u32[]{:S(2)}, u32[]{:S(2)}) collective-permute-start(f32[160,512]{1,0:T(8,128)S(1)} %collective-permute-done.3.refs_3_), channel_id=1, source_target_pairs={{0,8},{8,16},{16,24},{24,28},{28,20},{20,12},{12,4},{4,0},{1,9},{9... | collective-permute-start | bytes 983048 | tf_op jit(solution)/shard_map/ppermute | solution.py:410
  44.2 4.6 %collective-permute-done.20.refs_9_.refs_15_ = f32[160,512]{1,0:T(8,128)} collective-permute-done((f32[160,512]{1,0:T(8,128)S(1)}, f32[160,512]{1,0:T(8,128)}, u32[]{:S(2)}, u32[]{:S(2)}) %collective-permute-start.20) | collective-permute-done | bytes 327712 | tf_op jit(solution)/shard_map/ppermute | solution.py:410
  48.7 2.6 %collective-permute-start.22 = (f32[160,512]{1,0:T(8,128)}, f32[160,512]{1,0:T(8,128)}, u32[]{:S(2)}, u32[]{:S(2)}) collective-permute-start(f32[160,512]{1,0:T(8,128)} %collective-permute-done.20.refs_9_.refs_15_), channel_id=1, source_target_pairs={{0,8},{8,16},{16,24},{24,28},{28,20},{20,12},{12,4},{4,0},{1,9},{9... | collective-permute-start | bytes 983048 | tf_op jit(solution)/shard_map/ppermute | solution.py:410
  55.8 2.5 %collective-permute-start.27 = (f32[160,512]{1,0:T(8,128)S(1)}, f32[160,512]{1,0:T(8,128)}, u32[]{:S(2)}, u32[]{:S(2)}) collective-permute-start(f32[160,512]{1,0:T(8,128)S(1)} %get-tuple-element.15.refs_1_), channel_id=1, source_target_pairs={{0,8},{8,16},{16,24},{24,28},{28,20},{20,12},{12,4},{4,0},{1,9},{9... | collective-permute-start | bytes 983048 | tf_op jit(solution)/shard_map/ppermute | solution.py:410
  58.2 4.6 %collective-permute-done.22.refs_11_.refs_17_ = f32[160,512]{1,0:T(8,128)} collective-permute-done((f32[160,512]{1,0:T(8,128)}, f32[160,512]{1,0:T(8,128)}, u32[]{:S(2)}, u32[]{:S(2)}) %collective-permute-start.22) | collective-permute-done | bytes 327712 | tf_op jit(solution)/shard_map/ppermute | solution.py:410
  62.9 2.5 %collective-permute-start.8 = (f32[160,512]{1,0:T(8,128)S(1)}, f32[160,512]{1,0:T(8,128)S(1)}, u32[]{:S(2)}, u32[]{:S(2)}) collective-permute-start(f32[160,512]{1,0:T(8,128)S(1)} %collective-permute-done.4.refs_2_.refs_5_), channel_id=1, source_target_pairs={{0,8},{8,16},{16,24},{24,28},{28,20},{20,12},{12,4},{4,0},{1,9},{9... | collective-permute-start | bytes 983048 | tf_op jit(solution)/shard_map/ppermute | solution.py:410
  65.4 2.5 %collective-permute-start.24 = (f32[160,512]{1,0:T(8,128)}, f32[160,512]{1,0:T(8,128)S(1)}, u32[]{:S(2)}, u32[]{:S(2)}) collective-permute-start(f32[160,512]{1,0:T(8,128)} %collective-permute-done.22.refs_11_.refs_17_), channel_id=1, source_target_pairs={{0,8},{8,16},{16,24},{24,28},{28,20},{20,12},{12,4},{4,0},{1,9},{9... | collective-permute-start | bytes 983048 | tf_op jit(solution)/shard_map/ppermute | solution.py:410
  70.5 6.0 %collective-permute-done.5.refs_17_.refs_10_ = f32[160,512]{1,0:T(8,128)S(1)} collective-permute-done((f32[160,512]{1,0:T(8,128)S(1)}, f32[160,512]{1,0:T(8,128)S(1)}, u32[]{:S(2)}, u32[]{:S(2)}) %collective-permute-start.5) | collective-permute-done | bytes 327712 | tf_op jit(solution)/shard_map/ppermute | solution.py:410
  81.7 3.5 %collective-permute-done.26.refs_15_.refs_21_ = f32[160,512]{1,0:T(8,128)S(1)} collective-permute-done((f32[160,512]{1,0:T(8,128)}, f32[160,512]{1,0:T(8,128)S(1)}, u32[]{:S(2)}, u32[]{:S(2)}) %collective-permute-start.26) | collective-permute-done | bytes 327712 | tf_op jit(solution)/shard_map/ppermute | solution.py:410
  86.0 5.8 %shard_map.58.refs_17_.refs_29_.refs_5_ = f32[512,512]{1,0:T(8,128)} custom-call(s32[8]{0:T(128)S(1)} %get-tuple-element.25.ids, s32[1]{0:T(128)} %bitcast.place, f32[160,512]{1,0:T(8,128)S(1)} %get-tuple-element.21.refs_0_, f32[160,512]{1,0:T(8,128)S(1)} %collective-permute-done.2.refs_1_, f32[160,512]{1,0:T(8,128)S(1)} %collective-permute-done.17.refs_2_, ...), custom_call_target="tpu_custom_call" | custom-call | flops 3221225472 | bytes 3145728 | tf_op jit(solution)/shard_map/pallas_call | solution.py:228
  94.8 7.5 %shard_map.60.refs_33_.refs_9_ = f32[512,512]{1,0:T(8,128)} custom-call(s32[8]{0:T(128)S(1)} %get-tuple-element.25.ids, s32[1]{0:T(128)} %bitcast.place, f32[160,512]{1,0:T(8,128)S(1)} %get-tuple-element.21.refs_0_, f32[160,512]{1,0:T(8,128)S(1)} %collective-permute-done.2.refs_1_, f32[160,512]{1,0:T(8,128)S(1)} %collective-permute-done.17.refs_2_, ...), custom_call_target="tpu_custom_call" | custom-call | flops 6442450944 | bytes 3145728 | tf_op jit(solution)/shard_map/pallas_call | solution.py:228
  105.8 7.6 %collective-permute-done.30.refs_3_.refs_25_ = f32[160,512]{1,0:T(8,128)S(1)} collective-permute-done((f32[160,512]{1,0:T(8,128)}, f32[160,512]{1,0:T(8,128)S(1)}, u32[]{:S(2)}, u32[]{:S(2)}) %collective-permute-start.30) | collective-permute-done | bytes 327712 | tf_op jit(solution)/shard_map/ppermute | solution.py:410
  115.4 2.6 %collective-permute-done.10.refs_1_.refs_11_ = f32[160,512]{1,0:T(8,128)S(1)} collective-permute-done((f32[160,512]{1,0:T(8,128)}, f32[160,512]{1,0:T(8,128)S(1)}, u32[]{:S(2)}, u32[]{:S(2)}) %collective-permute-start.10) | collective-permute-done | bytes 327712 | tf_op jit(solution)/shard_map/ppermute | solution.py:410
  118.0 2.7 %collective-permute-done.14.refs_4_.refs_26_ = f32[160,512]{1,0:T(8,128)S(1)} collective-permute-done((f32[160,512]{1,0:T(8,128)}, f32[160,512]{1,0:T(8,128)S(1)}, u32[]{:S(2)}, u32[]{:S(2)}) %collective-permute-start.14) | collective-permute-done | bytes 327712 | tf_op jit(solution)/shard_map/ppermute | solution.py:410
  134.9 11.0 %shard_map.62.refs_13_ = f32[2560,512]{1,0:T(8,128)} custom-call(s32[14]{0:T(128)S(1)} %pad_add_fusion.ids, s32[1]{0:T(128)} %bitcast.place, f32[160,512]{1,0:T(8,128)S(1)} %get-tuple-element.21.refs_0_, f32[160,512]{1,0:T(8,128)S(1)} %collective-permute-done.2.refs_1_, f32[160,512]{1,0:T(8,128)S(1)} %collective-permute-done.17.refs_2_, ...), custom_call_target="tpu_custom_call" | custom-call | flops 7046430720 | bytes 18350080 | tf_op jit(solution)/shard_map/pallas_call | solution.py:355
  145.9 4.6 %shard_map.63 = f32[2560,512]{1,0:T(8,128)} custom-call(s32[2]{0:T(128)S(1)} %slice.17.ids, s32[1]{0:T(128)} %bitcast.place, f32[160,512]{1,0:T(8,128)S(1)} %collective-permute-done.7.refs_2_.refs_0_, f32[160,512]{1,0:T(8,128)S(1)} %collective-permute-done.12.refs_1_, ...), custom_call_target="tpu_custom_call", output_to_operand_aliasing={{}: (15, {})} | custom-call | flops 1006632960 | bytes 2621440 | tf_op jit(solution)/shard_map/pallas_call | solution.py:355
  (121 shorter events, 42.1 us)
Async XLA Ops:
  1.2 14.1 %collective-permute-start = (f32[160,512]{1,0:T(8,128)S(1)}, f32[160,512]{1,0:T(8,128)S(1)}, u32[]{:S(2)}, u32[]{:S(2)}) collective-permute-start(f32[160,512]{1,0:T(8,128)S(1)} %slice_select_fusion.1), channel_id=1, source_target_pairs={{0,24},{24,0},{4,28},{28,4},{8,16},{16,8}} | collective-permute-start | bytes 983048 | tf_op jit(solution)/shard_map/ppermute | solution.py:488
  12.1 10.9 %collective-permute-start.1 = (f32[160,512]{1,0:T(8,128)S(1)}, f32[160,512]{1,0:T(8,128)S(1)}, u32[]{:S(2)}, u32[]{:S(2)}) collective-permute-start(f32[160,512]{1,0:T(8,128)S(1)} %get-tuple-element.12), channel_id=1, source_target_pairs={{0,24},{24,0},{4,28},{28,4},{8,16},{16,8}} | collective-permute-start | bytes 983048 | tf_op jit(solution)/shard_map/ppermute | solution.py:488
  16.4 14.7 %collective-permute-start.2 = (f32[160,512]{1,0:T(8,128)S(1)}, f32[160,512]{1,0:T(8,128)S(1)}, u32[]{:S(2)}, u32[]{:S(2)}) collective-permute-start(f32[160,512]{1,0:T(8,128)S(1)} %get-tuple-element.21.refs_0_), channel_id=1, source_target_pairs={{0,8},{8,16},{16,24},{24,28},{28,20},{20,12},{12,4},{4,0},{1,9},{9... | collective-permute-start | bytes 983048 | tf_op jit(solution)/shard_map/ppermute | solution.py:410
  23.1 13.0 %collective-permute-start.21 = (f32[160,512]{1,0:T(8,128)S(1)}, f32[160,512]{1,0:T(8,128)S(1)}, u32[]{:S(2)}, u32[]{:S(2)}) collective-permute-start(f32[160,512]{1,0:T(8,128)S(1)} %get-tuple-element.23.refs_8_.refs_14_), channel_id=1, source_target_pairs={{8,0},{16,8},{24,16},{28,24},{20,28},{12,20},{4,12},{0,4},{9,1},{1... | collective-permute-start | bytes 983048 | tf_op jit(solution)/shard_map/ppermute | solution.py:410
  33.5 15.2 %collective-permute-start.20 = (f32[160,512]{1,0:T(8,128)S(1)}, f32[160,512]{1,0:T(8,128)}, u32[]{:S(2)}, u32[]{:S(2)}) collective-permute-start(f32[160,512]{1,0:T(8,128)S(1)} %get-tuple-element.23.refs_8_.refs_14_), channel_id=1, source_target_pairs={{0,8},{8,16},{16,24},{24,28},{28,20},{20,12},{12,4},{4,0},{1,9},{9... | collective-permute-start | bytes 983048 | tf_op jit(solution)/shard_map/ppermute | solution.py:410
  36.0 15.3 %collective-permute-start.17 = (f32[160,512]{1,0:T(8,128)S(1)}, f32[160,512]{1,0:T(8,128)S(1)}, u32[]{:S(2)}, u32[]{:S(2)}) collective-permute-start(f32[160,512]{1,0:T(8,128)S(1)} %get-tuple-element.21.refs_0_), channel_id=1, source_target_pairs={{8,0},{16,8},{24,16},{28,24},{20,28},{12,20},{4,12},{0,4},{9,1},{1... | collective-permute-start | bytes 983048 | tf_op jit(solution)/shard_map/ppermute | solution.py:410
  36.0 17.1 %collective-permute-start.23 = (f32[160,512]{1,0:T(8,128)S(1)}, f32[160,512]{1,0:T(8,128)}, u32[]{:S(2)}, u32[]{:S(2)}) collective-permute-start(f32[160,512]{1,0:T(8,128)S(1)} %collective-permute-done.21.refs_10_.refs_16_), channel_id=1, source_target_pairs={{8,0},{16,8},{24,16},{28,24},{20,28},{12,20},{4,12},{0,4},{9,1},{1... | collective-permute-start | bytes 983048 | tf_op jit(solution)/shard_map/ppermute | solution.py:410
  41.7 14.0 %collective-permute-start.4 = (f32[160,512]{1,0:T(8,128)S(1)}, f32[160,512]{1,0:T(8,128)S(1)}, u32[]{:S(2)}, u32[]{:S(2)}) collective-permute-start(f32[160,512]{1,0:T(8,128)S(1)} %collective-permute-done.3.refs_3_), channel_id=1, source_target_pairs={{0,8},{8,16},{16,24},{24,28},{28,20},{20,12},{12,4},{4,0},{1,9},{9... | collective-permute-start | bytes 983048 | tf_op jit(solution)/shard_map/ppermute | solution.py:410
  48.7 14.1 %collective-permute-start.22 = (f32[160,512]{1,0:T(8,128)}, f32[160,512]{1,0:T(8,128)}, u32[]{:S(2)}, u32[]{:S(2)}) collective-permute-start(f32[160,512]{1,0:T(8,128)} %collective-permute-done.20.refs_9_.refs_15_), channel_id=1, source_target_pairs={{0,8},{8,16},{16,24},{24,28},{28,20},{20,12},{12,4},{4,0},{1,9},{9... | collective-permute-start | bytes 983048 | tf_op jit(solution)/shard_map/ppermute | solution.py:410
  51.3 14.1 %collective-permute-start.18 = (f32[160,512]{1,0:T(8,128)S(1)}, f32[160,512]{1,0:T(8,128)S(1)}, u32[]{:S(2)}, u32[]{:S(2)}) collective-permute-start(f32[160,512]{1,0:T(8,128)S(1)} %collective-permute-done.17.refs_2_), channel_id=1, source_target_pairs={{8,0},{16,8},{24,16},{28,24},{20,28},{12,20},{4,12},{0,4},{9,1},{1... | collective-permute-start | bytes 983048 | tf_op jit(solution)/shard_map/ppermute | solution.py:410
  53.2 16.4 %collective-permute-start.25 = (f32[160,512]{1,0:T(8,128)}, f32[160,512]{1,0:T(8,128)}, u32[]{:S(2)}, u32[]{:S(2)}) collective-permute-start(f32[160,512]{1,0:T(8,128)} %collective-permute-done.23.refs_12_.refs_18_), channel_id=1, source_target_pairs={{8,0},{16,8},{24,16},{28,24},{20,28},{12,20},{4,12},{0,4},{9,1},{1... | collective-permute-start | bytes 983048 | tf_op jit(solution)/shard_map/ppermute | solution.py:410
  55.8 14.1 %collective-permute-start.27 = (f32[160,512]{1,0:T(8,128)S(1)}, f32[160,512]{1,0:T(8,128)}, u32[]{:S(2)}, u32[]{:S(2)}) collective-permute-start(f32[160,512]{1,0:T(8,128)S(1)} %get-tuple-element.15.refs_1_), channel_id=1, source_target_pairs={{0,8},{8,16},{16,24},{24,28},{28,20},{20,12},{12,4},{4,0},{1,9},{9... | collective-permute-start | bytes 983048 | tf_op jit(solution)/shard_map/ppermute | solution.py:410
  58.2 18.2 %collective-permute-start.5 = (f32[160,512]{1,0:T(8,128)S(1)}, f32[160,512]{1,0:T(8,128)S(1)}, u32[]{:S(2)}, u32[]{:S(2)}) collective-permute-start(f32[160,512]{1,0:T(8,128)S(1)} %get-tuple-element.14.refs_0_), channel_id=1, source_target_pairs={{8,0},{16,8},{24,16},{28,24},{20,28},{12,20},{4,12},{0,4},{9,1},{1... | collective-permute-start | bytes 983048 | tf_op jit(solution)/shard_map/ppermute | solution.py:410
  62.9 13.8 %collective-permute-start.8 = (f32[160,512]{1,0:T(8,128)S(1)}, f32[160,512]{1,0:T(8,128)S(1)}, u32[]{:S(2)}, u32[]{:S(2)}) collective-permute-start(f32[160,512]{1,0:T(8,128)S(1)} %collective-permute-done.4.refs_2_.refs_5_), channel_id=1, source_target_pairs={{0,8},{8,16},{16,24},{24,28},{28,20},{20,12},{12,4},{4,0},{1,9},{9... | collective-permute-start | bytes 983048 | tf_op jit(solution)/shard_map/ppermute | solution.py:410
  65.4 14.9 %collective-permute-start.24 = (f32[160,512]{1,0:T(8,128)}, f32[160,512]{1,0:T(8,128)S(1)}, u32[]{:S(2)}, u32[]{:S(2)}) collective-permute-start(f32[160,512]{1,0:T(8,128)} %collective-permute-done.22.refs_11_.refs_17_), channel_id=1, source_target_pairs={{0,8},{8,16},{16,24},{24,28},{28,20},{20,12},{12,4},{4,0},{1,9},{9... | collective-permute-start | bytes 983048 | tf_op jit(solution)/shard_map/ppermute | solution.py:410
  69.6 12.2 %collective-permute-start.19 = (f32[160,512]{1,0:T(8,128)S(1)}, f32[160,512]{1,0:T(8,128)S(1)}, u32[]{:S(2)}, u32[]{:S(2)}) collective-permute-start(f32[160,512]{1,0:T(8,128)S(1)} %collective-permute-done.18.refs_4_), channel_id=1, source_target_pairs={{8,0},{16,8},{24,16},{28,24},{20,28},{12,20},{4,12},{0,4},{9,1},{1... | collective-permute-start | bytes 983048 | tf_op jit(solution)/shard_map/ppermute | solution.py:410
  69.8 15.4 %collective-permute-start.26 = (f32[160,512]{1,0:T(8,128)}, f32[160,512]{1,0:T(8,128)S(1)}, u32[]{:S(2)}, u32[]{:S(2)}) collective-permute-start(f32[160,512]{1,0:T(8,128)} %collective-permute-done.25.refs_14_.refs_20_), channel_id=1, source_target_pairs={{8,0},{16,8},{24,16},{28,24},{20,28},{12,20},{4,12},{0,4},{9,1},{1... | collective-permute-start | bytes 983048 | tf_op jit(solution)/shard_map/ppermute | solution.py:410
  76.7 16.6 %collective-permute-start.13 = (f32[160,512]{1,0:T(8,128)S(1)}, f32[160,512]{1,0:T(8,128)S(1)}, u32[]{:S(2)}, u32[]{:S(2)}) collective-permute-start(f32[160,512]{1,0:T(8,128)S(1)} %get-tuple-element.17.refs_22_), channel_id=1, source_target_pairs={{8,0},{16,8},{24,16},{28,24},{20,28},{12,20},{4,12},{0,4},{9,1},{1... | collective-permute-start | bytes 983048 | tf_op jit(solution)/shard_map/ppermute | solution.py:410
  77.2 16.2 %collective-permute-start.9 = (f32[160,512]{1,0:T(8,128)S(1)}, f32[160,512]{1,0:T(8,128)S(1)}, u32[]{:S(2)}, u32[]{:S(2)}) collective-permute-start(f32[160,512]{1,0:T(8,128)S(1)} %get-tuple-element.16.refs_8_), channel_id=1, source_target_pairs={{0,8},{8,16},{16,24},{24,28},{28,20},{20,12},{12,4},{4,0},{1,9},{9... | collective-permute-start | bytes 983048 | tf_op jit(solution)/shard_map/ppermute | solution.py:410
  91.8 28.9 %collective-permute-start.29 = (f32[512,512]{1,0:T(8,128)}, f32[512,512]{1,0:T(8,128)S(1)}, u32[]{:S(2)}, u32[]{:S(2)}) collective-permute-start(f32[512,512]{1,0:T(8,128)} %shard_map.58.refs_17_.refs_29_.refs_5_), channel_id=1, source_target_pairs={{0,2},{4,6},{8,10},{12,14},{16,18},{20,22},{24,26},{28,30}} | collective-permute-start | bytes 3145736 | tf_op jit(solution)/shard_map/ppermute | solution.py:421
  102.3 26.3 %collective-permute-start.33 = (f32[512,512]{1,0:T(8,128)}, f32[512,512]{1,0:T(8,128)S(1)}, u32[]{:S(2)}, u32[]{:S(2)}) collective-permute-start(f32[512,512]{1,0:T(8,128)} %shard_map.60.refs_33_.refs_9_), channel_id=1, source_target_pairs={{0,2},{4,6},{8,10},{12,14},{16,18},{20,22},{24,26},{28,30}} | collective-permute-start | bytes 3145736 | tf_op jit(solution)/shard_map/ppermute | solution.py:421
  105.7 12.3 %collective-permute-start.10 = (f32[160,512]{1,0:T(8,128)}, f32[160,512]{1,0:T(8,128)S(1)}, u32[]{:S(2)}, u32[]{:S(2)}) collective-permute-start(f32[160,512]{1,0:T(8,128)} %copy-done.24), channel_id=1, source_target_pairs={{0,8},{8,16},{16,24},{24,28},{28,20},{20,12},{12,4},{4,0},{1,9},{9... | collective-permute-start | bytes 983048 | tf_op jit(solution)/shard_map/ppermute | solution.py:410
  130.5 15.4 %collective-permute-start.12 = (f32[160,512]{1,0:T(8,128)S(1)}, f32[160,512]{1,0:T(8,128)S(1)}, u32[]{:S(2)}, u32[]{:S(2)}) collective-permute-start(f32[160,512]{1,0:T(8,128)S(1)} %collective-permute-done.11.refs_1_.refs_13_), channel_id=1, source_target_pairs={{0,8},{8,16},{16,24},{24,28},{28,20},{20,12},{12,4},{4,0},{1,9},{9... | collective-permute-start | bytes 983048 | tf_op jit(solution)/shard_map/ppermute | solution.py:410
  130.5 15.4 %collective-permute-start.16 = (f32[160,512]{1,0:T(8,128)S(1)}, f32[160,512]{1,0:T(8,128)S(1)}, u32[]{:S(2)}, u32[]{:S(2)}) collective-permute-start(f32[160,512]{1,0:T(8,128)S(1)} %collective-permute-done.15.refs_4_.refs_2_), channel_id=1, source_target_pairs={{8,0},{16,8},{24,16},{28,24},{20,28},{12,20},{4,12},{0,4},{9,1},{1... | collective-permute-start | bytes 983048 | tf_op jit(solution)/shard_map/ppermute | solution.py:410
  (40 other events, 598.1 us)

commit v11 on v9

--- a/solution.py
+++ b/solution.py
@@ -490,7 +490,7 @@
             ]
             top, steps = ring_pass([[piece] * 2 for piece in own[0]], ring)
             free = gate(own[1], [steps[-2][0][0]])
-            full = gate(free, [steps[-1][0][0]])
+            full = gate(free, [steps[-1][0][0], steps[-1][1][1]])
             rest, steps = ring_pass([[full[0], free[0]], [free[1], full[1]]], ring)
             after, sends = [steps[0][0][1], steps[0][1][0]], [steps[0][0][0], steps[0][1][1]]
             near = [steps[i][0] + steps[i][1] for i in (0, -2)]

time: 154 us -> 158 us (1.026)
  waiting for transfers between devices: 55.9 us -> 57.8 us
    ppermute x28, waiting for transfers between devices: 54.4 us -> 56.4 us  [ring_pass(): going[k][way] = lax.ppermute(going[k][way], 'src', pairs)]
    unnamed x60 -> x62, local copies, waits for them, and re-layouts: 4.53 us -> 5.59 us
  transfers between devices with their start and end apart: 34 -> 34, of which waited for: 19 -> 18; matrix products, arithmetic and copies ran while one was open for 4% -> 4% of each run, Pallas kernels for 16% -> 15%
where the time goes in v11:
time: 158 us; the launch traced here: 156 us
  waiting for transfers between devices  57.8 us (37%)
  starting transfers between devices  56.2 us (36%)
  Pallas kernels  28.8 us (18%)
  other arithmetic  7.52 us (5%)
  local copies, waits for them, and re-layouts  5.66 us (4%)
    ppermute x28, waiting for transfers between devices, ring_pass(): going[k][way] = lax.ppermute(going[k][way], 'src', pairs)  56.4 us
    ppermute x28, starting transfers between devices, ring_pass(): going[k][way] = lax.ppermute(going[k][way], 'src', pairs)  39.9 us
    pallas_call x2, Pallas kernels, update(): pl.pallas_call(functools.partial(update_kernel, pieces, rows, width, grou...  15.7 us
    pallas_call x1, Pallas kernels, solve_panels(): pl.pallas_call(functools.partial(solve_kernel, pieces, rows, width, chunk...  9.08 us
    ppermute x2, starting transfers between devices, local(): got = [lax.ppermute(sent, axes, swap) for sent in (sent_first, sent_second)]  8.88 us
    unnamed x62, local copies, waits for them, and re-layouts  5.59 us
    select_n x2, other arithmetic, spread_far(): block = jnp.where(place[0] == r, found[r], block)  4.85 us
    ppermute x2, starting transfers between devices, spread_far(): found[r + stride] = lax.ppermute(found[r], 'row', [(r, r + stride)])  4.72 us
  transfers between devices with their start and end apart: 34, of which 18 were waited for; matrix products, arithmetic and copies ran while one was open for 4% of the time, Pallas kernels for 15%

profile of v11, /device:TPU:0, one launch (start us, length us, event | category | flops | bytes accessed | tf_op | source)
XLA Modules:
  0.0 156.5 jit_solution(7341220394538374620)
XLA Ops:
  1.2 7.0 %collective-permute-start = (f32[160,512]{1,0:T(8,128)S(1)}, f32[160,512]{1,0:T(8,128)S(1)}, u32[]{:S(2)}, u32[]{:S(2)}) collective-permute-start(f32[160,512]{1,0:T(8,128)S(1)} %slice_select_fusion.1), channel_id=1, source_target_pairs={{0,24},{24,0},{4,28},{28,4},{8,16},{16,8}} | collective-permute-start | bytes 983048 | tf_op jit(solution)/shard_map/ppermute | solution.py:471
  8.1 4.0 %shard_map.55 = (f32[160,512]{1,0:T(8,128)S(1)}, f32[160,512]{1,0:T(8,128)S(1)}, f32[160,512]{1,0:T(8,128)S(1)}) custom-call(s32[1]{0:T(128)} %bitcast.1.me, s32[1]{0:T(128)} %bitcast.place, f32[320,1024]{1,0:T(8,128)} %source.1), custom_call_target="tpu_custom_call" | custom-call | flops 1000 | bytes 1000 | tf_op jit(solution)/shard_map/pallas_call | solution.py:114
  16.4 6.6 %collective-permute-start.2 = (f32[160,512]{1,0:T(8,128)S(1)}, f32[160,512]{1,0:T(8,128)S(1)}, u32[]{:S(2)}, u32[]{:S(2)}) collective-permute-start(f32[160,512]{1,0:T(8,128)S(1)} %get-tuple-element.29.refs_0_), channel_id=1, source_target_pairs={{0,8},{8,16},{16,24},{24,28},{28,20},{20,12},{12,4},{4,0},{1,9},{9... | collective-permute-start | bytes 983048 | tf_op jit(solution)/shard_map/ppermute | solution.py:394
  23.1 3.5 %collective-permute-start.9 = (f32[160,512]{1,0:T(8,128)S(1)}, f32[160,512]{1,0:T(8,128)S(1)}, u32[]{:S(2)}, u32[]{:S(2)}) collective-permute-start(f32[160,512]{1,0:T(8,128)S(1)} %get-tuple-element.31.refs_8_.refs_14_), channel_id=1, source_target_pairs={{8,0},{16,8},{24,16},{28,24},{20,28},{12,20},{4,12},{0,4},{9,1},{1... | collective-permute-start | bytes 983048 | tf_op jit(solution)/shard_map/ppermute | solution.py:394
  26.5 4.5 %collective-permute-done.2.refs_1_ = f32[160,512]{1,0:T(8,128)S(1)} collective-permute-done((f32[160,512]{1,0:T(8,128)S(1)}, f32[160,512]{1,0:T(8,128)S(1)}, u32[]{:S(2)}, u32[]{:S(2)}) %collective-permute-start.2) | collective-permute-done | bytes 327712 | tf_op jit(solution)/shard_map/ppermute | solution.py:394
  31.1 2.5 %collective-permute-start.3 = (f32[160,512]{1,0:T(8,128)S(1)}, f32[160,512]{1,0:T(8,128)S(1)}, u32[]{:S(2)}, u32[]{:S(2)}) collective-permute-start(f32[160,512]{1,0:T(8,128)S(1)} %collective-permute-done.2.refs_1_), channel_id=1, source_target_pairs={{0,8},{8,16},{16,24},{24,28},{28,20},{20,12},{12,4},{4,0},{1,9},{9... | collective-permute-start | bytes 983048 | tf_op jit(solution)/shard_map/ppermute | solution.py:394
  33.5 2.5 %collective-permute-start.24 = (f32[160,512]{1,0:T(8,128)S(1)}, f32[160,512]{1,0:T(8,128)S(1)}, u32[]{:S(2)}, u32[]{:S(2)}) collective-permute-start(f32[160,512]{1,0:T(8,128)S(1)} %get-tuple-element.31.refs_8_.refs_14_), channel_id=1, source_target_pairs={{0,8},{8,16},{16,24},{24,28},{28,20},{20,12},{12,4},{4,0},{1,9},{9... | collective-permute-start | bytes 983048 | tf_op jit(solution)/shard_map/ppermute | solution.py:394
  37.2 4.6 %collective-permute-done.3.refs_3_ = f32[160,512]{1,0:T(8,128)S(1)} collective-permute-done((f32[160,512]{1,0:T(8,128)S(1)}, f32[160,512]{1,0:T(8,128)S(1)}, u32[]{:S(2)}, u32[]{:S(2)}) %collective-permute-start.3) | collective-permute-done | bytes 327712 | tf_op jit(solution)/shard_map/ppermute | solution.py:394
  41.7 2.5 %collective-permute-start.4 = (f32[160,512]{1,0:T(8,128)S(1)}, f32[160,512]{1,0:T(8,128)S(1)}, u32[]{:S(2)}, u32[]{:S(2)}) collective-permute-start(f32[160,512]{1,0:T(8,128)S(1)} %collective-permute-done.3.refs_3_), channel_id=1, source_target_pairs={{0,8},{8,16},{16,24},{24,28},{28,20},{20,12},{12,4},{4,0},{1,9},{9... | collective-permute-start | bytes 983048 | tf_op jit(solution)/shard_map/ppermute | solution.py:394
  44.2 4.5 %collective-permute-done.24.refs_9_.refs_15_ = f32[160,512]{1,0:T(8,128)S(1)} collective-permute-done((f32[160,512]{1,0:T(8,128)S(1)}, f32[160,512]{1,0:T(8,128)S(1)}, u32[]{:S(2)}, u32[]{:S(2)}) %collective-permute-start.24) | collective-permute-done | bytes 327712 | tf_op jit(solution)/shard_map/ppermute | solution.py:394
  48.7 2.5 %collective-permute-start.25 = (f32[160,512]{1,0:T(8,128)S(1)}, f32[160,512]{1,0:T(8,128)}, u32[]{:S(2)}, u32[]{:S(2)}) collective-permute-start(f32[160,512]{1,0:T(8,128)S(1)} %collective-permute-done.24.refs_9_.refs_15_), channel_id=1, source_target_pairs={{0,8},{8,16},{16,24},{24,28},{28,20},{20,12},{12,4},{4,0},{1,9},{9... | collective-permute-start | bytes 983048 | tf_op jit(solution)/shard_map/ppermute | solution.py:394
  55.8 2.5 %collective-permute-start.27 = (f32[160,512]{1,0:T(8,128)S(1)}, f32[160,512]{1,0:T(8,128)S(1)}, u32[]{:S(2)}, u32[]{:S(2)}) collective-permute-start(f32[160,512]{1,0:T(8,128)S(1)} %get-tuple-element.19.refs_1_), channel_id=1, source_target_pairs={{0,8},{8,16},{16,24},{24,28},{28,20},{20,12},{12,4},{4,0},{1,9},{9... | collective-permute-start | bytes 983048 | tf_op jit(solution)/shard_map/ppermute | solution.py:394
  58.3 4.5 %collective-permute-done.25.refs_11_.refs_17_ = f32[160,512]{1,0:T(8,128)} collective-permute-done((f32[160,512]{1,0:T(8,128)S(1)}, f32[160,512]{1,0:T(8,128)}, u32[]{:S(2)}, u32[]{:S(2)}) %collective-permute-start.25) | collective-permute-done | bytes 327712 | tf_op jit(solution)/shard_map/ppermute | solution.py:394
  62.8 2.6 %collective-permute-start.26 = (f32[160,512]{1,0:T(8,128)}, f32[160,512]{1,0:T(8,128)S(1)}, u32[]{:S(2)}, u32[]{:S(2)}) collective-permute-start(f32[160,512]{1,0:T(8,128)} %collective-permute-done.25.refs_11_.refs_17_), channel_id=1, source_target_pairs={{0,8},{8,16},{16,24},{24,28},{28,20},{20,12},{12,4},{4,0},{1,9},{9... | collective-permute-start | bytes 983048 | tf_op jit(solution)/shard_map/ppermute | solution.py:394
  65.4 4.0 %collective-permute-done.11.refs_14_.refs_20_ = f32[160,512]{1,0:T(8,128)} collective-permute-done((f32[160,512]{1,0:T(8,128)}, f32[160,512]{1,0:T(8,128)}, u32[]{:S(2)}, u32[]{:S(2)}) %collective-permute-start.11) | collective-permute-done | bytes 327712 | tf_op jit(solution)/shard_map/ppermute | solution.py:394
  71.7 7.9 %collective-permute-done.5.refs_17_.refs_2_.refs_10_ = f32[160,512]{1,0:T(8,128)S(1)} collective-permute-done((f32[160,512]{1,0:T(8,128)S(1)}, f32[160,512]{1,0:T(8,128)S(1)}, u32[]{:S(2)}, u32[]{:S(2)}) %collective-permute-start.5) | collective-permute-done | bytes 327712 | tf_op jit(solution)/shard_map/ppermute | solution.py:394
  79.7 6.3 %collective-permute-done.12.refs_3_.refs_15_.refs_21_ = f32[160,512]{1,0:T(8,128)S(1)} collective-permute-done((f32[160,512]{1,0:T(8,128)}, f32[160,512]{1,0:T(8,128)S(1)}, u32[]{:S(2)}, u32[]{:S(2)}) %collective-permute-start.12) | collective-permute-done | bytes 327712 | tf_op jit(solution)/shard_map/ppermute | solution.py:394
  91.9 9.1 %shard_map.58 = (f32[512,512]{1,0:T(8,128)}, f32[512,512]{1,0:T(8,128)}) custom-call(s32[8]{0:T(128)S(1)} %get-tuple-element.33.ids, s32[1]{0:T(128)} %bitcast.place, f32[160,512]{1,0:T(8,128)S(1)} %get-tuple-element.29.refs_0_, f32[160,512]{1,0:T(8,128)S(1)} %copy-done.13, f32[160,512]{1,0:T(8,128)S(1)} %copy-done.19, f32[160,512]{1,0:T(8,128)S(1)} %copy-done.16, ...), custom_call_target="tpu_custom_call" | custom-call | flops 9663676416 | bytes 6291456 | tf_op jit(solution)/shard_map/pallas_call | solution.py:213
  109.5 3.7 %collective-permute-done.31.refs_25_ = f32[160,512]{1,0:T(8,128)} collective-permute-done((f32[160,512]{1,0:T(8,128)}, f32[160,512]{1,0:T(8,128)}, u32[]{:S(2)}, u32[]{:S(2)}) %collective-permute-start.31) | collective-permute-done | bytes 327712 | tf_op jit(solution)/shard_map/ppermute | solution.py:394
  116.9 4.2 %collective-permute-done.18.refs_26_ = f32[160,512]{1,0:T(8,128)} collective-permute-done((f32[160,512]{1,0:T(8,128)S(1)}, f32[160,512]{1,0:T(8,128)}, u32[]{:S(2)}, u32[]{:S(2)}) %collective-permute-start.18) | collective-permute-done | bytes 327712 | tf_op jit(solution)/shard_map/ppermute | solution.py:394
  121.1 2.8 %collective-permute-start.15 = (f32[160,512]{1,0:T(8,128)}, f32[160,512]{1,0:T(8,128)S(1)}, u32[]{:S(2)}, u32[]{:S(2)}) collective-permute-start(f32[160,512]{1,0:T(8,128)} %collective-permute-done.14.refs_11_), channel_id=1, source_target_pairs={{0,8},{8,16},{16,24},{24,28},{28,20},{20,12},{12,4},{4,0},{1,9},{9... | collective-permute-start | bytes 983048 | tf_op jit(solution)/shard_map/ppermute | solution.py:394
  132.5 2.4 %broadcast_select_fusion.1.refs_0_ = f32[512,512]{1,0:T(8,128)} fusion(f32[512,512]{1,0:T(8,128)} %collective-permute-done.28, f32[512,512]{1,0:T(8,128)} %get-tuple-element.25, pred[]{:T(512)S(6)} %eq.54), kind=kLoop, calls=%fused_computation.1 | loop fusion | flops 262144 | bytes 3145729 | tf_op jit(solution)/shard_map/jit(_where)/select_n | solution.py:409
  140.6 11.2 %shard_map.62.refs_9_ = f32[2560,512]{1,0:T(8,128)} custom-call(s32[14]{0:T(128)S(1)} %pad_add_fusion.ids, s32[1]{0:T(128)} %bitcast.place, f32[160,512]{1,0:T(8,128)S(1)} %get-tuple-element.29.refs_0_, f32[160,512]{1,0:T(8,128)S(1)} %copy-done.14, f32[160,512]{1,0:T(8,128)S(1)} %copy-done.20, f32[160,512]{1,0:T(8,128)S(1)} %copy-done.17, ...), custom_call_target="tpu_custom_call" | custom-call | flops 7046430720 | bytes 18350080 | tf_op jit(solution)/shard_map/pallas_call | solution.py:339
  151.7 4.6 %shard_map.63 = f32[2560,512]{1,0:T(8,128)} custom-call(s32[2]{0:T(128)S(1)} %slice.17.ids, s32[1]{0:T(128)} %bitcast.place, f32[160,512]{1,0:T(8,128)S(1)} %collective-permute-done.7.refs_2_.refs_0_, f32[160,512]{1,0:T(8,128)S(1)} %collective-permute-done.16.refs_1_, ...), custom_call_target="tpu_custom_call", output_to_operand_aliasing={{}: (11, {})} | custom-call | flops 1006632960 | bytes 2621440 | tf_op jit(solution)/shard_map/pallas_call | solution.py:339
  (125 shorter events, 45.6 us)
Async XLA Ops:
  1.2 14.1 %collective-permute-start = (f32[160,512]{1,0:T(8,128)S(1)}, f32[160,512]{1,0:T(8,128)S(1)}, u32[]{:S(2)}, u32[]{:S(2)}) collective-permute-start(f32[160,512]{1,0:T(8,128)S(1)} %slice_select_fusion.1), channel_id=1, source_target_pairs={{0,24},{24,0},{4,28},{28,4},{8,16},{16,8}} | collective-permute-start | bytes 983048 | tf_op jit(solution)/shard_map/ppermute | solution.py:471
  12.1 10.9 %collective-permute-start.1 = (f32[160,512]{1,0:T(8,128)S(1)}, f32[160,512]{1,0:T(8,128)S(1)}, u32[]{:S(2)}, u32[]{:S(2)}) collective-permute-start(f32[160,512]{1,0:T(8,128)S(1)} %get-tuple-element.16), channel_id=1, source_target_pairs={{0,24},{24,0},{4,28},{28,4},{8,16},{16,8}} | collective-permute-start | bytes 983048 | tf_op jit(solution)/shard_map/ppermute | solution.py:471
  16.4 14.7 %collective-permute-start.2 = (f32[160,512]{1,0:T(8,128)S(1)}, f32[160,512]{1,0:T(8,128)S(1)}, u32[]{:S(2)}, u32[]{:S(2)}) collective-permute-start(f32[160,512]{1,0:T(8,128)S(1)} %get-tuple-element.29.refs_0_), channel_id=1, source_target_pairs={{0,8},{8,16},{16,24},{24,28},{28,20},{20,12},{12,4},{4,0},{1,9},{9... | collective-permute-start | bytes 983048 | tf_op jit(solution)/shard_map/ppermute | solution.py:394
  23.1 13.0 %collective-permute-start.9 = (f32[160,512]{1,0:T(8,128)S(1)}, f32[160,512]{1,0:T(8,128)S(1)}, u32[]{:S(2)}, u32[]{:S(2)}) collective-permute-start(f32[160,512]{1,0:T(8,128)S(1)} %get-tuple-element.31.refs_8_.refs_14_), channel_id=1, source_target_pairs={{8,0},{16,8},{24,16},{28,24},{20,28},{12,20},{4,12},{0,4},{9,1},{1... | collective-permute-start | bytes 983048 | tf_op jit(solution)/shard_map/ppermute | solution.py:394
  33.5 15.2 %collective-permute-start.24 = (f32[160,512]{1,0:T(8,128)S(1)}, f32[160,512]{1,0:T(8,128)S(1)}, u32[]{:S(2)}, u32[]{:S(2)}) collective-permute-start(f32[160,512]{1,0:T(8,128)S(1)} %get-tuple-element.31.refs_8_.refs_14_), channel_id=1, source_target_pairs={{0,8},{8,16},{16,24},{24,28},{28,20},{20,12},{12,4},{4,0},{1,9},{9... | collective-permute-start | bytes 983048 | tf_op jit(solution)/shard_map/ppermute | solution.py:394
  36.0 15.2 %collective-permute-start.21 = (f32[160,512]{1,0:T(8,128)S(1)}, f32[160,512]{1,0:T(8,128)S(1)}, u32[]{:S(2)}, u32[]{:S(2)}) collective-permute-start(f32[160,512]{1,0:T(8,128)S(1)} %get-tuple-element.29.refs_0_), channel_id=1, source_target_pairs={{8,0},{16,8},{24,16},{28,24},{20,28},{12,20},{4,12},{0,4},{9,1},{1... | collective-permute-start | bytes 983048 | tf_op jit(solution)/shard_map/ppermute | solution.py:394
  36.0 17.1 %collective-permute-start.10 = (f32[160,512]{1,0:T(8,128)S(1)}, f32[160,512]{1,0:T(8,128)}, u32[]{:S(2)}, u32[]{:S(2)}) collective-permute-start(f32[160,512]{1,0:T(8,128)S(1)} %collective-permute-done.9.refs_10_.refs_16_), channel_id=1, source_target_pairs={{8,0},{16,8},{24,16},{28,24},{20,28},{12,20},{4,12},{0,4},{9,1},{1... | collective-permute-start | bytes 983048 | tf_op jit(solution)/shard_map/ppermute | solution.py:394
  41.7 14.0 %collective-permute-start.4 = (f32[160,512]{1,0:T(8,128)S(1)}, f32[160,512]{1,0:T(8,128)S(1)}, u32[]{:S(2)}, u32[]{:S(2)}) collective-permute-start(f32[160,512]{1,0:T(8,128)S(1)} %collective-permute-done.3.refs_3_), channel_id=1, source_target_pairs={{0,8},{8,16},{16,24},{24,28},{28,20},{20,12},{12,4},{4,0},{1,9},{9... | collective-permute-start | bytes 983048 | tf_op jit(solution)/shard_map/ppermute | solution.py:394
  48.7 14.1 %collective-permute-start.25 = (f32[160,512]{1,0:T(8,128)S(1)}, f32[160,512]{1,0:T(8,128)}, u32[]{:S(2)}, u32[]{:S(2)}) collective-permute-start(f32[160,512]{1,0:T(8,128)S(1)} %collective-permute-done.24.refs_9_.refs_15_), channel_id=1, source_target_pairs={{0,8},{8,16},{16,24},{24,28},{28,20},{20,12},{12,4},{4,0},{1,9},{9... | collective-permute-start | bytes 983048 | tf_op jit(solution)/shard_map/ppermute | solution.py:394
  51.2 14.1 %collective-permute-start.22 = (f32[160,512]{1,0:T(8,128)S(1)}, f32[160,512]{1,0:T(8,128)}, u32[]{:S(2)}, u32[]{:S(2)}) collective-permute-start(f32[160,512]{1,0:T(8,128)S(1)} %collective-permute-done.21.refs_2_), channel_id=1, source_target_pairs={{8,0},{16,8},{24,16},{28,24},{20,28},{12,20},{4,12},{0,4},{9,1},{1... | collective-permute-start | bytes 983048 | tf_op jit(solution)/shard_map/ppermute | solution.py:394
  53.1 16.2 %collective-permute-start.11 = (f32[160,512]{1,0:T(8,128)}, f32[160,512]{1,0:T(8,128)}, u32[]{:S(2)}, u32[]{:S(2)}) collective-permute-start(f32[160,512]{1,0:T(8,128)} %collective-permute-done.10.refs_12_.refs_18_), channel_id=1, source_target_pairs={{8,0},{16,8},{24,16},{28,24},{20,28},{12,20},{4,12},{0,4},{9,1},{1... | collective-permute-start | bytes 983048 | tf_op jit(solution)/shard_map/ppermute | solution.py:394
  55.8 15.7 %collective-permute-start.27 = (f32[160,512]{1,0:T(8,128)S(1)}, f32[160,512]{1,0:T(8,128)S(1)}, u32[]{:S(2)}, u32[]{:S(2)}) collective-permute-start(f32[160,512]{1,0:T(8,128)S(1)} %get-tuple-element.19.refs_1_), channel_id=1, source_target_pairs={{0,8},{8,16},{16,24},{24,28},{28,20},{20,12},{12,4},{4,0},{1,9},{9... | collective-permute-start | bytes 983048 | tf_op jit(solution)/shard_map/ppermute | solution.py:394
  62.8 25.3 %collective-permute-start.26 = (f32[160,512]{1,0:T(8,128)}, f32[160,512]{1,0:T(8,128)S(1)}, u32[]{:S(2)}, u32[]{:S(2)}) collective-permute-start(f32[160,512]{1,0:T(8,128)} %collective-permute-done.25.refs_11_.refs_17_), channel_id=1, source_target_pairs={{0,8},{8,16},{16,24},{24,28},{28,20},{20,12},{12,4},{4,0},{1,9},{9... | collective-permute-start | bytes 983048 | tf_op jit(solution)/shard_map/ppermute | solution.py:394
  65.4 22.7 %collective-permute-start.23 = (f32[160,512]{1,0:T(8,128)}, f32[160,512]{1,0:T(8,128)S(1)}, u32[]{:S(2)}, u32[]{:S(2)}) collective-permute-start(f32[160,512]{1,0:T(8,128)} %collective-permute-done.22.refs_4_), channel_id=1, source_target_pairs={{8,0},{16,8},{24,16},{28,24},{20,28},{12,20},{4,12},{0,4},{9,1},{1... | collective-permute-start | bytes 983048 | tf_op jit(solution)/shard_map/ppermute | solution.py:394
  65.4 14.3 %collective-permute-start.5 = (f32[160,512]{1,0:T(8,128)S(1)}, f32[160,512]{1,0:T(8,128)S(1)}, u32[]{:S(2)}, u32[]{:S(2)}) collective-permute-start(f32[160,512]{1,0:T(8,128)S(1)} %get-tuple-element.18.refs_0_), channel_id=1, source_target_pairs={{8,0},{16,8},{24,16},{28,24},{20,28},{12,20},{4,12},{0,4},{9,1},{1... | collective-permute-start | bytes 983048 | tf_op jit(solution)/shard_map/ppermute | solution.py:394
  69.4 16.6 %collective-permute-start.8 = (f32[160,512]{1,0:T(8,128)S(1)}, f32[160,512]{1,0:T(8,128)S(1)}, u32[]{:S(2)}, u32[]{:S(2)}) collective-permute-start(f32[160,512]{1,0:T(8,128)S(1)} %collective-permute-done.4.refs_2_.refs_5_), channel_id=1, source_target_pairs={{0,8},{8,16},{16,24},{24,28},{28,20},{20,12},{12,4},{4,0},{1,9},{9... | collective-permute-start | bytes 983048 | tf_op jit(solution)/shard_map/ppermute | solution.py:394
  71.4 14.5 %collective-permute-start.12 = (f32[160,512]{1,0:T(8,128)}, f32[160,512]{1,0:T(8,128)S(1)}, u32[]{:S(2)}, u32[]{:S(2)}) collective-permute-start(f32[160,512]{1,0:T(8,128)} %collective-permute-done.11.refs_14_.refs_20_), channel_id=1, source_target_pairs={{8,0},{16,8},{24,16},{28,24},{20,28},{12,20},{4,12},{0,4},{9,1},{1... | collective-permute-start | bytes 983048 | tf_op jit(solution)/shard_map/ppermute | solution.py:394
  86.0 15.0 %collective-permute-start.13 = (f32[160,512]{1,0:T(8,128)S(1)}, f32[160,512]{1,0:T(8,128)S(1)}, u32[]{:S(2)}, u32[]{:S(2)}) collective-permute-start(f32[160,512]{1,0:T(8,128)S(1)} %get-tuple-element.21.refs_8_), channel_id=1, source_target_pairs={{0,8},{8,16},{16,24},{24,28},{28,20},{20,12},{12,4},{4,0},{1,9},{9... | collective-permute-start | bytes 983048 | tf_op jit(solution)/shard_map/ppermute | solution.py:394
  87.8 13.2 %collective-permute-start.17 = (f32[160,512]{1,0:T(8,128)S(1)}, f32[160,512]{1,0:T(8,128)S(1)}, u32[]{:S(2)}, u32[]{:S(2)}) collective-permute-start(f32[160,512]{1,0:T(8,128)S(1)} %get-tuple-element.22.refs_22_), channel_id=1, source_target_pairs={{8,0},{16,8},{24,16},{28,24},{20,28},{12,20},{4,12},{0,4},{9,1},{1... | collective-permute-start | bytes 983048 | tf_op jit(solution)/shard_map/ppermute | solution.py:394
  101.1 22.8 %collective-permute-start.30 = (f32[512,512]{1,0:T(8,128)}, f32[512,512]{1,0:T(8,128)}, u32[]{:S(2)}, u32[]{:S(2)}) collective-permute-start(f32[512,512]{1,0:T(8,128)} %get-tuple-element.26), channel_id=1, source_target_pairs={{0,2},{4,6},{8,10},{12,14},{16,18},{20,22},{24,26},{28,30}} | collective-permute-start | bytes 3145736 | tf_op jit(solution)/shard_map/ppermute | solution.py:405
  103.5 29.0 %collective-permute-start.28 = (f32[512,512]{1,0:T(8,128)}, f32[512,512]{1,0:T(8,128)}, u32[]{:S(2)}, u32[]{:S(2)}) collective-permute-start(f32[512,512]{1,0:T(8,128)} %get-tuple-element.25), channel_id=1, source_target_pairs={{0,2},{4,6},{8,10},{12,14},{16,18},{20,22},{24,26},{28,30}} | collective-permute-start | bytes 3145736 | tf_op jit(solution)/shard_map/ppermute | solution.py:405
  114.8 11.5 %collective-permute-start.32 = (f32[160,512]{1,0:T(8,128)}, f32[160,512]{1,0:T(8,128)S(1)}, u32[]{:S(2)}, u32[]{:S(2)}) collective-permute-start(f32[160,512]{1,0:T(8,128)} %collective-permute-done.31.refs_25_), channel_id=1, source_target_pairs={{0,8},{8,16},{16,24},{24,28},{28,20},{20,12},{12,4},{4,0},{1,9},{9... | collective-permute-start | bytes 983048 | tf_op jit(solution)/shard_map/ppermute | solution.py:394
  136.5 15.2 %collective-permute-start.16 = (f32[160,512]{1,0:T(8,128)S(1)}, f32[160,512]{1,0:T(8,128)S(1)}, u32[]{:S(2)}, u32[]{:S(2)}) collective-permute-start(f32[160,512]{1,0:T(8,128)S(1)} %collective-permute-done.15.refs_1_.refs_13_), channel_id=1, source_target_pairs={{0,8},{8,16},{16,24},{24,28},{28,20},{20,12},{12,4},{4,0},{1,9},{9... | collective-permute-start | bytes 983048 | tf_op jit(solution)/shard_map/ppermute | solution.py:394
  137.8 14.0 %collective-permute-start.20 = (f32[160,512]{1,0:T(8,128)S(1)}, f32[160,512]{1,0:T(8,128)S(1)}, u32[]{:S(2)}, u32[]{:S(2)}) collective-permute-start(f32[160,512]{1,0:T(8,128)S(1)} %collective-permute-done.19.refs_4_.refs_2_), channel_id=1, source_target_pairs={{8,0},{16,8},{24,16},{28,24},{20,28},{12,20},{4,12},{0,4},{9,1},{1... | collective-permute-start | bytes 983048 | tf_op jit(solution)/shard_map/ppermute | solution.py:394
  (41 other events, 753.7 us)

commit v12 on v8

--- a/solution.py
+++ b/solution.py
@@ -493,7 +493,7 @@
             full = gate(free, [steps[-1][0][0]])
             rest, steps = ring_pass([[full[0], free[0]], [free[1], full[1]]], ring)
             after = [steps[0][0][1], steps[0][1][0]]
-            near = [steps[i][0] + steps[i][1] for i in (0, -2)]
+            near = [steps[1][0] + steps[1][1], [steps[-2][0][0], steps[-2][1][1]]]
             top_spots, cut = spots[0], 2 * half - 2
             groups = [
                 (

time: 151 us -> 154 us (1.020)
  waiting for transfers between devices: 41.7 us -> 43.6 us
  starting transfers between devices: 68.8 us -> 70.6 us
    ppermute x28, waiting for transfers between devices: 36.1 us -> 38.2 us  [ring_pass(): going[k][way] = lax.ppermute(going[k][way], 'src', pairs)]
    ppermute x28, starting transfers between devices: 52.6 us -> 54.4 us  [ring_pass(): going[k][way] = lax.ppermute(going[k][way], 'src', pairs)]
    unnamed x56 -> x62, local copies, waits for them, and re-layouts: 3.67 us -> 3.93 us
  transfers between devices with their start and end apart: 34 -> 34, of which waited for: 23 -> 21; matrix products, arithmetic and copies ran while one was open for 4% -> 3% of each run, Pallas kernels for 10% -> 10%
where the time goes in v12:
time: 154 us; the launch traced here: 153 us
  starting transfers between devices  70.6 us (46%)
  waiting for transfers between devices  43.6 us (28%)
  Pallas kernels  28.9 us (19%)
  other arithmetic  5.34 us (3%)
  local copies, waits for them, and re-layouts  4 us (3%)
    ppermute x28, starting transfers between devices, ring_pass(): going[k][way] = lax.ppermute(going[k][way], 'src', pairs)  54.4 us
    ppermute x28, waiting for transfers between devices, ring_pass(): going[k][way] = lax.ppermute(going[k][way], 'src', pairs)  38.2 us
    pallas_call x2, Pallas kernels, update(): pl.pallas_call(functools.partial(update_kernel, pieces, rows, width, grou...  15.9 us
    pallas_call x1, Pallas kernels, solve_panels(): pl.pallas_call(functools.partial(solve_kernel, pieces, rows, width, chunk...  9.02 us
    ppermute x2, starting transfers between devices, local(): got = [lax.ppermute(sent, axes, swap) for sent in (sent_first, sent_second)]  8.88 us
    ppermute x2, waiting for transfers between devices, local(): got = [lax.ppermute(sent, axes, swap) for sent in (sent_first, sent_second)]  5.37 us
    ppermute x2, starting transfers between devices, spread_far(): found[r + stride] = lax.ppermute(found[r], 'row', [(r, r + stride)])  4.57 us
    pallas_call x1, Pallas kernels, prepare(): pl.pallas_call(functools.partial(prepare_kernel, rows, block, depth, cuts...  3.96 us
  transfers between devices with their start and end apart: 34, of which 21 were waited for; matrix products, arithmetic and copies ran while one was open for 3% of the time, Pallas kernels for 10%

profile of v12, /device:TPU:0, one launch (start us, length us, event | category | flops | bytes accessed | tf_op | source)
XLA Modules:
  0.0 152.9 jit_solution(11271698740524607730)
XLA Ops:
  1.2 7.0 %collective-permute-start = (f32[160,512]{1,0:T(8,128)S(1)}, f32[160,512]{1,0:T(8,128)S(1)}, u32[]{:S(2)}, u32[]{:S(2)}) collective-permute-start(f32[160,512]{1,0:T(8,128)S(1)} %slice_select_fusion.1), channel_id=1, source_target_pairs={{0,24},{24,0},{4,28},{28,4},{8,16},{16,8}} | collective-permute-start | bytes 983048 | tf_op jit(solution)/shard_map/ppermute | solution.py:471
  8.1 4.0 %shard_map.55 = (f32[160,512]{1,0:T(8,128)S(1)}, f32[160,512]{1,0:T(8,128)S(1)}, f32[160,512]{1,0:T(8,128)S(1)}) custom-call(s32[1]{0:T(128)} %bitcast.1.me, s32[1]{0:T(128)} %bitcast.place, f32[320,1024]{1,0:T(8,128)} %source.1), custom_call_target="tpu_custom_call" | custom-call | flops 1000 | bytes 1000 | tf_op jit(solution)/shard_map/pallas_call | solution.py:114
  17.4 3.3 %collective-permute-start.2 = (f32[160,512]{1,0:T(8,128)S(1)}, f32[160,512]{1,0:T(8,128)S(1)}, u32[]{:S(2)}, u32[]{:S(2)}) collective-permute-start(f32[160,512]{1,0:T(8,128)S(1)} %get-tuple-element.25.refs_0_), channel_id=1, source_target_pairs={{0,8},{8,16},{16,24},{24,28},{28,20},{20,12},{12,4},{4,0},{1,9},{9... | collective-permute-start | bytes 983048 | tf_op jit(solution)/shard_map/ppermute | solution.py:394
  20.6 3.2 %collective-permute-done.1 = f32[160,512]{1,0:T(8,128)S(1)} collective-permute-done((f32[160,512]{1,0:T(8,128)S(1)}, f32[160,512]{1,0:T(8,128)S(1)}, u32[]{:S(2)}, u32[]{:S(2)}) %collective-permute-start.1) | collective-permute-done | bytes 327712 | tf_op jit(solution)/shard_map/ppermute | solution.py:471
  24.0 4.1 %collective-permute-start.21 = (f32[160,512]{1,0:T(8,128)S(1)}, f32[160,512]{1,0:T(8,128)S(1)}, u32[]{:S(2)}, u32[]{:S(2)}) collective-permute-start(f32[160,512]{1,0:T(8,128)S(1)} %get-tuple-element.27.refs_8_.refs_14_), channel_id=1, source_target_pairs={{8,0},{16,8},{24,16},{28,24},{20,28},{12,20},{4,12},{0,4},{9,1},{1... | collective-permute-start | bytes 983048 | tf_op jit(solution)/shard_map/ppermute | solution.py:394
  30.2 5.6 %collective-permute-start.3 = (f32[160,512]{1,0:T(8,128)S(1)}, f32[160,512]{1,0:T(8,128)S(1)}, u32[]{:S(2)}, u32[]{:S(2)}) collective-permute-start(f32[160,512]{1,0:T(8,128)S(1)} %collective-permute-done.2.refs_1_), channel_id=1, source_target_pairs={{0,8},{8,16},{16,24},{24,28},{28,20},{20,12},{12,4},{4,0},{1,9},{9... | collective-permute-start | bytes 983048 | tf_op jit(solution)/shard_map/ppermute | solution.py:394
  38.1 4.7 %collective-permute-start.22 = (f32[160,512]{1,0:T(8,128)S(1)}, f32[160,512]{1,0:T(8,128)}, u32[]{:S(2)}, u32[]{:S(2)}) collective-permute-start(f32[160,512]{1,0:T(8,128)S(1)} %collective-permute-done.20.refs_9_.refs_15_), channel_id=1, source_target_pairs={{0,8},{8,16},{16,24},{24,28},{28,20},{20,12},{12,4},{4,0},{1,9},{9... | collective-permute-start | bytes 983048 | tf_op jit(solution)/shard_map/ppermute | solution.py:394
  45.0 4.8 %collective-permute-start.4 = (f32[160,512]{1,0:T(8,128)S(1)}, f32[160,512]{1,0:T(8,128)S(1)}, u32[]{:S(2)}, u32[]{:S(2)}) collective-permute-start(f32[160,512]{1,0:T(8,128)S(1)} %collective-permute-done.3.refs_3_), channel_id=1, source_target_pairs={{0,8},{8,16},{16,24},{24,28},{28,20},{20,12},{12,4},{4,0},{1,9},{9... | collective-permute-start | bytes 983048 | tf_op jit(solution)/shard_map/ppermute | solution.py:394
  51.9 5.0 %collective-permute-start.24 = (f32[160,512]{1,0:T(8,128)}, f32[160,512]{1,0:T(8,128)}, u32[]{:S(2)}, u32[]{:S(2)}) collective-permute-start(f32[160,512]{1,0:T(8,128)} %collective-permute-done.22.refs_11_.refs_17_), channel_id=1, source_target_pairs={{0,8},{8,16},{16,24},{24,28},{28,20},{20,12},{12,4},{4,0},{1,9},{9... | collective-permute-start | bytes 983048 | tf_op jit(solution)/shard_map/ppermute | solution.py:394
  58.9 5.0 %collective-permute-start.27 = (f32[160,512]{1,0:T(8,128)S(1)}, f32[160,512]{1,0:T(8,128)S(1)}, u32[]{:S(2)}, u32[]{:S(2)}) collective-permute-start(f32[160,512]{1,0:T(8,128)S(1)} %get-tuple-element.17.refs_1_), channel_id=1, source_target_pairs={{0,8},{8,16},{16,24},{24,28},{28,20},{20,12},{12,4},{4,0},{1,9},{9... | collective-permute-start | bytes 983048 | tf_op jit(solution)/shard_map/ppermute | solution.py:394
  64.4 3.4 %collective-permute-start.8 = (f32[160,512]{1,0:T(8,128)S(1)}, f32[160,512]{1,0:T(8,128)S(1)}, u32[]{:S(2)}, u32[]{:S(2)}) collective-permute-start(f32[160,512]{1,0:T(8,128)S(1)} %collective-permute-done.4.refs_2_.refs_5_), channel_id=1, source_target_pairs={{0,8},{8,16},{16,24},{24,28},{28,20},{20,12},{12,4},{4,0},{1,9},{9... | collective-permute-start | bytes 983048 | tf_op jit(solution)/shard_map/ppermute | solution.py:394
  68.0 2.3 %collective-permute-done.19.refs_6_ = f32[160,512]{1,0:T(8,128)S(1)} collective-permute-done((f32[160,512]{1,0:T(8,128)S(1)}, f32[160,512]{1,0:T(8,128)S(1)}, u32[]{:S(2)}, u32[]{:S(2)}) %collective-permute-start.19) | collective-permute-done | bytes 327712 | tf_op jit(solution)/shard_map/ppermute | solution.py:394
  70.3 3.5 %collective-permute-done.5.refs_17_.refs_10_ = f32[160,512]{1,0:T(8,128)S(1)} collective-permute-done((f32[160,512]{1,0:T(8,128)S(1)}, f32[160,512]{1,0:T(8,128)S(1)}, u32[]{:S(2)}, u32[]{:S(2)}) %collective-permute-start.5) | collective-permute-done | bytes 327712 | tf_op jit(solution)/shard_map/ppermute | solution.py:394
  73.8 3.5 %collective-permute-done.26.refs_15_.refs_21_ = f32[160,512]{1,0:T(8,128)S(1)} collective-permute-done((f32[160,512]{1,0:T(8,128)}, f32[160,512]{1,0:T(8,128)S(1)}, u32[]{:S(2)}, u32[]{:S(2)}) %collective-permute-start.26) | collective-permute-done | bytes 327712 | tf_op jit(solution)/shard_map/ppermute | solution.py:394
  78.2 9.0 %shard_map.58 = (f32[512,512]{1,0:T(8,128)}, f32[512,512]{1,0:T(8,128)}) custom-call(s32[8]{0:T(128)S(1)} %get-tuple-element.29.ids, s32[1]{0:T(128)} %bitcast.place, f32[160,512]{1,0:T(8,128)S(1)} %get-tuple-element.25.refs_0_, f32[160,512]{1,0:T(8,128)S(1)} %collective-permute-done.2.refs_1_, f32[160,512]{1,0:T(8,128)S(1)} %collective-permute-done.17.refs_2_, ...), custom_call_target="tpu_custom_call" | custom-call | flops 9663676416 | bytes 6291456 | tf_op jit(solution)/shard_map/pallas_call | solution.py:213
  92.8 2.5 %collective-permute-start.9 = (f32[160,512]{1,0:T(8,128)S(1)}, f32[160,512]{1,0:T(8,128)S(1)}, u32[]{:S(2)}, u32[]{:S(2)}) collective-permute-start(f32[160,512]{1,0:T(8,128)S(1)} %get-tuple-element.18.refs_8_), channel_id=1, source_target_pairs={{0,8},{8,16},{16,24},{24,28},{28,20},{20,12},{12,4},{4,0},{1,9},{9... | collective-permute-start | bytes 983048 | tf_op jit(solution)/shard_map/ppermute | solution.py:394
  95.3 6.7 %collective-permute-done.9.refs_9_ = f32[160,512]{1,0:T(8,128)S(1)} collective-permute-done((f32[160,512]{1,0:T(8,128)S(1)}, f32[160,512]{1,0:T(8,128)S(1)}, u32[]{:S(2)}, u32[]{:S(2)}) %collective-permute-start.9) | collective-permute-done | bytes 327712 | tf_op jit(solution)/shard_map/ppermute | solution.py:394
  104.6 6.5 %collective-permute-done.10.refs_1_.refs_11_ = f32[160,512]{1,0:T(8,128)S(1)} collective-permute-done((f32[160,512]{1,0:T(8,128)S(1)}, f32[160,512]{1,0:T(8,128)S(1)}, u32[]{:S(2)}, u32[]{:S(2)}) %collective-permute-start.10) | collective-permute-done | bytes 327712 | tf_op jit(solution)/shard_map/ppermute | solution.py:394
  111.1 3.3 %collective-permute-start.11 = (f32[160,512]{1,0:T(8,128)S(1)}, f32[160,512]{1,0:T(8,128)S(1)}, u32[]{:S(2)}, u32[]{:S(2)}) collective-permute-start(f32[160,512]{1,0:T(8,128)S(1)} %collective-permute-done.10.refs_1_.refs_11_), channel_id=1, source_target_pairs={{0,8},{8,16},{16,24},{24,28},{28,20},{20,12},{12,4},{4,0},{1,9},{9... | collective-permute-start | bytes 983048 | tf_op jit(solution)/shard_map/ppermute | solution.py:394
  114.5 2.5 %collective-permute-start.29 = (f32[160,512]{1,0:T(8,128)}, f32[160,512]{1,0:T(8,128)S(1)}, u32[]{:S(2)}, u32[]{:S(2)}) collective-permute-start(f32[160,512]{1,0:T(8,128)} %copy-done.25), channel_id=1, source_target_pairs={{0,8},{8,16},{16,24},{24,28},{28,20},{20,12},{12,4},{4,0},{1,9},{9... | collective-permute-start | bytes 983048 | tf_op jit(solution)/shard_map/ppermute | solution.py:394
  119.5 3.2 %collective-permute-done.15.refs_2_ = f32[160,512]{1,0:T(8,128)S(1)} collective-permute-done((f32[160,512]{1,0:T(8,128)S(1)}, f32[160,512]{1,0:T(8,128)S(1)}, u32[]{:S(2)}, u32[]{:S(2)}) %collective-permute-start.15) | collective-permute-done | bytes 327712 | tf_op jit(solution)/shard_map/ppermute | solution.py:394
  131.6 3.2 %collective-permute-done.33.refs_27_ = f32[160,512]{1,0:T(8,128)S(1)} collective-permute-done((f32[160,512]{1,0:T(8,128)S(1)}, f32[160,512]{1,0:T(8,128)S(1)}, u32[]{:S(2)}, u32[]{:S(2)}) %collective-permute-start.33) | collective-permute-done | bytes 327712 | tf_op jit(solution)/shard_map/ppermute | solution.py:394
  136.8 11.3 %shard_map.61.refs_9_ = f32[2560,512]{1,0:T(8,128)} custom-call(s32[14]{0:T(128)S(1)} %pad_add_fusion.ids, s32[1]{0:T(128)} %bitcast.place, f32[160,512]{1,0:T(8,128)S(1)} %get-tuple-element.25.refs_0_, f32[160,512]{1,0:T(8,128)S(1)} %collective-permute-done.2.refs_1_, f32[160,512]{1,0:T(8,128)S(1)} %collective-permute-done.17.refs_2_, ...), custom_call_target="tpu_custom_call" | custom-call | flops 7046430720 | bytes 18350080 | tf_op jit(solution)/shard_map/pallas_call | solution.py:339
  148.2 4.6 %shard_map.62 = f32[2560,512]{1,0:T(8,128)} custom-call(s32[2]{0:T(128)S(1)} %slice.17.ids, s32[1]{0:T(128)} %bitcast.place, f32[160,512]{1,0:T(8,128)S(1)} %collective-permute-done.7.refs_0_, f32[160,512]{1,0:T(8,128)S(1)} %collective-permute-done.12.refs_1_, f32[160,512]{1,0:T(8,128)S(1)} %collective-permute-done.15.refs_2_, ...), custom_call_target="tpu_custom_call", output_to_operand_aliasing={{}: (11, {})} | custom-call | flops 1006632960 | bytes 2621440 | tf_op jit(solution)/shard_map/pallas_call | solution.py:339
  (124 shorter events, 40.3 us)
Async XLA Ops:
  1.2 15.0 %collective-permute-start = (f32[160,512]{1,0:T(8,128)S(1)}, f32[160,512]{1,0:T(8,128)S(1)}, u32[]{:S(2)}, u32[]{:S(2)}) collective-permute-start(f32[160,512]{1,0:T(8,128)S(1)} %slice_select_fusion.1), channel_id=1, source_target_pairs={{0,24},{24,0},{4,28},{28,4},{8,16},{16,8}} | collective-permute-start | bytes 983048 | tf_op jit(solution)/shard_map/ppermute | solution.py:471
  12.1 11.8 %collective-permute-start.1 = (f32[160,512]{1,0:T(8,128)S(1)}, f32[160,512]{1,0:T(8,128)S(1)}, u32[]{:S(2)}, u32[]{:S(2)}) collective-permute-start(f32[160,512]{1,0:T(8,128)S(1)} %get-tuple-element.14), channel_id=1, source_target_pairs={{0,24},{24,0},{4,28},{28,4},{8,16},{16,8}} | collective-permute-start | bytes 983048 | tf_op jit(solution)/shard_map/ppermute | solution.py:471
  17.4 12.8 %collective-permute-start.2 = (f32[160,512]{1,0:T(8,128)S(1)}, f32[160,512]{1,0:T(8,128)S(1)}, u32[]{:S(2)}, u32[]{:S(2)}) collective-permute-start(f32[160,512]{1,0:T(8,128)S(1)} %get-tuple-element.25.refs_0_), channel_id=1, source_target_pairs={{0,8},{8,16},{16,24},{24,28},{28,20},{20,12},{12,4},{4,0},{1,9},{9... | collective-permute-start | bytes 983048 | tf_op jit(solution)/shard_map/ppermute | solution.py:394
  24.0 12.3 %collective-permute-start.21 = (f32[160,512]{1,0:T(8,128)S(1)}, f32[160,512]{1,0:T(8,128)S(1)}, u32[]{:S(2)}, u32[]{:S(2)}) collective-permute-start(f32[160,512]{1,0:T(8,128)S(1)} %get-tuple-element.27.refs_8_.refs_14_), channel_id=1, source_target_pairs={{8,0},{16,8},{24,16},{28,24},{20,28},{12,20},{4,12},{0,4},{9,1},{1... | collective-permute-start | bytes 983048 | tf_op jit(solution)/shard_map/ppermute | solution.py:394
  28.1 10.0 %collective-permute-start.20 = (f32[160,512]{1,0:T(8,128)S(1)}, f32[160,512]{1,0:T(8,128)S(1)}, u32[]{:S(2)}, u32[]{:S(2)}) collective-permute-start(f32[160,512]{1,0:T(8,128)S(1)} %get-tuple-element.27.refs_8_.refs_14_), channel_id=1, source_target_pairs={{0,8},{8,16},{16,24},{24,28},{28,20},{20,12},{12,4},{4,0},{1,9},{9... | collective-permute-start | bytes 983048 | tf_op jit(solution)/shard_map/ppermute | solution.py:394
  30.2 13.1 %collective-permute-start.17 = (f32[160,512]{1,0:T(8,128)S(1)}, f32[160,512]{1,0:T(8,128)S(1)}, u32[]{:S(2)}, u32[]{:S(2)}) collective-permute-start(f32[160,512]{1,0:T(8,128)S(1)} %get-tuple-element.25.refs_0_), channel_id=1, source_target_pairs={{8,0},{16,8},{24,16},{28,24},{20,28},{12,20},{4,12},{0,4},{9,1},{1... | collective-permute-start | bytes 983048 | tf_op jit(solution)/shard_map/ppermute | solution.py:394
  30.2 14.8 %collective-permute-start.3 = (f32[160,512]{1,0:T(8,128)S(1)}, f32[160,512]{1,0:T(8,128)S(1)}, u32[]{:S(2)}, u32[]{:S(2)}) collective-permute-start(f32[160,512]{1,0:T(8,128)S(1)} %collective-permute-done.2.refs_1_), channel_id=1, source_target_pairs={{0,8},{8,16},{16,24},{24,28},{28,20},{20,12},{12,4},{4,0},{1,9},{9... | collective-permute-start | bytes 983048 | tf_op jit(solution)/shard_map/ppermute | solution.py:394
  36.3 14.0 %collective-permute-start.23 = (f32[160,512]{1,0:T(8,128)S(1)}, f32[160,512]{1,0:T(8,128)S(1)}, u32[]{:S(2)}, u32[]{:S(2)}) collective-permute-start(f32[160,512]{1,0:T(8,128)S(1)} %collective-permute-done.21.refs_10_.refs_16_), channel_id=1, source_target_pairs={{8,0},{16,8},{24,16},{28,24},{20,28},{12,20},{4,12},{0,4},{9,1},{1... | collective-permute-start | bytes 983048 | tf_op jit(solution)/shard_map/ppermute | solution.py:394
  38.1 13.8 %collective-permute-start.22 = (f32[160,512]{1,0:T(8,128)S(1)}, f32[160,512]{1,0:T(8,128)}, u32[]{:S(2)}, u32[]{:S(2)}) collective-permute-start(f32[160,512]{1,0:T(8,128)S(1)} %collective-permute-done.20.refs_9_.refs_15_), channel_id=1, source_target_pairs={{0,8},{8,16},{16,24},{24,28},{28,20},{20,12},{12,4},{4,0},{1,9},{9... | collective-permute-start | bytes 983048 | tf_op jit(solution)/shard_map/ppermute | solution.py:394
  43.3 14.0 %collective-permute-start.18 = (f32[160,512]{1,0:T(8,128)S(1)}, f32[160,512]{1,0:T(8,128)S(1)}, u32[]{:S(2)}, u32[]{:S(2)}) collective-permute-start(f32[160,512]{1,0:T(8,128)S(1)} %collective-permute-done.17.refs_2_), channel_id=1, source_target_pairs={{8,0},{16,8},{24,16},{28,24},{20,28},{12,20},{4,12},{0,4},{9,1},{1... | collective-permute-start | bytes 983048 | tf_op jit(solution)/shard_map/ppermute | solution.py:394
  45.0 13.8 %collective-permute-start.4 = (f32[160,512]{1,0:T(8,128)S(1)}, f32[160,512]{1,0:T(8,128)S(1)}, u32[]{:S(2)}, u32[]{:S(2)}) collective-permute-start(f32[160,512]{1,0:T(8,128)S(1)} %collective-permute-done.3.refs_3_), channel_id=1, source_target_pairs={{0,8},{8,16},{16,24},{24,28},{28,20},{20,12},{12,4},{4,0},{1,9},{9... | collective-permute-start | bytes 983048 | tf_op jit(solution)/shard_map/ppermute | solution.py:394
  50.3 14.1 %collective-permute-start.25 = (f32[160,512]{1,0:T(8,128)S(1)}, f32[160,512]{1,0:T(8,128)}, u32[]{:S(2)}, u32[]{:S(2)}) collective-permute-start(f32[160,512]{1,0:T(8,128)S(1)} %collective-permute-done.23.refs_12_.refs_18_), channel_id=1, source_target_pairs={{8,0},{16,8},{24,16},{28,24},{20,28},{12,20},{4,12},{0,4},{9,1},{1... | collective-permute-start | bytes 983048 | tf_op jit(solution)/shard_map/ppermute | solution.py:394
  51.9 15.9 %collective-permute-start.24 = (f32[160,512]{1,0:T(8,128)}, f32[160,512]{1,0:T(8,128)}, u32[]{:S(2)}, u32[]{:S(2)}) collective-permute-start(f32[160,512]{1,0:T(8,128)} %collective-permute-done.22.refs_11_.refs_17_), channel_id=1, source_target_pairs={{0,8},{8,16},{16,24},{24,28},{28,20},{20,12},{12,4},{4,0},{1,9},{9... | collective-permute-start | bytes 983048 | tf_op jit(solution)/shard_map/ppermute | solution.py:394
  57.3 13.0 %collective-permute-start.19 = (f32[160,512]{1,0:T(8,128)S(1)}, f32[160,512]{1,0:T(8,128)S(1)}, u32[]{:S(2)}, u32[]{:S(2)}) collective-permute-start(f32[160,512]{1,0:T(8,128)S(1)} %collective-permute-done.18.refs_4_), channel_id=1, source_target_pairs={{8,0},{16,8},{24,16},{28,24},{20,28},{12,20},{4,12},{0,4},{9,1},{1... | collective-permute-start | bytes 983048 | tf_op jit(solution)/shard_map/ppermute | solution.py:394
  58.9 11.4 %collective-permute-start.27 = (f32[160,512]{1,0:T(8,128)S(1)}, f32[160,512]{1,0:T(8,128)S(1)}, u32[]{:S(2)}, u32[]{:S(2)}) collective-permute-start(f32[160,512]{1,0:T(8,128)S(1)} %get-tuple-element.17.refs_1_), channel_id=1, source_target_pairs={{0,8},{8,16},{16,24},{24,28},{28,20},{20,12},{12,4},{4,0},{1,9},{9... | collective-permute-start | bytes 983048 | tf_op jit(solution)/shard_map/ppermute | solution.py:394
  64.4 12.9 %collective-permute-start.8 = (f32[160,512]{1,0:T(8,128)S(1)}, f32[160,512]{1,0:T(8,128)S(1)}, u32[]{:S(2)}, u32[]{:S(2)}) collective-permute-start(f32[160,512]{1,0:T(8,128)S(1)} %collective-permute-done.4.refs_2_.refs_5_), channel_id=1, source_target_pairs={{0,8},{8,16},{16,24},{24,28},{28,20},{20,12},{12,4},{4,0},{1,9},{9... | collective-permute-start | bytes 983048 | tf_op jit(solution)/shard_map/ppermute | solution.py:394
  87.3 29.8 %collective-permute-start.31 = (f32[512,512]{1,0:T(8,128)}, f32[512,512]{1,0:T(8,128)}, u32[]{:S(2)}, u32[]{:S(2)}) collective-permute-start(f32[512,512]{1,0:T(8,128)} %get-tuple-element.22), channel_id=1, source_target_pairs={{0,2},{4,6},{8,10},{12,14},{16,18},{20,22},{24,26},{28,30}} | collective-permute-start | bytes 3145736 | tf_op jit(solution)/shard_map/ppermute | solution.py:405
  89.5 34.5 %collective-permute-start.28 = (f32[512,512]{1,0:T(8,128)}, f32[512,512]{1,0:T(8,128)}, u32[]{:S(2)}, u32[]{:S(2)}) collective-permute-start(f32[512,512]{1,0:T(8,128)} %get-tuple-element.21), channel_id=1, source_target_pairs={{0,2},{4,6},{8,10},{12,14},{16,18},{20,22},{24,26},{28,30}} | collective-permute-start | bytes 3145736 | tf_op jit(solution)/shard_map/ppermute | solution.py:405
  104.4 10.1 %collective-permute-start.14 = (f32[160,512]{1,0:T(8,128)S(1)}, f32[160,512]{1,0:T(8,128)S(1)}, u32[]{:S(2)}, u32[]{:S(2)}) collective-permute-start(f32[160,512]{1,0:T(8,128)S(1)} %collective-permute-done.13.refs_24_), channel_id=1, source_target_pairs={{8,0},{16,8},{24,16},{28,24},{20,28},{12,20},{4,12},{0,4},{9,1},{1... | collective-permute-start | bytes 983048 | tf_op jit(solution)/shard_map/ppermute | solution.py:394
  114.5 10.8 %collective-permute-start.29 = (f32[160,512]{1,0:T(8,128)}, f32[160,512]{1,0:T(8,128)S(1)}, u32[]{:S(2)}, u32[]{:S(2)}) collective-permute-start(f32[160,512]{1,0:T(8,128)} %copy-done.25), channel_id=1, source_target_pairs={{0,8},{8,16},{16,24},{24,28},{28,20},{20,12},{12,4},{4,0},{1,9},{9... | collective-permute-start | bytes 983048 | tf_op jit(solution)/shard_map/ppermute | solution.py:394
  122.7 12.0 %collective-permute-start.32 = (f32[512,512]{1,0:T(8,128)S(1)}, f32[512,512]{1,0:T(8,128)S(1)}, u32[]{:S(2)}, u32[]{:S(2)}) collective-permute-start(f32[512,512]{1,0:T(8,128)S(1)} %shard_map.60.refs_31_.refs_7_), channel_id=1, source_target_pairs={{0,1},{2,3},{4,5},{6,7},{8,9},{10,11},{12,13},{14,15},{16,17},{18,... | collective-permute-start | bytes 3145736 | tf_op jit(solution)/shard_map/ppermute | solution.py:416
  129.5 18.6 %collective-permute-start.7 = (f32[160,512]{1,0:T(8,128)S(1)}, f32[160,512]{1,0:T(8,128)S(1)}, u32[]{:S(2)}, u32[]{:S(2)}) collective-permute-start(f32[160,512]{1,0:T(8,128)S(1)} %collective-permute-done.6.refs_2_.refs_12_), channel_id=1, source_target_pairs={{8,0},{16,8},{24,16},{28,24},{20,28},{12,20},{4,12},{0,4},{9,1},{1... | collective-permute-start | bytes 983048 | tf_op jit(solution)/shard_map/ppermute | solution.py:394
  129.8 18.3 %collective-permute-start.12 = (f32[160,512]{1,0:T(8,128)S(1)}, f32[160,512]{1,0:T(8,128)S(1)}, u32[]{:S(2)}, u32[]{:S(2)}) collective-permute-start(f32[160,512]{1,0:T(8,128)S(1)} %collective-permute-done.11.refs_1_.refs_13_), channel_id=1, source_target_pairs={{0,8},{8,16},{16,24},{24,28},{28,20},{20,12},{12,4},{4,0},{1,9},{9... | collective-permute-start | bytes 983048 | tf_op jit(solution)/shard_map/ppermute | solution.py:394
  134.7 13.5 %collective-permute-start.16 = (f32[160,512]{1,0:T(8,128)S(1)}, f32[160,512]{1,0:T(8,128)S(1)}, u32[]{:S(2)}, u32[]{:S(2)}) collective-permute-start(f32[160,512]{1,0:T(8,128)S(1)} %collective-permute-done.15.refs_2_), channel_id=1, source_target_pairs={{8,0},{16,8},{24,16},{28,24},{20,28},{12,20},{4,12},{0,4},{9,1},{1... | collective-permute-start | bytes 983048 | tf_op jit(solution)/shard_map/ppermute | solution.py:394
  (41 other events, 675.9 us)
